TPU v7x, 32 devices: a whole 2x2x4 slice. The times are simulated.
32 devices in a mesh: member: 2 (over x), shard: 16 (over z, y, core).
Axes of the slice: x: 2, y: 2, z: 4, core: 2. Of those that a mesh axis runs over, the one named last changes fastest.
Arguments:
- tokens: bfloat16 [1024, 4096], P(('member', 'shard')), may hold values from -6 to 6
- key_weight: bfloat16 [4096, 16384], P(None, 'shard'), may hold values from -0.09375 to 0.09375
- value_weight: bfloat16 [16384, 4096], P('shard'), may hold values from -0.046875 to 0.046875
- shift_mix: bfloat16 [4096], replicated, may hold values from 0.049804688 to 0.94921875
- key_left: bfloat16 [16, 4096], P('member'), may hold values from -6 to 6
- key_right: bfloat16 [16, 16384], P('member', 'shard'), may hold values from -6 to 6
- value_left: bfloat16 [16, 16384], P('member', 'shard'), may hold values from -6 to 6
- value_right: bfloat16 [16, 4096], P('member'), may hold values from -6 to 6
- ranks: int32 [16], P('member'), may hold values from 0 to 15, each once
Outputs:
- mixed_out: bfloat16 [1024, 4096], P(('member', 'shard'))
- key_update: float32 [4096, 16384], P('member', 'shard')
- value_update: float32 [16384, 4096], P('shard', 'member')
Inputs may be any that keep to these rules, and one draw needn't show every extreme that they name: `ranks`: each value of 0 to 15 appears exactly once.
All inputs are finite; a program needn't handle non-finite values.
Results may differ from a plain program's by a relative error of at most 0.006.
Values may be sent and summed in bfloat16 or wider, within the bound.
No kernel may reach another device: no remote copies, remote signals or barrier semaphores. Data moves between devices by JAX's collectives and lax.ppermute only.
A program may use at most 128 MiB of HBM per device.

v0:
```python
import math

import jax
import jax.numpy as jnp
from jax import lax
from jax.sharding import PartitionSpec as P

D = 4096
FF = 16384
LEN = 64


def local(
    tokens, key_weight, value_weight, shift_mix, key_left, key_right, value_left, value_right, ranks
):
    group = lax.all_gather(tokens, "shard", axis=0, tiled=True)
    total_rows = group.shape[0]
    width = group.shape[1]
    memb = key_left.shape[0]
    place = lax.broadcasted_iota(jnp.int32, (total_rows, 1), 0)
    previous = jnp.concatenate([jnp.zeros((1, width), group.dtype), group[:-1]], 0)
    previous = jnp.where(place % LEN == 0, jnp.zeros_like(previous), previous)
    current = group.astype(jnp.float32)
    shifted = (
        current + (previous.astype(jnp.float32) - current) * shift_mix.astype(jnp.float32)
    ).astype(jnp.bfloat16)
    owner = place // LEN == lax.broadcasted_iota(jnp.int32, (1, memb), 1)
    select = owner.astype(jnp.float32)
    along = jnp.sum(jnp.dot(shifted, key_left.T, preferred_element_type=jnp.float32) * select, 1)
    right_rows = jnp.dot(owner.astype(jnp.bfloat16), key_right, preferred_element_type=jnp.float32)
    hidden = jnp.dot(shifted, key_weight, preferred_element_type=jnp.float32)
    hidden = hidden + 0.5 / math.sqrt(D) * along[:, None] * right_rows
    keyed = jnp.square(jnp.maximum(hidden, 0.0)).astype(jnp.bfloat16)
    dot_part = jnp.sum(jnp.dot(keyed, value_left.T, preferred_element_type=jnp.float32) * select, 1)
    partial_value = jnp.dot(keyed, value_weight, preferred_element_type=jnp.float32)
    count = total_rows // lax.axis_size("shard")
    dot_whole = lax.psum(dot_part, "shard")
    summed = lax.psum_scatter(partial_value, "shard", scatter_dimension=0, tiled=True)
    dot_mine = lax.dynamic_slice_in_dim(dot_whole, lax.axis_index("shard") * count, count)
    my_place = lax.axis_index("shard") * count + lax.broadcasted_iota(jnp.int32, (count, 1), 0)
    my_owner = (my_place // LEN == lax.broadcasted_iota(jnp.int32, (1, memb), 1)).astype(
        jnp.bfloat16
    )
    right_tokens = jnp.dot(my_owner, value_right, preferred_element_type=jnp.float32)
    mixed_out = (summed + 0.5 / math.sqrt(FF) * dot_mine[:, None] * right_tokens).astype(
        jnp.bfloat16
    )
    everyone = memb * lax.axis_size("member")
    fitness = ranks.astype(jnp.float32) / (everyone - 1) - 0.5
    factor = 2.0 / math.sqrt(everyone)
    weighted_left = fitness[:, None] * key_left.astype(jnp.float32)
    weighted_right = fitness[:, None] * value_right.astype(jnp.float32)
    key_block = jnp.dot(
        weighted_left.T, key_right.astype(jnp.float32), precision=lax.Precision.HIGHEST
    )
    value_block = jnp.dot(
        value_left.astype(jnp.float32).T, weighted_right, precision=lax.Precision.HIGHEST
    )
    key_update, value_update = (
        lax.psum_scatter(key_block, "member", scatter_dimension=0, tiled=True),
        lax.psum_scatter(value_block, "member", scatter_dimension=1, tiled=True),
    )
    return (mixed_out, key_update * factor, value_update * factor)


def solution(mesh):
    placed = (
        P(("member", "shard"), None),
        P(None, "shard"),
        P("shard", None),
        P(),
        P("member", None),
        P("member", "shard"),
        P("member", "shard"),
        P("member", None),
        P("member"),
    )
    return jax.shard_map(
        local,
        mesh=mesh,
        in_specs=placed,
        out_specs=(P(("member", "shard"), None), P("member", "shard"), P("shard", "member")),
        check_vma=False,
    )
```

profile of v0, /device:TPU:0, one launch (start us, length us, event | category | flops | bytes accessed | tf_op | source)
XLA Modules:
  0.0 584.7 jit_solution(8554288221559540847)
XLA Ops:
  7.2 0.0 copy-start
  7.2 0.0 all-gather.2.cloned.1.call-start
  7.2 0.7 all-gather.2.cloned.1.call-update
  7.9 0.0 reduce-scatter.4.cloned.1.call-start
  8.0 0.7 convert_element_type.34
  8.7 54.8 %all-gather.2.cloned.1.call-done = bf16[512,4096]{1,0:T(8,128)(2,1)} async-done(((bf16[32,4096]{1,0:T(8,128)(2,1)}), bf16[512,4096]{1,0:T(8,128)(2,1)}) %all-gather.2.cloned.1.call-update) | async-done | bytes 4194320 | tf_op jit(solution)/shard_map/all_gather | solution.py:16
  63.5 0.0 copy-start.4
  63.5 0.0 slice-start
  63.5 6.9 %fusion.1 = bf16[512,4096]{1,0:T(8,128)(2,1)S(1)} fusion(bf16[512,4096]{1,0:T(8,128)(2,1)} %all-gather.2.cloned.1.call-done, f32[4096]{0:T(1024)S(1)} %convert_element_type.34, bf16[511,4096]{1,0:T(8,128)(2,1)} %bitcast.15, pred[512]{0:T(512)(128)(4,1)S(1)} %fusion.15), kind=kLoop, calls=%fused_computation.4 | loop fusion | flops 14680064 | bytes 12591616 | tf_op jit(solution)/shard_map/convert_element_type | solution.py:26
  70.4 0.0 copy-done.4
  70.4 0.0 copy-start.1
  70.4 0.0 slice-start.1
  70.4 4.5 fusion.21
  74.9 0.0 copy-done.1
  74.9 1.2 fusion.4
  76.2 0.0 copy-done
  76.2 0.5 multiply_convert_fusion
  76.7 0.0 slice-done
  76.7 0.0 slice-done.1
  76.7 6.7 %fusion.22 = f32[512,4096]{1,0:T(8,128)} fusion(bf16[512,1024]{1,0:T(8,128)(2,1)S(1)} %multiply_convert_fusion, bf16[1024,4096]{1,0:T(8,128)(2,1)S(1)} %bitcast.17), kind=kOutput, calls=%fused_computation.45 | convolution fusion | flops 4294967296 | bytes 17825792 | tf_op jit(solution)/shard_map/dot_general | solution.py:35
  83.5 0.0 copy-start.5
  83.5 0.0 copy-start.2
  83.5 0.0 copy-start.3
  83.5 0.0 reduce-scatter.4.cloned.1.call-update
  83.5 0.2 reduce-scatter.8.cloned.1.call-start
  83.7 0.4 copy-done.5
  84.1 0.2 copy-done.2
  84.3 0.0 copy-done.3
  84.3 10.8 %convolution_bitcast_fusion = f32[1024,4096]{0,1:T(8,128)} fusion(bf16[8,1024]{1,0:T(8,128)(2,1)S(1)} %copy-done.3, bf16[8,4096]{1,0:T(8,128)(2,1)S(1)} %copy-done.2, f32[8]{0:T(128)S(1)} %multiply_add_fusion), kind=kOutput, calls=%fused_computation.2 | convolution fusion | flops 402718720 | bytes 16859168 | tf_op jit(solution)/shard_map/dot_general | solution.py:56
  95.2 0.0 reduce-scatter.8.cloned.1.call-update
  95.2 0.0 reduce-scatter.6.cloned.1.call-start
  95.2 10.4 %fusion.8 = f32[4096,1024]{1,0:T(8,128)} fusion(bf16[8,1024]{1,0:T(8,128)(2,1)S(1)} %copy-done, bf16[8,4096]{1,0:T(8,128)(2,1)S(1)} %copy-done.1, f32[8]{0:T(128)S(1)} %multiply_add_fusion), kind=kOutput, calls=%fused_computation.17 | convolution fusion | flops 402718720 | bytes 16859168 | tf_op jit(solution)/shard_map/dot_general | solution.py:53
  105.7 0.0 reduce-scatter.6.cloned.1.call-update
  105.7 0.4 fusion.5
  106.1 33.5 %psum.7 = f32[512]{0:T(512)S(1)} all-reduce(f32[512]{0:T(512)S(1)} %fusion.5), channel_id=1, replica_groups=mesh['member'=2,'shard'=16] {'shard'}, use_global_device_ids=true, to_apply=%region_3.4 | all-reduce | flops 512 | bytes 4096 | tf_op jit(solution)/shard_map/psum | solution.py:37
  139.6 0.1 dynamic-slice_multiply_fusion
  139.7 47.2 %reduce-scatter.4.cloned.1.call-done = f32[32,4096]{1,0:T(8,128)} async-done(((f32[512,4096]{1,0:T(8,128)}), f32[32,4096]{1,0:T(8,128)}) %reduce-scatter.4.cloned.1.call-update) | async-done | bytes 524304 | tf_op jit(solution)/shard_map/reduce_scatter | solution.py:38
  186.9 2.0 fusion.3
  188.9 189.2 %reduce-scatter.8.cloned.1.call-done = f32[1024,2048]{0,1:T(8,128)} async-done(((f32[1024,4096]{0,1:T(8,128)}), f32[1024,2048]{0,1:T(8,128)}) %reduce-scatter.8.cloned.1.call-update) | async-done | bytes 8388624 | tf_op jit(solution)/shard_map/reduce_scatter | solution.py:61
  378.1 8.8 %broadcast_multiply_fusion = f32[1024,2048]{0,1:T(8,128)} fusion(f32[1024,2048]{0,1:T(8,128)} %reduce-scatter.8.cloned.1.call-done), kind=kLoop, calls=%fused_computation.8 | loop fusion | flops 2097152 | bytes 16777216 | tf_op jit(solution)/shard_map/mul | solution.py:63
  386.9 9.1 %copy.12 = f32[1024,2048]{1,0:T(8,128)} copy(f32[1024,2048]{0,1:T(8,128)} %broadcast_multiply_fusion) | data formatting | bytes 16777216
  396.0 173.5 %reduce-scatter.6.cloned.1.call-done = f32[2048,1024]{1,0:T(8,128)} async-done(((f32[4096,1024]{1,0:T(8,128)}), f32[2048,1024]{1,0:T(8,128)}) %reduce-scatter.6.cloned.1.call-update) | async-done | bytes 8388624 | tf_op jit(solution)/shard_map/reduce_scatter | solution.py:60
  569.5 8.7 %broadcast_multiply_fusion.1 = f32[2048,1024]{1,0:T(8,128)} fusion(f32[2048,1024]{1,0:T(8,128)} %reduce-scatter.6.cloned.1.call-done), kind=kLoop, calls=%fused_computation.9 | loop fusion | flops 2097152 | bytes 16777216 | tf_op jit(solution)/shard_map/mul | solution.py:63
  (6 shorter events, 0.0 us)
Async XLA Ops:
  7.2 69.0 %copy-start = (bf16[8,1024]{1,0:T(8,128)(2,1)S(1)}, bf16[8,1024]{1,0:T(8,128)(2,1)}, u32[]{:S(2)}) copy-start(bf16[8,1024]{1,0:T(8,128)(2,1)} %param.14) | copy-start | bytes 49156
  7.2 56.3 %all-gather.2.cloned.1.call-start = ((), (), s32[]{:S(2)}) async-start(), calls=%async_computation.3 | async-start | bytes 4456448 | tf_op jit(solution)/shard_map/all_gather | solution.py:16
  7.9 179.0 %reduce-scatter.4.cloned.1.call-start = ((), (), s32[]{:S(2)}) async-start(), calls=%async_computation.4 | async-start | bytes 8912896 | tf_op jit(solution)/shard_map/reduce_scatter | solution.py:38
  63.5 6.9 %copy-start.4 = (bf16[4096,1024]{1,0:T(8,128)(2,1)S(1)}, bf16[4096,1024]{1,0:T(8,128)(2,1)}, u32[]{:S(2)}) copy-start(bf16[4096,1024]{1,0:T(8,128)(2,1)} %param.10) | copy-start | bytes 25165828
  63.5 13.2 %slice-start = ((s8[8388608]{0:T(1024)(128)(4,1)}), s8[4194304]{0:T(1024)(128)(4,1)S(1)}, s32[]{:S(2)}) async-start(s8[8388608]{0:T(1024)(128)(4,1)} %bitcast.16), calls=%async_computation.7 | async-start | bytes 8388608
  70.4 4.5 copy-start.1
  70.4 6.3 %slice-start.1 = ((s8[8388608]{0:T(1024)(128)(4,1)}), s8[4194304]{0:T(1024)(128)(4,1)S(1)}, s32[]{:S(2)}) async-start(s8[8388608]{0:T(1024)(128)(4,1)} %bitcast.16), calls=%async_computation.8 | async-start | bytes 8388608
  83.5 0.7 copy-start.5
  83.5 0.9 copy-start.2
  83.5 0.9 copy-start.3
  83.5 294.6 %reduce-scatter.8.cloned.1.call-start = ((), (), s32[]{:S(2)}) async-start(), calls=%async_computation.6 | async-start | bytes 25165824 | tf_op jit(solution)/shard_map/reduce_scatter | solution.py:61
  95.2 474.3 %reduce-scatter.6.cloned.1.call-start = ((), (), s32[]{:S(2)}) async-start(), calls=%async_computation.5 | async-start | bytes 25165824 | tf_op jit(solution)/shard_map/reduce_scatter | solution.py:60
Sparse Core Ops, SparseCore 0:
  10.2 53.2 all-gather.1
  83.6 103.2 reduce-scatter.3
  189.2 188.8 reduce-scatter.7
  380.4 189.0 reduce-scatter.5
where the time goes:
time: 585 us
  waiting for transfers between devices  465 us (79%)
  matrix products  36.6 us (6%)
  blocking collectives  33.5 us (6%)
  other arithmetic  25.2 us (4%)
  between operations  13.9 us (2%)
  local copies, waits for them, and re-layouts  9.77 us (2%)
    reduce_scatter x1, waiting for transfers between devices, local(): lax.psum_scatter(value_block, 'member', scatter_dimension=1, tiled=True)  189 us
    reduce_scatter x1, waiting for transfers between devices, local(): lax.psum_scatter(key_block, 'member', scatter_dimension=0, tiled=True)  173 us
    all_gather x1, waiting for transfers between devices, local(): group = lax.all_gather(tokens, 'shard', axis=0, tiled=True)  54.8 us
    reduce_scatter x1, waiting for transfers between devices, local(): lax.psum_scatter(partial_value, 'shard', scatter_dimension=0, tiled=True)  47.2 us
    psum x1, blocking collectives, local(): dot_whole = lax.psum(dot_part, 'shard')  33.5 us
    mul x2, other arithmetic, local(): return (mixed_out, key_update * factor, value_update * factor)  17.5 us
  transfers between devices with their start and end apart: 4, of which 4 were waited for; matrix products, arithmetic and copies ran while one was open for 7% of the time, Pallas kernels for 0%

commit v1 on v0

v1 whole, which is shorter than its diff:
```python
import functools
import math

import jax
import jax.numpy as jnp
from jax import lax
from jax.experimental import pallas as pl
from jax.experimental.pallas import tpu as pltpu
from jax.sharding import PartitionSpec as P

D = 4096
FF = 16384
LEN = 64
PLANES = 4
CORES = 2


def chunk_kernel(rows, columns, where, *refs):
    own, other = refs[:columns], refs[columns : 2 * columns]
    mix, key_left, key_right, value_left, value_right, key, value = refs[2 * columns : 2 * columns + 7]
    keep, send, whole, total, dots, natural, relative, across = refs[2 * columns + 7 :]
    step = pl.program_id(0)
    plane, y, core = where[0], where[1], where[2]
    depth, width = key.shape[0], value.shape[1]
    first = D // depth
    tokens = rows * columns * CORES

    def place(j, c):
        return pl.multiple_of(((y ^ j) * CORES + c) * rows, rows)

    def pick(array, member):
        at = lax.broadcasted_iota(jnp.int32, array.shape, 0) == member
        return jnp.sum(jnp.where(at, array.astype(jnp.float32), 0.0), 0, keepdims=True)

    def by_member(value_of):
        return [
            value_of(slice(m * LEN, (m + 1) * LEN), plane * (tokens // LEN) + m)
            for m in range(tokens // LEN)
        ]

    @pl.when(step == 0)
    def _():
        for j in range(columns):
            whole[pl.ds(place(j, core), rows), :] = own[j][...]
            whole[pl.ds(place(j, 1 - core), rows), :] = other[j][...]
        total[...] = jnp.zeros_like(total)
        dots[...] = jnp.zeros_like(dots)

    @pl.when(step < first)
    def _():
        at = pl.ds(pl.multiple_of(step * depth, depth), depth)
        current = whole[:, at].astype(jnp.float32)
        inside = lax.broadcasted_iota(jnp.int32, (tokens, 1), 0) % LEN != 0
        previous = jnp.where(inside, pltpu.roll(current, 1, 0), 0.0)
        shifted = (current + (previous - current) * mix[:, at].astype(jnp.float32)).astype(jnp.bfloat16)
        wide = shifted.astype(jnp.float32)
        left = key_left[:, at]
        products = jnp.concatenate(by_member(lambda at_rows, m: wide[at_rows] * pick(left, m)), 0)
        dots[...] += sum(products[:, i : i + 128] for i in range(0, depth, 128))
        total[...] += jnp.dot(shifted, key[...], preferred_element_type=jnp.float32)

    @pl.when(step == first - 1)
    def _():
        along = 0.5 / math.sqrt(D) * jnp.sum(dots[...], 1, keepdims=True)

        def finish(at_rows, m):
            hidden = total[at_rows, :] + along[at_rows] * pick(key_right[...], m)
            keyed = jnp.square(jnp.maximum(hidden, 0.0)).astype(jnp.bfloat16)
            natural[at_rows, :] = keyed
            sums = jnp.sum(keyed.astype(jnp.float32) * pick(value_left[...], m), 1, keepdims=True)
            dots[at_rows, :] = jnp.broadcast_to(0.5 / math.sqrt(FF) * sums, (LEN, 128))

        by_member(finish)
        for c in range(CORES):
            for j in range(columns):
                to = pl.ds((c * columns + j) * rows, rows)
                at_rows = pl.ds(place(j, core if c == 0 else 1 - core), rows)
                relative[to, :] = natural[at_rows, :]
                across[to, :] = dots[at_rows, :]

    @pl.when(step >= first)
    def _():
        result = jnp.dot(relative[...], value[...], preferred_element_type=jnp.float32)
        for c, out in enumerate((keep, send)):
            for j in range(columns):
                to = slice((c * columns + j) * rows, (c * columns + j + 1) * rows)
                m = plane * (tokens // LEN) + place(j, core if c == 0 else 1 - core) // LEN
                term = across[to, :1] * pick(value_right[...], m)
                out[j * rows : (j + 1) * rows, :] = (result[to] + term).astype(jnp.bfloat16)


def chunk(where, own, other, mix, key_left, key_right, value_left, value_right, key, value):
    columns, rows = len(own), own[0].shape[0]
    hidden = key.shape[1]
    memb = key_left.shape[0]
    depth = width = 1024
    first, second = D // depth, D // width
    tokens = rows * columns * CORES
    half = columns * rows

    def whole(shape):
        return pl.BlockSpec(shape, lambda i, _: (0, 0))

    return pl.pallas_call(
        functools.partial(chunk_kernel, rows, columns),
        out_shape=[jax.ShapeDtypeStruct((half, D), jnp.bfloat16)] * 2,
        grid_spec=pltpu.PrefetchScalarGridSpec(
            num_scalar_prefetch=1,
            grid=(first + second,),
            in_specs=[whole((rows, D))] * (2 * columns)
            + [whole((1, D)), whole((memb, D)), whole((memb, hidden)), whole((memb, hidden))]
            + [
                pl.BlockSpec((memb, width), lambda i, _: (0, jnp.maximum(i - first, 0))),
                pl.BlockSpec((depth, hidden), lambda i, _: (jnp.minimum(i, first - 1), 0)),
                pl.BlockSpec((hidden, width), lambda i, _: (0, jnp.maximum(i - first, 0))),
            ],
            out_specs=[pl.BlockSpec((half, width), lambda i, _: (0, jnp.maximum(i - first, 0)))] * 2,
            scratch_shapes=[
                pltpu.VMEM((tokens, D), jnp.bfloat16),
                pltpu.VMEM((tokens, hidden), jnp.float32),
                pltpu.VMEM((tokens, 128), jnp.float32),
                pltpu.VMEM((tokens, hidden), jnp.bfloat16),
                pltpu.VMEM((tokens, hidden), jnp.bfloat16),
                pltpu.VMEM((tokens, 128), jnp.float32),
            ],
        ),
        compiler_params=pltpu.CompilerParams(vmem_limit_bytes=32 * 1024 * 1024),
        cost_estimate=pl.CostEstimate(
            flops=4 * tokens * D * hidden, bytes_accessed=4 * D * hidden, transcendentals=0
        ),
    )(where, *own, *other, mix, key_left, key_right, value_left, value_right, key, value)


def updates(key_left, key_right, value_left, value_right, ranks):
    memb, hidden = key_right.shape
    marks = jnp.broadcast_to(ranks.astype(jnp.bfloat16)[:, None], (memb, 128))
    pack = jnp.concatenate([key_left, value_right, key_right, value_left, marks], 1)
    pack = lax.all_gather(pack, "member", axis=0, tiled=True)
    everyone = pack.shape[0]
    part = D // lax.axis_size("member")
    start = lax.axis_index("member") * part
    left = lax.dynamic_slice_in_dim(pack, start, part, 1)
    right = lax.dynamic_slice_in_dim(pack, D + start, part, 1)
    key_side, value_side = pack[:, 2 * D : 2 * D + hidden], pack[:, 2 * D + hidden : 2 * D + 2 * hidden]
    fitness = pack[:, -1:].astype(jnp.float32) / (everyone - 1) - 0.5
    weight = 2.0 / math.sqrt(everyone) * fitness

    def split(array):
        rest, terms = weight * array.astype(jnp.float32), []
        for _ in range(3):
            terms.append(lax.reduce_precision(rest, 8, 7).astype(jnp.bfloat16))
            rest = rest - terms[-1].astype(jnp.float32)
        return jnp.concatenate(terms, 0)

    def thrice(array):
        return jnp.concatenate([array] * 3, 0)

    def outer(a, b):
        return lax.dot_general(a, b, (((0,), (0,)), ((), ())), preferred_element_type=jnp.float32)

    return outer(split(left), thrice(key_side)), outer(thrice(value_side), split(right))


def local(
    tokens, key_weight, value_weight, shift_mix, key_left, key_right, value_left, value_right, ranks
):
    devices = lax.axis_size("shard")
    columns = devices // (PLANES * CORES)
    rows = tokens.shape[0]
    me = lax.axis_index("shard")
    z, y, core = me // (columns * CORES), me // CORES % columns, me % CORES

    def swap(array, bits):
        return lax.ppermute(array, "shard", [(i, i ^ bits) for i in range(devices)])

    key_update, value_update = updates(key_left, key_right, value_left, value_right, ranks)

    def plane_bits(k):
        return k * columns * CORES

    mix = shift_mix[None, :]
    arrived = [tokens] + [swap(tokens, plane_bits(k)) for k in range(1, PLANES)]
    partial = []
    for k in range(PLANES):
        own = [arrived[k]] + [swap(arrived[k], j * CORES) for j in range(1, columns)]
        other = [swap(block, 1) for block in own]
        where = jnp.stack([z ^ k, y, core]).astype(jnp.int32)
        partial.append(
            chunk(
                where, own, other, mix, key_left, key_right, value_left, value_right, key_weight, value_weight
            )
        )
    result = 0.0
    for k in reversed(range(PLANES)):
        keep, send = partial[k]
        both = keep.astype(jnp.float32) + swap(send, 1).astype(jnp.float32)
        mine = both[:rows]
        for j in range(1, columns):
            term = both[j * rows : (j + 1) * rows].astype(jnp.bfloat16)
            mine = mine + swap(term, j * CORES).astype(jnp.float32)
        if k:
            mine = swap(mine.astype(jnp.bfloat16), plane_bits(k)).astype(jnp.float32)
        result = result + mine
    return result.astype(jnp.bfloat16), key_update, value_update


def solution(mesh):
    placed = (
        P(("member", "shard"), None),
        P(None, "shard"),
        P("shard", None),
        P(),
        P("member", None),
        P("member", "shard"),
        P("member", "shard"),
        P("member", None),
        P("member"),
    )
    return jax.shard_map(
        local,
        mesh=mesh,
        in_specs=placed,
        out_specs=(P(("member", "shard"), None), P("member", "shard"), P("shard", "member")),
        check_vma=False,
    )
```

time: 585 us -> 122 us (0.21)
  waiting for transfers between devices: 465 us -> 31.9 us
  starting transfers between devices: 0.34 us -> 31.1 us
  matrix products: 36.6 us -> 9.35 us
  blocking collectives: 33.5 us -> 7.32 us
  Pallas kernels: 0 us -> 24.5 us
  other arithmetic: 25.2 us -> 2.76 us
  between operations: 13.9 us -> 0.88 us
    reduce_scatter x3 -> x0, waiting for transfers between devices: 410 us -> none  [the longest x1 189 us: local(): lax.psum_scatter(value_block, 'member', scatter_dimension=1, tiled=True)]
    all_gather x1 -> x0, waiting for transfers between devices: 54.8 us -> none  [local(): group = lax.all_gather(tokens, 'shard', axis=0, tiled=True)]
    psum x1 -> x0, blocking collectives: 33.5 us -> none  [local(): dot_whole = lax.psum(dot_part, 'shard')]
    ppermute x0 -> x26, waiting for transfers between devices: none -> 31.9 us  [swap(): return lax.ppermute(array, 'shard', [(i, i ^ bits) for i in range(devices)])]
    ppermute x0 -> x26, starting transfers between devices: none -> 31.1 us  [swap(): return lax.ppermute(array, 'shard', [(i, i ^ bits) for i in range(devices)])]
    dot_general x8 -> x2, matrix products: 36.6 us -> 9.35 us  [outer(): lax.dot_general(a, b, (((0,), (0,)), ((), ())), preferred_element_type=jn...]
    pallas_call x0 -> x4, Pallas kernels: none -> 24.5 us  [chunk(): pl.pallas_call(functools.partial(chunk_kernel, rows, columns), out_shape=...]
    mul x4 -> x1, other arithmetic: 17.5 us -> 0.18 us  [updates(): weight = 2.0 / math.sqrt(everyone) * fitness]
  transfers between devices with their start and end apart: 4 -> 26, of which waited for: 4 -> 8; matrix products, arithmetic and copies ran while one was open for 7% -> 12% of each run, Pallas kernels for 0% -> 20%
where the time goes in v1:
time: 122 us; the launch traced here: 121 us
  waiting for transfers between devices  31.9 us (26%)
  starting transfers between devices  31.1 us (25%)
  Pallas kernels  24.5 us (20%)
  local copies, waits for them, and re-layouts  13.5 us (11%)
  matrix products  9.35 us (8%)
  blocking collectives  7.32 us (6%)
  other arithmetic  2.76 us (2%)
    ppermute x26, waiting for transfers between devices, swap(): return lax.ppermute(array, 'shard', [(i, i ^ bits) for i in range(devices)])  31.9 us
    ppermute x26, starting transfers between devices, swap(): return lax.ppermute(array, 'shard', [(i, i ^ bits) for i in range(devices)])  31.1 us
    pallas_call x4, Pallas kernels, chunk(): pl.pallas_call(functools.partial(chunk_kernel, rows, columns), out_shape=...  24.5 us
    unnamed x24, local copies, waits for them, and re-layouts  13.3 us
    dot_general x2, matrix products, outer(): lax.dot_general(a, b, (((0,), (0,)), ((), ())), preferred_element_type=jn...  9.35 us
    all_gather x1, blocking collectives, updates(): pack = lax.all_gather(pack, 'member', axis=0, tiled=True)  7.32 us
  transfers between devices with their start and end apart: 26, of which 8 were waited for; matrix products, arithmetic and copies ran while one was open for 12% of the time, Pallas kernels for 20%

profile of v1, /device:TPU:0, one launch (start us, length us, event | category | flops | bytes accessed | tf_op | source)
XLA Modules:
  0.0 121.4 jit_solution(17037356787043434674)
XLA Ops:
  0.7 3.0 %collective-permute-start.21 = (bf16[32,4096]{1,0:T(8,128)(2,1)}, bf16[32,4096]{1,0:T(8,128)(2,1)S(1)}, u32[]{:S(2)}, u32[]{:S(2)}) collective-permute-start(bf16[32,4096]{1,0:T(8,128)(2,1)} %refs_0_.1), channel_id=1, source_target_pairs={{0,2},{1,3},{2,0},{3,1},{4,6},{5,7},{6,4},{7,5},{8,10},{9,11},{10,... | collective-permute-start | bytes 786440 | tf_op jit(solution)/shard_map/ppermute | solution.py:174
  3.7 1.6 %collective-permute-start.14 = (bf16[32,4096]{1,0:T(8,128)(2,1)}, bf16[32,4096]{1,0:T(8,128)(2,1)S(1)}, u32[]{:S(2)}, u32[]{:S(2)}) collective-permute-start(bf16[32,4096]{1,0:T(8,128)(2,1)} %refs_0_.1), channel_id=1, source_target_pairs={{0,4},{1,5},{2,6},{3,7},{4,0},{5,1},{6,2},{7,3},{8,12},{9,13},{10,... | collective-permute-start | bytes 786440 | tf_op jit(solution)/shard_map/ppermute | solution.py:174
  5.3 2.6 %collective-permute-start.7 = (bf16[32,4096]{1,0:T(8,128)(2,1)}, bf16[32,4096]{1,0:T(8,128)(2,1)S(1)}, u32[]{:S(2)}, u32[]{:S(2)}) collective-permute-start(bf16[32,4096]{1,0:T(8,128)(2,1)} %refs_0_.1), channel_id=1, source_target_pairs={{0,8},{1,9},{2,10},{3,11},{4,12},{5,13},{6,14},{7,15},{8,0},{9,1},... | collective-permute-start | bytes 786440 | tf_op jit(solution)/shard_map/ppermute | solution.py:174
  7.9 0.2 collective-permute-start
  8.1 0.7 convert_element_type.122
  8.8 0.8 constant_dynamic-update-slice_fusion.4
  9.6 0.8 constant_dynamic-update-slice_fusion.3
  10.5 0.7 constant_dynamic-update-slice_fusion.2
  11.2 0.7 constant_dynamic-update-slice_fusion.1
  12.0 7.3 %all_gather.3 = bf16[16,10368]{1,0:T(8,128)(2,1)S(1)} all-gather(bf16[8,10368]{1,0:T(8,128)(2,1)S(1)} %constant_dynamic-update-slice_fusion), channel_id=1, replica_groups=mesh['member'=2,'shard'=16] {'member'}, dimensions={0}, use_global_device_ids=true | all-gather | bytes 497664 | tf_op jit(solution)/shard_map/all_gather | solution.py:138
  19.3 0.2 multiply_reduce_fusion
  19.5 0.1 reduce-precision_convert_fusion.2
  19.6 4.7 %fusion.11 = f32[1024,2048]{1,0:T(8,128)} fusion(bf16[16,2048]{1,0:T(8,128)(2,1)S(1)} %get-tuple-element.23, bf16[16,2048]{1,0:T(8,128)(2,1)S(1)} %get-tuple-element.20, bf16[16,2048]{1,0:T(8,128)(2,1)S(1)} %get-tuple-element.19, bf16[16,1024]{1,0:T(8,128)(2,1)S(1)} %get-tuple-element.25), kind=kOutput, calls=%fused_computation.23 | convolution fusion | flops 202211328 | bytes 8617984 | tf_op jit(solution)/shard_map/dot_general | solution.py:159
  24.3 0.8 collective-permute-done.refs_0_
  25.1 0.5 collective-permute-start.1
  25.7 1.2 %collective-permute-done.7.refs_0_ = bf16[32,4096]{1,0:T(8,128)(2,1)S(1)} collective-permute-done((bf16[32,4096]{1,0:T(8,128)(2,1)}, bf16[32,4096]{1,0:T(8,128)(2,1)S(1)}, u32[]{:S(2)}, u32[]{:S(2)}) %collective-permute-start.7) | collective-permute-done | bytes 262176 | tf_op jit(solution)/shard_map/ppermute | solution.py:174
  26.9 0.5 collective-permute-start.8
  27.6 1.6 %collective-permute-start.15 = (bf16[32,4096]{1,0:T(8,128)(2,1)S(1)}, bf16[32,4096]{1,0:T(8,128)(2,1)S(1)}, u32[]{:S(2)}, u32[]{:S(2)}) collective-permute-start(bf16[32,4096]{1,0:T(8,128)(2,1)S(1)} %collective-permute-done.14.refs_0_), channel_id=1, source_target_pairs={{0,2},{1,3},{2,0},{3,1},{4,6},{5,7},{6,4},{7,5},{8,10},{9,11},{10,... | collective-permute-start | bytes 786440 | tf_op jit(solution)/shard_map/ppermute | solution.py:174
  29.2 5.1 %collective-permute-done.1.refs_1_ = bf16[32,4096]{1,0:T(8,128)(2,1)S(1)} collective-permute-done((bf16[32,4096]{1,0:T(8,128)(2,1)S(1)}, bf16[32,4096]{1,0:T(8,128)(2,1)S(1)}, u32[]{:S(2)}, u32[]{:S(2)}) %collective-permute-start.1) | collective-permute-done | bytes 262176 | tf_op jit(solution)/shard_map/ppermute | solution.py:174
  34.4 0.5 collective-permute-start.9
  34.9 5.0 %collective-permute-done.8.refs_1_ = bf16[32,4096]{1,0:T(8,128)(2,1)S(1)} collective-permute-done((bf16[32,4096]{1,0:T(8,128)(2,1)S(1)}, bf16[32,4096]{1,0:T(8,128)(2,1)S(1)}, u32[]{:S(2)}, u32[]{:S(2)}) %collective-permute-start.8) | collective-permute-done | bytes 262176 | tf_op jit(solution)/shard_map/ppermute | solution.py:174
  40.0 3.4 %copy-done = bf16[4096,1024]{1,0:T(8,128)(2,1)S(1)} copy-done((bf16[4096,1024]{1,0:T(8,128)(2,1)S(1)}, bf16[4096,1024]{1,0:T(8,128)(2,1)}, u32[]{:S(2)}) %copy-start) | copy-done | bytes 8388632
  43.4 3.4 %copy-done.2 = bf16[1024,4096]{1,0:T(8,128)(2,1)S(1)} copy-done((bf16[1024,4096]{1,0:T(8,128)(2,1)S(1)}, bf16[1024,4096]{1,0:T(8,128)(2,1)}, u32[]{:S(2)}) %copy-start.2) | copy-done | bytes 8388632
  46.7 6.1 %shard_map.115 = (bf16[64,4096]{1,0:T(8,128)(2,1)S(1)}, bf16[64,4096]{1,0:T(8,128)(2,1)S(1)}) custom-call(s32[3]{0:T(128)S(1)} %add_add_fusion.3.where, bf16[32,4096]{1,0:T(8,128)(2,1)S(1)} %copy-done.8, bf16[32,4096]{1,0:T(8,128)(2,1)S(1)} %collective-permute-done.21.refs_1_, bf16[32,4096]{1,0:T(8,128)(2,1)S(1)} %collective-permute-done.22.refs_2_, ...), custom_call_target="tpu_custom_call" | custom-call | flops 2147483648 | bytes 16777216 | tf_op jit(solution)/shard_map/pallas_call | solution.py:104
  52.9 0.6 collective-permute-start.16
  53.6 0.4 collective-permute-start.17
  54.0 3.4 %copy-done.3 = bf16[1024,4096]{1,0:T(8,128)(2,1)S(1)} copy-done((bf16[1024,4096]{1,0:T(8,128)(2,1)S(1)}, bf16[1024,4096]{1,0:T(8,128)(2,1)}, u32[]{:S(2)}) %copy-start.3) | copy-done | bytes 8388632
  57.4 6.2 %shard_map.112 = (bf16[64,4096]{1,0:T(8,128)(2,1)S(1)}, bf16[64,4096]{1,0:T(8,128)(2,1)S(1)}) custom-call(s32[3]{0:T(128)S(1)} %add_add_fusion.where, bf16[32,4096]{1,0:T(8,128)(2,1)S(1)} %collective-permute-done.refs_0_, bf16[32,4096]{1,0:T(8,128)(2,1)S(1)} %collective-permute-done.1.refs_1_, bf16[32,4096]{1,0:T(8,128)(2,1)S(1)} %collective-permute-done.2.refs_2_, ...), custom_call_target="tpu_custom_call" | custom-call | flops 2147483648 | bytes 16777216 | tf_op jit(solution)/shard_map/pallas_call | solution.py:104
  63.6 0.1 collective-permute-start.4
  63.7 6.1 %shard_map.113 = (bf16[64,4096]{1,0:T(8,128)(2,1)S(1)}, bf16[64,4096]{1,0:T(8,128)(2,1)S(1)}) custom-call(s32[3]{0:T(128)S(1)} %add_add_fusion.1.where, bf16[32,4096]{1,0:T(8,128)(2,1)S(1)} %collective-permute-done.7.refs_0_, bf16[32,4096]{1,0:T(8,128)(2,1)S(1)} %collective-permute-done.8.refs_1_, bf16[32,4096]{1,0:T(8,128)(2,1)S(1)} %collective-permute-done.9.refs_2_, ...), custom_call_target="tpu_custom_call" | custom-call | flops 2147483648 | bytes 16777216 | tf_op jit(solution)/shard_map/pallas_call | solution.py:104
  69.8 0.5 collective-permute-start.11
  70.3 6.1 %shard_map.114 = (bf16[64,4096]{1,0:T(8,128)(2,1)S(1)}, bf16[64,4096]{1,0:T(8,128)(2,1)S(1)}) custom-call(s32[3]{0:T(128)S(1)} %add_add_fusion.2.where, bf16[32,4096]{1,0:T(8,128)(2,1)S(1)} %collective-permute-done.14.refs_0_, bf16[32,4096]{1,0:T(8,128)(2,1)S(1)} %collective-permute-done.15.refs_1_, bf16[32,4096]{1,0:T(8,128)(2,1)S(1)} %collective-permute-done.16.refs_2_, ...), custom_call_target="tpu_custom_call" | custom-call | flops 2147483648 | bytes 16777216 | tf_op jit(solution)/shard_map/pallas_call | solution.py:104
  76.5 0.1 collective-permute-start.18
  76.6 0.1 convert_add_fusion
  76.8 0.5 collective-permute-start.25
  77.3 0.1 convert_add_fusion.3
  77.4 1.7 %collective-permute-start.5 = (bf16[32,4096]{1,0:T(8,128)(2,1)S(1)}, bf16[32,4096]{1,0:T(8,128)(2,1)S(1)}, u32[]{:S(2)}, u32[]{:S(2)}) collective-permute-start(bf16[32,4096]{1,0:T(8,128)(2,1)S(1)} %slice.81), channel_id=1, source_target_pairs={{0,2},{1,3},{2,0},{3,1},{4,6},{5,7},{6,4},{7,5},{8,10},{9,11},{10,... | collective-permute-start | bytes 786440 | tf_op jit(solution)/shard_map/ppermute | solution.py:174
  79.2 0.5 collective-permute-start.12
  79.9 1.7 %collective-permute-start.19 = (bf16[32,4096]{1,0:T(8,128)(2,1)S(1)}, bf16[32,4096]{1,0:T(8,128)(2,1)S(1)}, u32[]{:S(2)}, u32[]{:S(2)}) collective-permute-start(bf16[32,4096]{1,0:T(8,128)(2,1)S(1)} %slice.79), channel_id=1, source_target_pairs={{0,2},{1,3},{2,0},{3,1},{4,6},{5,7},{6,4},{7,5},{8,10},{9,11},{10,... | collective-permute-start | bytes 786440 | tf_op jit(solution)/shard_map/ppermute | solution.py:174
  81.5 10.0 %collective-permute-done.5 = bf16[32,4096]{1,0:T(8,128)(2,1)S(1)} collective-permute-done((bf16[32,4096]{1,0:T(8,128)(2,1)S(1)}, bf16[32,4096]{1,0:T(8,128)(2,1)S(1)}, u32[]{:S(2)}, u32[]{:S(2)}) %collective-permute-start.5) | collective-permute-done | bytes 262176 | tf_op jit(solution)/shard_map/ppermute | solution.py:174
  91.6 2.9 %collective-permute-start.6 = (bf16[32,4096]{1,0:T(8,128)(2,1)S(1)}, bf16[32,4096]{1,0:T(8,128)(2,1)S(1)}, u32[]{:S(2)}, u32[]{:S(2)}) collective-permute-start(bf16[32,4096]{1,0:T(8,128)(2,1)S(1)} %fusion.4), channel_id=1, source_target_pairs={{0,12},{1,13},{2,14},{3,15},{4,8},{5,9},{6,10},{7,11},{8,4},{9,5},... | collective-permute-start | bytes 786440 | tf_op jit(solution)/shard_map/ppermute | solution.py:174
  94.5 2.7 %collective-permute-done.12 = bf16[32,4096]{1,0:T(8,128)(2,1)S(1)} collective-permute-done((bf16[32,4096]{1,0:T(8,128)(2,1)S(1)}, bf16[32,4096]{1,0:T(8,128)(2,1)S(1)}, u32[]{:S(2)}, u32[]{:S(2)}) %collective-permute-start.12) | collective-permute-done | bytes 262176 | tf_op jit(solution)/shard_map/ppermute | solution.py:174
  97.2 7.3 %collective-permute-start.13 = (bf16[32,4096]{1,0:T(8,128)(2,1)S(1)}, bf16[32,4096]{1,0:T(8,128)(2,1)S(1)}, u32[]{:S(2)}, u32[]{:S(2)}) collective-permute-start(bf16[32,4096]{1,0:T(8,128)(2,1)S(1)} %fusion.3), channel_id=1, source_target_pairs={{0,8},{1,9},{2,10},{3,11},{4,12},{5,13},{6,14},{7,15},{8,0},{9,1},... | collective-permute-start | bytes 786440 | tf_op jit(solution)/shard_map/ppermute | solution.py:174
  104.7 4.1 %collective-permute-start.20 = (bf16[32,4096]{1,0:T(8,128)(2,1)S(1)}, bf16[32,4096]{1,0:T(8,128)(2,1)S(1)}, u32[]{:S(2)}, u32[]{:S(2)}) collective-permute-start(bf16[32,4096]{1,0:T(8,128)(2,1)S(1)} %fusion.2), channel_id=1, source_target_pairs={{0,4},{1,5},{2,6},{3,7},{4,0},{5,1},{6,2},{7,3},{8,12},{9,13},{10,... | collective-permute-start | bytes 786440 | tf_op jit(solution)/shard_map/ppermute | solution.py:174
  108.8 4.7 %fusion.5 = f32[2048,1024]{1,0:T(8,128)} fusion(bf16[16,2048]{1,0:T(8,128)(2,1)S(1)} %get-tuple-element.22, bf16[16,2048]{1,0:T(8,128)(2,1)S(1)} %get-tuple-element.21, bf16[16,2048]{1,0:T(8,128)(2,1)S(1)} %get-tuple-element.24, bf16[16,1024]{1,0:T(8,128)(2,1)S(1)} %get-tuple-element.26), kind=kOutput, calls=%fused_computation.17 | convolution fusion | flops 202211328 | bytes 8617984 | tf_op jit(solution)/shard_map/dot_general | solution.py:159
  113.5 4.4 %collective-permute-done.13 = bf16[32,4096]{1,0:T(8,128)(2,1)S(1)} collective-permute-done((bf16[32,4096]{1,0:T(8,128)(2,1)S(1)}, bf16[32,4096]{1,0:T(8,128)(2,1)S(1)}, u32[]{:S(2)}, u32[]{:S(2)}) %collective-permute-start.13) | collective-permute-done | bytes 262176 | tf_op jit(solution)/shard_map/ppermute | solution.py:174
  117.9 2.6 %collective-permute-done.20 = bf16[32,4096]{1,0:T(8,128)(2,1)S(1)} collective-permute-done((bf16[32,4096]{1,0:T(8,128)(2,1)S(1)}, bf16[32,4096]{1,0:T(8,128)(2,1)S(1)}, u32[]{:S(2)}, u32[]{:S(2)}) %collective-permute-start.20) | collective-permute-done | bytes 262176 | tf_op jit(solution)/shard_map/ppermute | solution.py:174
  120.5 0.9 fusion.1
  (57 shorter events, 1.2 us)
Async XLA Ops:
  0.6 39.3 %copy-start.8 = (bf16[32,4096]{1,0:T(8,128)(2,1)S(1)}, bf16[32,4096]{1,0:T(8,128)(2,1)}, u32[]{:S(2)}) copy-start(bf16[32,4096]{1,0:T(8,128)(2,1)} %refs_0_.1) | copy-start | bytes 786436
  0.6 39.3 %copy-start.4 = (bf16[8,4096]{1,0:T(8,128)(2,1)S(1)}, bf16[8,4096]{1,0:T(8,128)(2,1)}, u32[]{:S(2)}) copy-start(bf16[8,4096]{1,0:T(8,128)(2,1)} %refs_5_.7) | copy-start | bytes 196612
  0.7 39.3 %copy-start.5 = (bf16[8,4096]{1,0:T(8,128)(2,1)S(1)}, bf16[8,4096]{1,0:T(8,128)(2,1)}, u32[]{:S(2)}) copy-start(bf16[8,4096]{1,0:T(8,128)(2,1)} %refs_8_.7) | copy-start | bytes 196612
  0.7 39.3 %copy-start.6 = (bf16[8,1024]{1,0:T(8,128)(2,1)S(1)}, bf16[8,1024]{1,0:T(8,128)(2,1)}, u32[]{:S(2)}) copy-start(bf16[8,1024]{1,0:T(8,128)(2,1)} %refs_6_.7) | copy-start | bytes 49156
  0.7 39.3 %copy-start.7 = (bf16[8,1024]{1,0:T(8,128)(2,1)S(1)}, bf16[8,1024]{1,0:T(8,128)(2,1)}, u32[]{:S(2)}) copy-start(bf16[8,1024]{1,0:T(8,128)(2,1)} %refs_7_.7) | copy-start | bytes 49156
  0.7 26.8 %copy-start.9 = (bf16[4096]{0:T(1024)(128)(2,1)S(1)}, bf16[4096]{0:T(1024)(128)(2,1)}, u32[]{:S(2)}) copy-start(bf16[4096]{0:T(1024)(128)(2,1)} %param.12) | copy-start | bytes 24580
  0.7 25.0 %collective-permute-start.21 = (bf16[32,4096]{1,0:T(8,128)(2,1)}, bf16[32,4096]{1,0:T(8,128)(2,1)S(1)}, u32[]{:S(2)}, u32[]{:S(2)}) collective-permute-start(bf16[32,4096]{1,0:T(8,128)(2,1)} %refs_0_.1), channel_id=1, source_target_pairs={{0,2},{1,3},{2,0},{3,1},{4,6},{5,7},{6,4},{7,5},{8,10},{9,11},{10,... | collective-permute-start | bytes 786440 | tf_op jit(solution)/shard_map/ppermute | solution.py:174
  3.7 23.8 %collective-permute-start.14 = (bf16[32,4096]{1,0:T(8,128)(2,1)}, bf16[32,4096]{1,0:T(8,128)(2,1)S(1)}, u32[]{:S(2)}, u32[]{:S(2)}) collective-permute-start(bf16[32,4096]{1,0:T(8,128)(2,1)} %refs_0_.1), channel_id=1, source_target_pairs={{0,4},{1,5},{2,6},{3,7},{4,0},{5,1},{6,2},{7,3},{8,12},{9,13},{10,... | collective-permute-start | bytes 786440 | tf_op jit(solution)/shard_map/ppermute | solution.py:174
  5.3 21.6 %collective-permute-start.7 = (bf16[32,4096]{1,0:T(8,128)(2,1)}, bf16[32,4096]{1,0:T(8,128)(2,1)S(1)}, u32[]{:S(2)}, u32[]{:S(2)}) collective-permute-start(bf16[32,4096]{1,0:T(8,128)(2,1)} %refs_0_.1), channel_id=1, source_target_pairs={{0,8},{1,9},{2,10},{3,11},{4,12},{5,13},{6,14},{7,15},{8,0},{9,1},... | collective-permute-start | bytes 786440 | tf_op jit(solution)/shard_map/ppermute | solution.py:174
  7.9 17.2 %collective-permute-start = (bf16[32,4096]{1,0:T(8,128)(2,1)}, bf16[32,4096]{1,0:T(8,128)(2,1)S(1)}, u32[]{:S(2)}, u32[]{:S(2)}) collective-permute-start(bf16[32,4096]{1,0:T(8,128)(2,1)} %refs_0_.1), channel_id=1, source_target_pairs={{0,12},{1,13},{2,14},{3,15},{4,8},{5,9},{6,10},{7,11},{8,4},{9,5},... | collective-permute-start | bytes 786440 | tf_op jit(solution)/shard_map/ppermute | solution.py:174
  8.1 19.5 %collective-permute-start.22 = (bf16[32,4096]{1,0:T(8,128)(2,1)}, bf16[32,4096]{1,0:T(8,128)(2,1)S(1)}, u32[]{:S(2)}, u32[]{:S(2)}) collective-permute-start(bf16[32,4096]{1,0:T(8,128)(2,1)} %refs_0_.1), channel_id=1, source_target_pairs={{0,1},{1,0},{2,3},{3,2},{4,5},{5,4},{6,7},{7,6},{8,9},{9,8},{10,11... | collective-permute-start | bytes 786440 | tf_op jit(solution)/shard_map/ppermute | solution.py:174
  25.1 9.2 %collective-permute-start.1 = (bf16[32,4096]{1,0:T(8,128)(2,1)S(1)}, bf16[32,4096]{1,0:T(8,128)(2,1)S(1)}, u32[]{:S(2)}, u32[]{:S(2)}) collective-permute-start(bf16[32,4096]{1,0:T(8,128)(2,1)S(1)} %collective-permute-done.refs_0_), channel_id=1, source_target_pairs={{0,2},{1,3},{2,0},{3,1},{4,6},{5,7},{6,4},{7,5},{8,10},{9,11},{10,... | collective-permute-start | bytes 786440 | tf_op jit(solution)/shard_map/ppermute | solution.py:174
  25.7 8.7 %collective-permute-start.23 = (bf16[32,4096]{1,0:T(8,128)(2,1)S(1)}, bf16[32,4096]{1,0:T(8,128)(2,1)S(1)}, u32[]{:S(2)}, u32[]{:S(2)}) collective-permute-start(bf16[32,4096]{1,0:T(8,128)(2,1)S(1)} %collective-permute-done.21.refs_1_), channel_id=1, source_target_pairs={{0,1},{1,0},{2,3},{3,2},{4,5},{5,4},{6,7},{7,6},{8,9},{9,8},{10,11... | collective-permute-start | bytes 786440 | tf_op jit(solution)/shard_map/ppermute | solution.py:174
  26.9 13.0 %collective-permute-start.8 = (bf16[32,4096]{1,0:T(8,128)(2,1)S(1)}, bf16[32,4096]{1,0:T(8,128)(2,1)S(1)}, u32[]{:S(2)}, u32[]{:S(2)}) collective-permute-start(bf16[32,4096]{1,0:T(8,128)(2,1)S(1)} %collective-permute-done.7.refs_0_), channel_id=1, source_target_pairs={{0,2},{1,3},{2,0},{3,1},{4,6},{5,7},{6,4},{7,5},{8,10},{9,11},{10,... | collective-permute-start | bytes 786440 | tf_op jit(solution)/shard_map/ppermute | solution.py:174
  27.6 25.9 %collective-permute-start.2 = (bf16[32,4096]{1,0:T(8,128)(2,1)S(1)}, bf16[32,4096]{1,0:T(8,128)(2,1)S(1)}, u32[]{:S(2)}, u32[]{:S(2)}) collective-permute-start(bf16[32,4096]{1,0:T(8,128)(2,1)S(1)} %collective-permute-done.refs_0_), channel_id=1, source_target_pairs={{0,1},{1,0},{2,3},{3,2},{4,5},{5,4},{6,7},{7,6},{8,9},{9,8},{10,11... | collective-permute-start | bytes 786440 | tf_op jit(solution)/shard_map/ppermute | solution.py:174
  27.6 25.3 %collective-permute-start.15 = (bf16[32,4096]{1,0:T(8,128)(2,1)S(1)}, bf16[32,4096]{1,0:T(8,128)(2,1)S(1)}, u32[]{:S(2)}, u32[]{:S(2)}) collective-permute-start(bf16[32,4096]{1,0:T(8,128)(2,1)S(1)} %collective-permute-done.14.refs_0_), channel_id=1, source_target_pairs={{0,2},{1,3},{2,0},{3,1},{4,6},{5,7},{6,4},{7,5},{8,10},{9,11},{10,... | collective-permute-start | bytes 786440 | tf_op jit(solution)/shard_map/ppermute | solution.py:174
  34.3 19.3 %collective-permute-start.3 = (bf16[32,4096]{1,0:T(8,128)(2,1)S(1)}, bf16[32,4096]{1,0:T(8,128)(2,1)S(1)}, u32[]{:S(2)}, u32[]{:S(2)}) collective-permute-start(bf16[32,4096]{1,0:T(8,128)(2,1)S(1)} %collective-permute-done.1.refs_1_), channel_id=1, source_target_pairs={{0,1},{1,0},{2,3},{3,2},{4,5},{5,4},{6,7},{7,6},{8,9},{9,8},{10,11... | collective-permute-start | bytes 786440 | tf_op jit(solution)/shard_map/ppermute | solution.py:174
  34.4 29.1 %collective-permute-start.9 = (bf16[32,4096]{1,0:T(8,128)(2,1)S(1)}, bf16[32,4096]{1,0:T(8,128)(2,1)S(1)}, u32[]{:S(2)}, u32[]{:S(2)}) collective-permute-start(bf16[32,4096]{1,0:T(8,128)(2,1)S(1)} %collective-permute-done.7.refs_0_), channel_id=1, source_target_pairs={{0,1},{1,0},{2,3},{3,2},{4,5},{5,4},{6,7},{7,6},{8,9},{9,8},{10,11... | collective-permute-start | bytes 786440 | tf_op jit(solution)/shard_map/ppermute | solution.py:174
  39.9 23.8 %collective-permute-start.10 = (bf16[32,4096]{1,0:T(8,128)(2,1)S(1)}, bf16[32,4096]{1,0:T(8,128)(2,1)S(1)}, u32[]{:S(2)}, u32[]{:S(2)}) collective-permute-start(bf16[32,4096]{1,0:T(8,128)(2,1)S(1)} %collective-permute-done.8.refs_1_), channel_id=1, source_target_pairs={{0,1},{1,0},{2,3},{3,2},{4,5},{5,4},{6,7},{7,6},{8,9},{9,8},{10,11... | collective-permute-start | bytes 786440 | tf_op jit(solution)/shard_map/ppermute | solution.py:174
  40.0 3.4 %copy-start = (bf16[4096,1024]{1,0:T(8,128)(2,1)S(1)}, bf16[4096,1024]{1,0:T(8,128)(2,1)}, u32[]{:S(2)}) copy-start(bf16[4096,1024]{1,0:T(8,128)(2,1)} %refs_9_.7) | copy-start | bytes 25165828
  43.4 3.4 %copy-start.2 = (bf16[1024,4096]{1,0:T(8,128)(2,1)S(1)}, bf16[1024,4096]{1,0:T(8,128)(2,1)}, u32[]{:S(2)}) copy-start(bf16[1024,4096]{1,0:T(8,128)(2,1)} %refs_10_.7) | copy-start | bytes 25165828
  46.7 7.3 %copy-start.1 = (bf16[4096,1024]{1,0:T(8,128)(2,1)S(1)}, bf16[4096,1024]{1,0:T(8,128)(2,1)}, u32[]{:S(2)}) copy-start(bf16[4096,1024]{1,0:T(8,128)(2,1)} %refs_9_.7) | copy-start | bytes 25165828
  52.9 17.5 %collective-permute-start.16 = (bf16[32,4096]{1,0:T(8,128)(2,1)S(1)}, bf16[32,4096]{1,0:T(8,128)(2,1)S(1)}, u32[]{:S(2)}, u32[]{:S(2)}) collective-permute-start(bf16[32,4096]{1,0:T(8,128)(2,1)S(1)} %collective-permute-done.14.refs_0_), channel_id=1, source_target_pairs={{0,1},{1,0},{2,3},{3,2},{4,5},{5,4},{6,7},{7,6},{8,9},{9,8},{10,11... | collective-permute-start | bytes 786440 | tf_op jit(solution)/shard_map/ppermute | solution.py:174
  53.5 23.1 %collective-permute-start.24 = (bf16[64,4096]{1,0:T(8,128)(2,1)S(1)}, bf16[64,4096]{1,0:T(8,128)(2,1)S(1)}, u32[]{:S(2)}, u32[]{:S(2)}) collective-permute-start(bf16[64,4096]{1,0:T(8,128)(2,1)S(1)} %get-tuple-element.18), channel_id=1, source_target_pairs={{0,1},{1,0},{2,3},{3,2},{4,5},{5,4},{6,7},{7,6},{8,9},{9,8},{10,11... | collective-permute-start | bytes 1572872 | tf_op jit(solution)/shard_map/ppermute | solution.py:174
  53.6 16.8 %collective-permute-start.17 = (bf16[32,4096]{1,0:T(8,128)(2,1)S(1)}, bf16[32,4096]{1,0:T(8,128)(2,1)S(1)}, u32[]{:S(2)}, u32[]{:S(2)}) collective-permute-start(bf16[32,4096]{1,0:T(8,128)(2,1)S(1)} %collective-permute-done.15.refs_1_), channel_id=1, source_target_pairs={{0,1},{1,0},{2,3},{3,2},{4,5},{5,4},{6,7},{7,6},{8,9},{9,8},{10,11... | collective-permute-start | bytes 786440 | tf_op jit(solution)/shard_map/ppermute | solution.py:174
  54.0 3.4 %copy-start.3 = (bf16[1024,4096]{1,0:T(8,128)(2,1)S(1)}, bf16[1024,4096]{1,0:T(8,128)(2,1)}, u32[]{:S(2)}) copy-start(bf16[1024,4096]{1,0:T(8,128)(2,1)} %refs_10_.7) | copy-start | bytes 25165828
  63.6 13.7 %collective-permute-start.4 = (bf16[64,4096]{1,0:T(8,128)(2,1)S(1)}, bf16[64,4096]{1,0:T(8,128)(2,1)S(1)}, u32[]{:S(2)}, u32[]{:S(2)}) collective-permute-start(bf16[64,4096]{1,0:T(8,128)(2,1)S(1)} %get-tuple-element.12), channel_id=1, source_target_pairs={{0,1},{1,0},{2,3},{3,2},{4,5},{5,4},{6,7},{7,6},{8,9},{9,8},{10,11... | collective-permute-start | bytes 1572872 | tf_op jit(solution)/shard_map/ppermute | solution.py:174
  69.8 9.3 %collective-permute-start.11 = (bf16[64,4096]{1,0:T(8,128)(2,1)S(1)}, bf16[64,4096]{1,0:T(8,128)(2,1)S(1)}, u32[]{:S(2)}, u32[]{:S(2)}) collective-permute-start(bf16[64,4096]{1,0:T(8,128)(2,1)S(1)} %get-tuple-element.14), channel_id=1, source_target_pairs={{0,1},{1,0},{2,3},{3,2},{4,5},{5,4},{6,7},{7,6},{8,9},{9,8},{10,11... | collective-permute-start | bytes 1572872 | tf_op jit(solution)/shard_map/ppermute | solution.py:174
  76.5 3.2 %collective-permute-start.18 = (bf16[64,4096]{1,0:T(8,128)(2,1)S(1)}, bf16[64,4096]{1,0:T(8,128)(2,1)S(1)}, u32[]{:S(2)}, u32[]{:S(2)}) collective-permute-start(bf16[64,4096]{1,0:T(8,128)(2,1)S(1)} %get-tuple-element.16), channel_id=1, source_target_pairs={{0,1},{1,0},{2,3},{3,2},{4,5},{5,4},{6,7},{7,6},{8,9},{9,8},{10,11... | collective-permute-start | bytes 1572872 | tf_op jit(solution)/shard_map/ppermute | solution.py:174
  76.8 36.7 %collective-permute-start.25 = (bf16[32,4096]{1,0:T(8,128)(2,1)S(1)}, bf16[32,4096]{1,0:T(8,128)(2,1)S(1)}, u32[]{:S(2)}, u32[]{:S(2)}) collective-permute-start(bf16[32,4096]{1,0:T(8,128)(2,1)S(1)} %slice.78), channel_id=1, source_target_pairs={{0,2},{1,3},{2,0},{3,1},{4,6},{5,7},{6,4},{7,5},{8,10},{9,11},{10,... | collective-permute-start | bytes 786440 | tf_op jit(solution)/shard_map/ppermute | solution.py:174
  77.4 14.1 %collective-permute-start.5 = (bf16[32,4096]{1,0:T(8,128)(2,1)S(1)}, bf16[32,4096]{1,0:T(8,128)(2,1)S(1)}, u32[]{:S(2)}, u32[]{:S(2)}) collective-permute-start(bf16[32,4096]{1,0:T(8,128)(2,1)S(1)} %slice.81), channel_id=1, source_target_pairs={{0,2},{1,3},{2,0},{3,1},{4,6},{5,7},{6,4},{7,5},{8,10},{9,11},{10,... | collective-permute-start | bytes 786440 | tf_op jit(solution)/shard_map/ppermute | solution.py:174
  79.2 17.9 %collective-permute-start.12 = (bf16[32,4096]{1,0:T(8,128)(2,1)S(1)}, bf16[32,4096]{1,0:T(8,128)(2,1)S(1)}, u32[]{:S(2)}, u32[]{:S(2)}) collective-permute-start(bf16[32,4096]{1,0:T(8,128)(2,1)S(1)} %slice.80), channel_id=1, source_target_pairs={{0,2},{1,3},{2,0},{3,1},{4,6},{5,7},{6,4},{7,5},{8,10},{9,11},{10,... | collective-permute-start | bytes 786440 | tf_op jit(solution)/shard_map/ppermute | solution.py:174
  79.9 24.7 %collective-permute-start.19 = (bf16[32,4096]{1,0:T(8,128)(2,1)S(1)}, bf16[32,4096]{1,0:T(8,128)(2,1)S(1)}, u32[]{:S(2)}, u32[]{:S(2)}) collective-permute-start(bf16[32,4096]{1,0:T(8,128)(2,1)S(1)} %slice.79), channel_id=1, source_target_pairs={{0,2},{1,3},{2,0},{3,1},{4,6},{5,7},{6,4},{7,5},{8,10},{9,11},{10,... | collective-permute-start | bytes 786440 | tf_op jit(solution)/shard_map/ppermute | solution.py:174
  91.6 21.8 %collective-permute-start.6 = (bf16[32,4096]{1,0:T(8,128)(2,1)S(1)}, bf16[32,4096]{1,0:T(8,128)(2,1)S(1)}, u32[]{:S(2)}, u32[]{:S(2)}) collective-permute-start(bf16[32,4096]{1,0:T(8,128)(2,1)S(1)} %fusion.4), channel_id=1, source_target_pairs={{0,12},{1,13},{2,14},{3,15},{4,8},{5,9},{6,10},{7,11},{8,4},{9,5},... | collective-permute-start | bytes 786440 | tf_op jit(solution)/shard_map/ppermute | solution.py:174
  97.2 20.6 %collective-permute-start.13 = (bf16[32,4096]{1,0:T(8,128)(2,1)S(1)}, bf16[32,4096]{1,0:T(8,128)(2,1)S(1)}, u32[]{:S(2)}, u32[]{:S(2)}) collective-permute-start(bf16[32,4096]{1,0:T(8,128)(2,1)S(1)} %fusion.3), channel_id=1, source_target_pairs={{0,8},{1,9},{2,10},{3,11},{4,12},{5,13},{6,14},{7,15},{8,0},{9,1},... | collective-permute-start | bytes 786440 | tf_op jit(solution)/shard_map/ppermute | solution.py:174
  104.7 15.9 %collective-permute-start.20 = (bf16[32,4096]{1,0:T(8,128)(2,1)S(1)}, bf16[32,4096]{1,0:T(8,128)(2,1)S(1)}, u32[]{:S(2)}, u32[]{:S(2)}) collective-permute-start(bf16[32,4096]{1,0:T(8,128)(2,1)S(1)} %fusion.2), channel_id=1, source_target_pairs={{0,4},{1,5},{2,6},{3,7},{4,0},{5,1},{6,2},{7,3},{8,12},{9,13},{10,... | collective-permute-start | bytes 786440 | tf_op jit(solution)/shard_map/ppermute | solution.py:174

commit v2 on v0

v2 whole, which is shorter than its diff:
```python
import functools
import math

import jax
import jax.numpy as jnp
from jax import lax
from jax.experimental import pallas as pl
from jax.experimental.pallas import tpu as pltpu
from jax.sharding import PartitionSpec as P

D = 4096
FF = 16384
LEN = 64
PLANES = 4
CORES = 2
STEP = 1024


def chunk_kernel(rows, columns, where, *refs):
    own, other = refs[:columns], refs[columns : 2 * columns]
    mix, key_left, key_right, value_left, value_right, key, value = refs[2 * columns : 2 * columns + 7]
    keep, send, whole, natural, relative, natural_dots, dots = refs[2 * columns + 7 :]
    plane, y, core = where[0], where[1], where[2]
    tokens = rows * columns * CORES
    members = tokens // LEN

    def place(j, c):
        return pl.multiple_of(((y ^ j) * CORES + c) * rows, rows)

    def pick(array, member):
        at = lax.broadcasted_iota(jnp.int32, array.shape, 0) == member
        return jnp.sum(jnp.where(at, array.astype(jnp.float32), 0.0), 0, keepdims=True)

    for j in range(columns):
        whole[pl.ds(place(j, core), rows), :] = own[j][...]
        whole[pl.ds(place(j, 1 - core), rows), :] = other[j][...]

    inside = lax.broadcasted_iota(jnp.int32, (tokens, 1), 0) % LEN != 0
    total, along = None, [0.0] * members
    for start in range(0, D, STEP):
        at = slice(start, start + STEP)
        current = whole[:, at].astype(jnp.float32)
        previous = jnp.where(inside, pltpu.roll(current, 1, 0), 0.0)
        shifted = (current + (previous - current) * mix[:, at].astype(jnp.float32)).astype(jnp.bfloat16)
        part = jnp.dot(shifted, key[at, :], preferred_element_type=jnp.float32)
        total = part if total is None else total + part
        for m in range(members):
            wide = shifted[m * LEN : (m + 1) * LEN].astype(jnp.float32)
            products = wide * pick(key_left[:, at], plane * members + m)
            along[m] = along[m] + sum(products[:, i : i + 128] for i in range(0, STEP, 128))

    for m in range(members):
        at = slice(m * LEN, (m + 1) * LEN)
        dot = 0.5 / math.sqrt(D) * jnp.sum(along[m], 1, keepdims=True)
        hidden = total[at] + dot * pick(key_right[...], plane * members + m)
        keyed = jnp.square(jnp.maximum(hidden, 0.0)).astype(jnp.bfloat16)
        natural[at, :] = keyed
        dot = jnp.sum(keyed.astype(jnp.float32) * pick(value_left[...], plane * members + m), 1, keepdims=True)
        natural_dots[at, :] = jnp.broadcast_to(0.5 / math.sqrt(FF) * dot, (LEN, 128))

    cores = (core, 1 - core)
    for c in range(CORES):
        for j in range(columns):
            to = slice((c * columns + j) * rows, (c * columns + j + 1) * rows)
            relative[to, :] = natural[pl.ds(place(j, cores[c]), rows), :]
            dots[to, :] = natural_dots[pl.ds(place(j, cores[c]), rows), :]

    for start in range(0, D, STEP):
        at = slice(start, start + STEP)
        result = jnp.dot(relative[...], value[:, at], preferred_element_type=jnp.float32)
        for c, out in enumerate((keep, send)):
            for j in range(columns):
                to = slice((c * columns + j) * rows, (c * columns + j + 1) * rows)
                right = pick(value_right[:, at], plane * members + place(j, cores[c]) // LEN)
                out[j * rows : (j + 1) * rows, at] = (result[to] + dots[to, :1] * right).astype(jnp.bfloat16)


def chunk(where, own, other, mix, key_left, key_right, value_left, value_right, key, value):
    columns, rows = len(own), own[0].shape[0]
    hidden = key.shape[1]
    tokens = rows * columns * CORES
    operands = (*own, *other, mix, key_left, key_right, value_left, value_right, key, value)
    return pl.pallas_call(
        functools.partial(chunk_kernel, rows, columns),
        out_shape=[jax.ShapeDtypeStruct((columns * rows, D), jnp.bfloat16)] * 2,
        in_specs=[pl.BlockSpec(memory_space=pltpu.SMEM)]
        + [pl.BlockSpec(memory_space=pltpu.VMEM)] * len(operands),
        out_specs=[pl.BlockSpec(memory_space=pltpu.VMEM)] * 2,
        scratch_shapes=[
            pltpu.VMEM((tokens, D), jnp.bfloat16),
            pltpu.VMEM((tokens, hidden), jnp.bfloat16),
            pltpu.VMEM((tokens, hidden), jnp.bfloat16),
            pltpu.VMEM((tokens, 128), jnp.float32),
            pltpu.VMEM((tokens, 128), jnp.float32),
        ],
        compiler_params=pltpu.CompilerParams(vmem_limit_bytes=28 * 1024 * 1024),
        cost_estimate=pl.CostEstimate(
            flops=4 * tokens * D * hidden, bytes_accessed=4 * D * hidden, transcendentals=0
        ),
    )(where, *operands)


def pack_members(key_left, key_right, value_left, value_right, ranks):
    marks = jnp.broadcast_to(ranks.astype(jnp.bfloat16)[:, None], (ranks.shape[0], 128))
    return jnp.concatenate([key_left, value_right, key_right, value_left, marks], 1)


def member_sides(packs, hidden):
    pack = jnp.concatenate(packs, 0)
    everyone = pack.shape[0]
    part = D // lax.axis_size("member")
    start = lax.axis_index("member") * part
    left = lax.dynamic_slice_in_dim(pack, start, part, 1)
    right = lax.dynamic_slice_in_dim(pack, D + start, part, 1)
    key_side, value_side = pack[:, 2 * D : 2 * D + hidden], pack[:, 2 * D + hidden : 2 * D + 2 * hidden]
    fitness = pack[:, -1:].astype(jnp.float32) / (everyone - 1) - 0.5
    weight = 2.0 / math.sqrt(everyone) * fitness

    def split(array):
        rest, terms = weight * array.astype(jnp.float32), []
        for _ in range(3):
            terms.append(lax.reduce_precision(rest, 8, 7).astype(jnp.bfloat16))
            rest = rest - terms[-1].astype(jnp.float32)
        return jnp.concatenate(terms, 0)

    def thrice(array):
        return jnp.concatenate([array] * 3, 0)

    return (split(left), thrice(key_side)), (thrice(value_side), split(right))


def outer(sides):
    return lax.dot_general(*sides, (((0,), (0,)), ((), ())), preferred_element_type=jnp.float32)


def after(array, *others):
    return lax.optimization_barrier((array, *others))[0]


def local(
    tokens, key_weight, value_weight, shift_mix, key_left, key_right, value_left, value_right, ranks
):
    devices, groups = lax.axis_size("shard"), lax.axis_size("member")
    columns = devices // (PLANES * CORES)
    rows, hidden = tokens.shape[0], key_weight.shape[1]
    me = lax.axis_index("shard")
    z, y, core = me // (columns * CORES), me // CORES % columns, me % CORES
    mix = shift_mix[None, :]

    def swap(array, bits):
        return lax.ppermute(array, "shard", [(i, i ^ bits) for i in range(devices)])

    def over_z(array, k):
        return swap(array, k * columns * CORES)

    def over_y(array, j):
        return swap(array, j * CORES)

    def over_cores(array):
        return swap(array, 1)

    def partial(k, own, other):
        where = jnp.stack([z ^ k, y, core]).astype(jnp.int32)
        return chunk(
            where, own, other, mix, key_left, key_right, value_left, value_right, key_weight, value_weight
        )

    def spread(block):
        own = [block] + [over_y(block, j) for j in range(1, columns)]
        return own, [over_cores(part) for part in own]

    pack = pack_members(key_left, key_right, value_left, value_right, ranks)
    packs = [pack] + [
        lax.ppermute(pack, "member", [(i, i ^ bits) for i in range(groups)]) for bits in range(1, groups)
    ]
    key_sides, value_sides = member_sides(packs, hidden)

    arrived = [tokens, over_z(tokens, 1), over_z(tokens, 2), None]
    own0, other0 = spread(tokens)
    own1, other1 = spread(arrived[1])
    own0[0] = after(own0[0], arrived[1])
    keep0, send0 = partial(0, own0, other0)

    arrived[2] = after(arrived[2], keep0)
    arrived[3] = over_z(arrived[2], 1)
    own2, other2 = spread(arrived[2])
    key_update = outer((after(key_sides[0], keep0, arrived[2]), key_sides[1]))
    own1[0] = after(own1[0], key_update)
    keep1, send1 = partial(1, own1, other1)

    arrived[3] = after(arrived[3], keep1)
    own3, other3 = spread(arrived[3])
    own2[0] = after(own2[0], arrived[3], keep1)
    keep2, send2 = partial(2, own2, other2)

    def both_cores(keep, send):
        both = keep.astype(jnp.float32) + over_cores(send).astype(jnp.float32)
        return both[:rows], [
            both[j * rows : (j + 1) * rows].astype(jnp.bfloat16) for j in range(1, columns)
        ]

    def both_columns(mine, terms):
        for j, term in enumerate(terms, 1):
            mine = mine + over_y(term, j).astype(jnp.float32)
        return mine

    mine2, terms2 = both_cores(keep2, send2)
    own3[0] = after(own3[0], *terms2)
    keep3, send3 = partial(3, own3, other3)
    mine3, terms3 = both_cores(keep3, send3)
    send1 = after(send1, *terms3)
    send0 = after(send0, *terms3)
    value_update = outer((after(value_sides[0], *terms3), value_sides[1]))
    mine1, terms1 = both_cores(keep1, send1)
    mine0, terms0 = both_cores(keep0, send0)

    sum3 = over_z(both_columns(mine3, terms3).astype(jnp.bfloat16), 1)
    sum2 = both_columns(mine2, terms2) + sum3.astype(jnp.float32)
    sum2 = over_z(sum2.astype(jnp.bfloat16), 2)
    sum1 = over_z(both_columns(mine1, terms1).astype(jnp.bfloat16), 1)
    sum0 = both_columns(mine0, terms0)
    result = sum0 + sum1.astype(jnp.float32) + sum2.astype(jnp.float32)
    return result.astype(jnp.bfloat16), key_update, value_update


def solution(mesh):
    placed = (
        P(("member", "shard"), None),
        P(None, "shard"),
        P("shard", None),
        P(),
        P("member", None),
        P("member", "shard"),
        P("member", "shard"),
        P("member", None),
        P("member"),
    )
    return jax.shard_map(
        local,
        mesh=mesh,
        in_specs=placed,
        out_specs=(P(("member", "shard"), None), P("member", "shard"), P("shard", "member")),
        check_vma=False,
    )
```

time: 585 us -> 116 us (0.20)
  waiting for transfers between devices: 465 us -> 41.2 us
  blocking collectives: 33.5 us -> 0 us
  matrix products: 36.6 us -> 9.35 us
  other arithmetic: 25.2 us -> 4.69 us
  starting transfers between devices: 0.34 us -> 19.9 us
  Pallas kernels: 0 us -> 16 us
  local copies, waits for them, and re-layouts: 9.77 us -> 22.9 us
  between operations: 13.9 us -> 0.99 us
    reduce_scatter x3 -> x0, waiting for transfers between devices: 410 us -> none  [the longest x1 189 us: local(): lax.psum_scatter(value_block, 'member', scatter_dimension=1, tiled=True)]
    all_gather x1 -> x0, waiting for transfers between devices: 54.8 us -> none  [local(): group = lax.all_gather(tokens, 'shard', axis=0, tiled=True)]
    ppermute x0 -> x27, waiting for transfers between devices: none -> 41.2 us  [the longest x26 36.9 us: swap(): return lax.ppermute(array, 'shard', [(i, i ^ bits) for i in range(devices)])]
    psum x1 -> x0, blocking collectives: 33.5 us -> none  [local(): dot_whole = lax.psum(dot_part, 'shard')]
    dot_general x8 -> x2, matrix products: 36.6 us -> 9.35 us  [outer(): lax.dot_general(*sides, (((0,), (0,)), ((), ())), preferred_element_type=...]
    ppermute x0 -> x27, starting transfers between devices: none -> 19.9 us  [the longest x26 18.4 us: swap(): return lax.ppermute(array, 'shard', [(i, i ^ bits) for i in range(devices)])]
    mul x4 -> x1, other arithmetic: 17.5 us -> 0.18 us  [member_sides(): weight = 2.0 / math.sqrt(everyone) * fitness]
    pallas_call x0 -> x4, Pallas kernels: none -> 16 us  [chunk(): pl.pallas_call(functools.partial(chunk_kernel, rows, columns), out_shape=...]
  transfers between devices with their start and end apart: 4 -> 27, of which waited for: 4 -> 11; matrix products, arithmetic and copies ran while one was open for 7% -> 15% of each run, Pallas kernels for 0% -> 6%
where the time goes in v2:
time: 116 us; the launch traced here: 115 us
  waiting for transfers between devices  41.2 us (36%)
  local copies, waits for them, and re-layouts  22.9 us (20%)
  starting transfers between devices  19.9 us (17%)
  Pallas kernels  16 us (14%)
  matrix products  9.35 us (8%)
  other arithmetic  4.69 us (4%)
    ppermute x26, waiting for transfers between devices, swap(): return lax.ppermute(array, 'shard', [(i, i ^ bits) for i in range(devices)])  36.9 us
    unnamed x60, local copies, waits for them, and re-layouts  22 us
    ppermute x26, starting transfers between devices, swap(): return lax.ppermute(array, 'shard', [(i, i ^ bits) for i in range(devices)])  18.4 us
    pallas_call x4, Pallas kernels, chunk(): pl.pallas_call(functools.partial(chunk_kernel, rows, columns), out_shape=...  16 us
    dot_general x2, matrix products, outer(): lax.dot_general(*sides, (((0,), (0,)), ((), ())), preferred_element_type=...  9.35 us
    ppermute x1, waiting for transfers between devices, local(): lax.ppermute(pack, 'member', [(i, i ^ bits) for i in range(groups)])  4.22 us
  transfers between devices with their start and end apart: 27, of which 11 were waited for; matrix products, arithmetic and copies ran while one was open for 15% of the time, Pallas kernels for 6%

profile of v2, /device:TPU:0, one launch (start us, length us, event | category | flops | bytes accessed | tf_op | source)
XLA Modules:
  0.0 115.0 jit_solution(3470883422915186570)
XLA Ops:
  0.6 3.0 %collective-permute-start.1 = (bf16[32,4096]{1,0:T(8,128)(2,1)}, bf16[32,4096]{1,0:T(8,128)(2,1)S(1)}, u32[]{:S(2)}, u32[]{:S(2)}) collective-permute-start(bf16[32,4096]{1,0:T(8,128)(2,1)} %refs_0_), channel_id=1, source_target_pairs={{0,2},{1,3},{2,0},{3,1},{4,6},{5,7},{6,4},{7,5},{8,10},{9,11},{10,... | collective-permute-start | bytes 786440 | tf_op jit(solution)/shard_map/ppermute | solution.py:151
  3.7 1.6 %collective-permute-start = (bf16[32,4096]{1,0:T(8,128)(2,1)}, bf16[32,4096]{1,0:T(8,128)(2,1)S(1)}, u32[]{:S(2)}, u32[]{:S(2)}) collective-permute-start(bf16[32,4096]{1,0:T(8,128)(2,1)} %refs_0_), channel_id=1, source_target_pairs={{0,4},{1,5},{2,6},{3,7},{4,0},{5,1},{6,2},{7,3},{8,12},{9,13},{10,... | collective-permute-start | bytes 786440 | tf_op jit(solution)/shard_map/ppermute | solution.py:151
  5.2 2.6 %collective-permute-start.4 = (bf16[32,4096]{1,0:T(8,128)(2,1)}, bf16[32,4096]{1,0:T(8,128)(2,1)S(1)}, u32[]{:S(2)}, u32[]{:S(2)}) collective-permute-start(bf16[32,4096]{1,0:T(8,128)(2,1)} %refs_0_), channel_id=1, source_target_pairs={{0,8},{1,9},{2,10},{3,11},{4,12},{5,13},{6,14},{7,15},{8,0},{9,1},... | collective-permute-start | bytes 786440 | tf_op jit(solution)/shard_map/ppermute | solution.py:151
  7.8 0.7 convert_element_type.104
  8.5 0.8 constant_dynamic-update-slice_fusion.4
  9.3 0.8 constant_dynamic-update-slice_fusion.3
  10.2 0.7 constant_dynamic-update-slice_fusion.2
  10.9 0.7 constant_dynamic-update-slice_fusion.1
  11.7 1.5 %collective-permute-start.6 = (bf16[8,10368]{1,0:T(8,128)(2,1)S(1)}, bf16[8,10368]{1,0:T(8,128)(2,1)S(1)}, u32[]{:S(2)}, u32[]{:S(2)}) collective-permute-start(bf16[8,10368]{1,0:T(8,128)(2,1)S(1)} %constant_dynamic-update-slice_fusion), channel_id=1, source_target_pairs={{0,16},{16,0},{1,17},{17,1},{2,18},{18,2},{3,19},{19,3},{4,20},{20... | collective-permute-start | bytes 497672 | tf_op jit(solution)/shard_map/ppermute | solution.py:174
  13.3 0.7 broadcast_in_dim.4.refs_4_
  14.1 4.2 %collective-permute-done.6 = bf16[8,10368]{1,0:T(8,128)(2,1)S(1)} collective-permute-done((bf16[8,10368]{1,0:T(8,128)(2,1)S(1)}, bf16[8,10368]{1,0:T(8,128)(2,1)S(1)}, u32[]{:S(2)}, u32[]{:S(2)}) %collective-permute-start.6) | collective-permute-done | bytes 165920 | tf_op jit(solution)/shard_map/ppermute | solution.py:174
  18.5 0.7 reduce-precision_convert_fusion.2
  19.3 0.7 reduce-precision_convert_fusion.1
  20.8 3.4 %copy-done = bf16[4096,1024]{1,0:T(8,128)(2,1)S(1)} copy-done((bf16[4096,1024]{1,0:T(8,128)(2,1)S(1)}, bf16[4096,1024]{1,0:T(8,128)(2,1)}, u32[]{:S(2)}) %copy-start) | copy-done | bytes 8388632
  24.2 3.4 %copy-done.3 = bf16[1024,4096]{1,0:T(8,128)(2,1)S(1)} copy-done((bf16[1024,4096]{1,0:T(8,128)(2,1)S(1)}, bf16[1024,4096]{1,0:T(8,128)(2,1)}, u32[]{:S(2)}) %copy-start.3) | copy-done | bytes 8388632
  27.6 0.8 copy-done.6
  28.4 0.8 copy-done.8
  29.2 0.7 copy-done.10
  30.0 0.7 copy-done.12
  30.7 0.9 copy-done.14
  31.6 3.7 %shard_map.112 = (bf16[64,4096]{1,0:T(8,128)(2,1)S(1)}, bf16[64,4096]{1,0:T(8,128)(2,1)S(1)}) custom-call(s32[3]{0:T(128)S(1)} %add_add_fusion.where, bf16[32,4096]{1,0:T(8,128)(2,1)S(1)} %copy-done.14, bf16[32,4096]{1,0:T(8,128)(2,1)S(1)} %collective-permute-done.1.refs_1_, bf16[32,4096]{1,0:T(8,128)(2,1)S(1)} %collective-permute-done.2.refs_2_, ...), custom_call_target="tpu_custom_call" | custom-call | flops 2147483648 | bytes 16777216 | tf_op jit(solution)/shard_map/pallas_call | solution.py:83
  35.4 1.3 %collective-permute-start.10 = (bf16[32,4096]{1,0:T(8,128)(2,1)S(1)}, bf16[32,4096]{1,0:T(8,128)(2,1)S(1)}, u32[]{:S(2)}, u32[]{:S(2)}) collective-permute-start(bf16[32,4096]{1,0:T(8,128)(2,1)S(1)} %collective-permute-done.4.refs_0_), channel_id=1, source_target_pairs={{0,2},{1,3},{2,0},{3,1},{4,6},{5,7},{6,4},{7,5},{8,10},{9,11},{10,... | collective-permute-start | bytes 786440 | tf_op jit(solution)/shard_map/ppermute | solution.py:151
  36.7 0.6 fusion.22
  38.3 5.4 %collective-permute-done.10.refs_1_ = bf16[32,4096]{1,0:T(8,128)(2,1)S(1)} collective-permute-done((bf16[32,4096]{1,0:T(8,128)(2,1)S(1)}, bf16[32,4096]{1,0:T(8,128)(2,1)S(1)}, u32[]{:S(2)}, u32[]{:S(2)}) %collective-permute-start.10) | collective-permute-done | bytes 262176 | tf_op jit(solution)/shard_map/ppermute | solution.py:151
  43.8 4.7 %fusion.13 = f32[2048,1024]{1,0:T(8,128)} fusion(bf16[48,2048]{1,0:T(8,128)(2,1)S(1)} %pad_maximum_fusion, bf16[16,1024]{1,0:T(8,128)(2,1)S(1)} %get-tuple-element.46), kind=kOutput, calls=%fused_computation.46 | convolution fusion | flops 201621504 | bytes 8617984 | tf_op jit(solution)/shard_map/dot_general | solution.py:133
  48.5 3.7 %shard_map.113 = (bf16[64,4096]{1,0:T(8,128)(2,1)S(1)}, bf16[64,4096]{1,0:T(8,128)(2,1)S(1)}) custom-call(s32[3]{0:T(128)S(1)} %add_add_fusion.2.where, bf16[32,4096]{1,0:T(8,128)(2,1)S(1)} %collective-permute-done.refs_0_, bf16[32,4096]{1,0:T(8,128)(2,1)S(1)} %collective-permute-done.7.refs_1_, bf16[32,4096]{1,0:T(8,128)(2,1)S(1)} %collective-permute-done.8.refs_2_, ...), custom_call_target="tpu_custom_call" | custom-call | flops 2147483648 | bytes 16777216 | tf_op jit(solution)/shard_map/pallas_call | solution.py:83
  52.3 1.2 %copy-done.16 = bf16[32,4096]{1,0:T(8,128)(2,1)S(1)} copy-done((bf16[32,4096]{1,0:T(8,128)(2,1)S(1)}, bf16[32,4096]{1,0:T(8,128)(2,1)}, u32[]{:S(2)}) %copy-start.16) | copy-done | bytes 262168
  53.4 4.5 %shard_map.114 = (bf16[64,4096]{1,0:T(8,128)(2,1)S(1)}, bf16[64,4096]{1,0:T(8,128)(2,1)}) custom-call(s32[3]{0:T(128)S(1)} %add_add_fusion.3.where, bf16[32,4096]{1,0:T(8,128)(2,1)S(1)} %copy-done.16, bf16[32,4096]{1,0:T(8,128)(2,1)S(1)} %collective-permute-done.10.refs_1_, bf16[32,4096]{1,0:T(8,128)(2,1)S(1)} %collective-permute-done.11.refs_2_, ...), custom_call_target="tpu_custom_call" | custom-call | flops 2147483648 | bytes 16777216 | tf_op jit(solution)/shard_map/pallas_call | solution.py:83
  58.4 1.3 %collective-permute-start.14 = (bf16[32,4096]{1,0:T(8,128)(2,1)}, bf16[32,4096]{1,0:T(8,128)(2,1)S(1)}, u32[]{:S(2)}, u32[]{:S(2)}) collective-permute-start(bf16[32,4096]{1,0:T(8,128)(2,1)} %collective-permute-done.5.refs_0_), channel_id=1, source_target_pairs={{0,2},{1,3},{2,0},{3,1},{4,6},{5,7},{6,4},{7,5},{8,10},{9,11},{10,... | collective-permute-start | bytes 786440 | tf_op jit(solution)/shard_map/ppermute | solution.py:151
  59.9 7.0 %collective-permute-done.14.refs_1_ = bf16[32,4096]{1,0:T(8,128)(2,1)S(1)} collective-permute-done((bf16[32,4096]{1,0:T(8,128)(2,1)}, bf16[32,4096]{1,0:T(8,128)(2,1)S(1)}, u32[]{:S(2)}, u32[]{:S(2)}) %collective-permute-start.14) | collective-permute-done | bytes 262176 | tf_op jit(solution)/shard_map/ppermute | solution.py:151
  67.0 1.4 %collective-permute-done.16.refs_3_ = bf16[32,4096]{1,0:T(8,128)(2,1)S(1)} collective-permute-done((bf16[32,4096]{1,0:T(8,128)(2,1)S(1)}, bf16[32,4096]{1,0:T(8,128)(2,1)S(1)}, u32[]{:S(2)}, u32[]{:S(2)}) %collective-permute-start.16) | collective-permute-done | bytes 262176 | tf_op jit(solution)/shard_map/ppermute | solution.py:151
  68.4 3.4 %copy-done.2 = bf16[4096,1024]{1,0:T(8,128)(2,1)S(1)} copy-done((bf16[4096,1024]{1,0:T(8,128)(2,1)S(1)}, bf16[4096,1024]{1,0:T(8,128)(2,1)}, u32[]{:S(2)}) %copy-start.2) | copy-done | bytes 8388632
  71.8 3.4 %copy-done.5 = bf16[1024,4096]{1,0:T(8,128)(2,1)S(1)} copy-done((bf16[1024,4096]{1,0:T(8,128)(2,1)S(1)}, bf16[1024,4096]{1,0:T(8,128)(2,1)}, u32[]{:S(2)}) %copy-start.5) | copy-done | bytes 8388632
  75.2 4.2 %shard_map.115 = (bf16[64,4096]{1,0:T(8,128)(2,1)S(1)}, bf16[64,4096]{1,0:T(8,128)(2,1)S(1)}) custom-call(s32[3]{0:T(128)S(1)} %add_add_fusion.1.where, bf16[32,4096]{1,0:T(8,128)(2,1)} %collective-permute-done.5.refs_0_, bf16[32,4096]{1,0:T(8,128)(2,1)S(1)} %collective-permute-done.14.refs_1_, bf16[32,4096]{1,0:T(8,128)(2,1)S(1)} %collective-permute-done.15.refs_2_, ...), custom_call_target="tpu_custom_call" | custom-call | flops 2147483648 | bytes 16777216 | tf_op jit(solution)/shard_map/pallas_call | solution.py:83
  79.6 1.8 %collective-permute-done.17 = bf16[64,4096]{1,0:T(8,128)(2,1)S(1)} collective-permute-done((bf16[64,4096]{1,0:T(8,128)(2,1)S(1)}, bf16[64,4096]{1,0:T(8,128)(2,1)S(1)}, u32[]{:S(2)}, u32[]{:S(2)}) %collective-permute-start.17) | collective-permute-done | bytes 524320 | tf_op jit(solution)/shard_map/ppermute | solution.py:151
  81.5 1.4 %collective-permute-start.24 = (bf16[32,4096]{1,0:T(8,128)(2,1)S(1)}, bf16[32,4096]{1,0:T(8,128)(2,1)S(1)}, u32[]{:S(2)}, u32[]{:S(2)}) collective-permute-start(bf16[32,4096]{1,0:T(8,128)(2,1)S(1)} %slice.108), channel_id=1, source_target_pairs={{0,2},{1,3},{2,0},{3,1},{4,6},{5,7},{6,4},{7,5},{8,10},{9,11},{10,... | collective-permute-start | bytes 786440 | tf_op jit(solution)/shard_map/ppermute | solution.py:151
  83.0 0.7 collective-permute-start.23
  83.6 7.1 %collective-permute-done.24 = bf16[32,4096]{1,0:T(8,128)(2,1)S(1)} collective-permute-done((bf16[32,4096]{1,0:T(8,128)(2,1)S(1)}, bf16[32,4096]{1,0:T(8,128)(2,1)S(1)}, u32[]{:S(2)}, u32[]{:S(2)}) %collective-permute-start.24) | collective-permute-done | bytes 262176 | tf_op jit(solution)/shard_map/ppermute | solution.py:151
  90.8 0.5 collective-permute-start.25
  91.9 3.6 %collective-permute-done.23 = bf16[32,4096]{1,0:T(8,128)(2,1)S(1)} collective-permute-done((bf16[32,4096]{1,0:T(8,128)(2,1)S(1)}, bf16[32,4096]{1,0:T(8,128)(2,1)S(1)}, u32[]{:S(2)}, u32[]{:S(2)}) %collective-permute-start.23) | collective-permute-done | bytes 262176 | tf_op jit(solution)/shard_map/ppermute | solution.py:151
  95.6 2.0 %collective-permute-done.25 = bf16[32,4096]{1,0:T(8,128)(2,1)S(1)} collective-permute-done((bf16[32,4096]{1,0:T(8,128)(2,1)S(1)}, bf16[32,4096]{1,0:T(8,128)(2,1)S(1)}, u32[]{:S(2)}, u32[]{:S(2)}) %collective-permute-start.25) | collective-permute-done | bytes 262176 | tf_op jit(solution)/shard_map/ppermute | solution.py:151
  98.2 1.4 %collective-permute-start.21 = (bf16[32,4096]{1,0:T(8,128)(2,1)S(1)}, bf16[32,4096]{1,0:T(8,128)(2,1)S(1)}, u32[]{:S(2)}, u32[]{:S(2)}) collective-permute-start(bf16[32,4096]{1,0:T(8,128)(2,1)S(1)} %slice.106), channel_id=1, source_target_pairs={{0,2},{1,3},{2,0},{3,1},{4,6},{5,7},{6,4},{7,5},{8,10},{9,11},{10,... | collective-permute-start | bytes 786440 | tf_op jit(solution)/shard_map/ppermute | solution.py:151
  99.8 0.7 collective-permute-start.19
  100.6 6.1 %collective-permute-done.21 = bf16[32,4096]{1,0:T(8,128)(2,1)S(1)} collective-permute-done((bf16[32,4096]{1,0:T(8,128)(2,1)S(1)}, bf16[32,4096]{1,0:T(8,128)(2,1)S(1)}, u32[]{:S(2)}, u32[]{:S(2)}) %collective-permute-start.21) | collective-permute-done | bytes 262176 | tf_op jit(solution)/shard_map/ppermute | solution.py:151
  106.7 0.5 collective-permute-start.22
  107.2 4.7 %fusion.7 = f32[1024,2048]{1,0:T(8,128)} fusion(bf16[48,1024]{1,0:T(8,128)(2,1)S(1)} %pad_maximum_fusion.1, bf16[16,2048]{1,0:T(8,128)(2,1)S(1)} %copy-done.25, bf16[16,2048]{1,0:T(8,128)(2,1)S(1)} %get-tuple-element.47, bf16[16,2048]{1,0:T(8,128)(2,1)S(1)} %copy-done.26), kind=kOutput, calls=%fused_computation.30 | convolution fusion | flops 201916416 | bytes 8683520 | tf_op jit(solution)/shard_map/dot_general | solution.py:133
  111.9 2.2 %collective-permute-done.22 = bf16[32,4096]{1,0:T(8,128)(2,1)S(1)} collective-permute-done((bf16[32,4096]{1,0:T(8,128)(2,1)S(1)}, bf16[32,4096]{1,0:T(8,128)(2,1)S(1)}, u32[]{:S(2)}, u32[]{:S(2)}) %collective-permute-start.22) | collective-permute-done | bytes 262176 | tf_op jit(solution)/shard_map/ppermute | solution.py:151
  114.1 0.8 fusion.6
  (97 shorter events, 5.0 us)
Async XLA Ops:
  0.6 18.6 %collective-permute-start.1 = (bf16[32,4096]{1,0:T(8,128)(2,1)}, bf16[32,4096]{1,0:T(8,128)(2,1)S(1)}, u32[]{:S(2)}, u32[]{:S(2)}) collective-permute-start(bf16[32,4096]{1,0:T(8,128)(2,1)} %refs_0_), channel_id=1, source_target_pairs={{0,2},{1,3},{2,0},{3,1},{4,6},{5,7},{6,4},{7,5},{8,10},{9,11},{10,... | collective-permute-start | bytes 786440 | tf_op jit(solution)/shard_map/ppermute | solution.py:151
  3.7 16.3 %collective-permute-start = (bf16[32,4096]{1,0:T(8,128)(2,1)}, bf16[32,4096]{1,0:T(8,128)(2,1)S(1)}, u32[]{:S(2)}, u32[]{:S(2)}) collective-permute-start(bf16[32,4096]{1,0:T(8,128)(2,1)} %refs_0_), channel_id=1, source_target_pairs={{0,4},{1,5},{2,6},{3,7},{4,0},{5,1},{6,2},{7,3},{8,12},{9,13},{10,... | collective-permute-start | bytes 786440 | tf_op jit(solution)/shard_map/ppermute | solution.py:151
  5.2 30.1 %collective-permute-start.4 = (bf16[32,4096]{1,0:T(8,128)(2,1)}, bf16[32,4096]{1,0:T(8,128)(2,1)S(1)}, u32[]{:S(2)}, u32[]{:S(2)}) collective-permute-start(bf16[32,4096]{1,0:T(8,128)(2,1)} %refs_0_), channel_id=1, source_target_pairs={{0,8},{1,9},{2,10},{3,11},{4,12},{5,13},{6,14},{7,15},{8,0},{9,1},... | collective-permute-start | bytes 786440 | tf_op jit(solution)/shard_map/ppermute | solution.py:151
  7.8 12.7 %collective-permute-start.2 = (bf16[32,4096]{1,0:T(8,128)(2,1)}, bf16[32,4096]{1,0:T(8,128)(2,1)S(1)}, u32[]{:S(2)}, u32[]{:S(2)}) collective-permute-start(bf16[32,4096]{1,0:T(8,128)(2,1)} %refs_0_), channel_id=1, source_target_pairs={{0,1},{1,0},{2,3},{3,2},{4,5},{5,4},{6,7},{7,6},{8,9},{9,8},{10,11... | collective-permute-start | bytes 786440 | tf_op jit(solution)/shard_map/ppermute | solution.py:151
  11.7 8.8 %copy-start.21 = (bf16[8,10368]{1,0:T(8,128)(2,1)}, bf16[8,10368]{1,0:T(8,128)(2,1)S(1)}, u32[]{:S(2)}) copy-start(bf16[8,10368]{1,0:T(8,128)(2,1)S(1)} %constant_dynamic-update-slice_fusion) | copy-start | bytes 497668
  11.7 6.7 %collective-permute-start.6 = (bf16[8,10368]{1,0:T(8,128)(2,1)S(1)}, bf16[8,10368]{1,0:T(8,128)(2,1)S(1)}, u32[]{:S(2)}, u32[]{:S(2)}) collective-permute-start(bf16[8,10368]{1,0:T(8,128)(2,1)S(1)} %constant_dynamic-update-slice_fusion), channel_id=1, source_target_pairs={{0,16},{16,0},{1,17},{17,1},{2,18},{18,2},{3,19},{19,3},{4,20},{20... | collective-permute-start | bytes 497672 | tf_op jit(solution)/shard_map/ppermute | solution.py:174
  19.3 1.5 %collective-permute-start.3 = (bf16[32,4096]{1,0:T(8,128)(2,1)S(1)}, bf16[32,4096]{1,0:T(8,128)(2,1)S(1)}, u32[]{:S(2)}, u32[]{:S(2)}) collective-permute-start(bf16[32,4096]{1,0:T(8,128)(2,1)S(1)} %collective-permute-done.1.refs_1_), channel_id=1, source_target_pairs={{0,1},{1,0},{2,3},{3,2},{4,5},{5,4},{6,7},{7,6},{8,9},{9,8},{10,11... | collective-permute-start | bytes 786440 | tf_op jit(solution)/shard_map/ppermute | solution.py:151
  20.0 18.3 %collective-permute-start.7 = (bf16[32,4096]{1,0:T(8,128)(2,1)S(1)}, bf16[32,4096]{1,0:T(8,128)(2,1)S(1)}, u32[]{:S(2)}, u32[]{:S(2)}) collective-permute-start(bf16[32,4096]{1,0:T(8,128)(2,1)S(1)} %collective-permute-done.refs_0_), channel_id=1, source_target_pairs={{0,2},{1,3},{2,0},{3,1},{4,6},{5,7},{6,4},{7,5},{8,10},{9,11},{10,... | collective-permute-start | bytes 786440 | tf_op jit(solution)/shard_map/ppermute | solution.py:151
  20.8 3.4 %copy-start = (bf16[4096,1024]{1,0:T(8,128)(2,1)S(1)}, bf16[4096,1024]{1,0:T(8,128)(2,1)}, u32[]{:S(2)}) copy-start(bf16[4096,1024]{1,0:T(8,128)(2,1)} %refs_9_.7) | copy-start | bytes 25165828
  24.2 3.4 %copy-start.3 = (bf16[1024,4096]{1,0:T(8,128)(2,1)S(1)}, bf16[1024,4096]{1,0:T(8,128)(2,1)}, u32[]{:S(2)}) copy-start(bf16[1024,4096]{1,0:T(8,128)(2,1)} %refs_10_.7) | copy-start | bytes 25165828
  31.6 5.1 %copy-start.22 = (bf16[8,10368]{1,0:T(8,128)(2,1)S(1)}, bf16[8,10368]{1,0:T(8,128)(2,1)}, u32[]{:S(2)}) copy-start(bf16[8,10368]{1,0:T(8,128)(2,1)} %copy-done.21) | copy-start | bytes 497668
  31.6 5.1 %copy-start.24 = (bf16[8,10368]{1,0:T(8,128)(2,1)S(1)}, bf16[8,10368]{1,0:T(8,128)(2,1)}, u32[]{:S(2)}) copy-start(bf16[8,10368]{1,0:T(8,128)(2,1)} %copy-done.23) | copy-start | bytes 497668
  31.6 16.8 %copy-start.4 = (bf16[1024,4096]{1,0:T(8,128)(2,1)S(1)}, bf16[1024,4096]{1,0:T(8,128)(2,1)}, u32[]{:S(2)}) copy-start(bf16[1024,4096]{1,0:T(8,128)(2,1)} %refs_10_.7) | copy-start | bytes 25165828
  35.3 13.1 %copy-start.17 = (bf16[64,4096]{1,0:T(8,128)(2,1)}, bf16[64,4096]{1,0:T(8,128)(2,1)S(1)}, u32[]{:S(2)}) copy-start(bf16[64,4096]{1,0:T(8,128)(2,1)S(1)} %get-tuple-element.35) | copy-start | bytes 1572868
  35.3 13.2 %copy-start.1 = (bf16[4096,1024]{1,0:T(8,128)(2,1)S(1)}, bf16[4096,1024]{1,0:T(8,128)(2,1)}, u32[]{:S(2)}) copy-start(bf16[4096,1024]{1,0:T(8,128)(2,1)} %refs_9_.7) | copy-start | bytes 25165828
  35.3 16.8 %copy-start.15 = (bf16[32,4096]{1,0:T(8,128)(2,1)}, bf16[32,4096]{1,0:T(8,128)(2,1)S(1)}, u32[]{:S(2)}) copy-start(bf16[32,4096]{1,0:T(8,128)(2,1)S(1)} %collective-permute-done.4.refs_0_) | copy-start | bytes 786436
  35.4 8.4 %collective-permute-start.10 = (bf16[32,4096]{1,0:T(8,128)(2,1)S(1)}, bf16[32,4096]{1,0:T(8,128)(2,1)S(1)}, u32[]{:S(2)}, u32[]{:S(2)}) collective-permute-start(bf16[32,4096]{1,0:T(8,128)(2,1)S(1)} %collective-permute-done.4.refs_0_), channel_id=1, source_target_pairs={{0,2},{1,3},{2,0},{3,1},{4,6},{5,7},{6,4},{7,5},{8,10},{9,11},{10,... | collective-permute-start | bytes 786440 | tf_op jit(solution)/shard_map/ppermute | solution.py:151
  37.3 11.1 %collective-permute-start.8 = (bf16[32,4096]{1,0:T(8,128)(2,1)S(1)}, bf16[32,4096]{1,0:T(8,128)(2,1)S(1)}, u32[]{:S(2)}, u32[]{:S(2)}) collective-permute-start(bf16[32,4096]{1,0:T(8,128)(2,1)S(1)} %collective-permute-done.refs_0_), channel_id=1, source_target_pairs={{0,1},{1,0},{2,3},{3,2},{4,5},{5,4},{6,7},{7,6},{8,9},{9,8},{10,11... | collective-permute-start | bytes 786440 | tf_op jit(solution)/shard_map/ppermute | solution.py:151
  37.4 14.8 %collective-permute-start.11 = (bf16[32,4096]{1,0:T(8,128)(2,1)S(1)}, bf16[32,4096]{1,0:T(8,128)(2,1)S(1)}, u32[]{:S(2)}, u32[]{:S(2)}) collective-permute-start(bf16[32,4096]{1,0:T(8,128)(2,1)S(1)} %collective-permute-done.4.refs_0_), channel_id=1, source_target_pairs={{0,1},{1,0},{2,3},{3,2},{4,5},{5,4},{6,7},{7,6},{8,9},{9,8},{10,11... | collective-permute-start | bytes 786440 | tf_op jit(solution)/shard_map/ppermute | solution.py:151
  37.9 14.3 %collective-permute-start.5 = (bf16[32,4096]{1,0:T(8,128)(2,1)S(1)}, bf16[32,4096]{1,0:T(8,128)(2,1)}, u32[]{:S(2)}, u32[]{:S(2)}) collective-permute-start(bf16[32,4096]{1,0:T(8,128)(2,1)S(1)} %collective-permute-done.4.refs_0_), channel_id=1, source_target_pairs={{0,4},{1,5},{2,6},{3,7},{4,0},{5,1},{6,2},{7,3},{8,12},{9,13},{10,... | collective-permute-start | bytes 786440 | tf_op jit(solution)/shard_map/ppermute | solution.py:151
  38.3 10.1 %collective-permute-start.9 = (bf16[32,4096]{1,0:T(8,128)(2,1)S(1)}, bf16[32,4096]{1,0:T(8,128)(2,1)S(1)}, u32[]{:S(2)}, u32[]{:S(2)}) collective-permute-start(bf16[32,4096]{1,0:T(8,128)(2,1)S(1)} %collective-permute-done.7.refs_1_), channel_id=1, source_target_pairs={{0,1},{1,0},{2,3},{3,2},{4,5},{5,4},{6,7},{7,6},{8,9},{9,8},{10,11... | collective-permute-start | bytes 786440 | tf_op jit(solution)/shard_map/ppermute | solution.py:151
  43.8 8.5 %collective-permute-start.12 = (bf16[32,4096]{1,0:T(8,128)(2,1)S(1)}, bf16[32,4096]{1,0:T(8,128)(2,1)S(1)}, u32[]{:S(2)}, u32[]{:S(2)}) collective-permute-start(bf16[32,4096]{1,0:T(8,128)(2,1)S(1)} %collective-permute-done.10.refs_1_), channel_id=1, source_target_pairs={{0,1},{1,0},{2,3},{3,2},{4,5},{5,4},{6,7},{7,6},{8,9},{9,8},{10,11... | collective-permute-start | bytes 786440 | tf_op jit(solution)/shard_map/ppermute | solution.py:151
  52.2 5.7 %copy-start.19 = (bf16[64,4096]{1,0:T(8,128)(2,1)}, bf16[64,4096]{1,0:T(8,128)(2,1)S(1)}, u32[]{:S(2)}) copy-start(bf16[64,4096]{1,0:T(8,128)(2,1)S(1)} %get-tuple-element.37) | copy-start | bytes 1572868
  52.2 16.2 %copy-start.7 = (bf16[8,4096]{1,0:T(8,128)(2,1)S(1)}, bf16[8,4096]{1,0:T(8,128)(2,1)}, u32[]{:S(2)}) copy-start(bf16[8,4096]{1,0:T(8,128)(2,1)} %refs_5_.7) | copy-start | bytes 196612
  52.2 16.2 %copy-start.9 = (bf16[8,4096]{1,0:T(8,128)(2,1)S(1)}, bf16[8,4096]{1,0:T(8,128)(2,1)}, u32[]{:S(2)}) copy-start(bf16[8,4096]{1,0:T(8,128)(2,1)} %refs_8_.7) | copy-start | bytes 196612
  52.2 16.2 %copy-start.11 = (bf16[8,1024]{1,0:T(8,128)(2,1)S(1)}, bf16[8,1024]{1,0:T(8,128)(2,1)}, u32[]{:S(2)}) copy-start(bf16[8,1024]{1,0:T(8,128)(2,1)} %refs_6_.7) | copy-start | bytes 49156
  52.2 16.2 %copy-start.13 = (bf16[8,1024]{1,0:T(8,128)(2,1)S(1)}, bf16[8,1024]{1,0:T(8,128)(2,1)}, u32[]{:S(2)}) copy-start(bf16[8,1024]{1,0:T(8,128)(2,1)} %refs_7_.7) | copy-start | bytes 49156
  57.9 8.9 %collective-permute-start.13 = (bf16[64,4096]{1,0:T(8,128)(2,1)}, bf16[64,4096]{1,0:T(8,128)(2,1)S(1)}, u32[]{:S(2)}, u32[]{:S(2)}) collective-permute-start(bf16[64,4096]{1,0:T(8,128)(2,1)} %get-tuple-element.31), channel_id=1, source_target_pairs={{0,1},{1,0},{2,3},{3,2},{4,5},{5,4},{6,7},{7,6},{8,9},{9,8},{10,11... | collective-permute-start | bytes 1572872 | tf_op jit(solution)/shard_map/ppermute | solution.py:151
  58.4 8.4 %collective-permute-start.14 = (bf16[32,4096]{1,0:T(8,128)(2,1)}, bf16[32,4096]{1,0:T(8,128)(2,1)S(1)}, u32[]{:S(2)}, u32[]{:S(2)}) collective-permute-start(bf16[32,4096]{1,0:T(8,128)(2,1)} %collective-permute-done.5.refs_0_), channel_id=1, source_target_pairs={{0,2},{1,3},{2,0},{3,1},{4,6},{5,7},{6,4},{7,5},{8,10},{9,11},{10,... | collective-permute-start | bytes 786440 | tf_op jit(solution)/shard_map/ppermute | solution.py:151
  59.8 7.2 %collective-permute-start.15 = (bf16[32,4096]{1,0:T(8,128)(2,1)}, bf16[32,4096]{1,0:T(8,128)(2,1)S(1)}, u32[]{:S(2)}, u32[]{:S(2)}) collective-permute-start(bf16[32,4096]{1,0:T(8,128)(2,1)} %collective-permute-done.5.refs_0_), channel_id=1, source_target_pairs={{0,1},{1,0},{2,3},{3,2},{4,5},{5,4},{6,7},{7,6},{8,9},{9,8},{10,11... | collective-permute-start | bytes 786440 | tf_op jit(solution)/shard_map/ppermute | solution.py:151
  66.8 1.5 %collective-permute-start.16 = (bf16[32,4096]{1,0:T(8,128)(2,1)S(1)}, bf16[32,4096]{1,0:T(8,128)(2,1)S(1)}, u32[]{:S(2)}, u32[]{:S(2)}) collective-permute-start(bf16[32,4096]{1,0:T(8,128)(2,1)S(1)} %collective-permute-done.14.refs_1_), channel_id=1, source_target_pairs={{0,1},{1,0},{2,3},{3,2},{4,5},{5,4},{6,7},{7,6},{8,9},{9,8},{10,11... | collective-permute-start | bytes 786440 | tf_op jit(solution)/shard_map/ppermute | solution.py:151
  67.0 24.4 %copy-start.18 = (bf16[64,4096]{1,0:T(8,128)(2,1)S(1)}, bf16[64,4096]{1,0:T(8,128)(2,1)}, u32[]{:S(2)}) copy-start(bf16[64,4096]{1,0:T(8,128)(2,1)} %copy-done.17) | copy-start | bytes 1572868
  68.4 3.4 %copy-start.2 = (bf16[4096,1024]{1,0:T(8,128)(2,1)S(1)}, bf16[4096,1024]{1,0:T(8,128)(2,1)}, u32[]{:S(2)}) copy-start(bf16[4096,1024]{1,0:T(8,128)(2,1)} %refs_9_.7) | copy-start | bytes 25165828
  71.8 3.4 %copy-start.5 = (bf16[1024,4096]{1,0:T(8,128)(2,1)S(1)}, bf16[1024,4096]{1,0:T(8,128)(2,1)}, u32[]{:S(2)}) copy-start(bf16[1024,4096]{1,0:T(8,128)(2,1)} %refs_10_.7) | copy-start | bytes 25165828
  75.2 16.2 %copy-start.27 = (bf16[16,1024]{1,0:T(8,128)(2,1)S(1)}, bf16[16,1024]{1,0:T(8,128)(2,1)}, u32[]{:S(2)}) copy-start(bf16[16,1024]{1,0:T(8,128)(2,1)} %get-tuple-element.45) | copy-start | bytes 98308
  75.2 16.3 %copy-start.20 = (bf16[64,4096]{1,0:T(8,128)(2,1)S(1)}, bf16[64,4096]{1,0:T(8,128)(2,1)}, u32[]{:S(2)}) copy-start(bf16[64,4096]{1,0:T(8,128)(2,1)} %copy-done.19) | copy-start | bytes 1572868
  79.4 27.8 %copy-start.25 = (bf16[16,2048]{1,0:T(8,128)(2,1)S(1)}, bf16[16,2048]{1,0:T(8,128)(2,1)}, u32[]{:S(2)}) copy-start(bf16[16,2048]{1,0:T(8,128)(2,1)} %get-tuple-element.48) | copy-start | bytes 196612
  79.4 27.8 %copy-start.26 = (bf16[16,2048]{1,0:T(8,128)(2,1)S(1)}, bf16[16,2048]{1,0:T(8,128)(2,1)}, u32[]{:S(2)}) copy-start(bf16[16,2048]{1,0:T(8,128)(2,1)} %get-tuple-element.39) | copy-start | bytes 196612
  79.4 2.0 %collective-permute-start.17 = (bf16[64,4096]{1,0:T(8,128)(2,1)S(1)}, bf16[64,4096]{1,0:T(8,128)(2,1)S(1)}, u32[]{:S(2)}, u32[]{:S(2)}) collective-permute-start(bf16[64,4096]{1,0:T(8,128)(2,1)S(1)} %get-tuple-element.34), channel_id=1, source_target_pairs={{0,1},{1,0},{2,3},{3,2},{4,5},{5,4},{6,7},{7,6},{8,9},{9,8},{10,11... | collective-permute-start | bytes 1572872 | tf_op jit(solution)/shard_map/ppermute | solution.py:151
  81.5 9.2 %collective-permute-start.24 = (bf16[32,4096]{1,0:T(8,128)(2,1)S(1)}, bf16[32,4096]{1,0:T(8,128)(2,1)S(1)}, u32[]{:S(2)}, u32[]{:S(2)}) collective-permute-start(bf16[32,4096]{1,0:T(8,128)(2,1)S(1)} %slice.108), channel_id=1, source_target_pairs={{0,2},{1,3},{2,0},{3,1},{4,6},{5,7},{6,4},{7,5},{8,10},{9,11},{10,... | collective-permute-start | bytes 786440 | tf_op jit(solution)/shard_map/ppermute | solution.py:151
  83.0 12.6 %collective-permute-start.23 = (bf16[32,4096]{1,0:T(8,128)(2,1)S(1)}, bf16[32,4096]{1,0:T(8,128)(2,1)S(1)}, u32[]{:S(2)}, u32[]{:S(2)}) collective-permute-start(bf16[32,4096]{1,0:T(8,128)(2,1)S(1)} %slice.109), channel_id=1, source_target_pairs={{0,2},{1,3},{2,0},{3,1},{4,6},{5,7},{6,4},{7,5},{8,10},{9,11},{10,... | collective-permute-start | bytes 786440 | tf_op jit(solution)/shard_map/ppermute | solution.py:151
  90.8 6.8 %collective-permute-start.25 = (bf16[32,4096]{1,0:T(8,128)(2,1)S(1)}, bf16[32,4096]{1,0:T(8,128)(2,1)S(1)}, u32[]{:S(2)}, u32[]{:S(2)}) collective-permute-start(bf16[32,4096]{1,0:T(8,128)(2,1)S(1)} %fusion), channel_id=1, source_target_pairs={{0,4},{1,5},{2,6},{3,7},{4,0},{5,1},{6,2},{7,3},{8,12},{9,13},{10,... | collective-permute-start | bytes 786440 | tf_op jit(solution)/shard_map/ppermute | solution.py:151
  91.4 8.3 %collective-permute-start.18 = (bf16[64,4096]{1,0:T(8,128)(2,1)S(1)}, bf16[64,4096]{1,0:T(8,128)(2,1)S(1)}, u32[]{:S(2)}, u32[]{:S(2)}) collective-permute-start(bf16[64,4096]{1,0:T(8,128)(2,1)S(1)} %copy-done.18), channel_id=1, source_target_pairs={{0,1},{1,0},{2,3},{3,2},{4,5},{5,4},{6,7},{7,6},{8,9},{9,8},{10,11... | collective-permute-start | bytes 1572872 | tf_op jit(solution)/shard_map/ppermute | solution.py:151
  91.5 6.6 %collective-permute-start.20 = (bf16[64,4096]{1,0:T(8,128)(2,1)S(1)}, bf16[64,4096]{1,0:T(8,128)(2,1)S(1)}, u32[]{:S(2)}, u32[]{:S(2)}) collective-permute-start(bf16[64,4096]{1,0:T(8,128)(2,1)S(1)} %copy-done.20), channel_id=1, source_target_pairs={{0,1},{1,0},{2,3},{3,2},{4,5},{5,4},{6,7},{7,6},{8,9},{9,8},{10,11... | collective-permute-start | bytes 1572872 | tf_op jit(solution)/shard_map/ppermute | solution.py:151
  97.7 14.2 %collective-permute-start.26 = (bf16[32,4096]{1,0:T(8,128)(2,1)S(1)}, bf16[32,4096]{1,0:T(8,128)(2,1)S(1)}, u32[]{:S(2)}, u32[]{:S(2)}) collective-permute-start(bf16[32,4096]{1,0:T(8,128)(2,1)S(1)} %fusion.2), channel_id=1, source_target_pairs={{0,8},{1,9},{2,10},{3,11},{4,12},{5,13},{6,14},{7,15},{8,0},{9,1},... | collective-permute-start | bytes 786440 | tf_op jit(solution)/shard_map/ppermute | solution.py:151
  98.2 8.4 %collective-permute-start.21 = (bf16[32,4096]{1,0:T(8,128)(2,1)S(1)}, bf16[32,4096]{1,0:T(8,128)(2,1)S(1)}, u32[]{:S(2)}, u32[]{:S(2)}) collective-permute-start(bf16[32,4096]{1,0:T(8,128)(2,1)S(1)} %slice.106), channel_id=1, source_target_pairs={{0,2},{1,3},{2,0},{3,1},{4,6},{5,7},{6,4},{7,5},{8,10},{9,11},{10,... | collective-permute-start | bytes 786440 | tf_op jit(solution)/shard_map/ppermute | solution.py:151
  99.8 12.1 %collective-permute-start.19 = (bf16[32,4096]{1,0:T(8,128)(2,1)S(1)}, bf16[32,4096]{1,0:T(8,128)(2,1)S(1)}, u32[]{:S(2)}, u32[]{:S(2)}) collective-permute-start(bf16[32,4096]{1,0:T(8,128)(2,1)S(1)} %slice.107), channel_id=1, source_target_pairs={{0,2},{1,3},{2,0},{3,1},{4,6},{5,7},{6,4},{7,5},{8,10},{9,11},{10,... | collective-permute-start | bytes 786440 | tf_op jit(solution)/shard_map/ppermute | solution.py:151
  106.7 7.4 %collective-permute-start.22 = (bf16[32,4096]{1,0:T(8,128)(2,1)S(1)}, bf16[32,4096]{1,0:T(8,128)(2,1)S(1)}, u32[]{:S(2)}, u32[]{:S(2)}) collective-permute-start(bf16[32,4096]{1,0:T(8,128)(2,1)S(1)} %fusion.3), channel_id=1, source_target_pairs={{0,4},{1,5},{2,6},{3,7},{4,0},{5,1},{6,2},{7,3},{8,12},{9,13},{10,... | collective-permute-start | bytes 786440 | tf_op jit(solution)/shard_map/ppermute | solution.py:151
  (7 other events, 7.4 us)

commit v3 on v2

v3 whole, which is shorter than its diff:
```python
import functools
import math

import jax
import jax.numpy as jnp
from jax import lax
from jax.experimental import pallas as pl
from jax.experimental.pallas import tpu as pltpu
from jax.sharding import PartitionSpec as P

D = 4096
FF = 16384
LEN = 64
PLANES = 4
CORES = 2
STEP = 1024


def chunk_kernel(k, rows, columns, *refs):
    own, other = refs[:columns], refs[columns : 2 * columns]
    mix, key_left, key_right, value_left, value_right, key, value = refs[2 * columns : 2 * columns + 7]
    keep, send, whole, natural, relative, natural_dots, dots = refs[2 * columns + 7 :]
    me = lax.axis_index("shard")
    core, y, plane = me % CORES, me // CORES % columns, me // (CORES * columns) ^ k
    tokens = rows * columns * CORES
    members = tokens // LEN

    def place(j, c):
        return pl.multiple_of(((y ^ j) * CORES + c) * rows, rows)

    def pick(array, member):
        at = lax.broadcasted_iota(jnp.int32, array.shape, 0) == member
        return jnp.sum(jnp.where(at, array.astype(jnp.float32), 0.0), 0, keepdims=True)

    for j in range(columns):
        whole[pl.ds(place(j, core), rows), :] = own[j][...]
        whole[pl.ds(place(j, 1 - core), rows), :] = other[j][...]

    inside = lax.broadcasted_iota(jnp.int32, (tokens, 1), 0) % LEN != 0
    total, along = None, [0.0] * members
    for start in range(0, D, STEP):
        at = slice(start, start + STEP)
        current = whole[:, at].astype(jnp.float32)
        previous = jnp.where(inside, pltpu.roll(current, 1, 0), 0.0)
        shifted = (current + (previous - current) * mix[:, at].astype(jnp.float32)).astype(jnp.bfloat16)
        part = jnp.dot(shifted, key[at, :], preferred_element_type=jnp.float32)
        total = part if total is None else total + part
        for m in range(members):
            wide = shifted[m * LEN : (m + 1) * LEN].astype(jnp.float32)
            products = wide * pick(key_left[:, at], plane * members + m)
            along[m] = along[m] + sum(products[:, i : i + 128] for i in range(0, STEP, 128))

    for m in range(members):
        at = slice(m * LEN, (m + 1) * LEN)
        dot = 0.5 / math.sqrt(D) * jnp.sum(along[m], 1, keepdims=True)
        hidden = total[at] + dot * pick(key_right[...], plane * members + m)
        keyed = jnp.square(jnp.maximum(hidden, 0.0)).astype(jnp.bfloat16)
        natural[at, :] = keyed
        dot = jnp.sum(keyed.astype(jnp.float32) * pick(value_left[...], plane * members + m), 1, keepdims=True)
        natural_dots[at, :] = jnp.broadcast_to(0.5 / math.sqrt(FF) * dot, (LEN, 128))

    cores = (core, 1 - core)
    for c in range(CORES):
        for j in range(columns):
            to = slice((c * columns + j) * rows, (c * columns + j + 1) * rows)
            relative[to, :] = natural[pl.ds(place(j, cores[c]), rows), :]
            dots[to, :] = natural_dots[pl.ds(place(j, cores[c]), rows), :]

    for start in range(0, D, STEP):
        at = slice(start, start + STEP)
        result = jnp.dot(relative[...], value[:, at], preferred_element_type=jnp.float32)
        for c, out in enumerate((keep, send)):
            for j in range(columns):
                to = slice((c * columns + j) * rows, (c * columns + j + 1) * rows)
                right = pick(value_right[:, at], plane * members + place(j, cores[c]) // LEN)
                out[j * rows : (j + 1) * rows, at] = (result[to] + dots[to, :1] * right).astype(jnp.bfloat16)


def chunk(k, own, other, mix, key_left, key_right, value_left, value_right, key, value):
    columns, rows = len(own), own[0].shape[0]
    hidden = key.shape[1]
    tokens = rows * columns * CORES
    operands = (*own, *other, mix, key_left, key_right, value_left, value_right, key, value)
    return pl.pallas_call(
        functools.partial(chunk_kernel, k, rows, columns),
        out_shape=[jax.ShapeDtypeStruct((columns * rows, D), jnp.bfloat16)] * 2,
        in_specs=[pl.BlockSpec(memory_space=pltpu.VMEM)] * len(operands),
        out_specs=[pl.BlockSpec(memory_space=pltpu.VMEM)] * 2,
        scratch_shapes=[
            pltpu.VMEM((tokens, D), jnp.bfloat16),
            pltpu.VMEM((tokens, hidden), jnp.bfloat16),
            pltpu.VMEM((tokens, hidden), jnp.bfloat16),
            pltpu.VMEM((tokens, 128), jnp.float32),
            pltpu.VMEM((tokens, 128), jnp.float32),
        ],
        compiler_params=pltpu.CompilerParams(vmem_limit_bytes=8 * 1024 * 1024),
        cost_estimate=pl.CostEstimate(flops=tokens, bytes_accessed=tokens, transcendentals=0),
    )(*operands)


def sum_kernel(rows, keep, arrived, mine, *terms):
    both = keep[...].astype(jnp.float32) + arrived[...].astype(jnp.float32)
    mine[...] = both[:rows].astype(mine.dtype)
    per = D // terms[0].shape[1]
    for i, term in enumerate(terms):
        j, at = i // per + 1, i % per * term.shape[1]
        term[...] = both[j * rows : (j + 1) * rows, at : at + term.shape[1]].astype(jnp.bfloat16)


def sum_cores(keep, arrived, columns, per, kind=jnp.float32):
    rows = keep.shape[0] // columns
    terms = [jax.ShapeDtypeStruct((rows, D // per), jnp.bfloat16)] * ((columns - 1) * per)
    mine, *terms = pl.pallas_call(
        functools.partial(sum_kernel, rows),
        out_shape=[jax.ShapeDtypeStruct((rows, D), kind)] + terms,
        in_specs=[pl.BlockSpec(memory_space=pltpu.VMEM)] * 2,
        out_specs=[pl.BlockSpec(memory_space=pltpu.VMEM)] * (1 + len(terms)),
        compiler_params=pltpu.CompilerParams(vmem_limit_bytes=8 * 1024 * 1024),
        cost_estimate=pl.CostEstimate(flops=rows, bytes_accessed=rows, transcendentals=0),
    )(keep, arrived)
    return mine, [terms[i::per] for i in range(per)]


def pack_kernel(ranks, *refs):
    parts, out = refs[:-1], refs[-1]
    at = 0
    for part in parts:
        out[:, at : at + part.shape[1]] = part[...]
        at += part.shape[1]
    row = lax.broadcasted_iota(jnp.int32, (ranks.shape[0], 128), 0)
    marks = sum(jnp.where(row == m, ranks[m], 0) for m in range(ranks.shape[0]))
    out[:, at:] = marks.astype(jnp.float32).astype(jnp.bfloat16)


def pack_members(key_left, key_right, value_left, value_right, ranks):
    parts = (key_left, value_right, key_right, value_left)
    wide = sum(part.shape[1] for part in parts) + 128
    return pl.pallas_call(
        pack_kernel,
        out_shape=jax.ShapeDtypeStruct((ranks.shape[0], wide), jnp.bfloat16),
        in_specs=[pl.BlockSpec(memory_space=pltpu.SMEM)] + [pl.BlockSpec(memory_space=pltpu.VMEM)] * 4,
        out_specs=pl.BlockSpec(memory_space=pltpu.VMEM),
        compiler_params=pltpu.CompilerParams(vmem_limit_bytes=4 * 1024 * 1024),
        cost_estimate=pl.CostEstimate(flops=wide, bytes_accessed=wide, transcendentals=0),
    )(ranks, *parts)


def load_kernel(*refs):
    count = len(refs) // 2
    sems = refs[-1]
    copies = [pltpu.make_async_copy(refs[i], refs[count + i], sems.at[i]) for i in range(count)]
    for copy in copies:
        copy.start()
    for copy in copies:
        copy.wait()


def load(*arrays):
    size = sum(array.size * array.dtype.itemsize for array in arrays)
    return pl.pallas_call(
        load_kernel,
        out_shape=[jax.ShapeDtypeStruct(array.shape, array.dtype) for array in arrays],
        in_specs=[pl.BlockSpec(memory_space=pltpu.HBM)] * len(arrays),
        out_specs=[pl.BlockSpec(memory_space=pltpu.VMEM)] * len(arrays),
        scratch_shapes=[pltpu.SemaphoreType.DMA((len(arrays),))],
        compiler_params=pltpu.CompilerParams(vmem_limit_bytes=1024 * 1024),
        cost_estimate=pl.CostEstimate(flops=0, bytes_accessed=size, transcendentals=0),
    )(*arrays)


def update_kernel(fit_rows, groups, hidden, *refs):
    *packs, out, left, right = refs
    part, rows = D // groups, out.shape[0]

    def columns(start, size):
        at = pl.ds(pl.multiple_of(start, 128), size)
        return jnp.concatenate([ref[:, at].astype(jnp.float32) for ref in packs], 0)

    def split(array):
        everyone = array.shape[0]
        fitness = columns(packs[0].shape[1] - 128, 128)[:, :1] / (everyone - 1) - 0.5
        rest, terms = 2.0 / math.sqrt(everyone) * fitness * array, []
        for _ in range(3):
            terms.append(rest.astype(jnp.bfloat16).astype(jnp.float32))
            rest = rest - terms[-1]
        return jnp.concatenate(terms, 0).astype(jnp.bfloat16)

    def thrice(array):
        return jnp.concatenate([array] * 3, 0).astype(jnp.bfloat16)

    @pl.when(pl.program_id(0) == 0)
    def _():
        half = lax.axis_index("member") * part
        if fit_rows:
            left[...], right[...] = split(columns(half, part)), thrice(columns(2 * D, hidden))
        else:
            left[...], right[...] = thrice(columns(2 * D + hidden, hidden)), split(columns(D + half, part))

    at = pl.ds(pl.multiple_of(pl.program_id(0) * rows, rows), rows)
    out[...] = lax.dot_general(
        left[:, at], right[...], (((0,), (0,)), ((), ())), preferred_element_type=jnp.float32
    )


def update(fit_rows, packs, groups, hidden):
    part = D // groups
    shape, rows = ((part, hidden), 256) if fit_rows else ((hidden, part), 128)
    depth = 3 * packs[0].shape[0] * len(packs)
    return pl.pallas_call(
        functools.partial(update_kernel, fit_rows, groups, hidden),
        out_shape=jax.ShapeDtypeStruct(shape, jnp.float32),
        grid=(shape[0] // rows,),
        in_specs=[pl.BlockSpec(memory_space=pltpu.VMEM)] * len(packs),
        out_specs=pl.BlockSpec((rows, shape[1]), lambda i: (i, 0)),
        scratch_shapes=[pltpu.VMEM((depth, shape[0]), jnp.bfloat16), pltpu.VMEM((depth, shape[1]), jnp.bfloat16)],
        compiler_params=pltpu.CompilerParams(vmem_limit_bytes=12 * 1024 * 1024),
        cost_estimate=pl.CostEstimate(flops=0, bytes_accessed=8 * shape[0] * shape[1], transcendentals=0),
    )(*packs)


def together(*values):
    return lax.optimization_barrier(values)


def local(
    tokens, key_weight, value_weight, shift_mix, key_left, key_right, value_left, value_right, ranks
):
    devices, groups = lax.axis_size("shard"), lax.axis_size("member")
    columns = devices // (PLANES * CORES)
    rows, hidden = tokens.shape[0], key_weight.shape[1]
    mix = shift_mix[None, :]
    (key,) = load(key_weight)

    def swap(array, bits):
        return lax.ppermute(array, "shard", [(i, i ^ bits) for i in range(devices)])

    def over_z(array, k):
        return swap(array, k * columns * CORES)

    def over_y(array, j):
        return swap(array, j * CORES)

    def over_cores(array):
        return swap(array, 1)

    def partial(k, own, other):
        return chunk(k, own, other, mix, key_left, key_right, value_left, value_right, key, value)

    def all_y(block):
        return [over_y(block, j) for j in range(1, columns)]

    def all_cores(blocks):
        return [over_cores(block) for block in blocks]

    def exchange_y(terms):
        return [over_y(term, j) for j, term in enumerate(terms, 1)]

    def add(mine, arrived):
        return functools.reduce(lambda total, part: total + part.astype(jnp.float32), arrived, mine)

    near, far = over_z(tokens, 1), over_z(tokens, 2)
    y0, c0 = all_y(tokens), over_cores(tokens)
    mix, key, value = together(shift_mix[None, :], key_weight, value_weight)
    key, value = load(key, value)
    near, y0, c0, key, value, pack_of = together(near, y0, c0, key, value, key_left)

    y1, c1, cy0 = all_y(near), over_cores(near), all_cores(y0)
    pack = pack_members(pack_of, key_right, value_left, value_right, ranks)
    packs = [pack] + [
        lax.ppermute(pack, "member", [(i, i ^ bits) for i in range(groups)]) for bits in range(1, groups)
    ]
    far, y1, c1, cy0, packs = together(far, y1, c1, cy0, packs)

    farthest, y2, c2, cy1 = over_z(far, 1), all_y(far), over_cores(far), all_cores(y1)
    key_update = update(True, packs, groups, hidden)
    own, key_update = together(tokens, key_update)
    keep0, send0 = partial(0, [own] + y0, [c0] + cy0)
    farthest, y2, c2, cy1, keep0, send0 = together(farthest, y2, c2, cy1, keep0, send0)

    y3, c3, cy2 = all_y(farthest), over_cores(farthest), all_cores(y2)
    keep1, send1 = partial(1, [near] + y1, [c1] + cy1)
    far, keep1 = together(far, keep1)
    keep2, send2 = partial(2, [far] + y2, [c2] + cy2)
    y3, c3, keep1, send1, keep2, send2 = together(y3, c3, keep1, send1, keep2, send2)

    cy3 = all_cores(y3)
    mine2, (terms2,) = sum_cores(keep2, over_cores(send2), columns, 1)
    mine1, (terms1,) = sum_cores(keep1, over_cores(send1), columns, 1, jnp.bfloat16)
    farthest, mine2, terms2, mine1, terms1 = together(farthest, mine2, terms2, mine1, terms1)
    back2, mine1 = exchange_y(terms2), over_z(mine1, 1)
    keep3, send3 = partial(3, [farthest] + y3, [c3] + cy3)
    back2, mine1, terms1, send0, keep3, send3 = together(back2, mine1, terms1, send0, keep3, send3)

    terms1, back0 = [over_z(term, 1) for term in terms1], over_cores(send0)
    mine3, terms3 = sum_cores(keep3, over_cores(send3), columns, 2)
    back3 = exchange_y(terms3[0])
    back3, rest3, terms1, back0 = together(back3, terms3[1], terms1, back0)

    half = D // 2
    parts = (slice(0, half), slice(half, D))
    onward = over_z(add(mine3[:, parts[0]], back3).astype(jnp.bfloat16), 1)
    back3 = exchange_y(rest3)
    both = keep0.astype(jnp.float32) + back0.astype(jnp.float32)
    mine0 = add(both[:rows], [mine1])
    terms0 = [add(both[j * rows : (j + 1) * rows], [term]) for j, term in enumerate(terms1, 1)]
    sum2 = add(mine2, back2)
    onward, back3, mine0, terms0, sum2, packs = together(onward, back3, mine0, terms0, sum2, packs)

    first = over_z((sum2[:, parts[0]] + onward.astype(jnp.float32)).astype(jnp.bfloat16), 2)
    onward = over_z(add(mine3[:, parts[1]], back3).astype(jnp.bfloat16), 1)
    back0 = exchange_y([term.astype(jnp.bfloat16) for term in terms0])
    value_update = update(False, packs, groups, hidden)
    first, onward, back0, value_update = together(first, onward, back0, value_update)

    second = over_z((sum2[:, parts[1]] + onward.astype(jnp.float32)).astype(jnp.bfloat16), 2)
    result = add(mine0, back0)
    result = [add(result[:, at], [part]) for at, part in zip(parts, (first, second))]
    return jnp.concatenate(result, 1).astype(jnp.bfloat16), key_update, value_update


def solution(mesh):
    placed = (
        P(("member", "shard"), None),
        P(None, "shard"),
        P("shard", None),
        P(),
        P("member", None),
        P("member", "shard"),
        P("member", "shard"),
        P("member", None),
        P("member"),
    )
    return jax.shard_map(
        local,
        mesh=mesh,
        in_specs=placed,
        out_specs=(P(("member", "shard"), None), P("member", "shard"), P("shard", "member")),
        check_vma=False,
    )
```

time: 116 us -> 88.4 us (0.76)
  local copies, waits for them, and re-layouts: 22.9 us -> 7.49 us
  waiting for transfers between devices: 41.2 us -> 28.7 us
  matrix products: 9.35 us -> 0 us
  Pallas kernels: 16 us -> 25.2 us
  starting transfers between devices: 19.9 us -> 24.7 us
  other arithmetic: 4.69 us -> 1.2 us
    unnamed x60 -> x16, local copies, waits for them, and re-layouts: 22 us -> 6.79 us
    ppermute x26 -> x29, waiting for transfers between devices: 36.9 us -> 25 us  [swap(): return lax.ppermute(array, 'shard', [(i, i ^ bits) for i in range(devices)])]
    dot_general x2 -> x0, matrix products: 9.35 us -> none  [outer(): lax.dot_general(*sides, (((0,), (0,)), ((), ())), preferred_element_type=...]
    pallas_call x4 -> x11, Pallas kernels: 16 us -> 25.2 us  [the longest x4 11.9 us: chunk(): pl.pallas_call(functools.partial(chunk_kernel, k, rows, columns), out_sha...]
    ppermute x26 -> x29, starting transfers between devices: 18.4 us -> 23.1 us  [swap(): return lax.ppermute(array, 'shard', [(i, i ^ bits) for i in range(devices)])]
    convert_element_type x7 -> x4, other arithmetic: 3.15 us -> 0.11 us  [the longest x1 0.03 us: local(): (sum2[:, parts[1]] + onward.astype(jnp.float32)).astype(jnp.bfloat16)]
  transfers between devices with their start and end apart: 27 -> 30, of which waited for: 11 -> 13; matrix products, arithmetic and copies ran while one was open for 15% -> 1% of each run, Pallas kernels for 6% -> 29%
where the time goes in v3:
time: 88.4 us; the launch traced here: 88.2 us
  waiting for transfers between devices  28.7 us (32%)
  Pallas kernels  25.2 us (29%)
  starting transfers between devices  24.7 us (28%)
  local copies, waits for them, and re-layouts  7.49 us (8%)
  other arithmetic  1.2 us (1%)
    ppermute x29, waiting for transfers between devices, swap(): return lax.ppermute(array, 'shard', [(i, i ^ bits) for i in range(devices)])  25 us
    ppermute x29, starting transfers between devices, swap(): return lax.ppermute(array, 'shard', [(i, i ^ bits) for i in range(devices)])  23.1 us
    pallas_call x4, Pallas kernels, chunk(): pl.pallas_call(functools.partial(chunk_kernel, k, rows, columns), out_sha...  11.9 us
    pallas_call x2, Pallas kernels, update(): pl.pallas_call(functools.partial(update_kernel, fit_rows, groups, hidden)...  11.2 us
    unnamed x16, local copies, waits for them, and re-layouts  6.79 us
    ppermute x1, waiting for transfers between devices, local(): lax.ppermute(pack, 'member', [(i, i ^ bits) for i in range(groups)])  3.69 us
  transfers between devices with their start and end apart: 30, of which 13 were waited for; matrix products, arithmetic and copies ran while one was open for 1% of the time, Pallas kernels for 29%

profile of v3, /device:TPU:0, one launch (start us, length us, event | category | flops | bytes accessed | tf_op | source)
XLA Modules:
  0.0 88.2 jit_solution(15820937994216812607)
XLA Ops:
  0.6 3.1 %collective-permute-start.1 = (bf16[32,4096]{1,0:T(8,128)(2,1)}, bf16[32,4096]{1,0:T(8,128)(2,1)S(1)}, u32[]{:S(2)}, u32[]{:S(2)}) collective-permute-start(bf16[32,4096]{1,0:T(8,128)(2,1)} %refs_0_.2), channel_id=1, source_target_pairs={{0,4},{1,5},{2,6},{3,7},{4,0},{5,1},{6,2},{7,3},{8,12},{9,13},{10,... | collective-permute-start | bytes 786440 | tf_op jit(solution)/shard_map/ppermute | solution.py:235
  3.7 1.5 %collective-permute-start.2 = (bf16[32,4096]{1,0:T(8,128)(2,1)}, bf16[32,4096]{1,0:T(8,128)(2,1)S(1)}, u32[]{:S(2)}, u32[]{:S(2)}) collective-permute-start(bf16[32,4096]{1,0:T(8,128)(2,1)} %refs_0_.2), channel_id=1, source_target_pairs={{0,2},{1,3},{2,0},{3,1},{4,6},{5,7},{6,4},{7,5},{8,10},{9,11},{10,... | collective-permute-start | bytes 786440 | tf_op jit(solution)/shard_map/ppermute | solution.py:235
  5.2 2.6 %collective-permute-start = (bf16[32,4096]{1,0:T(8,128)(2,1)}, bf16[32,4096]{1,0:T(8,128)(2,1)S(1)}, u32[]{:S(2)}, u32[]{:S(2)}) collective-permute-start(bf16[32,4096]{1,0:T(8,128)(2,1)} %refs_0_.2), channel_id=1, source_target_pairs={{0,8},{1,9},{2,10},{3,11},{4,12},{5,13},{6,14},{7,15},{8,0},{9,1},... | collective-permute-start | bytes 786440 | tf_op jit(solution)/shard_map/ppermute | solution.py:235
  7.8 0.7 broadcast_in_dim.3.refs_4_
  8.6 3.4 %copy-done = bf16[4096,1024]{1,0:T(8,128)(2,1)S(1)} copy-done((bf16[4096,1024]{1,0:T(8,128)(2,1)S(1)}, bf16[4096,1024]{1,0:T(8,128)(2,1)}, u32[]{:S(2)}) %copy-start) | copy-done | bytes 8388632
  11.9 3.4 %copy-done.1 = bf16[1024,4096]{1,0:T(8,128)(2,1)S(1)} copy-done((bf16[1024,4096]{1,0:T(8,128)(2,1)S(1)}, bf16[1024,4096]{1,0:T(8,128)(2,1)}, u32[]{:S(2)}) %copy-start.1) | copy-done | bytes 8388632
  15.3 1.1 %shard_map.112 = (bf16[4096,1024]{1,0:T(8,128)(2,1)S(1)}, bf16[1024,4096]{1,0:T(8,128)(2,1)S(1)}) custom-call(bf16[4096,1024]{1,0:T(8,128)(2,1)S(1)} %copy-done, bf16[1024,4096]{1,0:T(8,128)(2,1)S(1)} %copy-done.1), custom_call_target="tpu_custom_call" | custom-call | bytes 16777216 | tf_op jit(solution)/shard_map/pallas_call | solution.py:160
  16.5 0.6 collective-permute-start.4
  17.1 0.5 collective-permute-start.6
  17.6 0.6 shard_map.113.refs_0_
  18.2 1.6 %collective-permute-start.7 = (bf16[8,10368]{1,0:T(8,128)(2,1)S(1)}, bf16[8,10368]{1,0:T(8,128)(2,1)S(1)}, u32[]{:S(2)}, u32[]{:S(2)}) collective-permute-start(bf16[8,10368]{1,0:T(8,128)(2,1)S(1)} %shard_map.113.refs_0_), channel_id=1, source_target_pairs={{0,16},{16,0},{1,17},{17,1},{2,18},{18,2},{3,19},{19,3},{4,20},{20... | collective-permute-start | bytes 497672 | tf_op jit(solution)/shard_map/ppermute | solution.py:270
  19.7 1.0 %collective-permute-done.refs_0_ = bf16[32,4096]{1,0:T(8,128)(2,1)S(1)} collective-permute-done((bf16[32,4096]{1,0:T(8,128)(2,1)}, bf16[32,4096]{1,0:T(8,128)(2,1)S(1)}, u32[]{:S(2)}, u32[]{:S(2)}) %collective-permute-start) | collective-permute-done | bytes 262176 | tf_op jit(solution)/shard_map/ppermute | solution.py:235
  20.7 3.7 %collective-permute-done.7.refs_1_ = bf16[8,10368]{1,0:T(8,128)(2,1)S(1)} collective-permute-done((bf16[8,10368]{1,0:T(8,128)(2,1)S(1)}, bf16[8,10368]{1,0:T(8,128)(2,1)S(1)}, u32[]{:S(2)}, u32[]{:S(2)}) %collective-permute-start.7) | collective-permute-done | bytes 165920 | tf_op jit(solution)/shard_map/ppermute | solution.py:270
  24.4 0.6 collective-permute-done.4.refs_1_
  25.0 0.5 collective-permute-start.8
  25.6 1.0 %collective-permute-start.9 = (bf16[32,4096]{1,0:T(8,128)(2,1)S(1)}, bf16[32,4096]{1,0:T(8,128)(2,1)S(1)}, u32[]{:S(2)}, u32[]{:S(2)}) collective-permute-start(bf16[32,4096]{1,0:T(8,128)(2,1)S(1)} %collective-permute-done.refs_0_), channel_id=1, source_target_pairs={{0,2},{1,3},{2,0},{3,1},{4,6},{5,7},{6,4},{7,5},{8,10},{9,11},{10,... | collective-permute-start | bytes 786440 | tf_op jit(solution)/shard_map/ppermute | solution.py:235
  26.6 5.6 %shard_map.114 = f32[2048,1024]{1,0:T(8,128)} custom-call(bf16[8,10368]{1,0:T(8,128)(2,1)S(1)} %shard_map.113.refs_0_, bf16[8,10368]{1,0:T(8,128)(2,1)S(1)} %collective-permute-done.7.refs_1_), custom_call_target="tpu_custom_call" | custom-call | bytes 16777216 | tf_op jit(solution)/shard_map/pallas_call | solution.py:209
  32.2 3.0 %shard_map.115 = (bf16[64,4096]{1,0:T(8,128)(2,1)S(1)}, bf16[64,4096]{1,0:T(8,128)(2,1)S(1)}) custom-call(bf16[32,4096]{1,0:T(8,128)(2,1)S(1)} %copy-done.6, bf16[32,4096]{1,0:T(8,128)(2,1)S(1)} %collective-permute-done.2.refs_1_, bf16[32,4096]{1,0:T(8,128)(2,1)S(1)} %collective-permute-done.3.refs_2_, bf16[32,4096]{1,0:T(8,128)(2,1)S(1)} %collective-permute-done.6.refs_3_, ...), custom_call_target="tpu_custom_call" | custom-call | flops 128 | bytes 128 | tf_op jit(solution)/shard_map/pallas_call | solution.py:84
  35.2 0.6 collective-permute-start.14
  35.8 1.0 %collective-permute-start.12 = (bf16[32,4096]{1,0:T(8,128)(2,1)S(1)}, bf16[32,4096]{1,0:T(8,128)(2,1)S(1)}, u32[]{:S(2)}, u32[]{:S(2)}) collective-permute-start(bf16[32,4096]{1,0:T(8,128)(2,1)S(1)} %collective-permute-done.8.refs_0_), channel_id=1, source_target_pairs={{0,2},{1,3},{2,0},{3,1},{4,6},{5,7},{6,4},{7,5},{8,10},{9,11},{10,... | collective-permute-start | bytes 786440 | tf_op jit(solution)/shard_map/ppermute | solution.py:235
  36.8 3.0 %shard_map.116 = (bf16[64,4096]{1,0:T(8,128)(2,1)S(1)}, bf16[64,4096]{1,0:T(8,128)(2,1)S(1)}) custom-call(bf16[32,4096]{1,0:T(8,128)(2,1)S(1)} %collective-permute-done.1.refs_0_, bf16[32,4096]{1,0:T(8,128)(2,1)S(1)} %collective-permute-done.4.refs_1_, bf16[32,4096]{1,0:T(8,128)(2,1)S(1)} %collective-permute-done.5.refs_2_, ...), custom_call_target="tpu_custom_call" | custom-call | flops 128 | bytes 128 | tf_op jit(solution)/shard_map/pallas_call | solution.py:84
  39.8 3.0 %shard_map.117 = (bf16[64,4096]{1,0:T(8,128)(2,1)S(1)}, bf16[64,4096]{1,0:T(8,128)(2,1)S(1)}) custom-call(bf16[32,4096]{1,0:T(8,128)(2,1)S(1)} %collective-permute-done.refs_0_, bf16[32,4096]{1,0:T(8,128)(2,1)S(1)} %collective-permute-done.9.refs_1_, bf16[32,4096]{1,0:T(8,128)(2,1)S(1)} %collective-permute-done.10.refs_2_, ...), custom_call_target="tpu_custom_call" | custom-call | flops 128 | bytes 128 | tf_op jit(solution)/shard_map/pallas_call | solution.py:84
  42.8 1.3 %collective-permute-done.12.refs_1_ = bf16[32,4096]{1,0:T(8,128)(2,1)S(1)} collective-permute-done((bf16[32,4096]{1,0:T(8,128)(2,1)S(1)}, bf16[32,4096]{1,0:T(8,128)(2,1)S(1)}, u32[]{:S(2)}, u32[]{:S(2)}) %collective-permute-start.12) | collective-permute-done | bytes 262176 | tf_op jit(solution)/shard_map/ppermute | solution.py:235
  44.1 0.5 collective-permute-start.15
  44.6 1.4 %collective-permute-done.16.arrived = bf16[64,4096]{1,0:T(8,128)(2,1)S(1)} collective-permute-done((bf16[64,4096]{1,0:T(8,128)(2,1)S(1)}, bf16[64,4096]{1,0:T(8,128)(2,1)S(1)}, u32[]{:S(2)}, u32[]{:S(2)}) %collective-permute-start.16) | collective-permute-done | bytes 524320 | tf_op jit(solution)/shard_map/ppermute | solution.py:235
  46.0 0.1 shard_map.119
  46.1 0.6 collective-permute-done.15.arrived
  46.9 1.1 %collective-permute-start.17 = (bf16[32,4096]{1,0:T(8,128)(2,1)S(1)}, bf16[32,4096]{1,0:T(8,128)(2,1)S(1)}, u32[]{:S(2)}, u32[]{:S(2)}) collective-permute-start(bf16[32,4096]{1,0:T(8,128)(2,1)S(1)} %get-tuple-element.115), channel_id=1, source_target_pairs={{0,2},{1,3},{2,0},{3,1},{4,6},{5,7},{6,4},{7,5},{8,10},{9,11},{10,... | collective-permute-start | bytes 786440 | tf_op jit(solution)/shard_map/ppermute | solution.py:235
  48.0 1.6 %collective-permute-start.18 = (bf16[32,4096]{1,0:T(8,128)(2,1)S(1)}, bf16[32,4096]{1,0:T(8,128)(2,1)S(1)}, u32[]{:S(2)}, u32[]{:S(2)}) collective-permute-start(bf16[32,4096]{1,0:T(8,128)(2,1)S(1)} %get-tuple-element.116), channel_id=1, source_target_pairs={{0,4},{1,5},{2,6},{3,7},{4,0},{5,1},{6,2},{7,3},{8,12},{9,13},{10,... | collective-permute-start | bytes 786440 | tf_op jit(solution)/shard_map/ppermute | solution.py:235
  49.5 3.0 %shard_map.120 = (bf16[64,4096]{1,0:T(8,128)(2,1)S(1)}, bf16[64,4096]{1,0:T(8,128)(2,1)S(1)}) custom-call(bf16[32,4096]{1,0:T(8,128)(2,1)S(1)} %collective-permute-done.8.refs_0_, bf16[32,4096]{1,0:T(8,128)(2,1)S(1)} %collective-permute-done.12.refs_1_, bf16[32,4096]{1,0:T(8,128)(2,1)S(1)} %collective-permute-done.13.refs_2_, ...), custom_call_target="tpu_custom_call" | custom-call | flops 128 | bytes 128 | tf_op jit(solution)/shard_map/pallas_call | solution.py:84
  52.5 2.7 %collective-permute-done.17 = bf16[32,4096]{1,0:T(8,128)(2,1)S(1)} collective-permute-done((bf16[32,4096]{1,0:T(8,128)(2,1)S(1)}, bf16[32,4096]{1,0:T(8,128)(2,1)S(1)}, u32[]{:S(2)}, u32[]{:S(2)}) %collective-permute-start.17) | collective-permute-done | bytes 262176 | tf_op jit(solution)/shard_map/ppermute | solution.py:235
  55.3 0.8 collective-permute-done.18
  56.0 0.5 collective-permute-start.23
  56.5 1.6 %collective-permute-start.22 = (bf16[32,4096]{1,0:T(8,128)(2,1)S(1)}, bf16[32,4096]{1,0:T(8,128)(2,1)S(1)}, u32[]{:S(2)}, u32[]{:S(2)}) collective-permute-start(bf16[32,4096]{1,0:T(8,128)(2,1)S(1)} %get-tuple-element.129), channel_id=1, source_target_pairs={{0,4},{1,5},{2,6},{3,7},{4,0},{5,1},{6,2},{7,3},{8,12},{9,13},{10,... | collective-permute-start | bytes 786440 | tf_op jit(solution)/shard_map/ppermute | solution.py:235
  58.2 1.1 %collective-permute-start.21 = (bf16[32,2048]{1,0:T(8,128)(2,1)S(1)}, bf16[32,2048]{1,0:T(8,128)(2,1)S(1)}, u32[]{:S(2)}, u32[]{:S(2)}) collective-permute-start(bf16[32,2048]{1,0:T(8,128)(2,1)S(1)} %get-tuple-element.127), channel_id=1, source_target_pairs={{0,2},{1,3},{2,0},{3,1},{4,6},{5,7},{6,4},{7,5},{8,10},{9,11},{10,... | collective-permute-start | bytes 393224 | tf_op jit(solution)/shard_map/ppermute | solution.py:235
  59.3 5.5 %collective-permute-done.22 = bf16[32,4096]{1,0:T(8,128)(2,1)S(1)} collective-permute-done((bf16[32,4096]{1,0:T(8,128)(2,1)S(1)}, bf16[32,4096]{1,0:T(8,128)(2,1)S(1)}, u32[]{:S(2)}, u32[]{:S(2)}) %collective-permute-start.22) | collective-permute-done | bytes 262176 | tf_op jit(solution)/shard_map/ppermute | solution.py:235
  64.8 1.6 %collective-permute-start.24 = (bf16[32,2048]{1,0:T(8,128)(2,1)S(1)}, bf16[32,2048]{1,0:T(8,128)(2,1)S(1)}, u32[]{:S(2)}, u32[]{:S(2)}) collective-permute-start(bf16[32,2048]{1,0:T(8,128)(2,1)S(1)} %add_convert_fusion.3), channel_id=1, source_target_pairs={{0,4},{1,5},{2,6},{3,7},{4,0},{5,1},{6,2},{7,3},{8,12},{9,13},{10,... | collective-permute-start | bytes 393224 | tf_op jit(solution)/shard_map/ppermute | solution.py:235
  66.4 1.0 %collective-permute-start.25 = (bf16[32,2048]{1,0:T(8,128)(2,1)S(1)}, bf16[32,2048]{1,0:T(8,128)(2,1)S(1)}, u32[]{:S(2)}, u32[]{:S(2)}) collective-permute-start(bf16[32,2048]{1,0:T(8,128)(2,1)S(1)} %get-tuple-element.132), channel_id=1, source_target_pairs={{0,2},{1,3},{2,0},{3,1},{4,6},{5,7},{6,4},{7,5},{8,10},{9,11},{10,... | collective-permute-start | bytes 393224 | tf_op jit(solution)/shard_map/ppermute | solution.py:235
  67.7 2.1 %collective-permute-done.24 = bf16[32,2048]{1,0:T(8,128)(2,1)S(1)} collective-permute-done((bf16[32,2048]{1,0:T(8,128)(2,1)S(1)}, bf16[32,2048]{1,0:T(8,128)(2,1)S(1)}, u32[]{:S(2)}, u32[]{:S(2)}) %collective-permute-start.24) | collective-permute-done | bytes 131104 | tf_op jit(solution)/shard_map/ppermute | solution.py:235
  69.8 1.6 %collective-permute-done.25 = bf16[32,2048]{1,0:T(8,128)(2,1)S(1)} collective-permute-done((bf16[32,2048]{1,0:T(8,128)(2,1)S(1)}, bf16[32,2048]{1,0:T(8,128)(2,1)S(1)}, u32[]{:S(2)}, u32[]{:S(2)}) %collective-permute-start.25) | collective-permute-done | bytes 131104 | tf_op jit(solution)/shard_map/ppermute | solution.py:235
  71.4 0.5 collective-permute-start.27
  71.9 1.0 %collective-permute-start.28 = (bf16[32,4096]{1,0:T(8,128)(2,1)S(1)}, bf16[32,4096]{1,0:T(8,128)(2,1)S(1)}, u32[]{:S(2)}, u32[]{:S(2)}) collective-permute-start(bf16[32,4096]{1,0:T(8,128)(2,1)S(1)} %slice_add_fusion), channel_id=1, source_target_pairs={{0,2},{1,3},{2,0},{3,1},{4,6},{5,7},{6,4},{7,5},{8,10},{9,11},{10,... | collective-permute-start | bytes 786440 | tf_op jit(solution)/shard_map/ppermute | solution.py:235
  73.0 0.4 collective-permute-start.26
  73.4 5.6 %shard_map.122 = f32[1024,2048]{1,0:T(8,128)} custom-call(bf16[8,10368]{1,0:T(8,128)(2,1)S(1)} %shard_map.113.refs_0_, bf16[8,10368]{1,0:T(8,128)(2,1)S(1)} %collective-permute-done.7.refs_1_), custom_call_target="tpu_custom_call" | custom-call | bytes 16777216 | tf_op jit(solution)/shard_map/pallas_call | solution.py:209
  79.0 1.8 %collective-permute-done.26 = bf16[32,2048]{1,0:T(8,128)(2,1)S(1)} collective-permute-done((bf16[32,2048]{1,0:T(8,128)(2,1)S(1)}, bf16[32,2048]{1,0:T(8,128)(2,1)S(1)}, u32[]{:S(2)}, u32[]{:S(2)}) %collective-permute-start.26) | collective-permute-done | bytes 131104 | tf_op jit(solution)/shard_map/ppermute | solution.py:235
  80.9 0.8 collective-permute-start.29
  81.8 5.7 %collective-permute-done.29 = bf16[32,2048]{1,0:T(8,128)(2,1)S(1)} collective-permute-done((bf16[32,2048]{1,0:T(8,128)(2,1)S(1)}, bf16[32,2048]{1,0:T(8,128)(2,1)S(1)}, u32[]{:S(2)}, u32[]{:S(2)}) %collective-permute-start.29) | collective-permute-done | bytes 131104 | tf_op jit(solution)/shard_map/ppermute | solution.py:235
  87.5 0.7 pad_maximum_fusion
  (50 shorter events, 0.8 us)
Async XLA Ops:
  0.6 15.9 %collective-permute-start.1 = (bf16[32,4096]{1,0:T(8,128)(2,1)}, bf16[32,4096]{1,0:T(8,128)(2,1)S(1)}, u32[]{:S(2)}, u32[]{:S(2)}) collective-permute-start(bf16[32,4096]{1,0:T(8,128)(2,1)} %refs_0_.2), channel_id=1, source_target_pairs={{0,4},{1,5},{2,6},{3,7},{4,0},{5,1},{6,2},{7,3},{8,12},{9,13},{10,... | collective-permute-start | bytes 786440 | tf_op jit(solution)/shard_map/ppermute | solution.py:235
  3.7 12.8 %collective-permute-start.2 = (bf16[32,4096]{1,0:T(8,128)(2,1)}, bf16[32,4096]{1,0:T(8,128)(2,1)S(1)}, u32[]{:S(2)}, u32[]{:S(2)}) collective-permute-start(bf16[32,4096]{1,0:T(8,128)(2,1)} %refs_0_.2), channel_id=1, source_target_pairs={{0,2},{1,3},{2,0},{3,1},{4,6},{5,7},{6,4},{7,5},{8,10},{9,11},{10,... | collective-permute-start | bytes 786440 | tf_op jit(solution)/shard_map/ppermute | solution.py:235
  5.2 11.3 %collective-permute-start.3 = (bf16[32,4096]{1,0:T(8,128)(2,1)}, bf16[32,4096]{1,0:T(8,128)(2,1)S(1)}, u32[]{:S(2)}, u32[]{:S(2)}) collective-permute-start(bf16[32,4096]{1,0:T(8,128)(2,1)} %refs_0_.2), channel_id=1, source_target_pairs={{0,1},{1,0},{2,3},{3,2},{4,5},{5,4},{6,7},{7,6},{8,9},{9,8},{10,11... | collective-permute-start | bytes 786440 | tf_op jit(solution)/shard_map/ppermute | solution.py:235
  5.2 15.5 %collective-permute-start = (bf16[32,4096]{1,0:T(8,128)(2,1)}, bf16[32,4096]{1,0:T(8,128)(2,1)S(1)}, u32[]{:S(2)}, u32[]{:S(2)}) collective-permute-start(bf16[32,4096]{1,0:T(8,128)(2,1)} %refs_0_.2), channel_id=1, source_target_pairs={{0,8},{1,9},{2,10},{3,11},{4,12},{5,13},{6,14},{7,15},{8,0},{9,1},... | collective-permute-start | bytes 786440 | tf_op jit(solution)/shard_map/ppermute | solution.py:235
  8.5 3.4 %copy-start = (bf16[4096,1024]{1,0:T(8,128)(2,1)S(1)}, bf16[4096,1024]{1,0:T(8,128)(2,1)}, u32[]{:S(2)}) copy-start(bf16[4096,1024]{1,0:T(8,128)(2,1)} %refs_0_) | copy-start | bytes 25165828
  11.9 3.4 %copy-start.1 = (bf16[1024,4096]{1,0:T(8,128)(2,1)S(1)}, bf16[1024,4096]{1,0:T(8,128)(2,1)}, u32[]{:S(2)}) copy-start(bf16[1024,4096]{1,0:T(8,128)(2,1)} %refs_1_.1) | copy-start | bytes 25165828
  15.3 2.3 %copy-start.2 = (bf16[8,4096]{1,0:T(8,128)(2,1)S(1)}, bf16[8,4096]{1,0:T(8,128)(2,1)}, u32[]{:S(2)}) copy-start(bf16[8,4096]{1,0:T(8,128)(2,1)} %refs_5_.7) | copy-start | bytes 196612
  15.3 2.3 %copy-start.3 = (bf16[8,4096]{1,0:T(8,128)(2,1)S(1)}, bf16[8,4096]{1,0:T(8,128)(2,1)}, u32[]{:S(2)}) copy-start(bf16[8,4096]{1,0:T(8,128)(2,1)} %refs_8_.7) | copy-start | bytes 196612
  15.3 2.3 %copy-start.4 = (bf16[8,1024]{1,0:T(8,128)(2,1)S(1)}, bf16[8,1024]{1,0:T(8,128)(2,1)}, u32[]{:S(2)}) copy-start(bf16[8,1024]{1,0:T(8,128)(2,1)} %refs_6_.7) | copy-start | bytes 49156
  15.3 2.3 %copy-start.5 = (bf16[8,1024]{1,0:T(8,128)(2,1)S(1)}, bf16[8,1024]{1,0:T(8,128)(2,1)}, u32[]{:S(2)}) copy-start(bf16[8,1024]{1,0:T(8,128)(2,1)} %refs_7_.7) | copy-start | bytes 49156
  15.3 2.3 %copy-start.7 = (s32[8]{0:T(128)S(1)}, s32[8]{0:T(128)}, u32[]{:S(2)}) copy-start(s32[8]{0:T(128)} %ranks.1) | copy-start | bytes 100
  16.5 15.7 %copy-start.6 = (bf16[32,4096]{1,0:T(8,128)(2,1)S(1)}, bf16[32,4096]{1,0:T(8,128)(2,1)}, u32[]{:S(2)}) copy-start(bf16[32,4096]{1,0:T(8,128)(2,1)} %refs_0_.2) | copy-start | bytes 786436
  16.5 8.5 %collective-permute-start.4 = (bf16[32,4096]{1,0:T(8,128)(2,1)S(1)}, bf16[32,4096]{1,0:T(8,128)(2,1)S(1)}, u32[]{:S(2)}, u32[]{:S(2)}) collective-permute-start(bf16[32,4096]{1,0:T(8,128)(2,1)S(1)} %collective-permute-done.1.refs_0_), channel_id=1, source_target_pairs={{0,2},{1,3},{2,0},{3,1},{4,6},{5,7},{6,4},{7,5},{8,10},{9,11},{10,... | collective-permute-start | bytes 786440 | tf_op jit(solution)/shard_map/ppermute | solution.py:235
  17.1 7.9 %collective-permute-start.5 = (bf16[32,4096]{1,0:T(8,128)(2,1)S(1)}, bf16[32,4096]{1,0:T(8,128)(2,1)S(1)}, u32[]{:S(2)}, u32[]{:S(2)}) collective-permute-start(bf16[32,4096]{1,0:T(8,128)(2,1)S(1)} %collective-permute-done.1.refs_0_), channel_id=1, source_target_pairs={{0,1},{1,0},{2,3},{3,2},{4,5},{5,4},{6,7},{7,6},{8,9},{9,8},{10,11... | collective-permute-start | bytes 786440 | tf_op jit(solution)/shard_map/ppermute | solution.py:235
  17.1 7.9 %collective-permute-start.6 = (bf16[32,4096]{1,0:T(8,128)(2,1)S(1)}, bf16[32,4096]{1,0:T(8,128)(2,1)S(1)}, u32[]{:S(2)}, u32[]{:S(2)}) collective-permute-start(bf16[32,4096]{1,0:T(8,128)(2,1)S(1)} %collective-permute-done.2.refs_1_), channel_id=1, source_target_pairs={{0,1},{1,0},{2,3},{3,2},{4,5},{5,4},{6,7},{7,6},{8,9},{9,8},{10,11... | collective-permute-start | bytes 786440 | tf_op jit(solution)/shard_map/ppermute | solution.py:235
  18.2 6.2 %collective-permute-start.7 = (bf16[8,10368]{1,0:T(8,128)(2,1)S(1)}, bf16[8,10368]{1,0:T(8,128)(2,1)S(1)}, u32[]{:S(2)}, u32[]{:S(2)}) collective-permute-start(bf16[8,10368]{1,0:T(8,128)(2,1)S(1)} %shard_map.113.refs_0_), channel_id=1, source_target_pairs={{0,16},{16,0},{1,17},{17,1},{2,18},{18,2},{3,19},{19,3},{4,20},{20... | collective-permute-start | bytes 497672 | tf_op jit(solution)/shard_map/ppermute | solution.py:270
  25.0 10.1 %collective-permute-start.10 = (bf16[32,4096]{1,0:T(8,128)(2,1)S(1)}, bf16[32,4096]{1,0:T(8,128)(2,1)S(1)}, u32[]{:S(2)}, u32[]{:S(2)}) collective-permute-start(bf16[32,4096]{1,0:T(8,128)(2,1)S(1)} %collective-permute-done.refs_0_), channel_id=1, source_target_pairs={{0,1},{1,0},{2,3},{3,2},{4,5},{5,4},{6,7},{7,6},{8,9},{9,8},{10,11... | collective-permute-start | bytes 786440 | tf_op jit(solution)/shard_map/ppermute | solution.py:235
  25.0 10.1 %collective-permute-start.8 = (bf16[32,4096]{1,0:T(8,128)(2,1)S(1)}, bf16[32,4096]{1,0:T(8,128)(2,1)S(1)}, u32[]{:S(2)}, u32[]{:S(2)}) collective-permute-start(bf16[32,4096]{1,0:T(8,128)(2,1)S(1)} %collective-permute-done.refs_0_), channel_id=1, source_target_pairs={{0,4},{1,5},{2,6},{3,7},{4,0},{5,1},{6,2},{7,3},{8,12},{9,13},{10,... | collective-permute-start | bytes 786440 | tf_op jit(solution)/shard_map/ppermute | solution.py:235
  25.6 9.6 %collective-permute-start.9 = (bf16[32,4096]{1,0:T(8,128)(2,1)S(1)}, bf16[32,4096]{1,0:T(8,128)(2,1)S(1)}, u32[]{:S(2)}, u32[]{:S(2)}) collective-permute-start(bf16[32,4096]{1,0:T(8,128)(2,1)S(1)} %collective-permute-done.refs_0_), channel_id=1, source_target_pairs={{0,2},{1,3},{2,0},{3,1},{4,6},{5,7},{6,4},{7,5},{8,10},{9,11},{10,... | collective-permute-start | bytes 786440 | tf_op jit(solution)/shard_map/ppermute | solution.py:235
  26.6 8.7 %collective-permute-start.11 = (bf16[32,4096]{1,0:T(8,128)(2,1)S(1)}, bf16[32,4096]{1,0:T(8,128)(2,1)S(1)}, u32[]{:S(2)}, u32[]{:S(2)}) collective-permute-start(bf16[32,4096]{1,0:T(8,128)(2,1)S(1)} %collective-permute-done.4.refs_1_), channel_id=1, source_target_pairs={{0,1},{1,0},{2,3},{3,2},{4,5},{5,4},{6,7},{7,6},{8,9},{9,8},{10,11... | collective-permute-start | bytes 786440 | tf_op jit(solution)/shard_map/ppermute | solution.py:235
  35.2 4.6 %collective-permute-start.14 = (bf16[32,4096]{1,0:T(8,128)(2,1)S(1)}, bf16[32,4096]{1,0:T(8,128)(2,1)S(1)}, u32[]{:S(2)}, u32[]{:S(2)}) collective-permute-start(bf16[32,4096]{1,0:T(8,128)(2,1)S(1)} %collective-permute-done.9.refs_1_), channel_id=1, source_target_pairs={{0,1},{1,0},{2,3},{3,2},{4,5},{5,4},{6,7},{7,6},{8,9},{9,8},{10,11... | collective-permute-start | bytes 786440 | tf_op jit(solution)/shard_map/ppermute | solution.py:235
  35.8 8.3 %collective-permute-start.12 = (bf16[32,4096]{1,0:T(8,128)(2,1)S(1)}, bf16[32,4096]{1,0:T(8,128)(2,1)S(1)}, u32[]{:S(2)}, u32[]{:S(2)}) collective-permute-start(bf16[32,4096]{1,0:T(8,128)(2,1)S(1)} %collective-permute-done.8.refs_0_), channel_id=1, source_target_pairs={{0,2},{1,3},{2,0},{3,1},{4,6},{5,7},{6,4},{7,5},{8,10},{9,11},{10,... | collective-permute-start | bytes 786440 | tf_op jit(solution)/shard_map/ppermute | solution.py:235
  36.8 7.3 %collective-permute-start.13 = (bf16[32,4096]{1,0:T(8,128)(2,1)S(1)}, bf16[32,4096]{1,0:T(8,128)(2,1)S(1)}, u32[]{:S(2)}, u32[]{:S(2)}) collective-permute-start(bf16[32,4096]{1,0:T(8,128)(2,1)S(1)} %collective-permute-done.8.refs_0_), channel_id=1, source_target_pairs={{0,1},{1,0},{2,3},{3,2},{4,5},{5,4},{6,7},{7,6},{8,9},{9,8},{10,11... | collective-permute-start | bytes 786440 | tf_op jit(solution)/shard_map/ppermute | solution.py:235
  44.1 1.9 %collective-permute-start.16 = (bf16[64,4096]{1,0:T(8,128)(2,1)S(1)}, bf16[64,4096]{1,0:T(8,128)(2,1)S(1)}, u32[]{:S(2)}, u32[]{:S(2)}) collective-permute-start(bf16[64,4096]{1,0:T(8,128)(2,1)S(1)} %get-tuple-element.112), channel_id=1, source_target_pairs={{0,1},{1,0},{2,3},{3,2},{4,5},{5,4},{6,7},{7,6},{8,9},{9,8},{10,11... | collective-permute-start | bytes 1572872 | tf_op jit(solution)/shard_map/ppermute | solution.py:235
  44.1 2.7 %collective-permute-start.15 = (bf16[64,4096]{1,0:T(8,128)(2,1)S(1)}, bf16[64,4096]{1,0:T(8,128)(2,1)S(1)}, u32[]{:S(2)}, u32[]{:S(2)}) collective-permute-start(bf16[64,4096]{1,0:T(8,128)(2,1)S(1)} %get-tuple-element.108), channel_id=1, source_target_pairs={{0,1},{1,0},{2,3},{3,2},{4,5},{5,4},{6,7},{7,6},{8,9},{9,8},{10,11... | collective-permute-start | bytes 1572872 | tf_op jit(solution)/shard_map/ppermute | solution.py:235
  44.6 4.9 %collective-permute-start.19 = (bf16[32,4096]{1,0:T(8,128)(2,1)S(1)}, bf16[32,4096]{1,0:T(8,128)(2,1)S(1)}, u32[]{:S(2)}, u32[]{:S(2)}) collective-permute-start(bf16[32,4096]{1,0:T(8,128)(2,1)S(1)} %collective-permute-done.12.refs_1_), channel_id=1, source_target_pairs={{0,1},{1,0},{2,3},{3,2},{4,5},{5,4},{6,7},{7,6},{8,9},{9,8},{10,11... | collective-permute-start | bytes 786440 | tf_op jit(solution)/shard_map/ppermute | solution.py:235
  46.9 8.4 %collective-permute-start.17 = (bf16[32,4096]{1,0:T(8,128)(2,1)S(1)}, bf16[32,4096]{1,0:T(8,128)(2,1)S(1)}, u32[]{:S(2)}, u32[]{:S(2)}) collective-permute-start(bf16[32,4096]{1,0:T(8,128)(2,1)S(1)} %get-tuple-element.115), channel_id=1, source_target_pairs={{0,2},{1,3},{2,0},{3,1},{4,6},{5,7},{6,4},{7,5},{8,10},{9,11},{10,... | collective-permute-start | bytes 786440 | tf_op jit(solution)/shard_map/ppermute | solution.py:235
  48.0 8.1 %collective-permute-start.18 = (bf16[32,4096]{1,0:T(8,128)(2,1)S(1)}, bf16[32,4096]{1,0:T(8,128)(2,1)S(1)}, u32[]{:S(2)}, u32[]{:S(2)}) collective-permute-start(bf16[32,4096]{1,0:T(8,128)(2,1)S(1)} %get-tuple-element.116), channel_id=1, source_target_pairs={{0,4},{1,5},{2,6},{3,7},{4,0},{5,1},{6,2},{7,3},{8,12},{9,13},{10,... | collective-permute-start | bytes 786440 | tf_op jit(solution)/shard_map/ppermute | solution.py:235
  56.0 2.1 %collective-permute-start.20 = (bf16[64,4096]{1,0:T(8,128)(2,1)S(1)}, bf16[64,4096]{1,0:T(8,128)(2,1)S(1)}, u32[]{:S(2)}, u32[]{:S(2)}) collective-permute-start(bf16[64,4096]{1,0:T(8,128)(2,1)S(1)} %get-tuple-element.125), channel_id=1, source_target_pairs={{0,1},{1,0},{2,3},{3,2},{4,5},{5,4},{6,7},{7,6},{8,9},{9,8},{10,11... | collective-permute-start | bytes 1572872 | tf_op jit(solution)/shard_map/ppermute | solution.py:235
  56.0 8.7 %collective-permute-start.23 = (bf16[64,4096]{1,0:T(8,128)(2,1)S(1)}, bf16[64,4096]{1,0:T(8,128)(2,1)S(1)}, u32[]{:S(2)}, u32[]{:S(2)}) collective-permute-start(bf16[64,4096]{1,0:T(8,128)(2,1)S(1)} %get-tuple-element.130), channel_id=1, source_target_pairs={{0,1},{1,0},{2,3},{3,2},{4,5},{5,4},{6,7},{7,6},{8,9},{9,8},{10,11... | collective-permute-start | bytes 1572872 | tf_op jit(solution)/shard_map/ppermute | solution.py:235
  56.5 8.2 %collective-permute-start.22 = (bf16[32,4096]{1,0:T(8,128)(2,1)S(1)}, bf16[32,4096]{1,0:T(8,128)(2,1)S(1)}, u32[]{:S(2)}, u32[]{:S(2)}) collective-permute-start(bf16[32,4096]{1,0:T(8,128)(2,1)S(1)} %get-tuple-element.129), channel_id=1, source_target_pairs={{0,4},{1,5},{2,6},{3,7},{4,0},{5,1},{6,2},{7,3},{8,12},{9,13},{10,... | collective-permute-start | bytes 786440 | tf_op jit(solution)/shard_map/ppermute | solution.py:235
  58.2 6.5 %collective-permute-start.21 = (bf16[32,2048]{1,0:T(8,128)(2,1)S(1)}, bf16[32,2048]{1,0:T(8,128)(2,1)S(1)}, u32[]{:S(2)}, u32[]{:S(2)}) collective-permute-start(bf16[32,2048]{1,0:T(8,128)(2,1)S(1)} %get-tuple-element.127), channel_id=1, source_target_pairs={{0,2},{1,3},{2,0},{3,1},{4,6},{5,7},{6,4},{7,5},{8,10},{9,11},{10,... | collective-permute-start | bytes 393224 | tf_op jit(solution)/shard_map/ppermute | solution.py:235
  64.8 5.0 %collective-permute-start.24 = (bf16[32,2048]{1,0:T(8,128)(2,1)S(1)}, bf16[32,2048]{1,0:T(8,128)(2,1)S(1)}, u32[]{:S(2)}, u32[]{:S(2)}) collective-permute-start(bf16[32,2048]{1,0:T(8,128)(2,1)S(1)} %add_convert_fusion.3), channel_id=1, source_target_pairs={{0,4},{1,5},{2,6},{3,7},{4,0},{5,1},{6,2},{7,3},{8,12},{9,13},{10,... | collective-permute-start | bytes 393224 | tf_op jit(solution)/shard_map/ppermute | solution.py:235
  66.4 5.0 %collective-permute-start.25 = (bf16[32,2048]{1,0:T(8,128)(2,1)S(1)}, bf16[32,2048]{1,0:T(8,128)(2,1)S(1)}, u32[]{:S(2)}, u32[]{:S(2)}) collective-permute-start(bf16[32,2048]{1,0:T(8,128)(2,1)S(1)} %get-tuple-element.132), channel_id=1, source_target_pairs={{0,2},{1,3},{2,0},{3,1},{4,6},{5,7},{6,4},{7,5},{8,10},{9,11},{10,... | collective-permute-start | bytes 393224 | tf_op jit(solution)/shard_map/ppermute | solution.py:235
  71.4 7.6 %collective-permute-start.27 = (bf16[32,2048]{1,0:T(8,128)(2,1)S(1)}, bf16[32,2048]{1,0:T(8,128)(2,1)S(1)}, u32[]{:S(2)}, u32[]{:S(2)}) collective-permute-start(bf16[32,2048]{1,0:T(8,128)(2,1)S(1)} %add_convert_fusion.1), channel_id=1, source_target_pairs={{0,4},{1,5},{2,6},{3,7},{4,0},{5,1},{6,2},{7,3},{8,12},{9,13},{10,... | collective-permute-start | bytes 393224 | tf_op jit(solution)/shard_map/ppermute | solution.py:235
  71.9 8.9 %collective-permute-start.28 = (bf16[32,4096]{1,0:T(8,128)(2,1)S(1)}, bf16[32,4096]{1,0:T(8,128)(2,1)S(1)}, u32[]{:S(2)}, u32[]{:S(2)}) collective-permute-start(bf16[32,4096]{1,0:T(8,128)(2,1)S(1)} %slice_add_fusion), channel_id=1, source_target_pairs={{0,2},{1,3},{2,0},{3,1},{4,6},{5,7},{6,4},{7,5},{8,10},{9,11},{10,... | collective-permute-start | bytes 786440 | tf_op jit(solution)/shard_map/ppermute | solution.py:235
  73.0 7.8 %collective-permute-start.26 = (bf16[32,2048]{1,0:T(8,128)(2,1)S(1)}, bf16[32,2048]{1,0:T(8,128)(2,1)S(1)}, u32[]{:S(2)}, u32[]{:S(2)}) collective-permute-start(bf16[32,2048]{1,0:T(8,128)(2,1)S(1)} %add_convert_fusion.2), channel_id=1, source_target_pairs={{0,8},{1,9},{2,10},{3,11},{4,12},{5,13},{6,14},{7,15},{8,0},{9,1},... | collective-permute-start | bytes 393224 | tf_op jit(solution)/shard_map/ppermute | solution.py:235
  80.9 6.5 %collective-permute-start.29 = (bf16[32,2048]{1,0:T(8,128)(2,1)S(1)}, bf16[32,2048]{1,0:T(8,128)(2,1)S(1)}, u32[]{:S(2)}, u32[]{:S(2)}) collective-permute-start(bf16[32,2048]{1,0:T(8,128)(2,1)S(1)} %add_convert_fusion), channel_id=1, source_target_pairs={{0,8},{1,9},{2,10},{3,11},{4,12},{5,13},{6,14},{7,15},{8,0},{9,1},... | collective-permute-start | bytes 393224 | tf_op jit(solution)/shard_map/ppermute | solution.py:235

commit v4 on v3

--- a/solution.py
+++ b/solution.py
@@ -14,6 +14,8 @@
 PLANES = 4
 CORES = 2
 STEP = 1024
+PARTS = 2
+PIECES = 4
 
 
 def chunk_kernel(k, rows, columns, *refs):
@@ -98,27 +100,28 @@
     )(*operands)
 
 
-def sum_kernel(rows, keep, arrived, mine, *terms):
+def sum_kernel(rows, keep, arrived, *outs):
     both = keep[...].astype(jnp.float32) + arrived[...].astype(jnp.float32)
-    mine[...] = both[:rows].astype(mine.dtype)
-    per = D // terms[0].shape[1]
-    for i, term in enumerate(terms):
-        j, at = i // per + 1, i % per * term.shape[1]
-        term[...] = both[j * rows : (j + 1) * rows, at : at + term.shape[1]].astype(jnp.bfloat16)
-
-
-def sum_cores(keep, arrived, columns, per, kind=jnp.float32):
+    at = 0
+    for out in outs:
+        block, start = at // D, at % D
+        out[...] = both[block * rows : (block + 1) * rows, start : start + out.shape[1]].astype(out.dtype)
+        at += out.shape[1]
+
+
+def sum_cores(keep, arrived, columns, kind, per):
     rows = keep.shape[0] // columns
-    terms = [jax.ShapeDtypeStruct((rows, D // per), jnp.bfloat16)] * ((columns - 1) * per)
-    mine, *terms = pl.pallas_call(
+    outs = [jax.ShapeDtypeStruct((rows, D // PARTS), kind)] * PARTS
+    outs += [jax.ShapeDtypeStruct((rows, D // per), jnp.bfloat16)] * ((columns - 1) * per)
+    sums = pl.pallas_call(
         functools.partial(sum_kernel, rows),
-        out_shape=[jax.ShapeDtypeStruct((rows, D), kind)] + terms,
+        out_shape=outs,
         in_specs=[pl.BlockSpec(memory_space=pltpu.VMEM)] * 2,
-        out_specs=[pl.BlockSpec(memory_space=pltpu.VMEM)] * (1 + len(terms)),
+        out_specs=[pl.BlockSpec(memory_space=pltpu.VMEM)] * len(outs),
         compiler_params=pltpu.CompilerParams(vmem_limit_bytes=8 * 1024 * 1024),
         cost_estimate=pl.CostEstimate(flops=rows, bytes_accessed=rows, transcendentals=0),
     )(keep, arrived)
-    return mine, [terms[i::per] for i in range(per)]
+    return sums[:PARTS], [sums[PARTS + part :: per] for part in range(per)]
 
 
 def pack_kernel(ranks, *refs):
@@ -164,12 +167,12 @@
         out_specs=[pl.BlockSpec(memory_space=pltpu.VMEM)] * len(arrays),
         scratch_shapes=[pltpu.SemaphoreType.DMA((len(arrays),))],
         compiler_params=pltpu.CompilerParams(vmem_limit_bytes=1024 * 1024),
-        cost_estimate=pl.CostEstimate(flops=0, bytes_accessed=size, transcendentals=0),
+        cost_estimate=pl.CostEstimate(flops=size // D, bytes_accessed=size // D, transcendentals=0),
     )(*arrays)
 
 
-def update_kernel(fit_rows, groups, hidden, *refs):
-    *packs, out, left, right = refs
+def update_kernel(fit_rows, piece, groups, hidden, count, *refs):
+    packs, out, right = refs[:count], refs[-2], refs[-1]
     part, rows = D // groups, out.shape[0]
 
     def columns(start, size):
@@ -188,34 +191,34 @@
     def thrice(array):
         return jnp.concatenate([array] * 3, 0).astype(jnp.bfloat16)
 
+    half = lax.axis_index("member") * part
+    step = (piece * pl.num_programs(0) + pl.program_id(0)) * rows
+
     @pl.when(pl.program_id(0) == 0)
     def _():
-        half = lax.axis_index("member") * part
-        if fit_rows:
-            left[...], right[...] = split(columns(half, part)), thrice(columns(2 * D, hidden))
-        else:
-            left[...], right[...] = thrice(columns(2 * D + hidden, hidden)), split(columns(D + half, part))
-
-    at = pl.ds(pl.multiple_of(pl.program_id(0) * rows, rows), rows)
-    out[...] = lax.dot_general(
-        left[:, at], right[...], (((0,), (0,)), ((), ())), preferred_element_type=jnp.float32
-    )
-
-
-def update(fit_rows, packs, groups, hidden):
+        right[...] = thrice(columns(2 * D, hidden)) if fit_rows else split(columns(D + half, part))
+
+    left = split(columns(half + step, rows)) if fit_rows else thrice(columns(2 * D + hidden + step, rows))
+    out[...] = lax.dot_general(left, right[...], (((0,), (0,)), ((), ())), preferred_element_type=jnp.float32)
+
+
+def update(fit_rows, packs, done, piece, groups, hidden):
     part = D // groups
     shape, rows = ((part, hidden), 256) if fit_rows else ((hidden, part), 128)
-    depth = 3 * packs[0].shape[0] * len(packs)
+    rows = min(rows, shape[0] // PIECES)
+    steps = shape[0] // rows // PIECES
+    done = [] if done is None else [done]
     return pl.pallas_call(
-        functools.partial(update_kernel, fit_rows, groups, hidden),
+        functools.partial(update_kernel, fit_rows, piece, groups, hidden, len(packs)),
         out_shape=jax.ShapeDtypeStruct(shape, jnp.float32),
-        grid=(shape[0] // rows,),
-        in_specs=[pl.BlockSpec(memory_space=pltpu.VMEM)] * len(packs),
-        out_specs=pl.BlockSpec((rows, shape[1]), lambda i: (i, 0)),
-        scratch_shapes=[pltpu.VMEM((depth, shape[0]), jnp.bfloat16), pltpu.VMEM((depth, shape[1]), jnp.bfloat16)],
+        grid=(steps,),
+        in_specs=[pl.BlockSpec(memory_space=pltpu.VMEM)] * len(packs) + [pl.BlockSpec(memory_space=pl.ANY)] * len(done),
+        out_specs=pl.BlockSpec((rows, shape[1]), lambda i: (piece * steps + i, 0)),
+        scratch_shapes=[pltpu.VMEM((3 * packs[0].shape[0] * len(packs), shape[1]), jnp.bfloat16)],
+        input_output_aliases={len(packs): 0} if done else {},
         compiler_params=pltpu.CompilerParams(vmem_limit_bytes=12 * 1024 * 1024),
-        cost_estimate=pl.CostEstimate(flops=0, bytes_accessed=8 * shape[0] * shape[1], transcendentals=0),
-    )(*packs)
+        cost_estimate=pl.CostEstimate(flops=rows, bytes_accessed=rows, transcendentals=0),
+    )(*packs, *done)
 
 
 def together(*values):
@@ -228,8 +231,7 @@
     devices, groups = lax.axis_size("shard"), lax.axis_size("member")
     columns = devices // (PLANES * CORES)
     rows, hidden = tokens.shape[0], key_weight.shape[1]
-    mix = shift_mix[None, :]
-    (key,) = load(key_weight)
+    parts = [slice(i * D // PARTS, (i + 1) * D // PARTS) for i in range(PARTS)]
 
     def swap(array, bits):
         return lax.ppermute(array, "shard", [(i, i ^ bits) for i in range(devices)])
@@ -237,85 +239,101 @@
     def over_z(array, k):
         return swap(array, k * columns * CORES)
 
-    def over_y(array, j):
-        return swap(array, j * CORES)
-
-    def over_cores(array):
-        return swap(array, 1)
+    def over_y(array):
+        return [swap(array, j * CORES) for j in range(1, columns)]
+
+    def over_cores(arrays):
+        return [swap(array, 1) for array in arrays]
+
+    def back_y(terms):
+        return [swap(term, j * CORES) for j, term in enumerate(terms, 1)]
+
+    def updates(fit_rows, packs, done, start, stop):
+        for piece in range(start, stop):
+            done = update(fit_rows, packs, done, piece, groups, hidden)
+        return done
+
+    def add(mine, arrived):
+        return functools.reduce(lambda total, part: total + part.astype(jnp.float32), arrived, mine)
+
+    def by_block(*blocks):
+        return [list(block) for block in zip(*blocks)]
+
+    def rounded(array):
+        return array.astype(jnp.bfloat16)
+
+    far, near, y0, c0 = over_z(tokens, 2), over_z(tokens, 1), over_y(tokens), over_cores([tokens])
+    mix, key = together(shift_mix[None, :], key_weight)
+    (key,) = load(key)
+    near, y0, c0, key, value = together(near, y0, c0, key, value_weight)
+
+    y1, cy0, c1 = over_y(near), over_cores(y0), over_cores([near])
+    (value,) = load(value)
+    far, y1, cy0, c1, key, value, left = together(far, y1, cy0, c1, key, value, key_left)
 
     def partial(k, own, other):
         return chunk(k, own, other, mix, key_left, key_right, value_left, value_right, key, value)
 
-    def all_y(block):
-        return [over_y(block, j) for j in range(1, columns)]
-
-    def all_cores(blocks):
-        return [over_cores(block) for block in blocks]
-
-    def exchange_y(terms):
-        return [over_y(term, j) for j, term in enumerate(terms, 1)]
-
-    def add(mine, arrived):
-        return functools.reduce(lambda total, part: total + part.astype(jnp.float32), arrived, mine)
-
-    near, far = over_z(tokens, 1), over_z(tokens, 2)
-    y0, c0 = all_y(tokens), over_cores(tokens)
-    mix, key, value = together(shift_mix[None, :], key_weight, value_weight)
-    key, value = load(key, value)
-    near, y0, c0, key, value, pack_of = together(near, y0, c0, key, value, key_left)
-
-    y1, c1, cy0 = all_y(near), over_cores(near), all_cores(y0)
-    pack = pack_members(pack_of, key_right, value_left, value_right, ranks)
+    pack = pack_members(left, key_right, value_left, value_right, ranks)
     packs = [pack] + [
         lax.ppermute(pack, "member", [(i, i ^ bits) for i in range(groups)]) for bits in range(1, groups)
     ]
-    far, y1, c1, cy0, packs = together(far, y1, c1, cy0, packs)
-
-    farthest, y2, c2, cy1 = over_z(far, 1), all_y(far), over_cores(far), all_cores(y1)
-    key_update = update(True, packs, groups, hidden)
-    own, key_update = together(tokens, key_update)
-    keep0, send0 = partial(0, [own] + y0, [c0] + cy0)
-    farthest, y2, c2, cy1, keep0, send0 = together(farthest, y2, c2, cy1, keep0, send0)
-
-    y3, c3, cy2 = all_y(farthest), over_cores(farthest), all_cores(y2)
-    keep1, send1 = partial(1, [near] + y1, [c1] + cy1)
+    farthest, y2, c2, cy1 = over_z(far, 1), over_y(far), over_cores([far]), over_cores(y1)
+    keep0, send0 = partial(0, [tokens] + y0, c0 + cy0)
+    farthest, y2, c2, cy1, keep0, send0, packs = together(farthest, y2, c2, cy1, keep0, send0, packs)
+
+    y3, c3, cy2 = over_y(farthest), over_cores([farthest]), over_cores(y2)
+    keep1, send1 = partial(1, [near] + y1, c1 + cy1)
     far, keep1 = together(far, keep1)
-    keep2, send2 = partial(2, [far] + y2, [c2] + cy2)
+    keep2, send2 = partial(2, [far] + y2, c2 + cy2)
     y3, c3, keep1, send1, keep2, send2 = together(y3, c3, keep1, send1, keep2, send2)
 
-    cy3 = all_cores(y3)
-    mine2, (terms2,) = sum_cores(keep2, over_cores(send2), columns, 1)
-    mine1, (terms1,) = sum_cores(keep1, over_cores(send1), columns, 1, jnp.bfloat16)
-    farthest, mine2, terms2, mine1, terms1 = together(farthest, mine2, terms2, mine1, terms1)
-    back2, mine1 = exchange_y(terms2), over_z(mine1, 1)
-    keep3, send3 = partial(3, [farthest] + y3, [c3] + cy3)
-    back2, mine1, terms1, send0, keep3, send3 = together(back2, mine1, terms1, send0, keep3, send3)
-
-    terms1, back0 = [over_z(term, 1) for term in terms1], over_cores(send0)
-    mine3, terms3 = sum_cores(keep3, over_cores(send3), columns, 2)
-    back3 = exchange_y(terms3[0])
-    back3, rest3, terms1, back0 = together(back3, terms3[1], terms1, back0)
-
-    half = D // 2
-    parts = (slice(0, half), slice(half, D))
-    onward = over_z(add(mine3[:, parts[0]], back3).astype(jnp.bfloat16), 1)
-    back3 = exchange_y(rest3)
+    cy3 = over_cores(y3)
+    mine2, terms2 = sum_cores(keep2, *over_cores([send2]), columns, jnp.float32, PARTS)
+    (other1,) = over_cores([send1])
+    farthest, mine2, terms2 = together(farthest, mine2, terms2)
+    back2a = back_y(terms2[0])
+    keep3, send3 = partial(3, [farthest] + y3, c3 + cy3)
+    back2a, other1, send0, keep3, send3 = together(back2a, other1, send0, keep3, send3)
+
+    mine1, (terms1,) = sum_cores(keep1, other1, columns, jnp.bfloat16, 1)
+    beside1 = [over_z(term, 1) for term in terms1]
+    (back0,) = over_cores([send0])
+    mine3, terms3 = sum_cores(keep3, *over_cores([send3]), columns, jnp.float32, PARTS)
+    packs, mine3, terms3 = together(packs, mine3, terms3)
+    back3 = back_y(terms3[0])
+    key_update = updates(True, packs, None, 0, 2)
+    back3, beside1, back0, rest3, key_update, mine1 = together(
+        back3, beside1, back0, terms3[1], key_update, mine1
+    )
+
+    onward, mine1a = over_z(rounded(add(mine3[0], back3)), 1), over_z(mine1[0], 1)
+    back3 = back_y(rest3)
     both = keep0.astype(jnp.float32) + back0.astype(jnp.float32)
-    mine0 = add(both[:rows], [mine1])
-    terms0 = [add(both[j * rows : (j + 1) * rows], [term]) for j, term in enumerate(terms1, 1)]
-    sum2 = add(mine2, back2)
-    onward, back3, mine0, terms0, sum2, packs = together(onward, back3, mine0, terms0, sum2, packs)
-
-    first = over_z((sum2[:, parts[0]] + onward.astype(jnp.float32)).astype(jnp.bfloat16), 2)
-    onward = over_z(add(mine3[:, parts[1]], back3).astype(jnp.bfloat16), 1)
-    back0 = exchange_y([term.astype(jnp.bfloat16) for term in terms0])
-    value_update = update(False, packs, groups, hidden)
-    first, onward, back0, value_update = together(first, onward, back0, value_update)
-
-    second = over_z((sum2[:, parts[1]] + onward.astype(jnp.float32)).astype(jnp.bfloat16), 2)
-    result = add(mine0, back0)
-    result = [add(result[:, at], [part]) for at, part in zip(parts, (first, second))]
-    return jnp.concatenate(result, 1).astype(jnp.bfloat16), key_update, value_update
+    terms0 = [
+        rounded(add(both[j * rows : (j + 1) * rows], [term])) for j, term in enumerate(beside1, 1)
+    ]
+    key_update = updates(True, packs, key_update, 2, 4)
+    onward, back3, terms0, packs, rest2, key_update, mine1a, rest1 = together(
+        onward, back3, terms0, packs, terms2[1], key_update, mine1a, mine1[1]
+    )
+
+    first = over_z(rounded(add(mine2[0], back2a + [onward])), 2)
+    onward = over_z(rounded(add(mine3[1], back3)), 1)
+    back2b = back_y(rest2)
+    value_update = updates(False, packs, None, 0, 2)
+    first, onward, back2b, value_update, packs, terms0, rest1 = together(
+        first, onward, back2b, value_update, packs, terms0, rest1
+    )
+
+    second = over_z(rounded(add(mine2[1], back2b + [onward])), 2)
+    back0, mine1b = back_y(terms0), over_z(rest1, 1)
+    value_update = updates(False, packs, value_update, 2, 4)
+    result = [
+        add(both[:rows, at], [side, arrived] + [term[:, at] for term in back0])
+        for at, side, arrived in zip(parts, (mine1a, mine1b), (first, second))
+    ]
+    return rounded(jnp.concatenate(result, 1)), key_update, value_update
 
 
 def solution(mesh):

time: 88.4 us -> 85.1 us (0.963)
  waiting for transfers between devices: 28.7 us -> 20.3 us
  starting transfers between devices: 24.7 us -> 30 us
  local copies, waits for them, and re-layouts: 7.49 us -> 4.13 us
  Pallas kernels: 25.2 us -> 28.4 us
    ppermute x29 -> x31, waiting for transfers between devices: 25 us -> 19 us  [swap(): return lax.ppermute(array, 'shard', [(i, i ^ bits) for i in range(devices)])]
    ppermute x29 -> x31, starting transfers between devices: 23.1 us -> 28.3 us  [swap(): return lax.ppermute(array, 'shard', [(i, i ^ bits) for i in range(devices)])]
    unnamed x16, local copies, waits for them, and re-layouts: 6.79 us -> 3.42 us
    pallas_call x5 -> x11, Pallas kernels: 11.6 us -> 14.6 us  [the longest x8 14.2 us: update(): pl.pallas_call(functools.partial(update_kernel, fit_rows, piece, groups,...]
    ppermute x1, waiting for transfers between devices: 3.69 us -> 1.26 us  [local(): lax.ppermute(pack, 'member', [(i, i ^ bits) for i in range(groups)])]
  transfers between devices with their start and end apart: 30 -> 32, of which waited for: 13 -> 13; matrix products, arithmetic and copies ran while one was open for 1% -> 1% of each run, Pallas kernels for 29% -> 33%
where the time goes in v4:
time: 85.1 us; the launch traced here: 84.9 us
  starting transfers between devices  30 us (35%)
  Pallas kernels  28.4 us (33%)
  waiting for transfers between devices  20.3 us (24%)
  local copies, waits for them, and re-layouts  4.13 us (5%)
  other arithmetic  1.14 us (1%)
  between operations  0.88 us (1%)
    ppermute x31, starting transfers between devices, swap(): return lax.ppermute(array, 'shard', [(i, i ^ bits) for i in range(devices)])  28.3 us
    ppermute x31, waiting for transfers between devices, swap(): return lax.ppermute(array, 'shard', [(i, i ^ bits) for i in range(devices)])  19 us
    pallas_call x8, Pallas kernels, update(): pl.pallas_call(functools.partial(update_kernel, fit_rows, piece, groups,...  14.2 us
    pallas_call x4, Pallas kernels, chunk(): pl.pallas_call(functools.partial(chunk_kernel, k, rows, columns), out_sha...  12.1 us
    unnamed x16, local copies, waits for them, and re-layouts  3.42 us
  transfers between devices with their start and end apart: 32, of which 13 were waited for; matrix products, arithmetic and copies ran while one was open for 1% of the time, Pallas kernels for 33%

profile of v4, /device:TPU:0, one launch (start us, length us, event | category | flops | bytes accessed | tf_op | source)
XLA Modules:
  0.0 84.9 jit_solution(6528828329481377458)
XLA Ops:
  0.6 3.0 %collective-permute-start.2 = (bf16[32,4096]{1,0:T(8,128)(2,1)}, bf16[32,4096]{1,0:T(8,128)(2,1)S(1)}, u32[]{:S(2)}, u32[]{:S(2)}) collective-permute-start(bf16[32,4096]{1,0:T(8,128)(2,1)} %refs_0_.3), channel_id=1, source_target_pairs={{0,2},{1,3},{2,0},{3,1},{4,6},{5,7},{6,4},{7,5},{8,10},{9,11},{10,... | collective-permute-start | bytes 786440 | tf_op jit(solution)/shard_map/ppermute | solution.py:237
  3.7 1.6 %collective-permute-start.1 = (bf16[32,4096]{1,0:T(8,128)(2,1)}, bf16[32,4096]{1,0:T(8,128)(2,1)S(1)}, u32[]{:S(2)}, u32[]{:S(2)}) collective-permute-start(bf16[32,4096]{1,0:T(8,128)(2,1)} %refs_0_.3), channel_id=1, source_target_pairs={{0,4},{1,5},{2,6},{3,7},{4,0},{5,1},{6,2},{7,3},{8,12},{9,13},{10,... | collective-permute-start | bytes 786440 | tf_op jit(solution)/shard_map/ppermute | solution.py:237
  5.2 2.6 %collective-permute-start = (bf16[32,4096]{1,0:T(8,128)(2,1)}, bf16[32,4096]{1,0:T(8,128)(2,1)S(1)}, u32[]{:S(2)}, u32[]{:S(2)}) collective-permute-start(bf16[32,4096]{1,0:T(8,128)(2,1)} %refs_0_.3), channel_id=1, source_target_pairs={{0,8},{1,9},{2,10},{3,11},{4,12},{5,13},{6,14},{7,15},{8,0},{9,1},... | collective-permute-start | bytes 786440 | tf_op jit(solution)/shard_map/ppermute | solution.py:237
  7.8 0.7 broadcast_in_dim.3.refs_4_
  8.6 3.4 %copy-done = bf16[4096,1024]{1,0:T(8,128)(2,1)S(1)} copy-done((bf16[4096,1024]{1,0:T(8,128)(2,1)S(1)}, bf16[4096,1024]{1,0:T(8,128)(2,1)}, u32[]{:S(2)}) %copy-start) | copy-done | bytes 8388632
  11.9 0.6 shard_map.112.refs_9_
  12.6 3.3 %collective-permute-done.1.refs_0_ = bf16[32,4096]{1,0:T(8,128)(2,1)S(1)} collective-permute-done((bf16[32,4096]{1,0:T(8,128)(2,1)}, bf16[32,4096]{1,0:T(8,128)(2,1)S(1)}, u32[]{:S(2)}, u32[]{:S(2)}) %collective-permute-start.1) | collective-permute-done | bytes 262176 | tf_op jit(solution)/shard_map/ppermute | solution.py:237
  15.9 0.5 collective-permute-start.6
  16.8 0.6 shard_map.113.refs_10_
  17.4 3.4 %collective-permute-done.refs_0_ = bf16[32,4096]{1,0:T(8,128)(2,1)S(1)} collective-permute-done((bf16[32,4096]{1,0:T(8,128)(2,1)}, bf16[32,4096]{1,0:T(8,128)(2,1)S(1)}, u32[]{:S(2)}, u32[]{:S(2)}) %collective-permute-start) | collective-permute-done | bytes 262176 | tf_op jit(solution)/shard_map/ppermute | solution.py:237
  20.7 3.9 %collective-permute-done.4.refs_1_ = bf16[32,4096]{1,0:T(8,128)(2,1)S(1)} collective-permute-done((bf16[32,4096]{1,0:T(8,128)(2,1)S(1)}, bf16[32,4096]{1,0:T(8,128)(2,1)S(1)}, u32[]{:S(2)}, u32[]{:S(2)}) %collective-permute-start.4) | collective-permute-done | bytes 262176 | tf_op jit(solution)/shard_map/ppermute | solution.py:237
  25.6 0.6 shard_map.115.refs_0_
  26.1 1.7 %collective-permute-start.11 = (bf16[8,10368]{1,0:T(8,128)(2,1)S(1)}, bf16[8,10368]{1,0:T(8,128)(2,1)S(1)}, u32[]{:S(2)}, u32[]{:S(2)}) collective-permute-start(bf16[8,10368]{1,0:T(8,128)(2,1)S(1)} %shard_map.115.refs_0_), channel_id=1, source_target_pairs={{0,16},{16,0},{1,17},{17,1},{2,18},{18,2},{3,19},{19,3},{4,20},{20... | collective-permute-start | bytes 497672 | tf_op jit(solution)/shard_map/ppermute | solution.py:279
  27.8 3.0 %shard_map.114 = (bf16[64,4096]{1,0:T(8,128)(2,1)S(1)}, bf16[64,4096]{1,0:T(8,128)(2,1)S(1)}) custom-call(bf16[32,4096]{1,0:T(8,128)(2,1)S(1)} %copy-done.6, bf16[32,4096]{1,0:T(8,128)(2,1)S(1)} %collective-permute-done.2.refs_1_, bf16[32,4096]{1,0:T(8,128)(2,1)S(1)} %collective-permute-done.3.refs_2_, bf16[32,4096]{1,0:T(8,128)(2,1)S(1)} %collective-permute-done.5.refs_3_, ...), custom_call_target="tpu_custom_call" | custom-call | flops 128 | bytes 128 | tf_op jit(solution)/shard_map/pallas_call | solution.py:86
  30.8 1.3 %collective-permute-done.11.refs_1_ = bf16[8,10368]{1,0:T(8,128)(2,1)S(1)} collective-permute-done((bf16[8,10368]{1,0:T(8,128)(2,1)S(1)}, bf16[8,10368]{1,0:T(8,128)(2,1)S(1)}, u32[]{:S(2)}, u32[]{:S(2)}) %collective-permute-start.11) | collective-permute-done | bytes 165920 | tf_op jit(solution)/shard_map/ppermute | solution.py:279
  32.1 1.3 %collective-permute-done.8.refs_1_ = bf16[32,4096]{1,0:T(8,128)(2,1)S(1)} collective-permute-done((bf16[32,4096]{1,0:T(8,128)(2,1)S(1)}, bf16[32,4096]{1,0:T(8,128)(2,1)S(1)}, u32[]{:S(2)}, u32[]{:S(2)}) %collective-permute-start.8) | collective-permute-done | bytes 262176 | tf_op jit(solution)/shard_map/ppermute | solution.py:237
  34.0 1.7 %collective-permute-start.12 = (bf16[32,4096]{1,0:T(8,128)(2,1)S(1)}, bf16[32,4096]{1,0:T(8,128)(2,1)S(1)}, u32[]{:S(2)}, u32[]{:S(2)}) collective-permute-start(bf16[32,4096]{1,0:T(8,128)(2,1)S(1)} %collective-permute-done.7.refs_0_), channel_id=1, source_target_pairs={{0,2},{1,3},{2,0},{3,1},{4,6},{5,7},{6,4},{7,5},{8,10},{9,11},{10,... | collective-permute-start | bytes 786440 | tf_op jit(solution)/shard_map/ppermute | solution.py:237
  35.6 3.0 %shard_map.116 = (bf16[64,4096]{1,0:T(8,128)(2,1)S(1)}, bf16[64,4096]{1,0:T(8,128)(2,1)S(1)}) custom-call(bf16[32,4096]{1,0:T(8,128)(2,1)S(1)} %collective-permute-done.1.refs_0_, bf16[32,4096]{1,0:T(8,128)(2,1)S(1)} %collective-permute-done.4.refs_1_, bf16[32,4096]{1,0:T(8,128)(2,1)S(1)} %collective-permute-done.6.refs_2_, ...), custom_call_target="tpu_custom_call" | custom-call | flops 128 | bytes 128 | tf_op jit(solution)/shard_map/pallas_call | solution.py:86
  38.6 3.0 %shard_map.117 = (bf16[64,4096]{1,0:T(8,128)(2,1)S(1)}, bf16[64,4096]{1,0:T(8,128)(2,1)S(1)}) custom-call(bf16[32,4096]{1,0:T(8,128)(2,1)S(1)} %collective-permute-done.refs_0_, bf16[32,4096]{1,0:T(8,128)(2,1)S(1)} %collective-permute-done.8.refs_1_, bf16[32,4096]{1,0:T(8,128)(2,1)S(1)} %collective-permute-done.9.refs_2_, ...), custom_call_target="tpu_custom_call" | custom-call | flops 128 | bytes 128 | tf_op jit(solution)/shard_map/pallas_call | solution.py:86
  41.6 0.6 collective-permute-done.12.refs_1_
  42.2 0.5 collective-permute-start.17
  42.7 1.4 %collective-permute-done.15.arrived = bf16[64,4096]{1,0:T(8,128)(2,1)S(1)} collective-permute-done((bf16[64,4096]{1,0:T(8,128)(2,1)S(1)}, bf16[64,4096]{1,0:T(8,128)(2,1)S(1)}, u32[]{:S(2)}, u32[]{:S(2)}) %collective-permute-start.15) | collective-permute-done | bytes 524320 | tf_op jit(solution)/shard_map/ppermute | solution.py:237
  44.2 1.7 %collective-permute-start.16 = (bf16[32,2048]{1,0:T(8,128)(2,1)S(1)}, bf16[32,2048]{1,0:T(8,128)(2,1)S(1)}, u32[]{:S(2)}, u32[]{:S(2)}) collective-permute-start(bf16[32,2048]{1,0:T(8,128)(2,1)S(1)} %get-tuple-element.127), channel_id=1, source_target_pairs={{0,2},{1,3},{2,0},{3,1},{4,6},{5,7},{6,4},{7,5},{8,10},{9,11},{10,... | collective-permute-start | bytes 393224 | tf_op jit(solution)/shard_map/ppermute | solution.py:237
  45.9 3.2 %shard_map.119 = (bf16[64,4096]{1,0:T(8,128)(2,1)S(1)}, bf16[64,4096]{1,0:T(8,128)(2,1)S(1)}) custom-call(bf16[32,4096]{1,0:T(8,128)(2,1)S(1)} %collective-permute-done.7.refs_0_, bf16[32,4096]{1,0:T(8,128)(2,1)S(1)} %collective-permute-done.12.refs_1_, bf16[32,4096]{1,0:T(8,128)(2,1)S(1)} %collective-permute-done.13.refs_2_, ...), custom_call_target="tpu_custom_call" | custom-call | flops 128 | bytes 128 | tf_op jit(solution)/shard_map/pallas_call | solution.py:86
  49.1 0.7 collective-permute-done.16
  50.4 0.6 collective-permute-start.21
  51.0 0.7 collective-permute-done.19.arrived
  51.8 1.7 %collective-permute-start.20 = (bf16[32,2048]{1,0:T(8,128)(2,1)S(1)}, bf16[32,2048]{1,0:T(8,128)(2,1)S(1)}, u32[]{:S(2)}, u32[]{:S(2)}) collective-permute-start(bf16[32,2048]{1,0:T(8,128)(2,1)S(1)} %get-tuple-element.141), channel_id=1, source_target_pairs={{0,2},{1,3},{2,0},{3,1},{4,6},{5,7},{6,4},{7,5},{8,10},{9,11},{10,... | collective-permute-start | bytes 393224 | tf_op jit(solution)/shard_map/ppermute | solution.py:237
  53.6 1.8 %shard_map.122.refs_2_ = f32[2048,1024]{1,0:T(8,128)} custom-call(bf16[8,10368]{1,0:T(8,128)(2,1)S(1)} %shard_map.115.refs_0_, bf16[8,10368]{1,0:T(8,128)(2,1)S(1)} %collective-permute-done.11.refs_1_), custom_call_target="tpu_custom_call" | custom-call | flops 256 | bytes 256 | tf_op jit(solution)/shard_map/pallas_call | solution.py:211
  55.3 1.8 %shard_map.123.refs_2_ = f32[2048,1024]{1,0:T(8,128)} custom-call(bf16[8,10368]{1,0:T(8,128)(2,1)S(1)} %shard_map.115.refs_0_, bf16[8,10368]{1,0:T(8,128)(2,1)S(1)} %collective-permute-done.11.refs_1_, f32[2048,1024]{1,0:T(8,128)} %shard_map.122.refs_2_), custom_call_target="tpu_custom_call", output_to_operand_aliasing={{}: (2, {})} | custom-call | flops 256 | bytes 256 | tf_op jit(solution)/shard_map/pallas_call | solution.py:211
  57.1 1.6 %collective-permute-done.21 = bf16[32,4096]{1,0:T(8,128)(2,1)S(1)} collective-permute-done((bf16[32,4096]{1,0:T(8,128)(2,1)S(1)}, bf16[32,4096]{1,0:T(8,128)(2,1)S(1)}, u32[]{:S(2)}, u32[]{:S(2)}) %collective-permute-start.21) | collective-permute-done | bytes 262176 | tf_op jit(solution)/shard_map/ppermute | solution.py:237
  58.8 0.6 collective-permute-start.23
  59.3 1.7 %collective-permute-start.24 = (bf16[32,2048]{1,0:T(8,128)(2,1)S(1)}, bf16[32,2048]{1,0:T(8,128)(2,1)S(1)}, u32[]{:S(2)}, u32[]{:S(2)}) collective-permute-start(bf16[32,2048]{1,0:T(8,128)(2,1)S(1)} %get-tuple-element.154), channel_id=1, source_target_pairs={{0,2},{1,3},{2,0},{3,1},{4,6},{5,7},{6,4},{7,5},{8,10},{9,11},{10,... | collective-permute-start | bytes 393224 | tf_op jit(solution)/shard_map/ppermute | solution.py:237
  61.0 1.5 %collective-permute-start.25 = (bf16[32,2048]{1,0:T(8,128)(2,1)S(1)}, bf16[32,2048]{1,0:T(8,128)(2,1)S(1)}, u32[]{:S(2)}, u32[]{:S(2)}) collective-permute-start(bf16[32,2048]{1,0:T(8,128)(2,1)S(1)} %get-tuple-element.158), channel_id=1, source_target_pairs={{0,4},{1,5},{2,6},{3,7},{4,0},{5,1},{6,2},{7,3},{8,12},{9,13},{10,... | collective-permute-start | bytes 393224 | tf_op jit(solution)/shard_map/ppermute | solution.py:237
  62.5 1.8 %shard_map.124.refs_2_ = f32[2048,1024]{1,0:T(8,128)} custom-call(bf16[8,10368]{1,0:T(8,128)(2,1)S(1)} %shard_map.115.refs_0_, bf16[8,10368]{1,0:T(8,128)(2,1)S(1)} %collective-permute-done.11.refs_1_, f32[2048,1024]{1,0:T(8,128)} %shard_map.123.refs_2_), custom_call_target="tpu_custom_call", output_to_operand_aliasing={{}: (2, {})} | custom-call | flops 256 | bytes 256 | tf_op jit(solution)/shard_map/pallas_call | solution.py:211
  64.5 1.8 %shard_map.125 = f32[2048,1024]{1,0:T(8,128)} custom-call(bf16[8,10368]{1,0:T(8,128)(2,1)S(1)} %shard_map.115.refs_0_, bf16[8,10368]{1,0:T(8,128)(2,1)S(1)} %collective-permute-done.11.refs_1_, f32[2048,1024]{1,0:T(8,128)} %shard_map.124.refs_2_), custom_call_target="tpu_custom_call", output_to_operand_aliasing={{}: (2, {})} | custom-call | flops 256 | bytes 256 | tf_op jit(solution)/shard_map/pallas_call | solution.py:211
  66.4 2.2 %collective-permute-start.26 = (bf16[32,2048]{1,0:T(8,128)(2,1)S(1)}, bf16[32,2048]{1,0:T(8,128)(2,1)S(1)}, u32[]{:S(2)}, u32[]{:S(2)}) collective-permute-start(bf16[32,2048]{1,0:T(8,128)(2,1)S(1)} %add_convert_fusion.2), channel_id=1, source_target_pairs={{0,8},{1,9},{2,10},{3,11},{4,12},{5,13},{6,14},{7,15},{8,0},{9,1},... | collective-permute-start | bytes 393224 | tf_op jit(solution)/shard_map/ppermute | solution.py:237
  68.6 1.0 %collective-permute-start.27 = (bf16[32,2048]{1,0:T(8,128)(2,1)S(1)}, bf16[32,2048]{1,0:T(8,128)(2,1)S(1)}, u32[]{:S(2)}, u32[]{:S(2)}) collective-permute-start(bf16[32,2048]{1,0:T(8,128)(2,1)S(1)} %add_convert_fusion.1), channel_id=1, source_target_pairs={{0,4},{1,5},{2,6},{3,7},{4,0},{5,1},{6,2},{7,3},{8,12},{9,13},{10,... | collective-permute-start | bytes 393224 | tf_op jit(solution)/shard_map/ppermute | solution.py:237
  69.6 1.5 %collective-permute-start.28 = (bf16[32,2048]{1,0:T(8,128)(2,1)S(1)}, bf16[32,2048]{1,0:T(8,128)(2,1)S(1)}, u32[]{:S(2)}, u32[]{:S(2)}) collective-permute-start(bf16[32,2048]{1,0:T(8,128)(2,1)S(1)} %get-tuple-element.166), channel_id=1, source_target_pairs={{0,2},{1,3},{2,0},{3,1},{4,6},{5,7},{6,4},{7,5},{8,10},{9,11},{10,... | collective-permute-start | bytes 393224 | tf_op jit(solution)/shard_map/ppermute | solution.py:237
  71.1 1.8 %shard_map.126.refs_2_ = f32[1024,2048]{1,0:T(8,128)} custom-call(bf16[8,10368]{1,0:T(8,128)(2,1)S(1)} %shard_map.115.refs_0_, bf16[8,10368]{1,0:T(8,128)(2,1)S(1)} %collective-permute-done.11.refs_1_), custom_call_target="tpu_custom_call" | custom-call | flops 128 | bytes 128 | tf_op jit(solution)/shard_map/pallas_call | solution.py:211
  72.9 1.8 %shard_map.127.refs_2_ = f32[1024,2048]{1,0:T(8,128)} custom-call(bf16[8,10368]{1,0:T(8,128)(2,1)S(1)} %shard_map.115.refs_0_, bf16[8,10368]{1,0:T(8,128)(2,1)S(1)} %collective-permute-done.11.refs_1_, f32[1024,2048]{1,0:T(8,128)} %shard_map.126.refs_2_), custom_call_target="tpu_custom_call", output_to_operand_aliasing={{}: (2, {})} | custom-call | flops 128 | bytes 128 | tf_op jit(solution)/shard_map/pallas_call | solution.py:211
  74.6 1.1 %collective-permute-start.30 = (bf16[32,2048]{1,0:T(8,128)(2,1)S(1)}, bf16[32,2048]{1,0:T(8,128)(2,1)S(1)}, u32[]{:S(2)}, u32[]{:S(2)}) collective-permute-start(bf16[32,2048]{1,0:T(8,128)(2,1)S(1)} %get-tuple-element.173), channel_id=1, source_target_pairs={{0,4},{1,5},{2,6},{3,7},{4,0},{5,1},{6,2},{7,3},{8,12},{9,13},{10,... | collective-permute-start | bytes 393224 | tf_op jit(solution)/shard_map/ppermute | solution.py:237
  75.7 0.9 %collective-permute-start.29 = (bf16[32,4096]{1,0:T(8,128)(2,1)S(1)}, bf16[32,4096]{1,0:T(8,128)(2,1)S(1)}, u32[]{:S(2)}, u32[]{:S(2)}) collective-permute-start(bf16[32,4096]{1,0:T(8,128)(2,1)S(1)} %fusion), channel_id=1, source_target_pairs={{0,2},{1,3},{2,0},{3,1},{4,6},{5,7},{6,4},{7,5},{8,10},{9,11},{10,... | collective-permute-start | bytes 786440 | tf_op jit(solution)/shard_map/ppermute | solution.py:237
  76.7 1.8 %collective-permute-start.31 = (bf16[32,2048]{1,0:T(8,128)(2,1)S(1)}, bf16[32,2048]{1,0:T(8,128)(2,1)S(1)}, u32[]{:S(2)}, u32[]{:S(2)}) collective-permute-start(bf16[32,2048]{1,0:T(8,128)(2,1)S(1)} %add_convert_fusion), channel_id=1, source_target_pairs={{0,8},{1,9},{2,10},{3,11},{4,12},{5,13},{6,14},{7,15},{8,0},{9,1},... | collective-permute-start | bytes 393224 | tf_op jit(solution)/shard_map/ppermute | solution.py:237
  78.5 1.8 %shard_map.128.refs_2_ = f32[1024,2048]{1,0:T(8,128)} custom-call(bf16[8,10368]{1,0:T(8,128)(2,1)S(1)} %shard_map.115.refs_0_, bf16[8,10368]{1,0:T(8,128)(2,1)S(1)} %collective-permute-done.11.refs_1_, f32[1024,2048]{1,0:T(8,128)} %shard_map.127.refs_2_), custom_call_target="tpu_custom_call", output_to_operand_aliasing={{}: (2, {})} | custom-call | flops 128 | bytes 128 | tf_op jit(solution)/shard_map/pallas_call | solution.py:211
  80.2 1.8 %shard_map.129 = f32[1024,2048]{1,0:T(8,128)} custom-call(bf16[8,10368]{1,0:T(8,128)(2,1)S(1)} %shard_map.115.refs_0_, bf16[8,10368]{1,0:T(8,128)(2,1)S(1)} %collective-permute-done.11.refs_1_, f32[1024,2048]{1,0:T(8,128)} %shard_map.128.refs_2_), custom_call_target="tpu_custom_call", output_to_operand_aliasing={{}: (2, {})} | custom-call | flops 128 | bytes 128 | tf_op jit(solution)/shard_map/pallas_call | solution.py:211
  82.0 2.0 %collective-permute-done.31 = bf16[32,2048]{1,0:T(8,128)(2,1)S(1)} collective-permute-done((bf16[32,2048]{1,0:T(8,128)(2,1)S(1)}, bf16[32,2048]{1,0:T(8,128)(2,1)S(1)}, u32[]{:S(2)}, u32[]{:S(2)}) %collective-permute-start.31) | collective-permute-done | bytes 131104 | tf_op jit(solution)/shard_map/ppermute | solution.py:237
  84.1 0.7 pad_maximum_fusion
  (59 shorter events, 3.3 us)
Async XLA Ops:
  0.6 11.9 %collective-permute-start.2 = (bf16[32,4096]{1,0:T(8,128)(2,1)}, bf16[32,4096]{1,0:T(8,128)(2,1)S(1)}, u32[]{:S(2)}, u32[]{:S(2)}) collective-permute-start(bf16[32,4096]{1,0:T(8,128)(2,1)} %refs_0_.3), channel_id=1, source_target_pairs={{0,2},{1,3},{2,0},{3,1},{4,6},{5,7},{6,4},{7,5},{8,10},{9,11},{10,... | collective-permute-start | bytes 786440 | tf_op jit(solution)/shard_map/ppermute | solution.py:237
  3.7 12.2 %collective-permute-start.1 = (bf16[32,4096]{1,0:T(8,128)(2,1)}, bf16[32,4096]{1,0:T(8,128)(2,1)S(1)}, u32[]{:S(2)}, u32[]{:S(2)}) collective-permute-start(bf16[32,4096]{1,0:T(8,128)(2,1)} %refs_0_.3), channel_id=1, source_target_pairs={{0,4},{1,5},{2,6},{3,7},{4,0},{5,1},{6,2},{7,3},{8,12},{9,13},{10,... | collective-permute-start | bytes 786440 | tf_op jit(solution)/shard_map/ppermute | solution.py:237
  5.2 10.7 %collective-permute-start.3 = (bf16[32,4096]{1,0:T(8,128)(2,1)}, bf16[32,4096]{1,0:T(8,128)(2,1)S(1)}, u32[]{:S(2)}, u32[]{:S(2)}) collective-permute-start(bf16[32,4096]{1,0:T(8,128)(2,1)} %refs_0_.3), channel_id=1, source_target_pairs={{0,1},{1,0},{2,3},{3,2},{4,5},{5,4},{6,7},{7,6},{8,9},{9,8},{10,11... | collective-permute-start | bytes 786440 | tf_op jit(solution)/shard_map/ppermute | solution.py:237
  5.2 15.5 %collective-permute-start = (bf16[32,4096]{1,0:T(8,128)(2,1)}, bf16[32,4096]{1,0:T(8,128)(2,1)S(1)}, u32[]{:S(2)}, u32[]{:S(2)}) collective-permute-start(bf16[32,4096]{1,0:T(8,128)(2,1)} %refs_0_.3), channel_id=1, source_target_pairs={{0,8},{1,9},{2,10},{3,11},{4,12},{5,13},{6,14},{7,15},{8,0},{9,1},... | collective-permute-start | bytes 786440 | tf_op jit(solution)/shard_map/ppermute | solution.py:237
  8.5 3.4 %copy-start = (bf16[4096,1024]{1,0:T(8,128)(2,1)S(1)}, bf16[4096,1024]{1,0:T(8,128)(2,1)}, u32[]{:S(2)}) copy-start(bf16[4096,1024]{1,0:T(8,128)(2,1)} %refs_0_.1) | copy-start | bytes 25165828
  11.9 4.9 %copy-start.1 = (bf16[1024,4096]{1,0:T(8,128)(2,1)S(1)}, bf16[1024,4096]{1,0:T(8,128)(2,1)}, u32[]{:S(2)}) copy-start(bf16[1024,4096]{1,0:T(8,128)(2,1)} %refs_0_.2) | copy-start | bytes 25165828
  12.5 13.0 %copy-start.2 = (bf16[8,4096]{1,0:T(8,128)(2,1)S(1)}, bf16[8,4096]{1,0:T(8,128)(2,1)}, u32[]{:S(2)}) copy-start(bf16[8,4096]{1,0:T(8,128)(2,1)} %refs_5_.7) | copy-start | bytes 196612
  12.5 13.0 %copy-start.3 = (bf16[8,4096]{1,0:T(8,128)(2,1)S(1)}, bf16[8,4096]{1,0:T(8,128)(2,1)}, u32[]{:S(2)}) copy-start(bf16[8,4096]{1,0:T(8,128)(2,1)} %refs_8_.7) | copy-start | bytes 196612
  12.5 13.0 %copy-start.4 = (bf16[8,1024]{1,0:T(8,128)(2,1)S(1)}, bf16[8,1024]{1,0:T(8,128)(2,1)}, u32[]{:S(2)}) copy-start(bf16[8,1024]{1,0:T(8,128)(2,1)} %refs_6_.7) | copy-start | bytes 49156
  12.5 13.0 %copy-start.5 = (bf16[8,1024]{1,0:T(8,128)(2,1)S(1)}, bf16[8,1024]{1,0:T(8,128)(2,1)}, u32[]{:S(2)}) copy-start(bf16[8,1024]{1,0:T(8,128)(2,1)} %refs_7_.7) | copy-start | bytes 49156
  12.6 13.0 %copy-start.7 = (s32[8]{0:T(128)S(1)}, s32[8]{0:T(128)}, u32[]{:S(2)}) copy-start(s32[8]{0:T(128)} %ranks.1) | copy-start | bytes 100
  12.6 15.3 %copy-start.6 = (bf16[32,4096]{1,0:T(8,128)(2,1)S(1)}, bf16[32,4096]{1,0:T(8,128)(2,1)}, u32[]{:S(2)}) copy-start(bf16[32,4096]{1,0:T(8,128)(2,1)} %refs_0_.3) | copy-start | bytes 786436
  15.9 4.8 %collective-permute-start.5 = (bf16[32,4096]{1,0:T(8,128)(2,1)S(1)}, bf16[32,4096]{1,0:T(8,128)(2,1)S(1)}, u32[]{:S(2)}, u32[]{:S(2)}) collective-permute-start(bf16[32,4096]{1,0:T(8,128)(2,1)S(1)} %collective-permute-done.2.refs_1_), channel_id=1, source_target_pairs={{0,1},{1,0},{2,3},{3,2},{4,5},{5,4},{6,7},{7,6},{8,9},{9,8},{10,11... | collective-permute-start | bytes 786440 | tf_op jit(solution)/shard_map/ppermute | solution.py:237
  15.9 4.8 %collective-permute-start.6 = (bf16[32,4096]{1,0:T(8,128)(2,1)S(1)}, bf16[32,4096]{1,0:T(8,128)(2,1)S(1)}, u32[]{:S(2)}, u32[]{:S(2)}) collective-permute-start(bf16[32,4096]{1,0:T(8,128)(2,1)S(1)} %collective-permute-done.1.refs_0_), channel_id=1, source_target_pairs={{0,1},{1,0},{2,3},{3,2},{4,5},{5,4},{6,7},{7,6},{8,9},{9,8},{10,11... | collective-permute-start | bytes 786440 | tf_op jit(solution)/shard_map/ppermute | solution.py:237
  16.4 8.2 %collective-permute-start.4 = (bf16[32,4096]{1,0:T(8,128)(2,1)S(1)}, bf16[32,4096]{1,0:T(8,128)(2,1)S(1)}, u32[]{:S(2)}, u32[]{:S(2)}) collective-permute-start(bf16[32,4096]{1,0:T(8,128)(2,1)S(1)} %collective-permute-done.1.refs_0_), channel_id=1, source_target_pairs={{0,2},{1,3},{2,0},{3,1},{4,6},{5,7},{6,4},{7,5},{8,10},{9,11},{10,... | collective-permute-start | bytes 786440 | tf_op jit(solution)/shard_map/ppermute | solution.py:237
  24.6 7.4 %collective-permute-start.10 = (bf16[32,4096]{1,0:T(8,128)(2,1)S(1)}, bf16[32,4096]{1,0:T(8,128)(2,1)S(1)}, u32[]{:S(2)}, u32[]{:S(2)}) collective-permute-start(bf16[32,4096]{1,0:T(8,128)(2,1)S(1)} %collective-permute-done.4.refs_1_), channel_id=1, source_target_pairs={{0,1},{1,0},{2,3},{3,2},{4,5},{5,4},{6,7},{7,6},{8,9},{9,8},{10,11... | collective-permute-start | bytes 786440 | tf_op jit(solution)/shard_map/ppermute | solution.py:237
  24.6 7.4 %collective-permute-start.9 = (bf16[32,4096]{1,0:T(8,128)(2,1)S(1)}, bf16[32,4096]{1,0:T(8,128)(2,1)S(1)}, u32[]{:S(2)}, u32[]{:S(2)}) collective-permute-start(bf16[32,4096]{1,0:T(8,128)(2,1)S(1)} %collective-permute-done.refs_0_), channel_id=1, source_target_pairs={{0,1},{1,0},{2,3},{3,2},{4,5},{5,4},{6,7},{7,6},{8,9},{9,8},{10,11... | collective-permute-start | bytes 786440 | tf_op jit(solution)/shard_map/ppermute | solution.py:237
  25.1 8.2 %collective-permute-start.8 = (bf16[32,4096]{1,0:T(8,128)(2,1)S(1)}, bf16[32,4096]{1,0:T(8,128)(2,1)S(1)}, u32[]{:S(2)}, u32[]{:S(2)}) collective-permute-start(bf16[32,4096]{1,0:T(8,128)(2,1)S(1)} %collective-permute-done.refs_0_), channel_id=1, source_target_pairs={{0,2},{1,3},{2,0},{3,1},{4,6},{5,7},{6,4},{7,5},{8,10},{9,11},{10,... | collective-permute-start | bytes 786440 | tf_op jit(solution)/shard_map/ppermute | solution.py:237
  25.5 7.9 %collective-permute-start.7 = (bf16[32,4096]{1,0:T(8,128)(2,1)S(1)}, bf16[32,4096]{1,0:T(8,128)(2,1)S(1)}, u32[]{:S(2)}, u32[]{:S(2)}) collective-permute-start(bf16[32,4096]{1,0:T(8,128)(2,1)S(1)} %collective-permute-done.refs_0_), channel_id=1, source_target_pairs={{0,4},{1,5},{2,6},{3,7},{4,0},{5,1},{6,2},{7,3},{8,12},{9,13},{10,... | collective-permute-start | bytes 786440 | tf_op jit(solution)/shard_map/ppermute | solution.py:237
  26.1 5.9 %collective-permute-start.11 = (bf16[8,10368]{1,0:T(8,128)(2,1)S(1)}, bf16[8,10368]{1,0:T(8,128)(2,1)S(1)}, u32[]{:S(2)}, u32[]{:S(2)}) collective-permute-start(bf16[8,10368]{1,0:T(8,128)(2,1)S(1)} %shard_map.115.refs_0_), channel_id=1, source_target_pairs={{0,16},{16,0},{1,17},{17,1},{2,18},{18,2},{3,19},{19,3},{4,20},{20... | collective-permute-start | bytes 497672 | tf_op jit(solution)/shard_map/ppermute | solution.py:279
  33.5 5.2 %collective-permute-start.14 = (bf16[32,4096]{1,0:T(8,128)(2,1)S(1)}, bf16[32,4096]{1,0:T(8,128)(2,1)S(1)}, u32[]{:S(2)}, u32[]{:S(2)}) collective-permute-start(bf16[32,4096]{1,0:T(8,128)(2,1)S(1)} %collective-permute-done.8.refs_1_), channel_id=1, source_target_pairs={{0,1},{1,0},{2,3},{3,2},{4,5},{5,4},{6,7},{7,6},{8,9},{9,8},{10,11... | collective-permute-start | bytes 786440 | tf_op jit(solution)/shard_map/ppermute | solution.py:237
  33.5 8.1 %collective-permute-start.13 = (bf16[32,4096]{1,0:T(8,128)(2,1)S(1)}, bf16[32,4096]{1,0:T(8,128)(2,1)S(1)}, u32[]{:S(2)}, u32[]{:S(2)}) collective-permute-start(bf16[32,4096]{1,0:T(8,128)(2,1)S(1)} %collective-permute-done.7.refs_0_), channel_id=1, source_target_pairs={{0,1},{1,0},{2,3},{3,2},{4,5},{5,4},{6,7},{7,6},{8,9},{9,8},{10,11... | collective-permute-start | bytes 786440 | tf_op jit(solution)/shard_map/ppermute | solution.py:237
  34.0 8.2 %collective-permute-start.12 = (bf16[32,4096]{1,0:T(8,128)(2,1)S(1)}, bf16[32,4096]{1,0:T(8,128)(2,1)S(1)}, u32[]{:S(2)}, u32[]{:S(2)}) collective-permute-start(bf16[32,4096]{1,0:T(8,128)(2,1)S(1)} %collective-permute-done.7.refs_0_), channel_id=1, source_target_pairs={{0,2},{1,3},{2,0},{3,1},{4,6},{5,7},{6,4},{7,5},{8,10},{9,11},{10,... | collective-permute-start | bytes 786440 | tf_op jit(solution)/shard_map/ppermute | solution.py:237
  42.2 1.9 %collective-permute-start.15 = (bf16[64,4096]{1,0:T(8,128)(2,1)S(1)}, bf16[64,4096]{1,0:T(8,128)(2,1)S(1)}, u32[]{:S(2)}, u32[]{:S(2)}) collective-permute-start(bf16[64,4096]{1,0:T(8,128)(2,1)S(1)} %get-tuple-element.122), channel_id=1, source_target_pairs={{0,1},{1,0},{2,3},{3,2},{4,5},{5,4},{6,7},{7,6},{8,9},{9,8},{10,11... | collective-permute-start | bytes 1572872 | tf_op jit(solution)/shard_map/ppermute | solution.py:237
  42.2 7.0 %collective-permute-start.17 = (bf16[64,4096]{1,0:T(8,128)(2,1)S(1)}, bf16[64,4096]{1,0:T(8,128)(2,1)S(1)}, u32[]{:S(2)}, u32[]{:S(2)}) collective-permute-start(bf16[64,4096]{1,0:T(8,128)(2,1)S(1)} %get-tuple-element.128), channel_id=1, source_target_pairs={{0,1},{1,0},{2,3},{3,2},{4,5},{5,4},{6,7},{7,6},{8,9},{9,8},{10,11... | collective-permute-start | bytes 1572872 | tf_op jit(solution)/shard_map/ppermute | solution.py:237
  42.7 3.2 %collective-permute-start.18 = (bf16[32,4096]{1,0:T(8,128)(2,1)S(1)}, bf16[32,4096]{1,0:T(8,128)(2,1)S(1)}, u32[]{:S(2)}, u32[]{:S(2)}) collective-permute-start(bf16[32,4096]{1,0:T(8,128)(2,1)S(1)} %collective-permute-done.12.refs_1_), channel_id=1, source_target_pairs={{0,1},{1,0},{2,3},{3,2},{4,5},{5,4},{6,7},{7,6},{8,9},{9,8},{10,11... | collective-permute-start | bytes 786440 | tf_op jit(solution)/shard_map/ppermute | solution.py:237
  44.2 5.6 %collective-permute-start.16 = (bf16[32,2048]{1,0:T(8,128)(2,1)S(1)}, bf16[32,2048]{1,0:T(8,128)(2,1)S(1)}, u32[]{:S(2)}, u32[]{:S(2)}) collective-permute-start(bf16[32,2048]{1,0:T(8,128)(2,1)S(1)} %get-tuple-element.127), channel_id=1, source_target_pairs={{0,2},{1,3},{2,0},{3,1},{4,6},{5,7},{6,4},{7,5},{8,10},{9,11},{10,... | collective-permute-start | bytes 393224 | tf_op jit(solution)/shard_map/ppermute | solution.py:237
  49.8 1.9 %collective-permute-start.19 = (bf16[64,4096]{1,0:T(8,128)(2,1)S(1)}, bf16[64,4096]{1,0:T(8,128)(2,1)S(1)}, u32[]{:S(2)}, u32[]{:S(2)}) collective-permute-start(bf16[64,4096]{1,0:T(8,128)(2,1)S(1)} %get-tuple-element.136), channel_id=1, source_target_pairs={{0,1},{1,0},{2,3},{3,2},{4,5},{5,4},{6,7},{7,6},{8,9},{9,8},{10,11... | collective-permute-start | bytes 1572872 | tf_op jit(solution)/shard_map/ppermute | solution.py:237
  49.8 8.9 %collective-permute-start.22 = (bf16[64,4096]{1,0:T(8,128)(2,1)S(1)}, bf16[64,4096]{1,0:T(8,128)(2,1)S(1)}, u32[]{:S(2)}, u32[]{:S(2)}) collective-permute-start(bf16[64,4096]{1,0:T(8,128)(2,1)S(1)} %get-tuple-element.145), channel_id=1, source_target_pairs={{0,1},{1,0},{2,3},{3,2},{4,5},{5,4},{6,7},{7,6},{8,9},{9,8},{10,11... | collective-permute-start | bytes 1572872 | tf_op jit(solution)/shard_map/ppermute | solution.py:237
  50.4 8.3 %collective-permute-start.21 = (bf16[32,4096]{1,0:T(8,128)(2,1)S(1)}, bf16[32,4096]{1,0:T(8,128)(2,1)S(1)}, u32[]{:S(2)}, u32[]{:S(2)}) collective-permute-start(bf16[32,4096]{1,0:T(8,128)(2,1)S(1)} %get-tuple-element.144), channel_id=1, source_target_pairs={{0,4},{1,5},{2,6},{3,7},{4,0},{5,1},{6,2},{7,3},{8,12},{9,13},{10,... | collective-permute-start | bytes 786440 | tf_op jit(solution)/shard_map/ppermute | solution.py:237
  51.8 6.9 %collective-permute-start.20 = (bf16[32,2048]{1,0:T(8,128)(2,1)S(1)}, bf16[32,2048]{1,0:T(8,128)(2,1)S(1)}, u32[]{:S(2)}, u32[]{:S(2)}) collective-permute-start(bf16[32,2048]{1,0:T(8,128)(2,1)S(1)} %get-tuple-element.141), channel_id=1, source_target_pairs={{0,2},{1,3},{2,0},{3,1},{4,6},{5,7},{6,4},{7,5},{8,10},{9,11},{10,... | collective-permute-start | bytes 393224 | tf_op jit(solution)/shard_map/ppermute | solution.py:237
  58.8 7.5 %collective-permute-start.23 = (bf16[32,2048]{1,0:T(8,128)(2,1)S(1)}, bf16[32,2048]{1,0:T(8,128)(2,1)S(1)}, u32[]{:S(2)}, u32[]{:S(2)}) collective-permute-start(bf16[32,2048]{1,0:T(8,128)(2,1)S(1)} %add_convert_fusion.3), channel_id=1, source_target_pairs={{0,4},{1,5},{2,6},{3,7},{4,0},{5,1},{6,2},{7,3},{8,12},{9,13},{10,... | collective-permute-start | bytes 393224 | tf_op jit(solution)/shard_map/ppermute | solution.py:237
  59.3 7.0 %collective-permute-start.24 = (bf16[32,2048]{1,0:T(8,128)(2,1)S(1)}, bf16[32,2048]{1,0:T(8,128)(2,1)S(1)}, u32[]{:S(2)}, u32[]{:S(2)}) collective-permute-start(bf16[32,2048]{1,0:T(8,128)(2,1)S(1)} %get-tuple-element.154), channel_id=1, source_target_pairs={{0,2},{1,3},{2,0},{3,1},{4,6},{5,7},{6,4},{7,5},{8,10},{9,11},{10,... | collective-permute-start | bytes 393224 | tf_op jit(solution)/shard_map/ppermute | solution.py:237
  61.0 5.4 %collective-permute-start.25 = (bf16[32,2048]{1,0:T(8,128)(2,1)S(1)}, bf16[32,2048]{1,0:T(8,128)(2,1)S(1)}, u32[]{:S(2)}, u32[]{:S(2)}) collective-permute-start(bf16[32,2048]{1,0:T(8,128)(2,1)S(1)} %get-tuple-element.158), channel_id=1, source_target_pairs={{0,4},{1,5},{2,6},{3,7},{4,0},{5,1},{6,2},{7,3},{8,12},{9,13},{10,... | collective-permute-start | bytes 393224 | tf_op jit(solution)/shard_map/ppermute | solution.py:237
  66.4 8.2 %collective-permute-start.26 = (bf16[32,2048]{1,0:T(8,128)(2,1)S(1)}, bf16[32,2048]{1,0:T(8,128)(2,1)S(1)}, u32[]{:S(2)}, u32[]{:S(2)}) collective-permute-start(bf16[32,2048]{1,0:T(8,128)(2,1)S(1)} %add_convert_fusion.2), channel_id=1, source_target_pairs={{0,8},{1,9},{2,10},{3,11},{4,12},{5,13},{6,14},{7,15},{8,0},{9,1},... | collective-permute-start | bytes 393224 | tf_op jit(solution)/shard_map/ppermute | solution.py:237
  68.6 6.0 %collective-permute-start.27 = (bf16[32,2048]{1,0:T(8,128)(2,1)S(1)}, bf16[32,2048]{1,0:T(8,128)(2,1)S(1)}, u32[]{:S(2)}, u32[]{:S(2)}) collective-permute-start(bf16[32,2048]{1,0:T(8,128)(2,1)S(1)} %add_convert_fusion.1), channel_id=1, source_target_pairs={{0,4},{1,5},{2,6},{3,7},{4,0},{5,1},{6,2},{7,3},{8,12},{9,13},{10,... | collective-permute-start | bytes 393224 | tf_op jit(solution)/shard_map/ppermute | solution.py:237
  69.6 5.0 %collective-permute-start.28 = (bf16[32,2048]{1,0:T(8,128)(2,1)S(1)}, bf16[32,2048]{1,0:T(8,128)(2,1)S(1)}, u32[]{:S(2)}, u32[]{:S(2)}) collective-permute-start(bf16[32,2048]{1,0:T(8,128)(2,1)S(1)} %get-tuple-element.166), channel_id=1, source_target_pairs={{0,2},{1,3},{2,0},{3,1},{4,6},{5,7},{6,4},{7,5},{8,10},{9,11},{10,... | collective-permute-start | bytes 393224 | tf_op jit(solution)/shard_map/ppermute | solution.py:237
  74.6 7.4 %collective-permute-start.30 = (bf16[32,2048]{1,0:T(8,128)(2,1)S(1)}, bf16[32,2048]{1,0:T(8,128)(2,1)S(1)}, u32[]{:S(2)}, u32[]{:S(2)}) collective-permute-start(bf16[32,2048]{1,0:T(8,128)(2,1)S(1)} %get-tuple-element.173), channel_id=1, source_target_pairs={{0,4},{1,5},{2,6},{3,7},{4,0},{5,1},{6,2},{7,3},{8,12},{9,13},{10,... | collective-permute-start | bytes 393224 | tf_op jit(solution)/shard_map/ppermute | solution.py:237
  75.7 8.3 %collective-permute-start.29 = (bf16[32,4096]{1,0:T(8,128)(2,1)S(1)}, bf16[32,4096]{1,0:T(8,128)(2,1)S(1)}, u32[]{:S(2)}, u32[]{:S(2)}) collective-permute-start(bf16[32,4096]{1,0:T(8,128)(2,1)S(1)} %fusion), channel_id=1, source_target_pairs={{0,2},{1,3},{2,0},{3,1},{4,6},{5,7},{6,4},{7,5},{8,10},{9,11},{10,... | collective-permute-start | bytes 786440 | tf_op jit(solution)/shard_map/ppermute | solution.py:237
  76.7 7.3 %collective-permute-start.31 = (bf16[32,2048]{1,0:T(8,128)(2,1)S(1)}, bf16[32,2048]{1,0:T(8,128)(2,1)S(1)}, u32[]{:S(2)}, u32[]{:S(2)}) collective-permute-start(bf16[32,2048]{1,0:T(8,128)(2,1)S(1)} %add_convert_fusion), channel_id=1, source_target_pairs={{0,8},{1,9},{2,10},{3,11},{4,12},{5,13},{6,14},{7,15},{8,0},{9,1},... | collective-permute-start | bytes 393224 | tf_op jit(solution)/shard_map/ppermute | solution.py:237

commit v5 on v4

--- a/solution.py
+++ b/solution.py
@@ -14,8 +14,7 @@
 PLANES = 4
 CORES = 2
 STEP = 1024
-PARTS = 2
-PIECES = 4
+PIECES = 2
 
 
 def chunk_kernel(k, rows, columns, *refs):
@@ -104,16 +103,14 @@
     both = keep[...].astype(jnp.float32) + arrived[...].astype(jnp.float32)
     at = 0
     for out in outs:
-        block, start = at // D, at % D
-        out[...] = both[block * rows : (block + 1) * rows, start : start + out.shape[1]].astype(out.dtype)
-        at += out.shape[1]
-
-
-def sum_cores(keep, arrived, columns, kind, per):
+        out[...] = both[at : at + out.shape[0]].astype(out.dtype)
+        at += out.shape[0]
+
+
+def sum_cores(keep, arrived, columns, kind):
     rows = keep.shape[0] // columns
-    outs = [jax.ShapeDtypeStruct((rows, D // PARTS), kind)] * PARTS
-    outs += [jax.ShapeDtypeStruct((rows, D // per), jnp.bfloat16)] * ((columns - 1) * per)
-    sums = pl.pallas_call(
+    outs = [jax.ShapeDtypeStruct((rows, D), k) for k in [kind] + [jnp.bfloat16] * (columns - 1)]
+    return pl.pallas_call(
         functools.partial(sum_kernel, rows),
         out_shape=outs,
         in_specs=[pl.BlockSpec(memory_space=pltpu.VMEM)] * 2,
@@ -121,7 +118,6 @@
         compiler_params=pltpu.CompilerParams(vmem_limit_bytes=8 * 1024 * 1024),
         cost_estimate=pl.CostEstimate(flops=rows, bytes_accessed=rows, transcendentals=0),
     )(keep, arrived)
-    return sums[:PARTS], [sums[PARTS + part :: per] for part in range(per)]
 
 
 def pack_kernel(ranks, *refs):
@@ -231,7 +227,6 @@
     devices, groups = lax.axis_size("shard"), lax.axis_size("member")
     columns = devices // (PLANES * CORES)
     rows, hidden = tokens.shape[0], key_weight.shape[1]
-    parts = [slice(i * D // PARTS, (i + 1) * D // PARTS) for i in range(PARTS)]
 
     def swap(array, bits):
         return lax.ppermute(array, "shard", [(i, i ^ bits) for i in range(devices)])
@@ -241,6 +236,9 @@
 
     def over_y(array):
         return [swap(array, j * CORES) for j in range(1, columns)]
+
+    def over_both(array):
+        return [swap(array, (columns + j) * CORES) for j in range(1, columns)]
 
     def over_cores(arrays):
         return [swap(array, 1) for array in arrays]
@@ -265,75 +263,59 @@
     far, near, y0, c0 = over_z(tokens, 2), over_z(tokens, 1), over_y(tokens), over_cores([tokens])
     mix, key = together(shift_mix[None, :], key_weight)
     (key,) = load(key)
-    near, y0, c0, key, value = together(near, y0, c0, key, value_weight)
+    near, y0, c0, key, value, left = together(near, y0, c0, key, value_weight, key_left)
 
     y1, cy0, c1 = over_y(near), over_cores(y0), over_cores([near])
     (value,) = load(value)
-    far, y1, cy0, c1, key, value, left = together(far, y1, cy0, c1, key, value, key_left)
-
-    def partial(k, own, other):
-        return chunk(k, own, other, mix, key_left, key_right, value_left, value_right, key, value)
-
     pack = pack_members(left, key_right, value_left, value_right, ranks)
     packs = [pack] + [
         lax.ppermute(pack, "member", [(i, i ^ bits) for i in range(groups)]) for bits in range(1, groups)
     ]
-    farthest, y2, c2, cy1 = over_z(far, 1), over_y(far), over_cores([far]), over_cores(y1)
-    keep0, send0 = partial(0, [tokens] + y0, c0 + cy0)
-    farthest, y2, c2, cy1, keep0, send0, packs = together(farthest, y2, c2, cy1, keep0, send0, packs)
-
-    y3, c3, cy2 = over_y(farthest), over_cores([farthest]), over_cores(y2)
+    far, y1, cy0, c1, key, value, packs = together(far, y1, cy0, c1, key, value, packs)
+
+    def partial(k, own, other):
+        return chunk(k, own, other, mix, key_left, key_right, value_left, value_right, key, value)
+
+    farthest, y2, y3, c2, cy1 = over_z(far, 1), over_y(far), over_both(far), over_cores([far]), over_cores(y1)
     keep1, send1 = partial(1, [near] + y1, c1 + cy1)
-    far, keep1 = together(far, keep1)
+    own, keep1 = together(tokens, keep1)
+    keep0, send0 = partial(0, [own] + y0, c0 + cy0)
+    packs, keep0 = together(packs, keep0)
+    key_update = updates(True, packs, None, 0, 1)
+    farthest, y2, y3, c2, keep1, send1, send0, key_update = together(
+        farthest, y2, y3, c2, keep1, send1, send0, key_update
+    )
+
+    c3, cy3, cy2, other1 = over_cores([farthest]), over_cores(y3), over_cores(y2), over_cores([send1])
+    keep3, send3 = partial(3, [farthest] + y3, c3 + cy3)
+    cy2, other1, keep3, send3 = together(cy2, other1, keep3, send3)
+
+    mine1, *terms1 = sum_cores(keep1, *other1, columns, jnp.bfloat16)
+    beside1 = [over_z(term, 1) for term in terms1]
+    mine3, *terms3 = sum_cores(keep3, *over_cores([send3]), columns, jnp.float32)
+    far, mine3, terms3 = together(far, mine3, terms3)
+    back3 = back_y(terms3)
     keep2, send2 = partial(2, [far] + y2, c2 + cy2)
-    y3, c3, keep1, send1, keep2, send2 = together(y3, c3, keep1, send1, keep2, send2)
-
-    cy3 = over_cores(y3)
-    mine2, terms2 = sum_cores(keep2, *over_cores([send2]), columns, jnp.float32, PARTS)
-    (other1,) = over_cores([send1])
-    farthest, mine2, terms2 = together(farthest, mine2, terms2)
-    back2a = back_y(terms2[0])
-    keep3, send3 = partial(3, [farthest] + y3, c3 + cy3)
-    back2a, other1, send0, keep3, send3 = together(back2a, other1, send0, keep3, send3)
-
-    mine1, (terms1,) = sum_cores(keep1, other1, columns, jnp.bfloat16, 1)
-    beside1 = [over_z(term, 1) for term in terms1]
-    (back0,) = over_cores([send0])
-    mine3, terms3 = sum_cores(keep3, *over_cores([send3]), columns, jnp.float32, PARTS)
-    packs, mine3, terms3 = together(packs, mine3, terms3)
-    back3 = back_y(terms3[0])
-    key_update = updates(True, packs, None, 0, 2)
-    back3, beside1, back0, rest3, key_update, mine1 = together(
-        back3, beside1, back0, terms3[1], key_update, mine1
-    )
-
-    onward, mine1a = over_z(rounded(add(mine3[0], back3)), 1), over_z(mine1[0], 1)
-    back3 = back_y(rest3)
-    both = keep0.astype(jnp.float32) + back0.astype(jnp.float32)
-    terms0 = [
-        rounded(add(both[j * rows : (j + 1) * rows], [term])) for j, term in enumerate(beside1, 1)
-    ]
-    key_update = updates(True, packs, key_update, 2, 4)
-    onward, back3, terms0, packs, rest2, key_update, mine1a, rest1 = together(
-        onward, back3, terms0, packs, terms2[1], key_update, mine1a, mine1[1]
-    )
-
-    first = over_z(rounded(add(mine2[0], back2a + [onward])), 2)
-    onward = over_z(rounded(add(mine3[1], back3)), 1)
-    back2b = back_y(rest2)
+    beside1, back3, keep2, send2, send0, packs, mine1 = together(
+        beside1, back3, keep2, send2, send0, packs, mine1
+    )
+
+    onward = over_z(rounded(add(mine3, back3)), 1)
+    other0, other2 = over_cores([send0, send2])
+    mine2, *terms2 = sum_cores(keep2, other2, columns, jnp.float32)
+    packs, mine2, terms2 = together(packs, mine2, terms2)
+    back2 = back_y(terms2)
+    key_update = updates(True, packs, key_update, 1, 2)
+    onward, mine2, back2, other0, key_update, packs, mine1 = together(
+        onward, mine2, back2, other0, key_update, packs, mine1
+    )
+
+    last = over_z(rounded(add(mine2, back2 + [onward])), 2)
+    both = keep0.astype(jnp.float32) + other0.astype(jnp.float32)
+    terms0 = [rounded(add(both[j * rows : (j + 1) * rows], [term])) for j, term in enumerate(beside1, 1)]
+    back0, mine1 = back_y(terms0), over_z(mine1, 1)
     value_update = updates(False, packs, None, 0, 2)
-    first, onward, back2b, value_update, packs, terms0, rest1 = together(
-        first, onward, back2b, value_update, packs, terms0, rest1
-    )
-
-    second = over_z(rounded(add(mine2[1], back2b + [onward])), 2)
-    back0, mine1b = back_y(terms0), over_z(rest1, 1)
-    value_update = updates(False, packs, value_update, 2, 4)
-    result = [
-        add(both[:rows, at], [side, arrived] + [term[:, at] for term in back0])
-        for at, side, arrived in zip(parts, (mine1a, mine1b), (first, second))
-    ]
-    return rounded(jnp.concatenate(result, 1)), key_update, value_update
+    return rounded(add(both[:rows], [last, mine1] + back0)), key_update, value_update
 
 
 def solution(mesh):

time: 85.1 us -> 81.2 us (0.954)
  starting transfers between devices: 30 us -> 22.5 us
  waiting for transfers between devices: 20.3 us -> 26 us
  Pallas kernels: 28.4 us -> 26.4 us
    ppermute x31 -> x26, starting transfers between devices: 28.3 us -> 20.9 us  [swap(): return lax.ppermute(array, 'shard', [(i, i ^ bits) for i in range(devices)])]
    ppermute x31 -> x26, waiting for transfers between devices: 19 us -> 23.4 us  [swap(): return lax.ppermute(array, 'shard', [(i, i ^ bits) for i in range(devices)])]
    pallas_call x8 -> x4, Pallas kernels: 14.2 us -> 12.4 us  [update(): pl.pallas_call(functools.partial(update_kernel, fit_rows, piece, groups,...]
    ppermute x1, waiting for transfers between devices: 1.26 us -> 2.57 us  [local(): lax.ppermute(pack, 'member', [(i, i ^ bits) for i in range(groups)])]
  transfers between devices with their start and end apart: 32 -> 27, of which waited for: 13 -> 15; matrix products, arithmetic and copies ran while one was open for 1% -> 1% of each run, Pallas kernels for 33% -> 33%
where the time goes in v5:
time: 81.2 us; the launch traced here: 81 us
  Pallas kernels  26.4 us (33%)
  waiting for transfers between devices  26 us (32%)
  starting transfers between devices  22.5 us (28%)
  local copies, waits for them, and re-layouts  4.12 us (5%)
  other arithmetic  1.13 us (1%)
  between operations  0.83 us (1%)
    ppermute x26, waiting for transfers between devices, swap(): return lax.ppermute(array, 'shard', [(i, i ^ bits) for i in range(devices)])  23.4 us
    ppermute x26, starting transfers between devices, swap(): return lax.ppermute(array, 'shard', [(i, i ^ bits) for i in range(devices)])  20.9 us
    pallas_call x4, Pallas kernels, update(): pl.pallas_call(functools.partial(update_kernel, fit_rows, piece, groups,...  12.4 us
    pallas_call x4, Pallas kernels, chunk(): pl.pallas_call(functools.partial(chunk_kernel, k, rows, columns), out_sha...  11.9 us
    unnamed x16, local copies, waits for them, and re-layouts  3.41 us
    ppermute x1, waiting for transfers between devices, local(): lax.ppermute(pack, 'member', [(i, i ^ bits) for i in range(groups)])  2.57 us
  transfers between devices with their start and end apart: 27, of which 15 were waited for; matrix products, arithmetic and copies ran while one was open for 1% of the time, Pallas kernels for 33%

profile of v5, /device:TPU:0, one launch (start us, length us, event | category | flops | bytes accessed | tf_op | source)
XLA Modules:
  0.0 81.0 jit_solution(11360949477342455569)
XLA Ops:
  0.6 3.1 %collective-permute-start.1 = (bf16[32,4096]{1,0:T(8,128)(2,1)}, bf16[32,4096]{1,0:T(8,128)(2,1)S(1)}, u32[]{:S(2)}, u32[]{:S(2)}) collective-permute-start(bf16[32,4096]{1,0:T(8,128)(2,1)} %refs_0_.3), channel_id=1, source_target_pairs={{0,4},{1,5},{2,6},{3,7},{4,0},{5,1},{6,2},{7,3},{8,12},{9,13},{10,... | collective-permute-start | bytes 786440 | tf_op jit(solution)/shard_map/ppermute | solution.py:232
  3.7 1.5 %collective-permute-start.2 = (bf16[32,4096]{1,0:T(8,128)(2,1)}, bf16[32,4096]{1,0:T(8,128)(2,1)S(1)}, u32[]{:S(2)}, u32[]{:S(2)}) collective-permute-start(bf16[32,4096]{1,0:T(8,128)(2,1)} %refs_0_.3), channel_id=1, source_target_pairs={{0,2},{1,3},{2,0},{3,1},{4,6},{5,7},{6,4},{7,5},{8,10},{9,11},{10,... | collective-permute-start | bytes 786440 | tf_op jit(solution)/shard_map/ppermute | solution.py:232
  5.2 2.6 %collective-permute-start = (bf16[32,4096]{1,0:T(8,128)(2,1)}, bf16[32,4096]{1,0:T(8,128)(2,1)S(1)}, u32[]{:S(2)}, u32[]{:S(2)}) collective-permute-start(bf16[32,4096]{1,0:T(8,128)(2,1)} %refs_0_.3), channel_id=1, source_target_pairs={{0,8},{1,9},{2,10},{3,11},{4,12},{5,13},{6,14},{7,15},{8,0},{9,1},... | collective-permute-start | bytes 786440 | tf_op jit(solution)/shard_map/ppermute | solution.py:232
  7.8 0.7 broadcast_in_dim.3.refs_4_
  8.6 3.4 %copy-done = bf16[4096,1024]{1,0:T(8,128)(2,1)S(1)} copy-done((bf16[4096,1024]{1,0:T(8,128)(2,1)S(1)}, bf16[4096,1024]{1,0:T(8,128)(2,1)}, u32[]{:S(2)}) %copy-start) | copy-done | bytes 8388632
  12.0 0.6 shard_map.112.refs_9_
  12.5 0.2 collective-permute-done.1.refs_0_
  12.8 3.2 %collective-permute-start.4 = (bf16[32,4096]{1,0:T(8,128)(2,1)S(1)}, bf16[32,4096]{1,0:T(8,128)(2,1)S(1)}, u32[]{:S(2)}, u32[]{:S(2)}) collective-permute-start(bf16[32,4096]{1,0:T(8,128)(2,1)S(1)} %collective-permute-done.1.refs_0_), channel_id=1, source_target_pairs={{0,2},{1,3},{2,0},{3,1},{4,6},{5,7},{6,4},{7,5},{8,10},{9,11},{10,... | collective-permute-start | bytes 786440 | tf_op jit(solution)/shard_map/ppermute | solution.py:232
  16.0 0.5 collective-permute-start.5
  16.5 0.6 shard_map.114.refs_0_
  17.1 1.6 %collective-permute-start.7 = (bf16[8,10368]{1,0:T(8,128)(2,1)S(1)}, bf16[8,10368]{1,0:T(8,128)(2,1)S(1)}, u32[]{:S(2)}, u32[]{:S(2)}) collective-permute-start(bf16[8,10368]{1,0:T(8,128)(2,1)S(1)} %shard_map.114.refs_0_), channel_id=1, source_target_pairs={{0,16},{16,0},{1,17},{17,1},{2,18},{18,2},{3,19},{19,3},{4,20},{20... | collective-permute-start | bytes 497672 | tf_op jit(solution)/shard_map/ppermute | solution.py:272
  18.6 0.6 shard_map.113.refs_10_
  19.2 1.5 %collective-permute-done.refs_0_ = bf16[32,4096]{1,0:T(8,128)(2,1)S(1)} collective-permute-done((bf16[32,4096]{1,0:T(8,128)(2,1)}, bf16[32,4096]{1,0:T(8,128)(2,1)S(1)}, u32[]{:S(2)}, u32[]{:S(2)}) %collective-permute-start) | collective-permute-done | bytes 262176 | tf_op jit(solution)/shard_map/ppermute | solution.py:232
  20.7 2.6 %collective-permute-done.7.refs_1_ = bf16[8,10368]{1,0:T(8,128)(2,1)S(1)} collective-permute-done((bf16[8,10368]{1,0:T(8,128)(2,1)S(1)}, bf16[8,10368]{1,0:T(8,128)(2,1)S(1)}, u32[]{:S(2)}, u32[]{:S(2)}) %collective-permute-start.7) | collective-permute-done | bytes 165920 | tf_op jit(solution)/shard_map/ppermute | solution.py:272
  23.4 0.2 collective-permute-start.10
  23.6 1.0 %collective-permute-start.11 = (bf16[32,4096]{1,0:T(8,128)(2,1)S(1)}, bf16[32,4096]{1,0:T(8,128)(2,1)S(1)}, u32[]{:S(2)}, u32[]{:S(2)}) collective-permute-start(bf16[32,4096]{1,0:T(8,128)(2,1)S(1)} %collective-permute-done.refs_0_), channel_id=1, source_target_pairs={{0,6},{1,7},{2,4},{3,5},{4,2},{5,3},{6,0},{7,1},{8,14},{9,15},{10,... | collective-permute-start | bytes 786440 | tf_op jit(solution)/shard_map/ppermute | solution.py:232
  24.6 2.4 %collective-permute-start.9 = (bf16[32,4096]{1,0:T(8,128)(2,1)S(1)}, bf16[32,4096]{1,0:T(8,128)(2,1)S(1)}, u32[]{:S(2)}, u32[]{:S(2)}) collective-permute-start(bf16[32,4096]{1,0:T(8,128)(2,1)S(1)} %collective-permute-done.refs_0_), channel_id=1, source_target_pairs={{0,4},{1,5},{2,6},{3,7},{4,0},{5,1},{6,2},{7,3},{8,12},{9,13},{10,... | collective-permute-start | bytes 786440 | tf_op jit(solution)/shard_map/ppermute | solution.py:232
  27.0 3.0 %shard_map.115 = (bf16[64,4096]{1,0:T(8,128)(2,1)S(1)}, bf16[64,4096]{1,0:T(8,128)(2,1)S(1)}) custom-call(bf16[32,4096]{1,0:T(8,128)(2,1)S(1)} %collective-permute-done.1.refs_0_, bf16[32,4096]{1,0:T(8,128)(2,1)S(1)} %collective-permute-done.4.refs_1_, bf16[32,4096]{1,0:T(8,128)(2,1)S(1)} %collective-permute-done.6.refs_2_, ...), custom_call_target="tpu_custom_call" | custom-call | flops 128 | bytes 128 | tf_op jit(solution)/shard_map/pallas_call | solution.py:85
  30.0 3.0 %shard_map.116 = (bf16[64,4096]{1,0:T(8,128)(2,1)S(1)}, bf16[64,4096]{1,0:T(8,128)(2,1)S(1)}) custom-call(bf16[32,4096]{1,0:T(8,128)(2,1)S(1)} %copy-done.6, bf16[32,4096]{1,0:T(8,128)(2,1)S(1)} %collective-permute-done.2.refs_1_, bf16[32,4096]{1,0:T(8,128)(2,1)S(1)} %collective-permute-done.3.refs_2_, bf16[32,4096]{1,0:T(8,128)(2,1)S(1)} %collective-permute-done.5.refs_3_, ...), custom_call_target="tpu_custom_call" | custom-call | flops 128 | bytes 128 | tf_op jit(solution)/shard_map/pallas_call | solution.py:85
  33.0 3.2 %shard_map.117.refs_2_ = f32[2048,1024]{1,0:T(8,128)} custom-call(bf16[8,10368]{1,0:T(8,128)(2,1)S(1)} %shard_map.114.refs_0_, bf16[8,10368]{1,0:T(8,128)(2,1)S(1)} %collective-permute-done.7.refs_1_), custom_call_target="tpu_custom_call" | custom-call | flops 256 | bytes 256 | tf_op jit(solution)/shard_map/pallas_call | solution.py:207
  36.1 1.6 %collective-permute-done.10.refs_1_ = bf16[32,4096]{1,0:T(8,128)(2,1)S(1)} collective-permute-done((bf16[32,4096]{1,0:T(8,128)(2,1)S(1)}, bf16[32,4096]{1,0:T(8,128)(2,1)S(1)}, u32[]{:S(2)}, u32[]{:S(2)}) %collective-permute-start.10) | collective-permute-done | bytes 262176 | tf_op jit(solution)/shard_map/ppermute | solution.py:232
  37.7 1.2 %collective-permute-done.9.refs_0_ = bf16[32,4096]{1,0:T(8,128)(2,1)S(1)} collective-permute-done((bf16[32,4096]{1,0:T(8,128)(2,1)S(1)}, bf16[32,4096]{1,0:T(8,128)(2,1)S(1)}, u32[]{:S(2)}, u32[]{:S(2)}) %collective-permute-start.9) | collective-permute-done | bytes 262176 | tf_op jit(solution)/shard_map/ppermute | solution.py:232
  39.0 0.5 collective-permute-start.15
  39.5 0.5 collective-permute-start.13
  40.0 1.3 %collective-permute-done.15.refs_2_ = bf16[32,4096]{1,0:T(8,128)(2,1)S(1)} collective-permute-done((bf16[32,4096]{1,0:T(8,128)(2,1)S(1)}, bf16[32,4096]{1,0:T(8,128)(2,1)S(1)}, u32[]{:S(2)}, u32[]{:S(2)}) %collective-permute-start.15) | collective-permute-done | bytes 262176 | tf_op jit(solution)/shard_map/ppermute | solution.py:232
  41.3 0.4 collective-permute-done.16.refs_3_
  41.6 3.0 %shard_map.118 = (bf16[64,4096]{1,0:T(8,128)(2,1)S(1)}, bf16[64,4096]{1,0:T(8,128)(2,1)S(1)}) custom-call(bf16[32,4096]{1,0:T(8,128)(2,1)S(1)} %collective-permute-done.9.refs_0_, bf16[32,4096]{1,0:T(8,128)(2,1)S(1)} %collective-permute-done.11.refs_1_, bf16[32,4096]{1,0:T(8,128)(2,1)S(1)} %collective-permute-done.15.refs_2_, ...), custom_call_target="tpu_custom_call" | custom-call | flops 128 | bytes 128 | tf_op jit(solution)/shard_map/pallas_call | solution.py:85
  44.6 0.2 collective-permute-start.17
  45.0 1.6 %collective-permute-done.17.arrived = bf16[64,4096]{1,0:T(8,128)(2,1)S(1)} collective-permute-done((bf16[64,4096]{1,0:T(8,128)(2,1)S(1)}, bf16[64,4096]{1,0:T(8,128)(2,1)S(1)}, u32[]{:S(2)}, u32[]{:S(2)}) %collective-permute-start.17) | collective-permute-done | bytes 524320 | tf_op jit(solution)/shard_map/ppermute | solution.py:232
  46.7 0.3 collective-permute-start.19
  47.1 3.0 %shard_map.121 = (bf16[64,4096]{1,0:T(8,128)(2,1)S(1)}, bf16[64,4096]{1,0:T(8,128)(2,1)S(1)}) custom-call(bf16[32,4096]{1,0:T(8,128)(2,1)S(1)} %collective-permute-done.refs_0_, bf16[32,4096]{1,0:T(8,128)(2,1)S(1)} %collective-permute-done.10.refs_1_, bf16[32,4096]{1,0:T(8,128)(2,1)S(1)} %collective-permute-done.12.refs_2_, ...), custom_call_target="tpu_custom_call" | custom-call | flops 128 | bytes 128 | tf_op jit(solution)/shard_map/pallas_call | solution.py:85
  50.0 3.6 %collective-permute-done.18 = bf16[32,4096]{1,0:T(8,128)(2,1)S(1)} collective-permute-done((bf16[32,4096]{1,0:T(8,128)(2,1)S(1)}, bf16[32,4096]{1,0:T(8,128)(2,1)S(1)}, u32[]{:S(2)}, u32[]{:S(2)}) %collective-permute-start.18) | collective-permute-done | bytes 262176 | tf_op jit(solution)/shard_map/ppermute | solution.py:232
  53.6 1.5 %collective-permute-done.19 = bf16[32,4096]{1,0:T(8,128)(2,1)S(1)} collective-permute-done((bf16[32,4096]{1,0:T(8,128)(2,1)S(1)}, bf16[32,4096]{1,0:T(8,128)(2,1)S(1)}, u32[]{:S(2)}, u32[]{:S(2)}) %collective-permute-start.19) | collective-permute-done | bytes 262176 | tf_op jit(solution)/shard_map/ppermute | solution.py:232
  55.1 0.5 collective-permute-start.23
  55.7 0.5 collective-permute-start.20
  56.2 0.9 %collective-permute-done.21.arrived = bf16[64,4096]{1,0:T(8,128)(2,1)S(1)} collective-permute-done((bf16[64,4096]{1,0:T(8,128)(2,1)S(1)}, bf16[64,4096]{1,0:T(8,128)(2,1)S(1)}, u32[]{:S(2)}, u32[]{:S(2)}) %collective-permute-start.21) | collective-permute-done | bytes 524320 | tf_op jit(solution)/shard_map/ppermute | solution.py:232
  57.2 0.4 collective-permute-start.22
  57.5 3.1 %shard_map.123 = f32[2048,1024]{1,0:T(8,128)} custom-call(bf16[8,10368]{1,0:T(8,128)(2,1)S(1)} %shard_map.114.refs_0_, bf16[8,10368]{1,0:T(8,128)(2,1)S(1)} %collective-permute-done.7.refs_1_, f32[2048,1024]{1,0:T(8,128)} %shard_map.117.refs_2_), custom_call_target="tpu_custom_call", output_to_operand_aliasing={{}: (2, {})} | custom-call | flops 256 | bytes 256 | tf_op jit(solution)/shard_map/pallas_call | solution.py:207
  60.7 3.3 %collective-permute-done.20 = bf16[32,4096]{1,0:T(8,128)(2,1)S(1)} collective-permute-done((bf16[32,4096]{1,0:T(8,128)(2,1)S(1)}, bf16[32,4096]{1,0:T(8,128)(2,1)S(1)}, u32[]{:S(2)}, u32[]{:S(2)}) %collective-permute-start.20) | collective-permute-done | bytes 262176 | tf_op jit(solution)/shard_map/ppermute | solution.py:232
  64.0 1.6 %collective-permute-done.22 = bf16[32,4096]{1,0:T(8,128)(2,1)S(1)} collective-permute-done((bf16[32,4096]{1,0:T(8,128)(2,1)S(1)}, bf16[32,4096]{1,0:T(8,128)(2,1)S(1)}, u32[]{:S(2)}, u32[]{:S(2)}) %collective-permute-start.22) | collective-permute-done | bytes 262176 | tf_op jit(solution)/shard_map/ppermute | solution.py:232
  65.7 1.5 %collective-permute-start.24 = (bf16[32,4096]{1,0:T(8,128)(2,1)S(1)}, bf16[32,4096]{1,0:T(8,128)(2,1)S(1)}, u32[]{:S(2)}, u32[]{:S(2)}) collective-permute-start(bf16[32,4096]{1,0:T(8,128)(2,1)S(1)} %add_convert_fusion), channel_id=1, source_target_pairs={{0,8},{1,9},{2,10},{3,11},{4,12},{5,13},{6,14},{7,15},{8,0},{9,1},... | collective-permute-start | bytes 786440 | tf_op jit(solution)/shard_map/ppermute | solution.py:232
  67.3 0.5 collective-permute-start.26
  67.8 1.5 %collective-permute-start.25 = (bf16[32,4096]{1,0:T(8,128)(2,1)S(1)}, bf16[32,4096]{1,0:T(8,128)(2,1)S(1)}, u32[]{:S(2)}, u32[]{:S(2)}) collective-permute-start(bf16[32,4096]{1,0:T(8,128)(2,1)S(1)} %get-tuple-element.138), channel_id=1, source_target_pairs={{0,4},{1,5},{2,6},{3,7},{4,0},{5,1},{6,2},{7,3},{8,12},{9,13},{10,... | collective-permute-start | bytes 786440 | tf_op jit(solution)/shard_map/ppermute | solution.py:232
  69.3 3.0 %shard_map.124.refs_2_ = f32[1024,2048]{1,0:T(8,128)} custom-call(bf16[8,10368]{1,0:T(8,128)(2,1)S(1)} %shard_map.114.refs_0_, bf16[8,10368]{1,0:T(8,128)(2,1)S(1)} %collective-permute-done.7.refs_1_), custom_call_target="tpu_custom_call" | custom-call | flops 128 | bytes 128 | tf_op jit(solution)/shard_map/pallas_call | solution.py:207
  72.4 3.0 %shard_map.125 = f32[1024,2048]{1,0:T(8,128)} custom-call(bf16[8,10368]{1,0:T(8,128)(2,1)S(1)} %shard_map.114.refs_0_, bf16[8,10368]{1,0:T(8,128)(2,1)S(1)} %collective-permute-done.7.refs_1_, f32[1024,2048]{1,0:T(8,128)} %shard_map.124.refs_2_), custom_call_target="tpu_custom_call", output_to_operand_aliasing={{}: (2, {})} | custom-call | flops 128 | bytes 128 | tf_op jit(solution)/shard_map/pallas_call | solution.py:207
  75.4 4.3 %collective-permute-done.24 = bf16[32,4096]{1,0:T(8,128)(2,1)S(1)} collective-permute-done((bf16[32,4096]{1,0:T(8,128)(2,1)S(1)}, bf16[32,4096]{1,0:T(8,128)(2,1)S(1)}, u32[]{:S(2)}, u32[]{:S(2)}) %collective-permute-start.24) | collective-permute-done | bytes 262176 | tf_op jit(solution)/shard_map/ppermute | solution.py:232
  79.7 0.4 collective-permute-done.25
  80.2 0.8 %fusion.3 = bf16[32,4096]{1,0:T(8,128)(2,1)} fusion(f32[64,4096]{1,0:T(8,128)S(1)} %convert_add_fusion, bf16[32,4096]{1,0:T(8,128)(2,1)S(1)} %collective-permute-done.26, bf16[32,4096]{1,0:T(8,128)(2,1)S(1)} %collective-permute-done.25, bf16[32,4096]{1,0:T(8,128)(2,1)S(1)} %collective-permute-done.24), kind=kLoop, calls=%fused_computation.6 | loop fusion | flops 917504 | bytes 1572864 | tf_op jit(solution)/shard_map/convert_element_type | solution.py:261
  (42 shorter events, 0.9 us)
Async XLA Ops:
  0.6 12.1 %collective-permute-start.1 = (bf16[32,4096]{1,0:T(8,128)(2,1)}, bf16[32,4096]{1,0:T(8,128)(2,1)S(1)}, u32[]{:S(2)}, u32[]{:S(2)}) collective-permute-start(bf16[32,4096]{1,0:T(8,128)(2,1)} %refs_0_.3), channel_id=1, source_target_pairs={{0,4},{1,5},{2,6},{3,7},{4,0},{5,1},{6,2},{7,3},{8,12},{9,13},{10,... | collective-permute-start | bytes 786440 | tf_op jit(solution)/shard_map/ppermute | solution.py:232
  3.7 9.0 %collective-permute-start.2 = (bf16[32,4096]{1,0:T(8,128)(2,1)}, bf16[32,4096]{1,0:T(8,128)(2,1)S(1)}, u32[]{:S(2)}, u32[]{:S(2)}) collective-permute-start(bf16[32,4096]{1,0:T(8,128)(2,1)} %refs_0_.3), channel_id=1, source_target_pairs={{0,2},{1,3},{2,0},{3,1},{4,6},{5,7},{6,4},{7,5},{8,10},{9,11},{10,... | collective-permute-start | bytes 786440 | tf_op jit(solution)/shard_map/ppermute | solution.py:232
  5.2 7.5 %collective-permute-start.3 = (bf16[32,4096]{1,0:T(8,128)(2,1)}, bf16[32,4096]{1,0:T(8,128)(2,1)S(1)}, u32[]{:S(2)}, u32[]{:S(2)}) collective-permute-start(bf16[32,4096]{1,0:T(8,128)(2,1)} %refs_0_.3), channel_id=1, source_target_pairs={{0,1},{1,0},{2,3},{3,2},{4,5},{5,4},{6,7},{7,6},{8,9},{9,8},{10,11... | collective-permute-start | bytes 786440 | tf_op jit(solution)/shard_map/ppermute | solution.py:232
  5.2 15.5 %collective-permute-start = (bf16[32,4096]{1,0:T(8,128)(2,1)}, bf16[32,4096]{1,0:T(8,128)(2,1)S(1)}, u32[]{:S(2)}, u32[]{:S(2)}) collective-permute-start(bf16[32,4096]{1,0:T(8,128)(2,1)} %refs_0_.3), channel_id=1, source_target_pairs={{0,8},{1,9},{2,10},{3,11},{4,12},{5,13},{6,14},{7,15},{8,0},{9,1},... | collective-permute-start | bytes 786440 | tf_op jit(solution)/shard_map/ppermute | solution.py:232
  8.5 3.4 %copy-start = (bf16[4096,1024]{1,0:T(8,128)(2,1)S(1)}, bf16[4096,1024]{1,0:T(8,128)(2,1)}, u32[]{:S(2)}) copy-start(bf16[4096,1024]{1,0:T(8,128)(2,1)} %refs_0_) | copy-start | bytes 25165828
  11.9 4.6 %copy-start.2 = (bf16[8,4096]{1,0:T(8,128)(2,1)S(1)}, bf16[8,4096]{1,0:T(8,128)(2,1)}, u32[]{:S(2)}) copy-start(bf16[8,4096]{1,0:T(8,128)(2,1)} %refs_5_.7) | copy-start | bytes 196612
  11.9 4.6 %copy-start.3 = (bf16[8,4096]{1,0:T(8,128)(2,1)S(1)}, bf16[8,4096]{1,0:T(8,128)(2,1)}, u32[]{:S(2)}) copy-start(bf16[8,4096]{1,0:T(8,128)(2,1)} %refs_8_.7) | copy-start | bytes 196612
  11.9 4.6 %copy-start.4 = (bf16[8,1024]{1,0:T(8,128)(2,1)S(1)}, bf16[8,1024]{1,0:T(8,128)(2,1)}, u32[]{:S(2)}) copy-start(bf16[8,1024]{1,0:T(8,128)(2,1)} %refs_6_.7) | copy-start | bytes 49156
  11.9 4.6 %copy-start.5 = (bf16[8,1024]{1,0:T(8,128)(2,1)S(1)}, bf16[8,1024]{1,0:T(8,128)(2,1)}, u32[]{:S(2)}) copy-start(bf16[8,1024]{1,0:T(8,128)(2,1)} %refs_7_.7) | copy-start | bytes 49156
  11.9 4.6 %copy-start.7 = (s32[8]{0:T(128)S(1)}, s32[8]{0:T(128)}, u32[]{:S(2)}) copy-start(s32[8]{0:T(128)} %ranks.1) | copy-start | bytes 100
  11.9 6.7 %copy-start.1 = (bf16[1024,4096]{1,0:T(8,128)(2,1)S(1)}, bf16[1024,4096]{1,0:T(8,128)(2,1)}, u32[]{:S(2)}) copy-start(bf16[1024,4096]{1,0:T(8,128)(2,1)} %refs_0_.1) | copy-start | bytes 25165828
  12.8 10.5 %collective-permute-start.4 = (bf16[32,4096]{1,0:T(8,128)(2,1)S(1)}, bf16[32,4096]{1,0:T(8,128)(2,1)S(1)}, u32[]{:S(2)}, u32[]{:S(2)}) collective-permute-start(bf16[32,4096]{1,0:T(8,128)(2,1)S(1)} %collective-permute-done.1.refs_0_), channel_id=1, source_target_pairs={{0,2},{1,3},{2,0},{3,1},{4,6},{5,7},{6,4},{7,5},{8,10},{9,11},{10,... | collective-permute-start | bytes 786440 | tf_op jit(solution)/shard_map/ppermute | solution.py:232
  16.0 7.3 %collective-permute-start.6 = (bf16[32,4096]{1,0:T(8,128)(2,1)S(1)}, bf16[32,4096]{1,0:T(8,128)(2,1)S(1)}, u32[]{:S(2)}, u32[]{:S(2)}) collective-permute-start(bf16[32,4096]{1,0:T(8,128)(2,1)S(1)} %collective-permute-done.1.refs_0_), channel_id=1, source_target_pairs={{0,1},{1,0},{2,3},{3,2},{4,5},{5,4},{6,7},{7,6},{8,9},{9,8},{10,11... | collective-permute-start | bytes 786440 | tf_op jit(solution)/shard_map/ppermute | solution.py:232
  16.0 7.3 %collective-permute-start.5 = (bf16[32,4096]{1,0:T(8,128)(2,1)S(1)}, bf16[32,4096]{1,0:T(8,128)(2,1)S(1)}, u32[]{:S(2)}, u32[]{:S(2)}) collective-permute-start(bf16[32,4096]{1,0:T(8,128)(2,1)S(1)} %collective-permute-done.2.refs_1_), channel_id=1, source_target_pairs={{0,1},{1,0},{2,3},{3,2},{4,5},{5,4},{6,7},{7,6},{8,9},{9,8},{10,11... | collective-permute-start | bytes 786440 | tf_op jit(solution)/shard_map/ppermute | solution.py:232
  17.1 6.2 %collective-permute-start.7 = (bf16[8,10368]{1,0:T(8,128)(2,1)S(1)}, bf16[8,10368]{1,0:T(8,128)(2,1)S(1)}, u32[]{:S(2)}, u32[]{:S(2)}) collective-permute-start(bf16[8,10368]{1,0:T(8,128)(2,1)S(1)} %shard_map.114.refs_0_), channel_id=1, source_target_pairs={{0,16},{16,0},{1,17},{17,1},{2,18},{18,2},{3,19},{19,3},{4,20},{20... | collective-permute-start | bytes 497672 | tf_op jit(solution)/shard_map/ppermute | solution.py:272
  19.2 10.8 %copy-start.6 = (bf16[32,4096]{1,0:T(8,128)(2,1)S(1)}, bf16[32,4096]{1,0:T(8,128)(2,1)}, u32[]{:S(2)}) copy-start(bf16[32,4096]{1,0:T(8,128)(2,1)} %refs_0_.3) | copy-start | bytes 786436
  23.3 3.6 %collective-permute-start.8 = (bf16[32,4096]{1,0:T(8,128)(2,1)S(1)}, bf16[32,4096]{1,0:T(8,128)(2,1)S(1)}, u32[]{:S(2)}, u32[]{:S(2)}) collective-permute-start(bf16[32,4096]{1,0:T(8,128)(2,1)S(1)} %collective-permute-done.4.refs_1_), channel_id=1, source_target_pairs={{0,1},{1,0},{2,3},{3,2},{4,5},{5,4},{6,7},{7,6},{8,9},{9,8},{10,11... | collective-permute-start | bytes 786440 | tf_op jit(solution)/shard_map/ppermute | solution.py:232
  23.4 14.3 %collective-permute-start.10 = (bf16[32,4096]{1,0:T(8,128)(2,1)S(1)}, bf16[32,4096]{1,0:T(8,128)(2,1)S(1)}, u32[]{:S(2)}, u32[]{:S(2)}) collective-permute-start(bf16[32,4096]{1,0:T(8,128)(2,1)S(1)} %collective-permute-done.refs_0_), channel_id=1, source_target_pairs={{0,2},{1,3},{2,0},{3,1},{4,6},{5,7},{6,4},{7,5},{8,10},{9,11},{10,... | collective-permute-start | bytes 786440 | tf_op jit(solution)/shard_map/ppermute | solution.py:232
  23.6 14.1 %collective-permute-start.11 = (bf16[32,4096]{1,0:T(8,128)(2,1)S(1)}, bf16[32,4096]{1,0:T(8,128)(2,1)S(1)}, u32[]{:S(2)}, u32[]{:S(2)}) collective-permute-start(bf16[32,4096]{1,0:T(8,128)(2,1)S(1)} %collective-permute-done.refs_0_), channel_id=1, source_target_pairs={{0,6},{1,7},{2,4},{3,5},{4,2},{5,3},{6,0},{7,1},{8,14},{9,15},{10,... | collective-permute-start | bytes 786440 | tf_op jit(solution)/shard_map/ppermute | solution.py:232
  24.6 13.2 %collective-permute-start.12 = (bf16[32,4096]{1,0:T(8,128)(2,1)S(1)}, bf16[32,4096]{1,0:T(8,128)(2,1)S(1)}, u32[]{:S(2)}, u32[]{:S(2)}) collective-permute-start(bf16[32,4096]{1,0:T(8,128)(2,1)S(1)} %collective-permute-done.refs_0_), channel_id=1, source_target_pairs={{0,1},{1,0},{2,3},{3,2},{4,5},{5,4},{6,7},{7,6},{8,9},{9,8},{10,11... | collective-permute-start | bytes 786440 | tf_op jit(solution)/shard_map/ppermute | solution.py:232
  24.6 14.4 %collective-permute-start.9 = (bf16[32,4096]{1,0:T(8,128)(2,1)S(1)}, bf16[32,4096]{1,0:T(8,128)(2,1)S(1)}, u32[]{:S(2)}, u32[]{:S(2)}) collective-permute-start(bf16[32,4096]{1,0:T(8,128)(2,1)S(1)} %collective-permute-done.refs_0_), channel_id=1, source_target_pairs={{0,4},{1,5},{2,6},{3,7},{4,0},{5,1},{6,2},{7,3},{8,12},{9,13},{10,... | collective-permute-start | bytes 786440 | tf_op jit(solution)/shard_map/ppermute | solution.py:232
  39.0 5.7 %collective-permute-start.14 = (bf16[64,4096]{1,0:T(8,128)(2,1)S(1)}, bf16[64,4096]{1,0:T(8,128)(2,1)S(1)}, u32[]{:S(2)}, u32[]{:S(2)}) collective-permute-start(bf16[64,4096]{1,0:T(8,128)(2,1)S(1)} %get-tuple-element.99), channel_id=1, source_target_pairs={{0,1},{1,0},{2,3},{3,2},{4,5},{5,4},{6,7},{7,6},{8,9},{9,8},{10,11... | collective-permute-start | bytes 1572872 | tf_op jit(solution)/shard_map/ppermute | solution.py:232
  39.0 2.3 %collective-permute-start.15 = (bf16[32,4096]{1,0:T(8,128)(2,1)S(1)}, bf16[32,4096]{1,0:T(8,128)(2,1)S(1)}, u32[]{:S(2)}, u32[]{:S(2)}) collective-permute-start(bf16[32,4096]{1,0:T(8,128)(2,1)S(1)} %collective-permute-done.9.refs_0_), channel_id=1, source_target_pairs={{0,1},{1,0},{2,3},{3,2},{4,5},{5,4},{6,7},{7,6},{8,9},{9,8},{10,11... | collective-permute-start | bytes 786440 | tf_op jit(solution)/shard_map/ppermute | solution.py:232
  39.5 2.1 %collective-permute-start.16 = (bf16[32,4096]{1,0:T(8,128)(2,1)S(1)}, bf16[32,4096]{1,0:T(8,128)(2,1)S(1)}, u32[]{:S(2)}, u32[]{:S(2)}) collective-permute-start(bf16[32,4096]{1,0:T(8,128)(2,1)S(1)} %collective-permute-done.11.refs_1_), channel_id=1, source_target_pairs={{0,1},{1,0},{2,3},{3,2},{4,5},{5,4},{6,7},{7,6},{8,9},{9,8},{10,11... | collective-permute-start | bytes 786440 | tf_op jit(solution)/shard_map/ppermute | solution.py:232
  39.5 5.1 %collective-permute-start.13 = (bf16[32,4096]{1,0:T(8,128)(2,1)S(1)}, bf16[32,4096]{1,0:T(8,128)(2,1)S(1)}, u32[]{:S(2)}, u32[]{:S(2)}) collective-permute-start(bf16[32,4096]{1,0:T(8,128)(2,1)S(1)} %collective-permute-done.10.refs_1_), channel_id=1, source_target_pairs={{0,1},{1,0},{2,3},{3,2},{4,5},{5,4},{6,7},{7,6},{8,9},{9,8},{10,11... | collective-permute-start | bytes 786440 | tf_op jit(solution)/shard_map/ppermute | solution.py:232
  44.6 2.0 %collective-permute-start.17 = (bf16[64,4096]{1,0:T(8,128)(2,1)S(1)}, bf16[64,4096]{1,0:T(8,128)(2,1)S(1)}, u32[]{:S(2)}, u32[]{:S(2)}) collective-permute-start(bf16[64,4096]{1,0:T(8,128)(2,1)S(1)} %get-tuple-element.105), channel_id=1, source_target_pairs={{0,1},{1,0},{2,3},{3,2},{4,5},{5,4},{6,7},{7,6},{8,9},{9,8},{10,11... | collective-permute-start | bytes 1572872 | tf_op jit(solution)/shard_map/ppermute | solution.py:232
  45.0 8.7 %collective-permute-start.18 = (bf16[32,4096]{1,0:T(8,128)(2,1)S(1)}, bf16[32,4096]{1,0:T(8,128)(2,1)S(1)}, u32[]{:S(2)}, u32[]{:S(2)}) collective-permute-start(bf16[32,4096]{1,0:T(8,128)(2,1)S(1)} %get-tuple-element.111), channel_id=1, source_target_pairs={{0,4},{1,5},{2,6},{3,7},{4,0},{5,1},{6,2},{7,3},{8,12},{9,13},{10,... | collective-permute-start | bytes 786440 | tf_op jit(solution)/shard_map/ppermute | solution.py:232
  46.7 8.4 %collective-permute-start.19 = (bf16[32,4096]{1,0:T(8,128)(2,1)S(1)}, bf16[32,4096]{1,0:T(8,128)(2,1)S(1)}, u32[]{:S(2)}, u32[]{:S(2)}) collective-permute-start(bf16[32,4096]{1,0:T(8,128)(2,1)S(1)} %get-tuple-element.112), channel_id=1, source_target_pairs={{0,2},{1,3},{2,0},{3,1},{4,6},{5,7},{6,4},{7,5},{8,10},{9,11},{10,... | collective-permute-start | bytes 786440 | tf_op jit(solution)/shard_map/ppermute | solution.py:232
  55.1 1.9 %collective-permute-start.21 = (bf16[64,4096]{1,0:T(8,128)(2,1)S(1)}, bf16[64,4096]{1,0:T(8,128)(2,1)S(1)}, u32[]{:S(2)}, u32[]{:S(2)}) collective-permute-start(bf16[64,4096]{1,0:T(8,128)(2,1)S(1)} %get-tuple-element.124), channel_id=1, source_target_pairs={{0,1},{1,0},{2,3},{3,2},{4,5},{5,4},{6,7},{7,6},{8,9},{9,8},{10,11... | collective-permute-start | bytes 1572872 | tf_op jit(solution)/shard_map/ppermute | solution.py:232
  55.1 8.9 %collective-permute-start.23 = (bf16[64,4096]{1,0:T(8,128)(2,1)S(1)}, bf16[64,4096]{1,0:T(8,128)(2,1)S(1)}, u32[]{:S(2)}, u32[]{:S(2)}) collective-permute-start(bf16[64,4096]{1,0:T(8,128)(2,1)S(1)} %get-tuple-element.129), channel_id=1, source_target_pairs={{0,1},{1,0},{2,3},{3,2},{4,5},{5,4},{6,7},{7,6},{8,9},{9,8},{10,11... | collective-permute-start | bytes 1572872 | tf_op jit(solution)/shard_map/ppermute | solution.py:232
  55.7 8.3 %collective-permute-start.20 = (bf16[32,4096]{1,0:T(8,128)(2,1)S(1)}, bf16[32,4096]{1,0:T(8,128)(2,1)S(1)}, u32[]{:S(2)}, u32[]{:S(2)}) collective-permute-start(bf16[32,4096]{1,0:T(8,128)(2,1)S(1)} %add_convert_fusion.1), channel_id=1, source_target_pairs={{0,4},{1,5},{2,6},{3,7},{4,0},{5,1},{6,2},{7,3},{8,12},{9,13},{10,... | collective-permute-start | bytes 786440 | tf_op jit(solution)/shard_map/ppermute | solution.py:232
  57.2 8.4 %collective-permute-start.22 = (bf16[32,4096]{1,0:T(8,128)(2,1)S(1)}, bf16[32,4096]{1,0:T(8,128)(2,1)S(1)}, u32[]{:S(2)}, u32[]{:S(2)}) collective-permute-start(bf16[32,4096]{1,0:T(8,128)(2,1)S(1)} %get-tuple-element.128), channel_id=1, source_target_pairs={{0,2},{1,3},{2,0},{3,1},{4,6},{5,7},{6,4},{7,5},{8,10},{9,11},{10,... | collective-permute-start | bytes 786440 | tf_op jit(solution)/shard_map/ppermute | solution.py:232
  65.7 14.0 %collective-permute-start.24 = (bf16[32,4096]{1,0:T(8,128)(2,1)S(1)}, bf16[32,4096]{1,0:T(8,128)(2,1)S(1)}, u32[]{:S(2)}, u32[]{:S(2)}) collective-permute-start(bf16[32,4096]{1,0:T(8,128)(2,1)S(1)} %add_convert_fusion), channel_id=1, source_target_pairs={{0,8},{1,9},{2,10},{3,11},{4,12},{5,13},{6,14},{7,15},{8,0},{9,1},... | collective-permute-start | bytes 786440 | tf_op jit(solution)/shard_map/ppermute | solution.py:232
  67.3 12.4 %collective-permute-start.26 = (bf16[32,4096]{1,0:T(8,128)(2,1)S(1)}, bf16[32,4096]{1,0:T(8,128)(2,1)S(1)}, u32[]{:S(2)}, u32[]{:S(2)}) collective-permute-start(bf16[32,4096]{1,0:T(8,128)(2,1)S(1)} %fusion), channel_id=1, source_target_pairs={{0,2},{1,3},{2,0},{3,1},{4,6},{5,7},{6,4},{7,5},{8,10},{9,11},{10,... | collective-permute-start | bytes 786440 | tf_op jit(solution)/shard_map/ppermute | solution.py:232
  67.8 12.3 %collective-permute-start.25 = (bf16[32,4096]{1,0:T(8,128)(2,1)S(1)}, bf16[32,4096]{1,0:T(8,128)(2,1)S(1)}, u32[]{:S(2)}, u32[]{:S(2)}) collective-permute-start(bf16[32,4096]{1,0:T(8,128)(2,1)S(1)} %get-tuple-element.138), channel_id=1, source_target_pairs={{0,4},{1,5},{2,6},{3,7},{4,0},{5,1},{6,2},{7,3},{8,12},{9,13},{10,... | collective-permute-start | bytes 786440 | tf_op jit(solution)/shard_map/ppermute | solution.py:232

commit v6 on v5

--- a/solution.py
+++ b/solution.py
@@ -14,7 +14,7 @@
 PLANES = 4
 CORES = 2
 STEP = 1024
-PIECES = 2
+PIECES = 4
 
 
 def chunk_kernel(k, rows, columns, *refs):
@@ -261,17 +261,17 @@
         return array.astype(jnp.bfloat16)
 
     far, near, y0, c0 = over_z(tokens, 2), over_z(tokens, 1), over_y(tokens), over_cores([tokens])
-    mix, key = together(shift_mix[None, :], key_weight)
+    near, y0, c0, mix, key = together(near, y0, c0, shift_mix[None, :], key_weight)
+
+    y1, cy0, c1 = over_y(near), over_cores(y0), over_cores([near])
     (key,) = load(key)
-    near, y0, c0, key, value, left = together(near, y0, c0, key, value_weight, key_left)
-
-    y1, cy0, c1 = over_y(near), over_cores(y0), over_cores([near])
+    far, y1, cy0, c1, key, value, left = together(far, y1, cy0, c1, key, value_weight, key_left)
+
     (value,) = load(value)
     pack = pack_members(left, key_right, value_left, value_right, ranks)
     packs = [pack] + [
         lax.ppermute(pack, "member", [(i, i ^ bits) for i in range(groups)]) for bits in range(1, groups)
     ]
-    far, y1, cy0, c1, key, value, packs = together(far, y1, cy0, c1, key, value, packs)
 
     def partial(k, own, other):
         return chunk(k, own, other, mix, key_left, key_right, value_left, value_right, key, value)
@@ -296,8 +296,10 @@
     far, mine3, terms3 = together(far, mine3, terms3)
     back3 = back_y(terms3)
     keep2, send2 = partial(2, [far] + y2, c2 + cy2)
-    beside1, back3, keep2, send2, send0, packs, mine1 = together(
-        beside1, back3, keep2, send2, send0, packs, mine1
+    packs, keep2 = together(packs, keep2)
+    key_update = updates(True, packs, key_update, 1, 2)
+    beside1, back3, keep2, send2, send0, packs, mine1, key_update = together(
+        beside1, back3, keep2, send2, send0, packs, mine1, key_update
     )
 
     onward = over_z(rounded(add(mine3, back3)), 1)
@@ -305,7 +307,7 @@
     mine2, *terms2 = sum_cores(keep2, other2, columns, jnp.float32)
     packs, mine2, terms2 = together(packs, mine2, terms2)
     back2 = back_y(terms2)
-    key_update = updates(True, packs, key_update, 1, 2)
+    key_update = updates(True, packs, key_update, 2, 4)
     onward, mine2, back2, other0, key_update, packs, mine1 = together(
         onward, mine2, back2, other0, key_update, packs, mine1
     )
@@ -314,7 +316,7 @@
     both = keep0.astype(jnp.float32) + other0.astype(jnp.float32)
     terms0 = [rounded(add(both[j * rows : (j + 1) * rows], [term])) for j, term in enumerate(beside1, 1)]
     back0, mine1 = back_y(terms0), over_z(mine1, 1)
-    value_update = updates(False, packs, None, 0, 2)
+    value_update = updates(False, packs, None, 0, 4)
     return rounded(add(both[:rows], [last, mine1] + back0)), key_update, value_update
 
 

time: 81.2 us -> 80.2 us (0.988)
  waiting for transfers between devices: 26 us -> 17.7 us
  starting transfers between devices: 22.5 us -> 28 us
  Pallas kernels: 26.4 us -> 28.2 us
    ppermute x26, waiting for transfers between devices: 23.4 us -> 17.7 us  [swap(): return lax.ppermute(array, 'shard', [(i, i ^ bits) for i in range(devices)])]
    ppermute x26, starting transfers between devices: 20.9 us -> 26.5 us  [swap(): return lax.ppermute(array, 'shard', [(i, i ^ bits) for i in range(devices)])]
    ppermute x1, waiting for transfers between devices: 2.57 us -> 0.01 us  [local(): lax.ppermute(pack, 'member', [(i, i ^ bits) for i in range(groups)])]
    pallas_call x4 -> x8, Pallas kernels: 12.4 us -> 14.2 us  [update(): pl.pallas_call(functools.partial(update_kernel, fit_rows, piece, groups,...]
  transfers between devices with their start and end apart: 27 -> 27, of which waited for: 15 -> 15; matrix products, arithmetic and copies ran while one was open for 1% -> 1% of each run, Pallas kernels for 33% -> 35%
where the time goes in v6:
time: 80.2 us; the launch traced here: 80 us
  Pallas kernels  28.2 us (35%)
  starting transfers between devices  28 us (35%)
  waiting for transfers between devices  17.7 us (22%)
  local copies, waits for them, and re-layouts  4.14 us (5%)
  other arithmetic  1.13 us (1%)
  between operations  0.82 us (1%)
    ppermute x26, starting transfers between devices, swap(): return lax.ppermute(array, 'shard', [(i, i ^ bits) for i in range(devices)])  26.5 us
    ppermute x26, waiting for transfers between devices, swap(): return lax.ppermute(array, 'shard', [(i, i ^ bits) for i in range(devices)])  17.7 us
    pallas_call x8, Pallas kernels, update(): pl.pallas_call(functools.partial(update_kernel, fit_rows, piece, groups,...  14.2 us
    pallas_call x4, Pallas kernels, chunk(): pl.pallas_call(functools.partial(chunk_kernel, k, rows, columns), out_sha...  11.9 us
    unnamed x16, local copies, waits for them, and re-layouts  3.41 us
  transfers between devices with their start and end apart: 27, of which 15 were waited for; matrix products, arithmetic and copies ran while one was open for 1% of the time, Pallas kernels for 35%

profile of v6, /device:TPU:0, one launch (start us, length us, event | category | flops | bytes accessed | tf_op | source)
XLA Modules:
  0.0 80.0 jit_solution(10469579831072637610)
XLA Ops:
  0.6 3.1 %collective-permute-start.1 = (bf16[32,4096]{1,0:T(8,128)(2,1)}, bf16[32,4096]{1,0:T(8,128)(2,1)S(1)}, u32[]{:S(2)}, u32[]{:S(2)}) collective-permute-start(bf16[32,4096]{1,0:T(8,128)(2,1)} %refs_0_.3), channel_id=1, source_target_pairs={{0,4},{1,5},{2,6},{3,7},{4,0},{5,1},{6,2},{7,3},{8,12},{9,13},{10,... | collective-permute-start | bytes 786440 | tf_op jit(solution)/shard_map/ppermute | solution.py:232
  3.7 1.5 %collective-permute-start.2 = (bf16[32,4096]{1,0:T(8,128)(2,1)}, bf16[32,4096]{1,0:T(8,128)(2,1)S(1)}, u32[]{:S(2)}, u32[]{:S(2)}) collective-permute-start(bf16[32,4096]{1,0:T(8,128)(2,1)} %refs_0_.3), channel_id=1, source_target_pairs={{0,2},{1,3},{2,0},{3,1},{4,6},{5,7},{6,4},{7,5},{8,10},{9,11},{10,... | collective-permute-start | bytes 786440 | tf_op jit(solution)/shard_map/ppermute | solution.py:232
  5.2 2.6 %collective-permute-start = (bf16[32,4096]{1,0:T(8,128)(2,1)}, bf16[32,4096]{1,0:T(8,128)(2,1)S(1)}, u32[]{:S(2)}, u32[]{:S(2)}) collective-permute-start(bf16[32,4096]{1,0:T(8,128)(2,1)} %refs_0_.3), channel_id=1, source_target_pairs={{0,8},{1,9},{2,10},{3,11},{4,12},{5,13},{6,14},{7,15},{8,0},{9,1},... | collective-permute-start | bytes 786440 | tf_op jit(solution)/shard_map/ppermute | solution.py:232
  7.8 0.7 broadcast_in_dim.3.refs_4_
  8.6 4.2 %collective-permute-done.1.refs_0_ = bf16[32,4096]{1,0:T(8,128)(2,1)S(1)} collective-permute-done((bf16[32,4096]{1,0:T(8,128)(2,1)}, bf16[32,4096]{1,0:T(8,128)(2,1)S(1)}, u32[]{:S(2)}, u32[]{:S(2)}) %collective-permute-start.1) | collective-permute-done | bytes 262176 | tf_op jit(solution)/shard_map/ppermute | solution.py:232
  12.8 3.2 %collective-permute-start.4 = (bf16[32,4096]{1,0:T(8,128)(2,1)S(1)}, bf16[32,4096]{1,0:T(8,128)(2,1)S(1)}, u32[]{:S(2)}, u32[]{:S(2)}) collective-permute-start(bf16[32,4096]{1,0:T(8,128)(2,1)S(1)} %collective-permute-done.1.refs_0_), channel_id=1, source_target_pairs={{0,2},{1,3},{2,0},{3,1},{4,6},{5,7},{6,4},{7,5},{8,10},{9,11},{10,... | collective-permute-start | bytes 786440 | tf_op jit(solution)/shard_map/ppermute | solution.py:232
  16.0 0.5 collective-permute-start.5
  16.5 3.4 %copy-done = bf16[4096,1024]{1,0:T(8,128)(2,1)S(1)} copy-done((bf16[4096,1024]{1,0:T(8,128)(2,1)S(1)}, bf16[4096,1024]{1,0:T(8,128)(2,1)}, u32[]{:S(2)}) %copy-start) | copy-done | bytes 8388632
  19.9 0.6 shard_map.112.refs_9_
  20.5 0.3 collective-permute-done.refs_0_
  20.9 1.8 %collective-permute-start.10 = (bf16[32,4096]{1,0:T(8,128)(2,1)S(1)}, bf16[32,4096]{1,0:T(8,128)(2,1)S(1)}, u32[]{:S(2)}, u32[]{:S(2)}) collective-permute-start(bf16[32,4096]{1,0:T(8,128)(2,1)S(1)} %collective-permute-done.refs_0_), channel_id=1, source_target_pairs={{0,2},{1,3},{2,0},{3,1},{4,6},{5,7},{6,4},{7,5},{8,10},{9,11},{10,... | collective-permute-start | bytes 786440 | tf_op jit(solution)/shard_map/ppermute | solution.py:232
  22.9 1.6 %collective-permute-start.9 = (bf16[32,4096]{1,0:T(8,128)(2,1)S(1)}, bf16[32,4096]{1,0:T(8,128)(2,1)S(1)}, u32[]{:S(2)}, u32[]{:S(2)}) collective-permute-start(bf16[32,4096]{1,0:T(8,128)(2,1)S(1)} %collective-permute-done.refs_0_), channel_id=1, source_target_pairs={{0,4},{1,5},{2,6},{3,7},{4,0},{5,1},{6,2},{7,3},{8,12},{9,13},{10,... | collective-permute-start | bytes 786440 | tf_op jit(solution)/shard_map/ppermute | solution.py:232
  24.5 0.6 shard_map.113.refs_0_
  25.1 1.6 %collective-permute-start.7 = (bf16[8,10368]{1,0:T(8,128)(2,1)S(1)}, bf16[8,10368]{1,0:T(8,128)(2,1)S(1)}, u32[]{:S(2)}, u32[]{:S(2)}) collective-permute-start(bf16[8,10368]{1,0:T(8,128)(2,1)S(1)} %shard_map.113.refs_0_), channel_id=1, source_target_pairs={{0,16},{16,0},{1,17},{17,1},{2,18},{18,2},{3,19},{19,3},{4,20},{20... | collective-permute-start | bytes 497672 | tf_op jit(solution)/shard_map/ppermute | solution.py:273
  26.6 0.6 shard_map.114.refs_10_
  27.2 3.0 %shard_map.115 = (bf16[64,4096]{1,0:T(8,128)(2,1)S(1)}, bf16[64,4096]{1,0:T(8,128)(2,1)S(1)}) custom-call(bf16[32,4096]{1,0:T(8,128)(2,1)S(1)} %collective-permute-done.1.refs_0_, bf16[32,4096]{1,0:T(8,128)(2,1)S(1)} %collective-permute-done.4.refs_1_, bf16[32,4096]{1,0:T(8,128)(2,1)S(1)} %collective-permute-done.6.refs_2_, ...), custom_call_target="tpu_custom_call" | custom-call | flops 128 | bytes 128 | tf_op jit(solution)/shard_map/pallas_call | solution.py:85
  30.2 3.0 %shard_map.116 = (bf16[64,4096]{1,0:T(8,128)(2,1)S(1)}, bf16[64,4096]{1,0:T(8,128)(2,1)S(1)}) custom-call(bf16[32,4096]{1,0:T(8,128)(2,1)S(1)} %copy-done.6, bf16[32,4096]{1,0:T(8,128)(2,1)S(1)} %collective-permute-done.2.refs_1_, bf16[32,4096]{1,0:T(8,128)(2,1)S(1)} %collective-permute-done.3.refs_2_, bf16[32,4096]{1,0:T(8,128)(2,1)S(1)} %collective-permute-done.5.refs_3_, ...), custom_call_target="tpu_custom_call" | custom-call | flops 128 | bytes 128 | tf_op jit(solution)/shard_map/pallas_call | solution.py:85
  33.2 1.8 %shard_map.117.refs_2_ = f32[2048,1024]{1,0:T(8,128)} custom-call(bf16[8,10368]{1,0:T(8,128)(2,1)S(1)} %shard_map.113.refs_0_, bf16[8,10368]{1,0:T(8,128)(2,1)S(1)} %collective-permute-done.7.refs_1_), custom_call_target="tpu_custom_call" | custom-call | flops 256 | bytes 256 | tf_op jit(solution)/shard_map/pallas_call | solution.py:207
  35.3 1.2 %collective-permute-done.9.refs_0_ = bf16[32,4096]{1,0:T(8,128)(2,1)S(1)} collective-permute-done((bf16[32,4096]{1,0:T(8,128)(2,1)S(1)}, bf16[32,4096]{1,0:T(8,128)(2,1)S(1)}, u32[]{:S(2)}, u32[]{:S(2)}) %collective-permute-start.9) | collective-permute-done | bytes 262176 | tf_op jit(solution)/shard_map/ppermute | solution.py:232
  36.5 0.5 collective-permute-start.15
  37.0 0.5 collective-permute-start.13
  37.5 1.3 %collective-permute-done.15.refs_2_ = bf16[32,4096]{1,0:T(8,128)(2,1)S(1)} collective-permute-done((bf16[32,4096]{1,0:T(8,128)(2,1)S(1)}, bf16[32,4096]{1,0:T(8,128)(2,1)S(1)}, u32[]{:S(2)}, u32[]{:S(2)}) %collective-permute-start.15) | collective-permute-done | bytes 262176 | tf_op jit(solution)/shard_map/ppermute | solution.py:232
  38.8 0.4 collective-permute-done.16.refs_3_
  39.2 3.0 %shard_map.118 = (bf16[64,4096]{1,0:T(8,128)(2,1)S(1)}, bf16[64,4096]{1,0:T(8,128)(2,1)S(1)}) custom-call(bf16[32,4096]{1,0:T(8,128)(2,1)S(1)} %collective-permute-done.9.refs_0_, bf16[32,4096]{1,0:T(8,128)(2,1)S(1)} %collective-permute-done.11.refs_1_, bf16[32,4096]{1,0:T(8,128)(2,1)S(1)} %collective-permute-done.15.refs_2_, ...), custom_call_target="tpu_custom_call" | custom-call | flops 128 | bytes 128 | tf_op jit(solution)/shard_map/pallas_call | solution.py:85
  42.5 0.6 collective-permute-start.18
  43.1 1.0 %collective-permute-done.17.arrived = bf16[64,4096]{1,0:T(8,128)(2,1)S(1)} collective-permute-done((bf16[64,4096]{1,0:T(8,128)(2,1)S(1)}, bf16[64,4096]{1,0:T(8,128)(2,1)S(1)}, u32[]{:S(2)}, u32[]{:S(2)}) %collective-permute-start.17) | collective-permute-done | bytes 524320 | tf_op jit(solution)/shard_map/ppermute | solution.py:232
  44.3 1.8 %collective-permute-start.19 = (bf16[32,4096]{1,0:T(8,128)(2,1)S(1)}, bf16[32,4096]{1,0:T(8,128)(2,1)S(1)}, u32[]{:S(2)}, u32[]{:S(2)}) collective-permute-start(bf16[32,4096]{1,0:T(8,128)(2,1)S(1)} %get-tuple-element.108), channel_id=1, source_target_pairs={{0,2},{1,3},{2,0},{3,1},{4,6},{5,7},{6,4},{7,5},{8,10},{9,11},{10,... | collective-permute-start | bytes 786440 | tf_op jit(solution)/shard_map/ppermute | solution.py:232
  46.1 3.0 %shard_map.121 = (bf16[64,4096]{1,0:T(8,128)(2,1)S(1)}, bf16[64,4096]{1,0:T(8,128)(2,1)S(1)}) custom-call(bf16[32,4096]{1,0:T(8,128)(2,1)S(1)} %collective-permute-done.refs_0_, bf16[32,4096]{1,0:T(8,128)(2,1)S(1)} %collective-permute-done.10.refs_1_, bf16[32,4096]{1,0:T(8,128)(2,1)S(1)} %collective-permute-done.12.refs_2_, ...), custom_call_target="tpu_custom_call" | custom-call | flops 128 | bytes 128 | tf_op jit(solution)/shard_map/pallas_call | solution.py:85
  49.1 1.8 %shard_map.122.refs_2_ = f32[2048,1024]{1,0:T(8,128)} custom-call(bf16[8,10368]{1,0:T(8,128)(2,1)S(1)} %shard_map.113.refs_0_, bf16[8,10368]{1,0:T(8,128)(2,1)S(1)} %collective-permute-done.7.refs_1_, f32[2048,1024]{1,0:T(8,128)} %shard_map.117.refs_2_), custom_call_target="tpu_custom_call", output_to_operand_aliasing={{}: (2, {})} | custom-call | flops 256 | bytes 256 | tf_op jit(solution)/shard_map/pallas_call | solution.py:207
  51.1 1.5 %collective-permute-done.19 = bf16[32,4096]{1,0:T(8,128)(2,1)S(1)} collective-permute-done((bf16[32,4096]{1,0:T(8,128)(2,1)S(1)}, bf16[32,4096]{1,0:T(8,128)(2,1)S(1)}, u32[]{:S(2)}, u32[]{:S(2)}) %collective-permute-start.19) | collective-permute-done | bytes 262176 | tf_op jit(solution)/shard_map/ppermute | solution.py:232
  52.7 0.5 collective-permute-start.23
  53.3 0.6 collective-permute-start.20
  53.9 0.7 collective-permute-done.21.arrived
  54.7 1.8 %collective-permute-start.22 = (bf16[32,4096]{1,0:T(8,128)(2,1)S(1)}, bf16[32,4096]{1,0:T(8,128)(2,1)S(1)}, u32[]{:S(2)}, u32[]{:S(2)}) collective-permute-start(bf16[32,4096]{1,0:T(8,128)(2,1)S(1)} %get-tuple-element.128), channel_id=1, source_target_pairs={{0,2},{1,3},{2,0},{3,1},{4,6},{5,7},{6,4},{7,5},{8,10},{9,11},{10,... | collective-permute-start | bytes 786440 | tf_op jit(solution)/shard_map/ppermute | solution.py:232
  56.5 1.8 %shard_map.124.refs_2_ = f32[2048,1024]{1,0:T(8,128)} custom-call(bf16[8,10368]{1,0:T(8,128)(2,1)S(1)} %shard_map.113.refs_0_, bf16[8,10368]{1,0:T(8,128)(2,1)S(1)} %collective-permute-done.7.refs_1_, f32[2048,1024]{1,0:T(8,128)} %shard_map.122.refs_2_), custom_call_target="tpu_custom_call", output_to_operand_aliasing={{}: (2, {})} | custom-call | flops 256 | bytes 256 | tf_op jit(solution)/shard_map/pallas_call | solution.py:207
  58.3 1.8 %shard_map.125 = f32[2048,1024]{1,0:T(8,128)} custom-call(bf16[8,10368]{1,0:T(8,128)(2,1)S(1)} %shard_map.113.refs_0_, bf16[8,10368]{1,0:T(8,128)(2,1)S(1)} %collective-permute-done.7.refs_1_, f32[2048,1024]{1,0:T(8,128)} %shard_map.124.refs_2_), custom_call_target="tpu_custom_call", output_to_operand_aliasing={{}: (2, {})} | custom-call | flops 256 | bytes 256 | tf_op jit(solution)/shard_map/pallas_call | solution.py:207
  60.1 1.5 %collective-permute-done.20 = bf16[32,4096]{1,0:T(8,128)(2,1)S(1)} collective-permute-done((bf16[32,4096]{1,0:T(8,128)(2,1)S(1)}, bf16[32,4096]{1,0:T(8,128)(2,1)S(1)}, u32[]{:S(2)}, u32[]{:S(2)}) %collective-permute-start.20) | collective-permute-done | bytes 262176 | tf_op jit(solution)/shard_map/ppermute | solution.py:232
  61.5 1.6 %collective-permute-done.22 = bf16[32,4096]{1,0:T(8,128)(2,1)S(1)} collective-permute-done((bf16[32,4096]{1,0:T(8,128)(2,1)S(1)}, bf16[32,4096]{1,0:T(8,128)(2,1)S(1)}, u32[]{:S(2)}, u32[]{:S(2)}) %collective-permute-start.22) | collective-permute-done | bytes 262176 | tf_op jit(solution)/shard_map/ppermute | solution.py:232
  63.2 2.1 %collective-permute-start.24 = (bf16[32,4096]{1,0:T(8,128)(2,1)S(1)}, bf16[32,4096]{1,0:T(8,128)(2,1)S(1)}, u32[]{:S(2)}, u32[]{:S(2)}) collective-permute-start(bf16[32,4096]{1,0:T(8,128)(2,1)S(1)} %add_convert_fusion), channel_id=1, source_target_pairs={{0,8},{1,9},{2,10},{3,11},{4,12},{5,13},{6,14},{7,15},{8,0},{9,1},... | collective-permute-start | bytes 786440 | tf_op jit(solution)/shard_map/ppermute | solution.py:232
  65.5 1.6 %collective-permute-start.26 = (bf16[32,4096]{1,0:T(8,128)(2,1)S(1)}, bf16[32,4096]{1,0:T(8,128)(2,1)S(1)}, u32[]{:S(2)}, u32[]{:S(2)}) collective-permute-start(bf16[32,4096]{1,0:T(8,128)(2,1)S(1)} %fusion), channel_id=1, source_target_pairs={{0,2},{1,3},{2,0},{3,1},{4,6},{5,7},{6,4},{7,5},{8,10},{9,11},{10,... | collective-permute-start | bytes 786440 | tf_op jit(solution)/shard_map/ppermute | solution.py:232
  67.2 1.6 %collective-permute-start.25 = (bf16[32,4096]{1,0:T(8,128)(2,1)S(1)}, bf16[32,4096]{1,0:T(8,128)(2,1)S(1)}, u32[]{:S(2)}, u32[]{:S(2)}) collective-permute-start(bf16[32,4096]{1,0:T(8,128)(2,1)S(1)} %get-tuple-element.138), channel_id=1, source_target_pairs={{0,4},{1,5},{2,6},{3,7},{4,0},{5,1},{6,2},{7,3},{8,12},{9,13},{10,... | collective-permute-start | bytes 786440 | tf_op jit(solution)/shard_map/ppermute | solution.py:232
  68.8 1.8 %shard_map.126.refs_2_ = f32[1024,2048]{1,0:T(8,128)} custom-call(bf16[8,10368]{1,0:T(8,128)(2,1)S(1)} %shard_map.113.refs_0_, bf16[8,10368]{1,0:T(8,128)(2,1)S(1)} %collective-permute-done.7.refs_1_), custom_call_target="tpu_custom_call" | custom-call | flops 128 | bytes 128 | tf_op jit(solution)/shard_map/pallas_call | solution.py:207
  70.5 1.8 %shard_map.127.refs_2_ = f32[1024,2048]{1,0:T(8,128)} custom-call(bf16[8,10368]{1,0:T(8,128)(2,1)S(1)} %shard_map.113.refs_0_, bf16[8,10368]{1,0:T(8,128)(2,1)S(1)} %collective-permute-done.7.refs_1_, f32[1024,2048]{1,0:T(8,128)} %shard_map.126.refs_2_), custom_call_target="tpu_custom_call", output_to_operand_aliasing={{}: (2, {})} | custom-call | flops 128 | bytes 128 | tf_op jit(solution)/shard_map/pallas_call | solution.py:207
  72.3 1.8 %shard_map.128.refs_2_ = f32[1024,2048]{1,0:T(8,128)} custom-call(bf16[8,10368]{1,0:T(8,128)(2,1)S(1)} %shard_map.113.refs_0_, bf16[8,10368]{1,0:T(8,128)(2,1)S(1)} %collective-permute-done.7.refs_1_, f32[1024,2048]{1,0:T(8,128)} %shard_map.127.refs_2_), custom_call_target="tpu_custom_call", output_to_operand_aliasing={{}: (2, {})} | custom-call | flops 128 | bytes 128 | tf_op jit(solution)/shard_map/pallas_call | solution.py:207
  74.1 1.8 %shard_map.129 = f32[1024,2048]{1,0:T(8,128)} custom-call(bf16[8,10368]{1,0:T(8,128)(2,1)S(1)} %shard_map.113.refs_0_, bf16[8,10368]{1,0:T(8,128)(2,1)S(1)} %collective-permute-done.7.refs_1_, f32[1024,2048]{1,0:T(8,128)} %shard_map.128.refs_2_), custom_call_target="tpu_custom_call", output_to_operand_aliasing={{}: (2, {})} | custom-call | flops 128 | bytes 128 | tf_op jit(solution)/shard_map/pallas_call | solution.py:207
  75.8 1.6 %collective-permute-done.24 = bf16[32,4096]{1,0:T(8,128)(2,1)S(1)} collective-permute-done((bf16[32,4096]{1,0:T(8,128)(2,1)S(1)}, bf16[32,4096]{1,0:T(8,128)(2,1)S(1)}, u32[]{:S(2)}, u32[]{:S(2)}) %collective-permute-start.24) | collective-permute-done | bytes 262176 | tf_op jit(solution)/shard_map/ppermute | solution.py:232
  77.4 1.8 %collective-permute-done.25 = bf16[32,4096]{1,0:T(8,128)(2,1)S(1)} collective-permute-done((bf16[32,4096]{1,0:T(8,128)(2,1)S(1)}, bf16[32,4096]{1,0:T(8,128)(2,1)S(1)}, u32[]{:S(2)}, u32[]{:S(2)}) %collective-permute-start.25) | collective-permute-done | bytes 262176 | tf_op jit(solution)/shard_map/ppermute | solution.py:232
  79.2 0.8 %fusion.3 = bf16[32,4096]{1,0:T(8,128)(2,1)} fusion(f32[64,4096]{1,0:T(8,128)S(1)} %convert_add_fusion, bf16[32,4096]{1,0:T(8,128)(2,1)S(1)} %collective-permute-done.26, bf16[32,4096]{1,0:T(8,128)(2,1)S(1)} %collective-permute-done.25, bf16[32,4096]{1,0:T(8,128)(2,1)S(1)} %collective-permute-done.24), kind=kLoop, calls=%fused_computation.6 | loop fusion | flops 917504 | bytes 1572864 | tf_op jit(solution)/shard_map/convert_element_type | solution.py:261
  (46 shorter events, 1.8 us)
Async XLA Ops:
  0.6 12.1 %collective-permute-start.1 = (bf16[32,4096]{1,0:T(8,128)(2,1)}, bf16[32,4096]{1,0:T(8,128)(2,1)S(1)}, u32[]{:S(2)}, u32[]{:S(2)}) collective-permute-start(bf16[32,4096]{1,0:T(8,128)(2,1)} %refs_0_.3), channel_id=1, source_target_pairs={{0,4},{1,5},{2,6},{3,7},{4,0},{5,1},{6,2},{7,3},{8,12},{9,13},{10,... | collective-permute-start | bytes 786440 | tf_op jit(solution)/shard_map/ppermute | solution.py:232
  3.7 9.0 %collective-permute-start.2 = (bf16[32,4096]{1,0:T(8,128)(2,1)}, bf16[32,4096]{1,0:T(8,128)(2,1)S(1)}, u32[]{:S(2)}, u32[]{:S(2)}) collective-permute-start(bf16[32,4096]{1,0:T(8,128)(2,1)} %refs_0_.3), channel_id=1, source_target_pairs={{0,2},{1,3},{2,0},{3,1},{4,6},{5,7},{6,4},{7,5},{8,10},{9,11},{10,... | collective-permute-start | bytes 786440 | tf_op jit(solution)/shard_map/ppermute | solution.py:232
  5.2 7.5 %collective-permute-start.3 = (bf16[32,4096]{1,0:T(8,128)(2,1)}, bf16[32,4096]{1,0:T(8,128)(2,1)S(1)}, u32[]{:S(2)}, u32[]{:S(2)}) collective-permute-start(bf16[32,4096]{1,0:T(8,128)(2,1)} %refs_0_.3), channel_id=1, source_target_pairs={{0,1},{1,0},{2,3},{3,2},{4,5},{5,4},{6,7},{7,6},{8,9},{9,8},{10,11... | collective-permute-start | bytes 786440 | tf_op jit(solution)/shard_map/ppermute | solution.py:232
  5.2 15.5 %collective-permute-start = (bf16[32,4096]{1,0:T(8,128)(2,1)}, bf16[32,4096]{1,0:T(8,128)(2,1)S(1)}, u32[]{:S(2)}, u32[]{:S(2)}) collective-permute-start(bf16[32,4096]{1,0:T(8,128)(2,1)} %refs_0_.3), channel_id=1, source_target_pairs={{0,8},{1,9},{2,10},{3,11},{4,12},{5,13},{6,14},{7,15},{8,0},{9,1},... | collective-permute-start | bytes 786440 | tf_op jit(solution)/shard_map/ppermute | solution.py:232
  7.8 16.7 %copy-start.4 = (bf16[8,1024]{1,0:T(8,128)(2,1)S(1)}, bf16[8,1024]{1,0:T(8,128)(2,1)}, u32[]{:S(2)}) copy-start(bf16[8,1024]{1,0:T(8,128)(2,1)} %refs_6_.7) | copy-start | bytes 49156
  7.8 16.7 %copy-start.7 = (s32[8]{0:T(128)S(1)}, s32[8]{0:T(128)}, u32[]{:S(2)}) copy-start(s32[8]{0:T(128)} %ranks.1) | copy-start | bytes 100
  12.8 8.2 %collective-permute-start.4 = (bf16[32,4096]{1,0:T(8,128)(2,1)S(1)}, bf16[32,4096]{1,0:T(8,128)(2,1)S(1)}, u32[]{:S(2)}, u32[]{:S(2)}) collective-permute-start(bf16[32,4096]{1,0:T(8,128)(2,1)S(1)} %collective-permute-done.1.refs_0_), channel_id=1, source_target_pairs={{0,2},{1,3},{2,0},{3,1},{4,6},{5,7},{6,4},{7,5},{8,10},{9,11},{10,... | collective-permute-start | bytes 786440 | tf_op jit(solution)/shard_map/ppermute | solution.py:232
  16.0 4.9 %collective-permute-start.6 = (bf16[32,4096]{1,0:T(8,128)(2,1)S(1)}, bf16[32,4096]{1,0:T(8,128)(2,1)S(1)}, u32[]{:S(2)}, u32[]{:S(2)}) collective-permute-start(bf16[32,4096]{1,0:T(8,128)(2,1)S(1)} %collective-permute-done.1.refs_0_), channel_id=1, source_target_pairs={{0,1},{1,0},{2,3},{3,2},{4,5},{5,4},{6,7},{7,6},{8,9},{9,8},{10,11... | collective-permute-start | bytes 786440 | tf_op jit(solution)/shard_map/ppermute | solution.py:232
  16.0 4.9 %collective-permute-start.5 = (bf16[32,4096]{1,0:T(8,128)(2,1)S(1)}, bf16[32,4096]{1,0:T(8,128)(2,1)S(1)}, u32[]{:S(2)}, u32[]{:S(2)}) collective-permute-start(bf16[32,4096]{1,0:T(8,128)(2,1)S(1)} %collective-permute-done.2.refs_1_), channel_id=1, source_target_pairs={{0,1},{1,0},{2,3},{3,2},{4,5},{5,4},{6,7},{7,6},{8,9},{9,8},{10,11... | collective-permute-start | bytes 786440 | tf_op jit(solution)/shard_map/ppermute | solution.py:232
  16.5 3.4 %copy-start = (bf16[4096,1024]{1,0:T(8,128)(2,1)S(1)}, bf16[4096,1024]{1,0:T(8,128)(2,1)}, u32[]{:S(2)}) copy-start(bf16[4096,1024]{1,0:T(8,128)(2,1)} %refs_0_) | copy-start | bytes 25165828
  19.9 4.6 %copy-start.2 = (bf16[8,4096]{1,0:T(8,128)(2,1)S(1)}, bf16[8,4096]{1,0:T(8,128)(2,1)}, u32[]{:S(2)}) copy-start(bf16[8,4096]{1,0:T(8,128)(2,1)} %refs_5_.7) | copy-start | bytes 196612
  19.9 4.6 %copy-start.3 = (bf16[8,4096]{1,0:T(8,128)(2,1)S(1)}, bf16[8,4096]{1,0:T(8,128)(2,1)}, u32[]{:S(2)}) copy-start(bf16[8,4096]{1,0:T(8,128)(2,1)} %refs_8_.7) | copy-start | bytes 196612
  19.9 4.6 %copy-start.5 = (bf16[8,1024]{1,0:T(8,128)(2,1)S(1)}, bf16[8,1024]{1,0:T(8,128)(2,1)}, u32[]{:S(2)}) copy-start(bf16[8,1024]{1,0:T(8,128)(2,1)} %refs_7_.7) | copy-start | bytes 49156
  19.9 6.8 %copy-start.1 = (bf16[1024,4096]{1,0:T(8,128)(2,1)S(1)}, bf16[1024,4096]{1,0:T(8,128)(2,1)}, u32[]{:S(2)}) copy-start(bf16[1024,4096]{1,0:T(8,128)(2,1)} %refs_0_.2) | copy-start | bytes 25165828
  20.9 4.2 %collective-permute-start.8 = (bf16[32,4096]{1,0:T(8,128)(2,1)S(1)}, bf16[32,4096]{1,0:T(8,128)(2,1)S(1)}, u32[]{:S(2)}, u32[]{:S(2)}) collective-permute-start(bf16[32,4096]{1,0:T(8,128)(2,1)S(1)} %collective-permute-done.4.refs_1_), channel_id=1, source_target_pairs={{0,1},{1,0},{2,3},{3,2},{4,5},{5,4},{6,7},{7,6},{8,9},{9,8},{10,11... | collective-permute-start | bytes 786440 | tf_op jit(solution)/shard_map/ppermute | solution.py:232
  20.9 14.3 %collective-permute-start.10 = (bf16[32,4096]{1,0:T(8,128)(2,1)S(1)}, bf16[32,4096]{1,0:T(8,128)(2,1)S(1)}, u32[]{:S(2)}, u32[]{:S(2)}) collective-permute-start(bf16[32,4096]{1,0:T(8,128)(2,1)S(1)} %collective-permute-done.refs_0_), channel_id=1, source_target_pairs={{0,2},{1,3},{2,0},{3,1},{4,6},{5,7},{6,4},{7,5},{8,10},{9,11},{10,... | collective-permute-start | bytes 786440 | tf_op jit(solution)/shard_map/ppermute | solution.py:232
  22.7 12.5 %collective-permute-start.11 = (bf16[32,4096]{1,0:T(8,128)(2,1)S(1)}, bf16[32,4096]{1,0:T(8,128)(2,1)S(1)}, u32[]{:S(2)}, u32[]{:S(2)}) collective-permute-start(bf16[32,4096]{1,0:T(8,128)(2,1)S(1)} %collective-permute-done.refs_0_), channel_id=1, source_target_pairs={{0,6},{1,7},{2,4},{3,5},{4,2},{5,3},{6,0},{7,1},{8,14},{9,15},{10,... | collective-permute-start | bytes 786440 | tf_op jit(solution)/shard_map/ppermute | solution.py:232
  22.7 12.5 %collective-permute-start.12 = (bf16[32,4096]{1,0:T(8,128)(2,1)S(1)}, bf16[32,4096]{1,0:T(8,128)(2,1)S(1)}, u32[]{:S(2)}, u32[]{:S(2)}) collective-permute-start(bf16[32,4096]{1,0:T(8,128)(2,1)S(1)} %collective-permute-done.refs_0_), channel_id=1, source_target_pairs={{0,1},{1,0},{2,3},{3,2},{4,5},{5,4},{6,7},{7,6},{8,9},{9,8},{10,11... | collective-permute-start | bytes 786440 | tf_op jit(solution)/shard_map/ppermute | solution.py:232
  22.9 13.6 %collective-permute-start.9 = (bf16[32,4096]{1,0:T(8,128)(2,1)S(1)}, bf16[32,4096]{1,0:T(8,128)(2,1)S(1)}, u32[]{:S(2)}, u32[]{:S(2)}) collective-permute-start(bf16[32,4096]{1,0:T(8,128)(2,1)S(1)} %collective-permute-done.refs_0_), channel_id=1, source_target_pairs={{0,4},{1,5},{2,6},{3,7},{4,0},{5,1},{6,2},{7,3},{8,12},{9,13},{10,... | collective-permute-start | bytes 786440 | tf_op jit(solution)/shard_map/ppermute | solution.py:232
  25.1 8.1 %collective-permute-start.7 = (bf16[8,10368]{1,0:T(8,128)(2,1)S(1)}, bf16[8,10368]{1,0:T(8,128)(2,1)S(1)}, u32[]{:S(2)}, u32[]{:S(2)}) collective-permute-start(bf16[8,10368]{1,0:T(8,128)(2,1)S(1)} %shard_map.113.refs_0_), channel_id=1, source_target_pairs={{0,16},{16,0},{1,17},{17,1},{2,18},{18,2},{3,19},{19,3},{4,20},{20... | collective-permute-start | bytes 497672 | tf_op jit(solution)/shard_map/ppermute | solution.py:273
  27.2 3.0 %copy-start.6 = (bf16[32,4096]{1,0:T(8,128)(2,1)S(1)}, bf16[32,4096]{1,0:T(8,128)(2,1)}, u32[]{:S(2)}) copy-start(bf16[32,4096]{1,0:T(8,128)(2,1)} %refs_0_.3) | copy-start | bytes 786436
  36.5 5.7 %collective-permute-start.14 = (bf16[64,4096]{1,0:T(8,128)(2,1)S(1)}, bf16[64,4096]{1,0:T(8,128)(2,1)S(1)}, u32[]{:S(2)}, u32[]{:S(2)}) collective-permute-start(bf16[64,4096]{1,0:T(8,128)(2,1)S(1)} %get-tuple-element.95), channel_id=1, source_target_pairs={{0,1},{1,0},{2,3},{3,2},{4,5},{5,4},{6,7},{7,6},{8,9},{9,8},{10,11... | collective-permute-start | bytes 1572872 | tf_op jit(solution)/shard_map/ppermute | solution.py:232
  36.5 2.3 %collective-permute-start.15 = (bf16[32,4096]{1,0:T(8,128)(2,1)S(1)}, bf16[32,4096]{1,0:T(8,128)(2,1)S(1)}, u32[]{:S(2)}, u32[]{:S(2)}) collective-permute-start(bf16[32,4096]{1,0:T(8,128)(2,1)S(1)} %collective-permute-done.9.refs_0_), channel_id=1, source_target_pairs={{0,1},{1,0},{2,3},{3,2},{4,5},{5,4},{6,7},{7,6},{8,9},{9,8},{10,11... | collective-permute-start | bytes 786440 | tf_op jit(solution)/shard_map/ppermute | solution.py:232
  37.0 2.1 %collective-permute-start.16 = (bf16[32,4096]{1,0:T(8,128)(2,1)S(1)}, bf16[32,4096]{1,0:T(8,128)(2,1)S(1)}, u32[]{:S(2)}, u32[]{:S(2)}) collective-permute-start(bf16[32,4096]{1,0:T(8,128)(2,1)S(1)} %collective-permute-done.11.refs_1_), channel_id=1, source_target_pairs={{0,1},{1,0},{2,3},{3,2},{4,5},{5,4},{6,7},{7,6},{8,9},{9,8},{10,11... | collective-permute-start | bytes 786440 | tf_op jit(solution)/shard_map/ppermute | solution.py:232
  37.0 5.1 %collective-permute-start.13 = (bf16[32,4096]{1,0:T(8,128)(2,1)S(1)}, bf16[32,4096]{1,0:T(8,128)(2,1)S(1)}, u32[]{:S(2)}, u32[]{:S(2)}) collective-permute-start(bf16[32,4096]{1,0:T(8,128)(2,1)S(1)} %collective-permute-done.10.refs_1_), channel_id=1, source_target_pairs={{0,1},{1,0},{2,3},{3,2},{4,5},{5,4},{6,7},{7,6},{8,9},{9,8},{10,11... | collective-permute-start | bytes 786440 | tf_op jit(solution)/shard_map/ppermute | solution.py:232
  42.2 2.0 %collective-permute-start.17 = (bf16[64,4096]{1,0:T(8,128)(2,1)S(1)}, bf16[64,4096]{1,0:T(8,128)(2,1)S(1)}, u32[]{:S(2)}, u32[]{:S(2)}) collective-permute-start(bf16[64,4096]{1,0:T(8,128)(2,1)S(1)} %get-tuple-element.101), channel_id=1, source_target_pairs={{0,1},{1,0},{2,3},{3,2},{4,5},{5,4},{6,7},{7,6},{8,9},{9,8},{10,11... | collective-permute-start | bytes 1572872 | tf_op jit(solution)/shard_map/ppermute | solution.py:232
  42.5 8.6 %collective-permute-start.18 = (bf16[32,4096]{1,0:T(8,128)(2,1)S(1)}, bf16[32,4096]{1,0:T(8,128)(2,1)S(1)}, u32[]{:S(2)}, u32[]{:S(2)}) collective-permute-start(bf16[32,4096]{1,0:T(8,128)(2,1)S(1)} %get-tuple-element.107), channel_id=1, source_target_pairs={{0,4},{1,5},{2,6},{3,7},{4,0},{5,1},{6,2},{7,3},{8,12},{9,13},{10,... | collective-permute-start | bytes 786440 | tf_op jit(solution)/shard_map/ppermute | solution.py:232
  44.3 8.4 %collective-permute-start.19 = (bf16[32,4096]{1,0:T(8,128)(2,1)S(1)}, bf16[32,4096]{1,0:T(8,128)(2,1)S(1)}, u32[]{:S(2)}, u32[]{:S(2)}) collective-permute-start(bf16[32,4096]{1,0:T(8,128)(2,1)S(1)} %get-tuple-element.108), channel_id=1, source_target_pairs={{0,2},{1,3},{2,0},{3,1},{4,6},{5,7},{6,4},{7,5},{8,10},{9,11},{10,... | collective-permute-start | bytes 786440 | tf_op jit(solution)/shard_map/ppermute | solution.py:232
  52.7 1.9 %collective-permute-start.21 = (bf16[64,4096]{1,0:T(8,128)(2,1)S(1)}, bf16[64,4096]{1,0:T(8,128)(2,1)S(1)}, u32[]{:S(2)}, u32[]{:S(2)}) collective-permute-start(bf16[64,4096]{1,0:T(8,128)(2,1)S(1)} %get-tuple-element.124), channel_id=1, source_target_pairs={{0,1},{1,0},{2,3},{3,2},{4,5},{5,4},{6,7},{7,6},{8,9},{9,8},{10,11... | collective-permute-start | bytes 1572872 | tf_op jit(solution)/shard_map/ppermute | solution.py:232
  52.7 8.9 %collective-permute-start.23 = (bf16[64,4096]{1,0:T(8,128)(2,1)S(1)}, bf16[64,4096]{1,0:T(8,128)(2,1)S(1)}, u32[]{:S(2)}, u32[]{:S(2)}) collective-permute-start(bf16[64,4096]{1,0:T(8,128)(2,1)S(1)} %get-tuple-element.129), channel_id=1, source_target_pairs={{0,1},{1,0},{2,3},{3,2},{4,5},{5,4},{6,7},{7,6},{8,9},{9,8},{10,11... | collective-permute-start | bytes 1572872 | tf_op jit(solution)/shard_map/ppermute | solution.py:232
  53.3 8.3 %collective-permute-start.20 = (bf16[32,4096]{1,0:T(8,128)(2,1)S(1)}, bf16[32,4096]{1,0:T(8,128)(2,1)S(1)}, u32[]{:S(2)}, u32[]{:S(2)}) collective-permute-start(bf16[32,4096]{1,0:T(8,128)(2,1)S(1)} %add_convert_fusion.1), channel_id=1, source_target_pairs={{0,4},{1,5},{2,6},{3,7},{4,0},{5,1},{6,2},{7,3},{8,12},{9,13},{10,... | collective-permute-start | bytes 786440 | tf_op jit(solution)/shard_map/ppermute | solution.py:232
  54.7 8.4 %collective-permute-start.22 = (bf16[32,4096]{1,0:T(8,128)(2,1)S(1)}, bf16[32,4096]{1,0:T(8,128)(2,1)S(1)}, u32[]{:S(2)}, u32[]{:S(2)}) collective-permute-start(bf16[32,4096]{1,0:T(8,128)(2,1)S(1)} %get-tuple-element.128), channel_id=1, source_target_pairs={{0,2},{1,3},{2,0},{3,1},{4,6},{5,7},{6,4},{7,5},{8,10},{9,11},{10,... | collective-permute-start | bytes 786440 | tf_op jit(solution)/shard_map/ppermute | solution.py:232
  63.2 14.2 %collective-permute-start.24 = (bf16[32,4096]{1,0:T(8,128)(2,1)S(1)}, bf16[32,4096]{1,0:T(8,128)(2,1)S(1)}, u32[]{:S(2)}, u32[]{:S(2)}) collective-permute-start(bf16[32,4096]{1,0:T(8,128)(2,1)S(1)} %add_convert_fusion), channel_id=1, source_target_pairs={{0,8},{1,9},{2,10},{3,11},{4,12},{5,13},{6,14},{7,15},{8,0},{9,1},... | collective-permute-start | bytes 786440 | tf_op jit(solution)/shard_map/ppermute | solution.py:232
  65.5 11.9 %collective-permute-start.26 = (bf16[32,4096]{1,0:T(8,128)(2,1)S(1)}, bf16[32,4096]{1,0:T(8,128)(2,1)S(1)}, u32[]{:S(2)}, u32[]{:S(2)}) collective-permute-start(bf16[32,4096]{1,0:T(8,128)(2,1)S(1)} %fusion), channel_id=1, source_target_pairs={{0,2},{1,3},{2,0},{3,1},{4,6},{5,7},{6,4},{7,5},{8,10},{9,11},{10,... | collective-permute-start | bytes 786440 | tf_op jit(solution)/shard_map/ppermute | solution.py:232
  67.2 12.0 %collective-permute-start.25 = (bf16[32,4096]{1,0:T(8,128)(2,1)S(1)}, bf16[32,4096]{1,0:T(8,128)(2,1)S(1)}, u32[]{:S(2)}, u32[]{:S(2)}) collective-permute-start(bf16[32,4096]{1,0:T(8,128)(2,1)S(1)} %get-tuple-element.138), channel_id=1, source_target_pairs={{0,4},{1,5},{2,6},{3,7},{4,0},{5,1},{6,2},{7,3},{8,12},{9,13},{10,... | collective-permute-start | bytes 786440 | tf_op jit(solution)/shard_map/ppermute | solution.py:232

commit v7 on v6

--- a/solution.py
+++ b/solution.py
@@ -302,20 +302,20 @@
         beside1, back3, keep2, send2, send0, packs, mine1, key_update
     )
 
-    onward = over_z(rounded(add(mine3, back3)), 1)
+    onward, early = over_z(rounded(add(mine3, back3)), 1), over_z(mine1[:, :STEP], 1)
     other0, other2 = over_cores([send0, send2])
     mine2, *terms2 = sum_cores(keep2, other2, columns, jnp.float32)
     packs, mine2, terms2 = together(packs, mine2, terms2)
     back2 = back_y(terms2)
     key_update = updates(True, packs, key_update, 2, 4)
-    onward, mine2, back2, other0, key_update, packs, mine1 = together(
-        onward, mine2, back2, other0, key_update, packs, mine1
+    onward, mine2, back2, other0, key_update, packs, mine1, early = together(
+        onward, mine2, back2, other0, key_update, packs, mine1, early
     )
 
     last = over_z(rounded(add(mine2, back2 + [onward])), 2)
     both = keep0.astype(jnp.float32) + other0.astype(jnp.float32)
     terms0 = [rounded(add(both[j * rows : (j + 1) * rows], [term])) for j, term in enumerate(beside1, 1)]
-    back0, mine1 = back_y(terms0), over_z(mine1, 1)
+    back0, mine1 = back_y(terms0), jnp.concatenate([early, over_z(mine1[:, STEP:], 1)], 1)
     value_update = updates(False, packs, None, 0, 4)
     return rounded(add(both[:rows], [last, mine1] + back0)), key_update, value_update
 

time: 80.2 us -> 79.1 us (0.986)
  waiting for transfers between devices: 17.7 us -> 15.7 us
  starting transfers between devices: 28 us -> 28.9 us
    ppermute x26 -> x27, waiting for transfers between devices: 17.7 us -> 15.7 us  [swap(): return lax.ppermute(array, 'shard', [(i, i ^ bits) for i in range(devices)])]
    ppermute x26 -> x27, starting transfers between devices: 26.5 us -> 27.3 us  [swap(): return lax.ppermute(array, 'shard', [(i, i ^ bits) for i in range(devices)])]
  transfers between devices with their start and end apart: 27 -> 28, of which waited for: 15 -> 14; matrix products, arithmetic and copies ran while one was open for 1% -> 1% of each run, Pallas kernels for 35% -> 36%
where the time goes in v7:
time: 79.1 us; the launch traced here: 78.9 us
  starting transfers between devices  28.9 us (37%)
  Pallas kernels  28.2 us (36%)
  waiting for transfers between devices  15.7 us (20%)
  local copies, waits for them, and re-layouts  4.16 us (5%)
  other arithmetic  1.13 us (1%)
  between operations  0.82 us (1%)
    ppermute x27, starting transfers between devices, swap(): return lax.ppermute(array, 'shard', [(i, i ^ bits) for i in range(devices)])  27.3 us
    ppermute x27, waiting for transfers between devices, swap(): return lax.ppermute(array, 'shard', [(i, i ^ bits) for i in range(devices)])  15.7 us
    pallas_call x8, Pallas kernels, update(): pl.pallas_call(functools.partial(update_kernel, fit_rows, piece, groups,...  14.2 us
    pallas_call x4, Pallas kernels, chunk(): pl.pallas_call(functools.partial(chunk_kernel, k, rows, columns), out_sha...  11.9 us
    unnamed x16, local copies, waits for them, and re-layouts  3.41 us
  transfers between devices with their start and end apart: 28, of which 14 were waited for; matrix products, arithmetic and copies ran while one was open for 1% of the time, Pallas kernels for 36%

profile of v7, /device:TPU:0, one launch (start us, length us, event | category | flops | bytes accessed | tf_op | source)
XLA Modules:
  0.0 78.9 jit_solution(18384099004269883175)
XLA Ops:
  0.6 3.1 %collective-permute-start.1 = (bf16[32,4096]{1,0:T(8,128)(2,1)}, bf16[32,4096]{1,0:T(8,128)(2,1)S(1)}, u32[]{:S(2)}, u32[]{:S(2)}) collective-permute-start(bf16[32,4096]{1,0:T(8,128)(2,1)} %refs_0_.3), channel_id=1, source_target_pairs={{0,4},{1,5},{2,6},{3,7},{4,0},{5,1},{6,2},{7,3},{8,12},{9,13},{10,... | collective-permute-start | bytes 786440 | tf_op jit(solution)/shard_map/ppermute | solution.py:232
  3.7 1.5 %collective-permute-start.2 = (bf16[32,4096]{1,0:T(8,128)(2,1)}, bf16[32,4096]{1,0:T(8,128)(2,1)S(1)}, u32[]{:S(2)}, u32[]{:S(2)}) collective-permute-start(bf16[32,4096]{1,0:T(8,128)(2,1)} %refs_0_.3), channel_id=1, source_target_pairs={{0,2},{1,3},{2,0},{3,1},{4,6},{5,7},{6,4},{7,5},{8,10},{9,11},{10,... | collective-permute-start | bytes 786440 | tf_op jit(solution)/shard_map/ppermute | solution.py:232
  5.2 2.6 %collective-permute-start = (bf16[32,4096]{1,0:T(8,128)(2,1)}, bf16[32,4096]{1,0:T(8,128)(2,1)S(1)}, u32[]{:S(2)}, u32[]{:S(2)}) collective-permute-start(bf16[32,4096]{1,0:T(8,128)(2,1)} %refs_0_.3), channel_id=1, source_target_pairs={{0,8},{1,9},{2,10},{3,11},{4,12},{5,13},{6,14},{7,15},{8,0},{9,1},... | collective-permute-start | bytes 786440 | tf_op jit(solution)/shard_map/ppermute | solution.py:232
  7.8 0.7 broadcast_in_dim.3.refs_4_
  8.6 4.2 %collective-permute-done.1.refs_0_ = bf16[32,4096]{1,0:T(8,128)(2,1)S(1)} collective-permute-done((bf16[32,4096]{1,0:T(8,128)(2,1)}, bf16[32,4096]{1,0:T(8,128)(2,1)S(1)}, u32[]{:S(2)}, u32[]{:S(2)}) %collective-permute-start.1) | collective-permute-done | bytes 262176 | tf_op jit(solution)/shard_map/ppermute | solution.py:232
  12.8 3.2 %collective-permute-start.4 = (bf16[32,4096]{1,0:T(8,128)(2,1)S(1)}, bf16[32,4096]{1,0:T(8,128)(2,1)S(1)}, u32[]{:S(2)}, u32[]{:S(2)}) collective-permute-start(bf16[32,4096]{1,0:T(8,128)(2,1)S(1)} %collective-permute-done.1.refs_0_), channel_id=1, source_target_pairs={{0,2},{1,3},{2,0},{3,1},{4,6},{5,7},{6,4},{7,5},{8,10},{9,11},{10,... | collective-permute-start | bytes 786440 | tf_op jit(solution)/shard_map/ppermute | solution.py:232
  16.0 0.5 collective-permute-start.5
  16.5 3.4 %copy-done = bf16[4096,1024]{1,0:T(8,128)(2,1)S(1)} copy-done((bf16[4096,1024]{1,0:T(8,128)(2,1)S(1)}, bf16[4096,1024]{1,0:T(8,128)(2,1)}, u32[]{:S(2)}) %copy-start) | copy-done | bytes 8388632
  19.9 0.6 shard_map.112.refs_9_
  20.5 0.3 collective-permute-done.refs_0_
  20.9 1.8 %collective-permute-start.10 = (bf16[32,4096]{1,0:T(8,128)(2,1)S(1)}, bf16[32,4096]{1,0:T(8,128)(2,1)S(1)}, u32[]{:S(2)}, u32[]{:S(2)}) collective-permute-start(bf16[32,4096]{1,0:T(8,128)(2,1)S(1)} %collective-permute-done.refs_0_), channel_id=1, source_target_pairs={{0,2},{1,3},{2,0},{3,1},{4,6},{5,7},{6,4},{7,5},{8,10},{9,11},{10,... | collective-permute-start | bytes 786440 | tf_op jit(solution)/shard_map/ppermute | solution.py:232
  22.9 1.6 %collective-permute-start.9 = (bf16[32,4096]{1,0:T(8,128)(2,1)S(1)}, bf16[32,4096]{1,0:T(8,128)(2,1)S(1)}, u32[]{:S(2)}, u32[]{:S(2)}) collective-permute-start(bf16[32,4096]{1,0:T(8,128)(2,1)S(1)} %collective-permute-done.refs_0_), channel_id=1, source_target_pairs={{0,4},{1,5},{2,6},{3,7},{4,0},{5,1},{6,2},{7,3},{8,12},{9,13},{10,... | collective-permute-start | bytes 786440 | tf_op jit(solution)/shard_map/ppermute | solution.py:232
  24.5 0.6 shard_map.113.refs_0_
  25.1 1.6 %collective-permute-start.7 = (bf16[8,10368]{1,0:T(8,128)(2,1)S(1)}, bf16[8,10368]{1,0:T(8,128)(2,1)S(1)}, u32[]{:S(2)}, u32[]{:S(2)}) collective-permute-start(bf16[8,10368]{1,0:T(8,128)(2,1)S(1)} %shard_map.113.refs_0_), channel_id=1, source_target_pairs={{0,16},{16,0},{1,17},{17,1},{2,18},{18,2},{3,19},{19,3},{4,20},{20... | collective-permute-start | bytes 497672 | tf_op jit(solution)/shard_map/ppermute | solution.py:273
  26.6 0.6 shard_map.114.refs_10_
  27.2 3.0 %shard_map.115 = (bf16[64,4096]{1,0:T(8,128)(2,1)S(1)}, bf16[64,4096]{1,0:T(8,128)(2,1)S(1)}) custom-call(bf16[32,4096]{1,0:T(8,128)(2,1)S(1)} %collective-permute-done.1.refs_0_, bf16[32,4096]{1,0:T(8,128)(2,1)S(1)} %collective-permute-done.4.refs_1_, bf16[32,4096]{1,0:T(8,128)(2,1)S(1)} %collective-permute-done.6.refs_2_, ...), custom_call_target="tpu_custom_call" | custom-call | flops 128 | bytes 128 | tf_op jit(solution)/shard_map/pallas_call | solution.py:85
  30.2 3.0 %shard_map.116 = (bf16[64,4096]{1,0:T(8,128)(2,1)S(1)}, bf16[64,4096]{1,0:T(8,128)(2,1)S(1)}) custom-call(bf16[32,4096]{1,0:T(8,128)(2,1)S(1)} %copy-done.6, bf16[32,4096]{1,0:T(8,128)(2,1)S(1)} %collective-permute-done.2.refs_1_, bf16[32,4096]{1,0:T(8,128)(2,1)S(1)} %collective-permute-done.3.refs_2_, bf16[32,4096]{1,0:T(8,128)(2,1)S(1)} %collective-permute-done.5.refs_3_, ...), custom_call_target="tpu_custom_call" | custom-call | flops 128 | bytes 128 | tf_op jit(solution)/shard_map/pallas_call | solution.py:85
  33.2 1.8 %shard_map.117.refs_2_ = f32[2048,1024]{1,0:T(8,128)} custom-call(bf16[8,10368]{1,0:T(8,128)(2,1)S(1)} %shard_map.113.refs_0_, bf16[8,10368]{1,0:T(8,128)(2,1)S(1)} %collective-permute-done.7.refs_1_), custom_call_target="tpu_custom_call" | custom-call | flops 256 | bytes 256 | tf_op jit(solution)/shard_map/pallas_call | solution.py:207
  35.3 1.2 %collective-permute-done.9.refs_0_ = bf16[32,4096]{1,0:T(8,128)(2,1)S(1)} collective-permute-done((bf16[32,4096]{1,0:T(8,128)(2,1)S(1)}, bf16[32,4096]{1,0:T(8,128)(2,1)S(1)}, u32[]{:S(2)}, u32[]{:S(2)}) %collective-permute-start.9) | collective-permute-done | bytes 262176 | tf_op jit(solution)/shard_map/ppermute | solution.py:232
  36.5 0.5 collective-permute-start.15
  37.0 0.5 collective-permute-start.13
  37.5 1.3 %collective-permute-done.15.refs_2_ = bf16[32,4096]{1,0:T(8,128)(2,1)S(1)} collective-permute-done((bf16[32,4096]{1,0:T(8,128)(2,1)S(1)}, bf16[32,4096]{1,0:T(8,128)(2,1)S(1)}, u32[]{:S(2)}, u32[]{:S(2)}) %collective-permute-start.15) | collective-permute-done | bytes 262176 | tf_op jit(solution)/shard_map/ppermute | solution.py:232
  38.8 0.4 collective-permute-done.16.refs_3_
  39.2 3.0 %shard_map.118 = (bf16[64,4096]{1,0:T(8,128)(2,1)S(1)}, bf16[64,4096]{1,0:T(8,128)(2,1)S(1)}) custom-call(bf16[32,4096]{1,0:T(8,128)(2,1)S(1)} %collective-permute-done.9.refs_0_, bf16[32,4096]{1,0:T(8,128)(2,1)S(1)} %collective-permute-done.11.refs_1_, bf16[32,4096]{1,0:T(8,128)(2,1)S(1)} %collective-permute-done.15.refs_2_, ...), custom_call_target="tpu_custom_call" | custom-call | flops 128 | bytes 128 | tf_op jit(solution)/shard_map/pallas_call | solution.py:85
  42.5 0.6 collective-permute-start.18
  43.1 1.0 %collective-permute-done.17.arrived = bf16[64,4096]{1,0:T(8,128)(2,1)S(1)} collective-permute-done((bf16[64,4096]{1,0:T(8,128)(2,1)S(1)}, bf16[64,4096]{1,0:T(8,128)(2,1)S(1)}, u32[]{:S(2)}, u32[]{:S(2)}) %collective-permute-start.17) | collective-permute-done | bytes 524320 | tf_op jit(solution)/shard_map/ppermute | solution.py:232
  44.3 1.8 %collective-permute-start.19 = (bf16[32,4096]{1,0:T(8,128)(2,1)S(1)}, bf16[32,4096]{1,0:T(8,128)(2,1)S(1)}, u32[]{:S(2)}, u32[]{:S(2)}) collective-permute-start(bf16[32,4096]{1,0:T(8,128)(2,1)S(1)} %get-tuple-element.109), channel_id=1, source_target_pairs={{0,2},{1,3},{2,0},{3,1},{4,6},{5,7},{6,4},{7,5},{8,10},{9,11},{10,... | collective-permute-start | bytes 786440 | tf_op jit(solution)/shard_map/ppermute | solution.py:232
  46.1 3.0 %shard_map.121 = (bf16[64,4096]{1,0:T(8,128)(2,1)S(1)}, bf16[64,4096]{1,0:T(8,128)(2,1)S(1)}) custom-call(bf16[32,4096]{1,0:T(8,128)(2,1)S(1)} %collective-permute-done.refs_0_, bf16[32,4096]{1,0:T(8,128)(2,1)S(1)} %collective-permute-done.10.refs_1_, bf16[32,4096]{1,0:T(8,128)(2,1)S(1)} %collective-permute-done.12.refs_2_, ...), custom_call_target="tpu_custom_call" | custom-call | flops 128 | bytes 128 | tf_op jit(solution)/shard_map/pallas_call | solution.py:85
  49.1 1.8 %shard_map.122.refs_2_ = f32[2048,1024]{1,0:T(8,128)} custom-call(bf16[8,10368]{1,0:T(8,128)(2,1)S(1)} %shard_map.113.refs_0_, bf16[8,10368]{1,0:T(8,128)(2,1)S(1)} %collective-permute-done.7.refs_1_, f32[2048,1024]{1,0:T(8,128)} %shard_map.117.refs_2_), custom_call_target="tpu_custom_call", output_to_operand_aliasing={{}: (2, {})} | custom-call | flops 256 | bytes 256 | tf_op jit(solution)/shard_map/pallas_call | solution.py:207
  50.9 0.3 collective-permute-done.18
  51.1 1.5 %collective-permute-done.19 = bf16[32,4096]{1,0:T(8,128)(2,1)S(1)} collective-permute-done((bf16[32,4096]{1,0:T(8,128)(2,1)S(1)}, bf16[32,4096]{1,0:T(8,128)(2,1)S(1)}, u32[]{:S(2)}, u32[]{:S(2)}) %collective-permute-start.19) | collective-permute-done | bytes 262176 | tf_op jit(solution)/shard_map/ppermute | solution.py:232
  52.7 0.5 collective-permute-start.23
  53.3 0.6 collective-permute-start.20
  53.9 0.7 collective-permute-done.21.arrived
  54.7 1.8 %collective-permute-start.22 = (bf16[32,4096]{1,0:T(8,128)(2,1)S(1)}, bf16[32,4096]{1,0:T(8,128)(2,1)S(1)}, u32[]{:S(2)}, u32[]{:S(2)}) collective-permute-start(bf16[32,4096]{1,0:T(8,128)(2,1)S(1)} %get-tuple-element.129), channel_id=1, source_target_pairs={{0,2},{1,3},{2,0},{3,1},{4,6},{5,7},{6,4},{7,5},{8,10},{9,11},{10,... | collective-permute-start | bytes 786440 | tf_op jit(solution)/shard_map/ppermute | solution.py:232
  56.5 0.8 collective-permute-start.24
  57.3 1.8 %shard_map.124.refs_2_ = f32[2048,1024]{1,0:T(8,128)} custom-call(bf16[8,10368]{1,0:T(8,128)(2,1)S(1)} %shard_map.113.refs_0_, bf16[8,10368]{1,0:T(8,128)(2,1)S(1)} %collective-permute-done.7.refs_1_, f32[2048,1024]{1,0:T(8,128)} %shard_map.122.refs_2_), custom_call_target="tpu_custom_call", output_to_operand_aliasing={{}: (2, {})} | custom-call | flops 256 | bytes 256 | tf_op jit(solution)/shard_map/pallas_call | solution.py:207
  59.1 1.8 %shard_map.125 = f32[2048,1024]{1,0:T(8,128)} custom-call(bf16[8,10368]{1,0:T(8,128)(2,1)S(1)} %shard_map.113.refs_0_, bf16[8,10368]{1,0:T(8,128)(2,1)S(1)} %collective-permute-done.7.refs_1_, f32[2048,1024]{1,0:T(8,128)} %shard_map.124.refs_2_), custom_call_target="tpu_custom_call", output_to_operand_aliasing={{}: (2, {})} | custom-call | flops 256 | bytes 256 | tf_op jit(solution)/shard_map/pallas_call | solution.py:207
  60.8 2.1 %collective-permute-done.24 = bf16[32,1024]{1,0:T(8,128)(2,1)S(1)} collective-permute-done((bf16[32,1024]{1,0:T(8,128)(2,1)S(1)}, bf16[32,1024]{1,0:T(8,128)(2,1)S(1)}, u32[]{:S(2)}, u32[]{:S(2)}) %collective-permute-start.24) | collective-permute-done | bytes 65568 | tf_op jit(solution)/shard_map/ppermute | solution.py:232
  63.2 2.1 %collective-permute-start.25 = (bf16[32,4096]{1,0:T(8,128)(2,1)S(1)}, bf16[32,4096]{1,0:T(8,128)(2,1)S(1)}, u32[]{:S(2)}, u32[]{:S(2)}) collective-permute-start(bf16[32,4096]{1,0:T(8,128)(2,1)S(1)} %add_convert_fusion), channel_id=1, source_target_pairs={{0,8},{1,9},{2,10},{3,11},{4,12},{5,13},{6,14},{7,15},{8,0},{9,1},... | collective-permute-start | bytes 786440 | tf_op jit(solution)/shard_map/ppermute | solution.py:232
  65.5 1.6 %collective-permute-start.27 = (bf16[32,4096]{1,0:T(8,128)(2,1)S(1)}, bf16[32,4096]{1,0:T(8,128)(2,1)S(1)}, u32[]{:S(2)}, u32[]{:S(2)}) collective-permute-start(bf16[32,4096]{1,0:T(8,128)(2,1)S(1)} %fusion), channel_id=1, source_target_pairs={{0,2},{1,3},{2,0},{3,1},{4,6},{5,7},{6,4},{7,5},{8,10},{9,11},{10,... | collective-permute-start | bytes 786440 | tf_op jit(solution)/shard_map/ppermute | solution.py:232
  67.2 1.7 %collective-permute-start.26 = (bf16[32,3072]{1,0:T(8,128)(2,1)S(1)}, bf16[32,3072]{1,0:T(8,128)(2,1)S(1)}, u32[]{:S(2)}, u32[]{:S(2)}) collective-permute-start(bf16[32,3072]{1,0:T(8,128)(2,1)S(1)} %slice.14), channel_id=1, source_target_pairs={{0,4},{1,5},{2,6},{3,7},{4,0},{5,1},{6,2},{7,3},{8,12},{9,13},{10,... | collective-permute-start | bytes 589832 | tf_op jit(solution)/shard_map/ppermute | solution.py:232
  68.9 1.8 %shard_map.126.refs_2_ = f32[1024,2048]{1,0:T(8,128)} custom-call(bf16[8,10368]{1,0:T(8,128)(2,1)S(1)} %shard_map.113.refs_0_, bf16[8,10368]{1,0:T(8,128)(2,1)S(1)} %collective-permute-done.7.refs_1_), custom_call_target="tpu_custom_call" | custom-call | flops 128 | bytes 128 | tf_op jit(solution)/shard_map/pallas_call | solution.py:207
  70.6 1.8 %shard_map.127.refs_2_ = f32[1024,2048]{1,0:T(8,128)} custom-call(bf16[8,10368]{1,0:T(8,128)(2,1)S(1)} %shard_map.113.refs_0_, bf16[8,10368]{1,0:T(8,128)(2,1)S(1)} %collective-permute-done.7.refs_1_, f32[1024,2048]{1,0:T(8,128)} %shard_map.126.refs_2_), custom_call_target="tpu_custom_call", output_to_operand_aliasing={{}: (2, {})} | custom-call | flops 128 | bytes 128 | tf_op jit(solution)/shard_map/pallas_call | solution.py:207
  72.4 1.8 %shard_map.128.refs_2_ = f32[1024,2048]{1,0:T(8,128)} custom-call(bf16[8,10368]{1,0:T(8,128)(2,1)S(1)} %shard_map.113.refs_0_, bf16[8,10368]{1,0:T(8,128)(2,1)S(1)} %collective-permute-done.7.refs_1_, f32[1024,2048]{1,0:T(8,128)} %shard_map.127.refs_2_), custom_call_target="tpu_custom_call", output_to_operand_aliasing={{}: (2, {})} | custom-call | flops 128 | bytes 128 | tf_op jit(solution)/shard_map/pallas_call | solution.py:207
  74.1 1.8 %shard_map.129 = f32[1024,2048]{1,0:T(8,128)} custom-call(bf16[8,10368]{1,0:T(8,128)(2,1)S(1)} %shard_map.113.refs_0_, bf16[8,10368]{1,0:T(8,128)(2,1)S(1)} %collective-permute-done.7.refs_1_, f32[1024,2048]{1,0:T(8,128)} %shard_map.128.refs_2_), custom_call_target="tpu_custom_call", output_to_operand_aliasing={{}: (2, {})} | custom-call | flops 128 | bytes 128 | tf_op jit(solution)/shard_map/pallas_call | solution.py:207
  75.9 2.2 %collective-permute-done.26 = bf16[32,3072]{1,0:T(8,128)(2,1)S(1)} collective-permute-done((bf16[32,3072]{1,0:T(8,128)(2,1)S(1)}, bf16[32,3072]{1,0:T(8,128)(2,1)S(1)}, u32[]{:S(2)}, u32[]{:S(2)}) %collective-permute-start.26) | collective-permute-done | bytes 196640 | tf_op jit(solution)/shard_map/ppermute | solution.py:232
  78.1 0.8 %fusion.3 = bf16[32,4096]{1,0:T(8,128)(2,1)} fusion(f32[64,4096]{1,0:T(8,128)S(1)} %convert_add_fusion, bf16[32,4096]{1,0:T(8,128)(2,1)S(1)} %collective-permute-done.27, bf16[32,4096]{1,0:T(8,128)(2,1)S(1)} %collective-permute-done.25, bf16[32,3072]{1,0:T(8,128)(2,1)S(1)} %collective-permute-done.26, bf16[32,1024]{1,0:T(8,128)(2,1)S(1)} %collective-permute-done.24), kind=kLoop, calls=%fused_computation.6 | loop fusion | flops 1310720 | bytes 1572864 | tf_op jit(solution)/shard_map/convert_element_type | solution.py:261
  (50 shorter events, 1.7 us)
Async XLA Ops:
  0.6 12.1 %collective-permute-start.1 = (bf16[32,4096]{1,0:T(8,128)(2,1)}, bf16[32,4096]{1,0:T(8,128)(2,1)S(1)}, u32[]{:S(2)}, u32[]{:S(2)}) collective-permute-start(bf16[32,4096]{1,0:T(8,128)(2,1)} %refs_0_.3), channel_id=1, source_target_pairs={{0,4},{1,5},{2,6},{3,7},{4,0},{5,1},{6,2},{7,3},{8,12},{9,13},{10,... | collective-permute-start | bytes 786440 | tf_op jit(solution)/shard_map/ppermute | solution.py:232
  3.7 9.0 %collective-permute-start.2 = (bf16[32,4096]{1,0:T(8,128)(2,1)}, bf16[32,4096]{1,0:T(8,128)(2,1)S(1)}, u32[]{:S(2)}, u32[]{:S(2)}) collective-permute-start(bf16[32,4096]{1,0:T(8,128)(2,1)} %refs_0_.3), channel_id=1, source_target_pairs={{0,2},{1,3},{2,0},{3,1},{4,6},{5,7},{6,4},{7,5},{8,10},{9,11},{10,... | collective-permute-start | bytes 786440 | tf_op jit(solution)/shard_map/ppermute | solution.py:232
  5.2 7.5 %collective-permute-start.3 = (bf16[32,4096]{1,0:T(8,128)(2,1)}, bf16[32,4096]{1,0:T(8,128)(2,1)S(1)}, u32[]{:S(2)}, u32[]{:S(2)}) collective-permute-start(bf16[32,4096]{1,0:T(8,128)(2,1)} %refs_0_.3), channel_id=1, source_target_pairs={{0,1},{1,0},{2,3},{3,2},{4,5},{5,4},{6,7},{7,6},{8,9},{9,8},{10,11... | collective-permute-start | bytes 786440 | tf_op jit(solution)/shard_map/ppermute | solution.py:232
  5.2 15.5 %collective-permute-start = (bf16[32,4096]{1,0:T(8,128)(2,1)}, bf16[32,4096]{1,0:T(8,128)(2,1)S(1)}, u32[]{:S(2)}, u32[]{:S(2)}) collective-permute-start(bf16[32,4096]{1,0:T(8,128)(2,1)} %refs_0_.3), channel_id=1, source_target_pairs={{0,8},{1,9},{2,10},{3,11},{4,12},{5,13},{6,14},{7,15},{8,0},{9,1},... | collective-permute-start | bytes 786440 | tf_op jit(solution)/shard_map/ppermute | solution.py:232
  7.8 16.7 %copy-start.4 = (bf16[8,1024]{1,0:T(8,128)(2,1)S(1)}, bf16[8,1024]{1,0:T(8,128)(2,1)}, u32[]{:S(2)}) copy-start(bf16[8,1024]{1,0:T(8,128)(2,1)} %refs_6_.7) | copy-start | bytes 49156
  7.8 16.7 %copy-start.7 = (s32[8]{0:T(128)S(1)}, s32[8]{0:T(128)}, u32[]{:S(2)}) copy-start(s32[8]{0:T(128)} %ranks.1) | copy-start | bytes 100
  12.8 8.2 %collective-permute-start.4 = (bf16[32,4096]{1,0:T(8,128)(2,1)S(1)}, bf16[32,4096]{1,0:T(8,128)(2,1)S(1)}, u32[]{:S(2)}, u32[]{:S(2)}) collective-permute-start(bf16[32,4096]{1,0:T(8,128)(2,1)S(1)} %collective-permute-done.1.refs_0_), channel_id=1, source_target_pairs={{0,2},{1,3},{2,0},{3,1},{4,6},{5,7},{6,4},{7,5},{8,10},{9,11},{10,... | collective-permute-start | bytes 786440 | tf_op jit(solution)/shard_map/ppermute | solution.py:232
  16.0 4.9 %collective-permute-start.6 = (bf16[32,4096]{1,0:T(8,128)(2,1)S(1)}, bf16[32,4096]{1,0:T(8,128)(2,1)S(1)}, u32[]{:S(2)}, u32[]{:S(2)}) collective-permute-start(bf16[32,4096]{1,0:T(8,128)(2,1)S(1)} %collective-permute-done.1.refs_0_), channel_id=1, source_target_pairs={{0,1},{1,0},{2,3},{3,2},{4,5},{5,4},{6,7},{7,6},{8,9},{9,8},{10,11... | collective-permute-start | bytes 786440 | tf_op jit(solution)/shard_map/ppermute | solution.py:232
  16.0 4.9 %collective-permute-start.5 = (bf16[32,4096]{1,0:T(8,128)(2,1)S(1)}, bf16[32,4096]{1,0:T(8,128)(2,1)S(1)}, u32[]{:S(2)}, u32[]{:S(2)}) collective-permute-start(bf16[32,4096]{1,0:T(8,128)(2,1)S(1)} %collective-permute-done.2.refs_1_), channel_id=1, source_target_pairs={{0,1},{1,0},{2,3},{3,2},{4,5},{5,4},{6,7},{7,6},{8,9},{9,8},{10,11... | collective-permute-start | bytes 786440 | tf_op jit(solution)/shard_map/ppermute | solution.py:232
  16.5 3.4 %copy-start = (bf16[4096,1024]{1,0:T(8,128)(2,1)S(1)}, bf16[4096,1024]{1,0:T(8,128)(2,1)}, u32[]{:S(2)}) copy-start(bf16[4096,1024]{1,0:T(8,128)(2,1)} %refs_0_) | copy-start | bytes 25165828
  19.9 4.6 %copy-start.2 = (bf16[8,4096]{1,0:T(8,128)(2,1)S(1)}, bf16[8,4096]{1,0:T(8,128)(2,1)}, u32[]{:S(2)}) copy-start(bf16[8,4096]{1,0:T(8,128)(2,1)} %refs_5_.7) | copy-start | bytes 196612
  19.9 4.6 %copy-start.3 = (bf16[8,4096]{1,0:T(8,128)(2,1)S(1)}, bf16[8,4096]{1,0:T(8,128)(2,1)}, u32[]{:S(2)}) copy-start(bf16[8,4096]{1,0:T(8,128)(2,1)} %refs_8_.7) | copy-start | bytes 196612
  19.9 4.6 %copy-start.5 = (bf16[8,1024]{1,0:T(8,128)(2,1)S(1)}, bf16[8,1024]{1,0:T(8,128)(2,1)}, u32[]{:S(2)}) copy-start(bf16[8,1024]{1,0:T(8,128)(2,1)} %refs_7_.7) | copy-start | bytes 49156
  19.9 6.8 %copy-start.1 = (bf16[1024,4096]{1,0:T(8,128)(2,1)S(1)}, bf16[1024,4096]{1,0:T(8,128)(2,1)}, u32[]{:S(2)}) copy-start(bf16[1024,4096]{1,0:T(8,128)(2,1)} %refs_0_.2) | copy-start | bytes 25165828
  20.9 4.2 %collective-permute-start.8 = (bf16[32,4096]{1,0:T(8,128)(2,1)S(1)}, bf16[32,4096]{1,0:T(8,128)(2,1)S(1)}, u32[]{:S(2)}, u32[]{:S(2)}) collective-permute-start(bf16[32,4096]{1,0:T(8,128)(2,1)S(1)} %collective-permute-done.4.refs_1_), channel_id=1, source_target_pairs={{0,1},{1,0},{2,3},{3,2},{4,5},{5,4},{6,7},{7,6},{8,9},{9,8},{10,11... | collective-permute-start | bytes 786440 | tf_op jit(solution)/shard_map/ppermute | solution.py:232
  20.9 14.3 %collective-permute-start.10 = (bf16[32,4096]{1,0:T(8,128)(2,1)S(1)}, bf16[32,4096]{1,0:T(8,128)(2,1)S(1)}, u32[]{:S(2)}, u32[]{:S(2)}) collective-permute-start(bf16[32,4096]{1,0:T(8,128)(2,1)S(1)} %collective-permute-done.refs_0_), channel_id=1, source_target_pairs={{0,2},{1,3},{2,0},{3,1},{4,6},{5,7},{6,4},{7,5},{8,10},{9,11},{10,... | collective-permute-start | bytes 786440 | tf_op jit(solution)/shard_map/ppermute | solution.py:232
  22.7 12.5 %collective-permute-start.11 = (bf16[32,4096]{1,0:T(8,128)(2,1)S(1)}, bf16[32,4096]{1,0:T(8,128)(2,1)S(1)}, u32[]{:S(2)}, u32[]{:S(2)}) collective-permute-start(bf16[32,4096]{1,0:T(8,128)(2,1)S(1)} %collective-permute-done.refs_0_), channel_id=1, source_target_pairs={{0,6},{1,7},{2,4},{3,5},{4,2},{5,3},{6,0},{7,1},{8,14},{9,15},{10,... | collective-permute-start | bytes 786440 | tf_op jit(solution)/shard_map/ppermute | solution.py:232
  22.7 12.5 %collective-permute-start.12 = (bf16[32,4096]{1,0:T(8,128)(2,1)S(1)}, bf16[32,4096]{1,0:T(8,128)(2,1)S(1)}, u32[]{:S(2)}, u32[]{:S(2)}) collective-permute-start(bf16[32,4096]{1,0:T(8,128)(2,1)S(1)} %collective-permute-done.refs_0_), channel_id=1, source_target_pairs={{0,1},{1,0},{2,3},{3,2},{4,5},{5,4},{6,7},{7,6},{8,9},{9,8},{10,11... | collective-permute-start | bytes 786440 | tf_op jit(solution)/shard_map/ppermute | solution.py:232
  22.9 13.6 %collective-permute-start.9 = (bf16[32,4096]{1,0:T(8,128)(2,1)S(1)}, bf16[32,4096]{1,0:T(8,128)(2,1)S(1)}, u32[]{:S(2)}, u32[]{:S(2)}) collective-permute-start(bf16[32,4096]{1,0:T(8,128)(2,1)S(1)} %collective-permute-done.refs_0_), channel_id=1, source_target_pairs={{0,4},{1,5},{2,6},{3,7},{4,0},{5,1},{6,2},{7,3},{8,12},{9,13},{10,... | collective-permute-start | bytes 786440 | tf_op jit(solution)/shard_map/ppermute | solution.py:232
  25.1 8.1 %collective-permute-start.7 = (bf16[8,10368]{1,0:T(8,128)(2,1)S(1)}, bf16[8,10368]{1,0:T(8,128)(2,1)S(1)}, u32[]{:S(2)}, u32[]{:S(2)}) collective-permute-start(bf16[8,10368]{1,0:T(8,128)(2,1)S(1)} %shard_map.113.refs_0_), channel_id=1, source_target_pairs={{0,16},{16,0},{1,17},{17,1},{2,18},{18,2},{3,19},{19,3},{4,20},{20... | collective-permute-start | bytes 497672 | tf_op jit(solution)/shard_map/ppermute | solution.py:273
  27.2 3.0 %copy-start.6 = (bf16[32,4096]{1,0:T(8,128)(2,1)S(1)}, bf16[32,4096]{1,0:T(8,128)(2,1)}, u32[]{:S(2)}) copy-start(bf16[32,4096]{1,0:T(8,128)(2,1)} %refs_0_.3) | copy-start | bytes 786436
  36.5 5.7 %collective-permute-start.14 = (bf16[64,4096]{1,0:T(8,128)(2,1)S(1)}, bf16[64,4096]{1,0:T(8,128)(2,1)S(1)}, u32[]{:S(2)}, u32[]{:S(2)}) collective-permute-start(bf16[64,4096]{1,0:T(8,128)(2,1)S(1)} %get-tuple-element.96), channel_id=1, source_target_pairs={{0,1},{1,0},{2,3},{3,2},{4,5},{5,4},{6,7},{7,6},{8,9},{9,8},{10,11... | collective-permute-start | bytes 1572872 | tf_op jit(solution)/shard_map/ppermute | solution.py:232
  36.5 2.3 %collective-permute-start.15 = (bf16[32,4096]{1,0:T(8,128)(2,1)S(1)}, bf16[32,4096]{1,0:T(8,128)(2,1)S(1)}, u32[]{:S(2)}, u32[]{:S(2)}) collective-permute-start(bf16[32,4096]{1,0:T(8,128)(2,1)S(1)} %collective-permute-done.9.refs_0_), channel_id=1, source_target_pairs={{0,1},{1,0},{2,3},{3,2},{4,5},{5,4},{6,7},{7,6},{8,9},{9,8},{10,11... | collective-permute-start | bytes 786440 | tf_op jit(solution)/shard_map/ppermute | solution.py:232
  37.0 2.1 %collective-permute-start.16 = (bf16[32,4096]{1,0:T(8,128)(2,1)S(1)}, bf16[32,4096]{1,0:T(8,128)(2,1)S(1)}, u32[]{:S(2)}, u32[]{:S(2)}) collective-permute-start(bf16[32,4096]{1,0:T(8,128)(2,1)S(1)} %collective-permute-done.11.refs_1_), channel_id=1, source_target_pairs={{0,1},{1,0},{2,3},{3,2},{4,5},{5,4},{6,7},{7,6},{8,9},{9,8},{10,11... | collective-permute-start | bytes 786440 | tf_op jit(solution)/shard_map/ppermute | solution.py:232
  37.0 5.1 %collective-permute-start.13 = (bf16[32,4096]{1,0:T(8,128)(2,1)S(1)}, bf16[32,4096]{1,0:T(8,128)(2,1)S(1)}, u32[]{:S(2)}, u32[]{:S(2)}) collective-permute-start(bf16[32,4096]{1,0:T(8,128)(2,1)S(1)} %collective-permute-done.10.refs_1_), channel_id=1, source_target_pairs={{0,1},{1,0},{2,3},{3,2},{4,5},{5,4},{6,7},{7,6},{8,9},{9,8},{10,11... | collective-permute-start | bytes 786440 | tf_op jit(solution)/shard_map/ppermute | solution.py:232
  42.2 2.0 %collective-permute-start.17 = (bf16[64,4096]{1,0:T(8,128)(2,1)S(1)}, bf16[64,4096]{1,0:T(8,128)(2,1)S(1)}, u32[]{:S(2)}, u32[]{:S(2)}) collective-permute-start(bf16[64,4096]{1,0:T(8,128)(2,1)S(1)} %get-tuple-element.102), channel_id=1, source_target_pairs={{0,1},{1,0},{2,3},{3,2},{4,5},{5,4},{6,7},{7,6},{8,9},{9,8},{10,11... | collective-permute-start | bytes 1572872 | tf_op jit(solution)/shard_map/ppermute | solution.py:232
  42.5 8.6 %collective-permute-start.18 = (bf16[32,4096]{1,0:T(8,128)(2,1)S(1)}, bf16[32,4096]{1,0:T(8,128)(2,1)S(1)}, u32[]{:S(2)}, u32[]{:S(2)}) collective-permute-start(bf16[32,4096]{1,0:T(8,128)(2,1)S(1)} %get-tuple-element.108), channel_id=1, source_target_pairs={{0,4},{1,5},{2,6},{3,7},{4,0},{5,1},{6,2},{7,3},{8,12},{9,13},{10,... | collective-permute-start | bytes 786440 | tf_op jit(solution)/shard_map/ppermute | solution.py:232
  44.3 8.4 %collective-permute-start.19 = (bf16[32,4096]{1,0:T(8,128)(2,1)S(1)}, bf16[32,4096]{1,0:T(8,128)(2,1)S(1)}, u32[]{:S(2)}, u32[]{:S(2)}) collective-permute-start(bf16[32,4096]{1,0:T(8,128)(2,1)S(1)} %get-tuple-element.109), channel_id=1, source_target_pairs={{0,2},{1,3},{2,0},{3,1},{4,6},{5,7},{6,4},{7,5},{8,10},{9,11},{10,... | collective-permute-start | bytes 786440 | tf_op jit(solution)/shard_map/ppermute | solution.py:232
  52.7 1.9 %collective-permute-start.21 = (bf16[64,4096]{1,0:T(8,128)(2,1)S(1)}, bf16[64,4096]{1,0:T(8,128)(2,1)S(1)}, u32[]{:S(2)}, u32[]{:S(2)}) collective-permute-start(bf16[64,4096]{1,0:T(8,128)(2,1)S(1)} %get-tuple-element.125), channel_id=1, source_target_pairs={{0,1},{1,0},{2,3},{3,2},{4,5},{5,4},{6,7},{7,6},{8,9},{9,8},{10,11... | collective-permute-start | bytes 1572872 | tf_op jit(solution)/shard_map/ppermute | solution.py:232
  52.7 10.3 %collective-permute-start.23 = (bf16[64,4096]{1,0:T(8,128)(2,1)S(1)}, bf16[64,4096]{1,0:T(8,128)(2,1)S(1)}, u32[]{:S(2)}, u32[]{:S(2)}) collective-permute-start(bf16[64,4096]{1,0:T(8,128)(2,1)S(1)} %get-tuple-element.130), channel_id=1, source_target_pairs={{0,1},{1,0},{2,3},{3,2},{4,5},{5,4},{6,7},{7,6},{8,9},{9,8},{10,11... | collective-permute-start | bytes 1572872 | tf_op jit(solution)/shard_map/ppermute | solution.py:232
  53.3 9.7 %collective-permute-start.20 = (bf16[32,4096]{1,0:T(8,128)(2,1)S(1)}, bf16[32,4096]{1,0:T(8,128)(2,1)S(1)}, u32[]{:S(2)}, u32[]{:S(2)}) collective-permute-start(bf16[32,4096]{1,0:T(8,128)(2,1)S(1)} %add_convert_fusion.1), channel_id=1, source_target_pairs={{0,4},{1,5},{2,6},{3,7},{4,0},{5,1},{6,2},{7,3},{8,12},{9,13},{10,... | collective-permute-start | bytes 786440 | tf_op jit(solution)/shard_map/ppermute | solution.py:232
  54.7 8.4 %collective-permute-start.22 = (bf16[32,4096]{1,0:T(8,128)(2,1)S(1)}, bf16[32,4096]{1,0:T(8,128)(2,1)S(1)}, u32[]{:S(2)}, u32[]{:S(2)}) collective-permute-start(bf16[32,4096]{1,0:T(8,128)(2,1)S(1)} %get-tuple-element.129), channel_id=1, source_target_pairs={{0,2},{1,3},{2,0},{3,1},{4,6},{5,7},{6,4},{7,5},{8,10},{9,11},{10,... | collective-permute-start | bytes 786440 | tf_op jit(solution)/shard_map/ppermute | solution.py:232
  56.5 6.4 %collective-permute-start.24 = (bf16[32,1024]{1,0:T(8,128)(2,1)S(1)}, bf16[32,1024]{1,0:T(8,128)(2,1)S(1)}, u32[]{:S(2)}, u32[]{:S(2)}) collective-permute-start(bf16[32,1024]{1,0:T(8,128)(2,1)S(1)} %slice.12), channel_id=1, source_target_pairs={{0,4},{1,5},{2,6},{3,7},{4,0},{5,1},{6,2},{7,3},{8,12},{9,13},{10,... | collective-permute-start | bytes 196616 | tf_op jit(solution)/shard_map/ppermute | solution.py:232
  63.2 14.9 %collective-permute-start.25 = (bf16[32,4096]{1,0:T(8,128)(2,1)S(1)}, bf16[32,4096]{1,0:T(8,128)(2,1)S(1)}, u32[]{:S(2)}, u32[]{:S(2)}) collective-permute-start(bf16[32,4096]{1,0:T(8,128)(2,1)S(1)} %add_convert_fusion), channel_id=1, source_target_pairs={{0,8},{1,9},{2,10},{3,11},{4,12},{5,13},{6,14},{7,15},{8,0},{9,1},... | collective-permute-start | bytes 786440 | tf_op jit(solution)/shard_map/ppermute | solution.py:232
  65.5 12.6 %collective-permute-start.27 = (bf16[32,4096]{1,0:T(8,128)(2,1)S(1)}, bf16[32,4096]{1,0:T(8,128)(2,1)S(1)}, u32[]{:S(2)}, u32[]{:S(2)}) collective-permute-start(bf16[32,4096]{1,0:T(8,128)(2,1)S(1)} %fusion), channel_id=1, source_target_pairs={{0,2},{1,3},{2,0},{3,1},{4,6},{5,7},{6,4},{7,5},{8,10},{9,11},{10,... | collective-permute-start | bytes 786440 | tf_op jit(solution)/shard_map/ppermute | solution.py:232
  67.2 10.9 %collective-permute-start.26 = (bf16[32,3072]{1,0:T(8,128)(2,1)S(1)}, bf16[32,3072]{1,0:T(8,128)(2,1)S(1)}, u32[]{:S(2)}, u32[]{:S(2)}) collective-permute-start(bf16[32,3072]{1,0:T(8,128)(2,1)S(1)} %slice.14), channel_id=1, source_target_pairs={{0,4},{1,5},{2,6},{3,7},{4,0},{5,1},{6,2},{7,3},{8,12},{9,13},{10,... | collective-permute-start | bytes 589832 | tf_op jit(solution)/shard_map/ppermute | solution.py:232

commit v8 on v7

--- a/solution.py
+++ b/solution.py
@@ -99,19 +99,22 @@
     )(*operands)
 
 
-def sum_kernel(rows, keep, arrived, *outs):
+def sum_kernel(rows, count, keep, arrived, *outs):
     both = keep[...].astype(jnp.float32) + arrived[...].astype(jnp.float32)
     at = 0
-    for out in outs:
-        out[...] = both[at : at + out.shape[0]].astype(out.dtype)
-        at += out.shape[0]
-
-
-def sum_cores(keep, arrived, columns, kind):
+    for out in outs[:count]:
+        out[...] = both[:rows, at : at + out.shape[1]].astype(out.dtype)
+        at += out.shape[1]
+    for j, out in enumerate(outs[count:], 1):
+        out[...] = both[j * rows : (j + 1) * rows].astype(out.dtype)
+
+
+def sum_cores(keep, arrived, columns, kind, widths=(D,)):
     rows = keep.shape[0] // columns
-    outs = [jax.ShapeDtypeStruct((rows, D), k) for k in [kind] + [jnp.bfloat16] * (columns - 1)]
-    return pl.pallas_call(
-        functools.partial(sum_kernel, rows),
+    outs = [jax.ShapeDtypeStruct((rows, width), kind) for width in widths]
+    outs += [jax.ShapeDtypeStruct((rows, D), jnp.bfloat16)] * (columns - 1)
+    return pl.pallas_call(
+        functools.partial(sum_kernel, rows, len(widths)),
         out_shape=outs,
         in_specs=[pl.BlockSpec(memory_space=pltpu.VMEM)] * 2,
         out_specs=[pl.BlockSpec(memory_space=pltpu.VMEM)] * len(outs),
@@ -290,19 +293,21 @@
     keep3, send3 = partial(3, [farthest] + y3, c3 + cy3)
     cy2, other1, keep3, send3 = together(cy2, other1, keep3, send3)
 
-    mine1, *terms1 = sum_cores(keep1, *other1, columns, jnp.bfloat16)
-    beside1 = [over_z(term, 1) for term in terms1]
+    first1, second1, mine1, *terms1 = sum_cores(
+        keep1, *other1, columns, jnp.bfloat16, (D // 4, D // 4, D // 2)
+    )
+    beside1, first1 = [over_z(term, 1) for term in terms1], over_z(first1, 1)
     mine3, *terms3 = sum_cores(keep3, *over_cores([send3]), columns, jnp.float32)
     far, mine3, terms3 = together(far, mine3, terms3)
     back3 = back_y(terms3)
     keep2, send2 = partial(2, [far] + y2, c2 + cy2)
     packs, keep2 = together(packs, keep2)
     key_update = updates(True, packs, key_update, 1, 2)
-    beside1, back3, keep2, send2, send0, packs, mine1, key_update = together(
-        beside1, back3, keep2, send2, send0, packs, mine1, key_update
-    )
-
-    onward, early = over_z(rounded(add(mine3, back3)), 1), over_z(mine1[:, :STEP], 1)
+    beside1, back3, keep2, send2, send0, packs, mine1, key_update, first1, second1 = together(
+        beside1, back3, keep2, send2, send0, packs, mine1, key_update, first1, second1
+    )
+
+    onward, early = over_z(rounded(add(mine3, back3)), 1), over_z(second1, 1)
     other0, other2 = over_cores([send0, send2])
     mine2, *terms2 = sum_cores(keep2, other2, columns, jnp.float32)
     packs, mine2, terms2 = together(packs, mine2, terms2)
@@ -315,7 +320,7 @@
     last = over_z(rounded(add(mine2, back2 + [onward])), 2)
     both = keep0.astype(jnp.float32) + other0.astype(jnp.float32)
     terms0 = [rounded(add(both[j * rows : (j + 1) * rows], [term])) for j, term in enumerate(beside1, 1)]
-    back0, mine1 = back_y(terms0), jnp.concatenate([early, over_z(mine1[:, STEP:], 1)], 1)
+    back0, mine1 = back_y(terms0), jnp.concatenate([first1, early, over_z(mine1, 1)], 1)
     value_update = updates(False, packs, None, 0, 4)
     return rounded(add(both[:rows], [last, mine1] + back0)), key_update, value_update
 

time: 79.1 us -> 78.3 us (0.990)
  waiting for transfers between devices: 15.7 us -> 14.6 us
    ppermute x27 -> x28, waiting for transfers between devices: 15.7 us -> 14.6 us  [swap(): return lax.ppermute(array, 'shard', [(i, i ^ bits) for i in range(devices)])]
    ppermute x27 -> x28, starting transfers between devices: 27.3 us -> 27.7 us  [swap(): return lax.ppermute(array, 'shard', [(i, i ^ bits) for i in range(devices)])]
  transfers between devices with their start and end apart: 28 -> 29, of which waited for: 14 -> 14; matrix products, arithmetic and copies ran while one was open for 1% -> 1% of each run, Pallas kernels for 36% -> 36%
where the time goes in v8:
time: 78.3 us; the launch traced here: 78.1 us
  starting transfers between devices  29.3 us (37%)
  Pallas kernels  28.2 us (36%)
  waiting for transfers between devices  14.6 us (19%)
  local copies, waits for them, and re-layouts  4.14 us (5%)
  other arithmetic  1.13 us (1%)
  between operations  0.82 us (1%)
    ppermute x28, starting transfers between devices, swap(): return lax.ppermute(array, 'shard', [(i, i ^ bits) for i in range(devices)])  27.7 us
    ppermute x28, waiting for transfers between devices, swap(): return lax.ppermute(array, 'shard', [(i, i ^ bits) for i in range(devices)])  14.6 us
    pallas_call x8, Pallas kernels, update(): pl.pallas_call(functools.partial(update_kernel, fit_rows, piece, groups,...  14.3 us
    pallas_call x4, Pallas kernels, chunk(): pl.pallas_call(functools.partial(chunk_kernel, k, rows, columns), out_sha...  11.9 us
    unnamed x16, local copies, waits for them, and re-layouts  3.41 us
  transfers between devices with their start and end apart: 29, of which 14 were waited for; matrix products, arithmetic and copies ran while one was open for 1% of the time, Pallas kernels for 36%

profile of v8, /device:TPU:0, one launch (start us, length us, event | category | flops | bytes accessed | tf_op | source)
XLA Modules:
  0.0 78.1 jit_solution(6297525691628191298)
XLA Ops:
  0.6 3.1 %collective-permute-start.1 = (bf16[32,4096]{1,0:T(8,128)(2,1)}, bf16[32,4096]{1,0:T(8,128)(2,1)S(1)}, u32[]{:S(2)}, u32[]{:S(2)}) collective-permute-start(bf16[32,4096]{1,0:T(8,128)(2,1)} %refs_0_.3), channel_id=1, source_target_pairs={{0,4},{1,5},{2,6},{3,7},{4,0},{5,1},{6,2},{7,3},{8,12},{9,13},{10,... | collective-permute-start | bytes 786440 | tf_op jit(solution)/shard_map/ppermute | solution.py:235
  3.7 1.5 %collective-permute-start.2 = (bf16[32,4096]{1,0:T(8,128)(2,1)}, bf16[32,4096]{1,0:T(8,128)(2,1)S(1)}, u32[]{:S(2)}, u32[]{:S(2)}) collective-permute-start(bf16[32,4096]{1,0:T(8,128)(2,1)} %refs_0_.3), channel_id=1, source_target_pairs={{0,2},{1,3},{2,0},{3,1},{4,6},{5,7},{6,4},{7,5},{8,10},{9,11},{10,... | collective-permute-start | bytes 786440 | tf_op jit(solution)/shard_map/ppermute | solution.py:235
  5.2 2.6 %collective-permute-start = (bf16[32,4096]{1,0:T(8,128)(2,1)}, bf16[32,4096]{1,0:T(8,128)(2,1)S(1)}, u32[]{:S(2)}, u32[]{:S(2)}) collective-permute-start(bf16[32,4096]{1,0:T(8,128)(2,1)} %refs_0_.3), channel_id=1, source_target_pairs={{0,8},{1,9},{2,10},{3,11},{4,12},{5,13},{6,14},{7,15},{8,0},{9,1},... | collective-permute-start | bytes 786440 | tf_op jit(solution)/shard_map/ppermute | solution.py:235
  7.8 0.7 broadcast_in_dim.3.refs_4_
  8.6 4.2 %collective-permute-done.1.refs_0_ = bf16[32,4096]{1,0:T(8,128)(2,1)S(1)} collective-permute-done((bf16[32,4096]{1,0:T(8,128)(2,1)}, bf16[32,4096]{1,0:T(8,128)(2,1)S(1)}, u32[]{:S(2)}, u32[]{:S(2)}) %collective-permute-start.1) | collective-permute-done | bytes 262176 | tf_op jit(solution)/shard_map/ppermute | solution.py:235
  12.8 3.2 %collective-permute-start.4 = (bf16[32,4096]{1,0:T(8,128)(2,1)S(1)}, bf16[32,4096]{1,0:T(8,128)(2,1)S(1)}, u32[]{:S(2)}, u32[]{:S(2)}) collective-permute-start(bf16[32,4096]{1,0:T(8,128)(2,1)S(1)} %collective-permute-done.1.refs_0_), channel_id=1, source_target_pairs={{0,2},{1,3},{2,0},{3,1},{4,6},{5,7},{6,4},{7,5},{8,10},{9,11},{10,... | collective-permute-start | bytes 786440 | tf_op jit(solution)/shard_map/ppermute | solution.py:235
  16.0 0.5 collective-permute-start.5
  16.5 3.4 %copy-done = bf16[4096,1024]{1,0:T(8,128)(2,1)S(1)} copy-done((bf16[4096,1024]{1,0:T(8,128)(2,1)S(1)}, bf16[4096,1024]{1,0:T(8,128)(2,1)}, u32[]{:S(2)}) %copy-start) | copy-done | bytes 8388632
  19.9 0.6 shard_map.112.refs_9_
  20.5 0.3 collective-permute-done.refs_0_
  20.9 1.8 %collective-permute-start.10 = (bf16[32,4096]{1,0:T(8,128)(2,1)S(1)}, bf16[32,4096]{1,0:T(8,128)(2,1)S(1)}, u32[]{:S(2)}, u32[]{:S(2)}) collective-permute-start(bf16[32,4096]{1,0:T(8,128)(2,1)S(1)} %collective-permute-done.refs_0_), channel_id=1, source_target_pairs={{0,2},{1,3},{2,0},{3,1},{4,6},{5,7},{6,4},{7,5},{8,10},{9,11},{10,... | collective-permute-start | bytes 786440 | tf_op jit(solution)/shard_map/ppermute | solution.py:235
  22.9 1.6 %collective-permute-start.9 = (bf16[32,4096]{1,0:T(8,128)(2,1)S(1)}, bf16[32,4096]{1,0:T(8,128)(2,1)S(1)}, u32[]{:S(2)}, u32[]{:S(2)}) collective-permute-start(bf16[32,4096]{1,0:T(8,128)(2,1)S(1)} %collective-permute-done.refs_0_), channel_id=1, source_target_pairs={{0,4},{1,5},{2,6},{3,7},{4,0},{5,1},{6,2},{7,3},{8,12},{9,13},{10,... | collective-permute-start | bytes 786440 | tf_op jit(solution)/shard_map/ppermute | solution.py:235
  24.5 0.6 shard_map.113.refs_0_
  25.1 1.6 %collective-permute-start.7 = (bf16[8,10368]{1,0:T(8,128)(2,1)S(1)}, bf16[8,10368]{1,0:T(8,128)(2,1)S(1)}, u32[]{:S(2)}, u32[]{:S(2)}) collective-permute-start(bf16[8,10368]{1,0:T(8,128)(2,1)S(1)} %shard_map.113.refs_0_), channel_id=1, source_target_pairs={{0,16},{16,0},{1,17},{17,1},{2,18},{18,2},{3,19},{19,3},{4,20},{20... | collective-permute-start | bytes 497672 | tf_op jit(solution)/shard_map/ppermute | solution.py:276
  26.6 0.6 shard_map.114.refs_10_
  27.2 3.0 %shard_map.115 = (bf16[64,4096]{1,0:T(8,128)(2,1)S(1)}, bf16[64,4096]{1,0:T(8,128)(2,1)S(1)}) custom-call(bf16[32,4096]{1,0:T(8,128)(2,1)S(1)} %collective-permute-done.1.refs_0_, bf16[32,4096]{1,0:T(8,128)(2,1)S(1)} %collective-permute-done.4.refs_1_, bf16[32,4096]{1,0:T(8,128)(2,1)S(1)} %collective-permute-done.6.refs_2_, ...), custom_call_target="tpu_custom_call" | custom-call | flops 128 | bytes 128 | tf_op jit(solution)/shard_map/pallas_call | solution.py:85
  30.2 3.0 %shard_map.116 = (bf16[64,4096]{1,0:T(8,128)(2,1)S(1)}, bf16[64,4096]{1,0:T(8,128)(2,1)S(1)}) custom-call(bf16[32,4096]{1,0:T(8,128)(2,1)S(1)} %copy-done.6, bf16[32,4096]{1,0:T(8,128)(2,1)S(1)} %collective-permute-done.2.refs_1_, bf16[32,4096]{1,0:T(8,128)(2,1)S(1)} %collective-permute-done.3.refs_2_, bf16[32,4096]{1,0:T(8,128)(2,1)S(1)} %collective-permute-done.5.refs_3_, ...), custom_call_target="tpu_custom_call" | custom-call | flops 128 | bytes 128 | tf_op jit(solution)/shard_map/pallas_call | solution.py:85
  33.2 1.8 %shard_map.117.refs_2_ = f32[2048,1024]{1,0:T(8,128)} custom-call(bf16[8,10368]{1,0:T(8,128)(2,1)S(1)} %shard_map.113.refs_0_, bf16[8,10368]{1,0:T(8,128)(2,1)S(1)} %collective-permute-done.7.refs_1_), custom_call_target="tpu_custom_call" | custom-call | flops 256 | bytes 256 | tf_op jit(solution)/shard_map/pallas_call | solution.py:210
  35.3 1.2 %collective-permute-done.9.refs_0_ = bf16[32,4096]{1,0:T(8,128)(2,1)S(1)} collective-permute-done((bf16[32,4096]{1,0:T(8,128)(2,1)S(1)}, bf16[32,4096]{1,0:T(8,128)(2,1)S(1)}, u32[]{:S(2)}, u32[]{:S(2)}) %collective-permute-start.9) | collective-permute-done | bytes 262176 | tf_op jit(solution)/shard_map/ppermute | solution.py:235
  36.5 0.5 collective-permute-start.15
  37.0 0.5 collective-permute-start.13
  37.5 1.3 %collective-permute-done.15.refs_2_ = bf16[32,4096]{1,0:T(8,128)(2,1)S(1)} collective-permute-done((bf16[32,4096]{1,0:T(8,128)(2,1)S(1)}, bf16[32,4096]{1,0:T(8,128)(2,1)S(1)}, u32[]{:S(2)}, u32[]{:S(2)}) %collective-permute-start.15) | collective-permute-done | bytes 262176 | tf_op jit(solution)/shard_map/ppermute | solution.py:235
  38.8 0.4 collective-permute-done.16.refs_3_
  39.2 3.0 %shard_map.118 = (bf16[64,4096]{1,0:T(8,128)(2,1)S(1)}, bf16[64,4096]{1,0:T(8,128)(2,1)S(1)}) custom-call(bf16[32,4096]{1,0:T(8,128)(2,1)S(1)} %collective-permute-done.9.refs_0_, bf16[32,4096]{1,0:T(8,128)(2,1)S(1)} %collective-permute-done.11.refs_1_, bf16[32,4096]{1,0:T(8,128)(2,1)S(1)} %collective-permute-done.15.refs_2_, ...), custom_call_target="tpu_custom_call" | custom-call | flops 128 | bytes 128 | tf_op jit(solution)/shard_map/pallas_call | solution.py:85
  42.5 0.6 collective-permute-start.18
  43.1 1.0 %collective-permute-done.17.arrived = bf16[64,4096]{1,0:T(8,128)(2,1)S(1)} collective-permute-done((bf16[64,4096]{1,0:T(8,128)(2,1)S(1)}, bf16[64,4096]{1,0:T(8,128)(2,1)S(1)}, u32[]{:S(2)}, u32[]{:S(2)}) %collective-permute-start.17) | collective-permute-done | bytes 524320 | tf_op jit(solution)/shard_map/ppermute | solution.py:235
  44.3 1.8 %collective-permute-start.19 = (bf16[32,4096]{1,0:T(8,128)(2,1)S(1)}, bf16[32,4096]{1,0:T(8,128)(2,1)S(1)}, u32[]{:S(2)}, u32[]{:S(2)}) collective-permute-start(bf16[32,4096]{1,0:T(8,128)(2,1)S(1)} %get-tuple-element.113), channel_id=1, source_target_pairs={{0,2},{1,3},{2,0},{3,1},{4,6},{5,7},{6,4},{7,5},{8,10},{9,11},{10,... | collective-permute-start | bytes 786440 | tf_op jit(solution)/shard_map/ppermute | solution.py:235
  46.1 0.5 collective-permute-start.20
  46.5 3.0 %shard_map.121 = (bf16[64,4096]{1,0:T(8,128)(2,1)S(1)}, bf16[64,4096]{1,0:T(8,128)(2,1)S(1)}) custom-call(bf16[32,4096]{1,0:T(8,128)(2,1)S(1)} %collective-permute-done.refs_0_, bf16[32,4096]{1,0:T(8,128)(2,1)S(1)} %collective-permute-done.10.refs_1_, bf16[32,4096]{1,0:T(8,128)(2,1)S(1)} %collective-permute-done.12.refs_2_, ...), custom_call_target="tpu_custom_call" | custom-call | flops 128 | bytes 128 | tf_op jit(solution)/shard_map/pallas_call | solution.py:85
  49.5 1.8 %shard_map.122.refs_2_ = f32[2048,1024]{1,0:T(8,128)} custom-call(bf16[8,10368]{1,0:T(8,128)(2,1)S(1)} %shard_map.113.refs_0_, bf16[8,10368]{1,0:T(8,128)(2,1)S(1)} %collective-permute-done.7.refs_1_, f32[2048,1024]{1,0:T(8,128)} %shard_map.117.refs_2_), custom_call_target="tpu_custom_call", output_to_operand_aliasing={{}: (2, {})} | custom-call | flops 256 | bytes 256 | tf_op jit(solution)/shard_map/pallas_call | solution.py:210
  51.3 1.2 %collective-permute-done.20 = bf16[32,1024]{1,0:T(8,128)(2,1)S(1)} collective-permute-done((bf16[32,1024]{1,0:T(8,128)(2,1)S(1)}, bf16[32,1024]{1,0:T(8,128)(2,1)S(1)}, u32[]{:S(2)}, u32[]{:S(2)}) %collective-permute-start.20) | collective-permute-done | bytes 65568 | tf_op jit(solution)/shard_map/ppermute | solution.py:235
  52.7 0.5 collective-permute-start.24
  53.3 0.6 collective-permute-start.21
  53.9 0.7 collective-permute-done.22.arrived
  54.7 1.8 %collective-permute-start.23 = (bf16[32,4096]{1,0:T(8,128)(2,1)S(1)}, bf16[32,4096]{1,0:T(8,128)(2,1)S(1)}, u32[]{:S(2)}, u32[]{:S(2)}) collective-permute-start(bf16[32,4096]{1,0:T(8,128)(2,1)S(1)} %get-tuple-element.135), channel_id=1, source_target_pairs={{0,2},{1,3},{2,0},{3,1},{4,6},{5,7},{6,4},{7,5},{8,10},{9,11},{10,... | collective-permute-start | bytes 786440 | tf_op jit(solution)/shard_map/ppermute | solution.py:235
  56.5 0.8 collective-permute-start.25
  57.3 1.8 %shard_map.124.refs_2_ = f32[2048,1024]{1,0:T(8,128)} custom-call(bf16[8,10368]{1,0:T(8,128)(2,1)S(1)} %shard_map.113.refs_0_, bf16[8,10368]{1,0:T(8,128)(2,1)S(1)} %collective-permute-done.7.refs_1_, f32[2048,1024]{1,0:T(8,128)} %shard_map.122.refs_2_), custom_call_target="tpu_custom_call", output_to_operand_aliasing={{}: (2, {})} | custom-call | flops 256 | bytes 256 | tf_op jit(solution)/shard_map/pallas_call | solution.py:210
  59.1 1.8 %shard_map.125 = f32[2048,1024]{1,0:T(8,128)} custom-call(bf16[8,10368]{1,0:T(8,128)(2,1)S(1)} %shard_map.113.refs_0_, bf16[8,10368]{1,0:T(8,128)(2,1)S(1)} %collective-permute-done.7.refs_1_, f32[2048,1024]{1,0:T(8,128)} %shard_map.124.refs_2_), custom_call_target="tpu_custom_call", output_to_operand_aliasing={{}: (2, {})} | custom-call | flops 256 | bytes 256 | tf_op jit(solution)/shard_map/pallas_call | solution.py:210
  60.8 2.1 %collective-permute-done.25 = bf16[32,1024]{1,0:T(8,128)(2,1)S(1)} collective-permute-done((bf16[32,1024]{1,0:T(8,128)(2,1)S(1)}, bf16[32,1024]{1,0:T(8,128)(2,1)S(1)}, u32[]{:S(2)}, u32[]{:S(2)}) %collective-permute-start.25) | collective-permute-done | bytes 65568 | tf_op jit(solution)/shard_map/ppermute | solution.py:235
  63.2 2.1 %collective-permute-start.26 = (bf16[32,4096]{1,0:T(8,128)(2,1)S(1)}, bf16[32,4096]{1,0:T(8,128)(2,1)S(1)}, u32[]{:S(2)}, u32[]{:S(2)}) collective-permute-start(bf16[32,4096]{1,0:T(8,128)(2,1)S(1)} %add_convert_fusion), channel_id=1, source_target_pairs={{0,8},{1,9},{2,10},{3,11},{4,12},{5,13},{6,14},{7,15},{8,0},{9,1},... | collective-permute-start | bytes 786440 | tf_op jit(solution)/shard_map/ppermute | solution.py:235
  65.5 1.6 %collective-permute-start.28 = (bf16[32,4096]{1,0:T(8,128)(2,1)S(1)}, bf16[32,4096]{1,0:T(8,128)(2,1)S(1)}, u32[]{:S(2)}, u32[]{:S(2)}) collective-permute-start(bf16[32,4096]{1,0:T(8,128)(2,1)S(1)} %fusion), channel_id=1, source_target_pairs={{0,2},{1,3},{2,0},{3,1},{4,6},{5,7},{6,4},{7,5},{8,10},{9,11},{10,... | collective-permute-start | bytes 786440 | tf_op jit(solution)/shard_map/ppermute | solution.py:235
  67.2 1.6 %collective-permute-start.27 = (bf16[32,2048]{1,0:T(8,128)(2,1)S(1)}, bf16[32,2048]{1,0:T(8,128)(2,1)S(1)}, u32[]{:S(2)}, u32[]{:S(2)}) collective-permute-start(bf16[32,2048]{1,0:T(8,128)(2,1)S(1)} %get-tuple-element.148), channel_id=1, source_target_pairs={{0,4},{1,5},{2,6},{3,7},{4,0},{5,1},{6,2},{7,3},{8,12},{9,13},{10,... | collective-permute-start | bytes 393224 | tf_op jit(solution)/shard_map/ppermute | solution.py:235
  68.8 1.8 %shard_map.126.refs_2_ = f32[1024,2048]{1,0:T(8,128)} custom-call(bf16[8,10368]{1,0:T(8,128)(2,1)S(1)} %shard_map.113.refs_0_, bf16[8,10368]{1,0:T(8,128)(2,1)S(1)} %collective-permute-done.7.refs_1_), custom_call_target="tpu_custom_call" | custom-call | flops 128 | bytes 128 | tf_op jit(solution)/shard_map/pallas_call | solution.py:210
  70.5 1.8 %shard_map.127.refs_2_ = f32[1024,2048]{1,0:T(8,128)} custom-call(bf16[8,10368]{1,0:T(8,128)(2,1)S(1)} %shard_map.113.refs_0_, bf16[8,10368]{1,0:T(8,128)(2,1)S(1)} %collective-permute-done.7.refs_1_, f32[1024,2048]{1,0:T(8,128)} %shard_map.126.refs_2_), custom_call_target="tpu_custom_call", output_to_operand_aliasing={{}: (2, {})} | custom-call | flops 128 | bytes 128 | tf_op jit(solution)/shard_map/pallas_call | solution.py:210
  72.3 1.8 %shard_map.128.refs_2_ = f32[1024,2048]{1,0:T(8,128)} custom-call(bf16[8,10368]{1,0:T(8,128)(2,1)S(1)} %shard_map.113.refs_0_, bf16[8,10368]{1,0:T(8,128)(2,1)S(1)} %collective-permute-done.7.refs_1_, f32[1024,2048]{1,0:T(8,128)} %shard_map.127.refs_2_), custom_call_target="tpu_custom_call", output_to_operand_aliasing={{}: (2, {})} | custom-call | flops 128 | bytes 128 | tf_op jit(solution)/shard_map/pallas_call | solution.py:210
  74.1 1.8 %shard_map.129 = f32[1024,2048]{1,0:T(8,128)} custom-call(bf16[8,10368]{1,0:T(8,128)(2,1)S(1)} %shard_map.113.refs_0_, bf16[8,10368]{1,0:T(8,128)(2,1)S(1)} %collective-permute-done.7.refs_1_, f32[1024,2048]{1,0:T(8,128)} %shard_map.128.refs_2_), custom_call_target="tpu_custom_call", output_to_operand_aliasing={{}: (2, {})} | custom-call | flops 128 | bytes 128 | tf_op jit(solution)/shard_map/pallas_call | solution.py:210
  75.8 1.5 %collective-permute-done.26 = bf16[32,4096]{1,0:T(8,128)(2,1)S(1)} collective-permute-done((bf16[32,4096]{1,0:T(8,128)(2,1)S(1)}, bf16[32,4096]{1,0:T(8,128)(2,1)S(1)}, u32[]{:S(2)}, u32[]{:S(2)}) %collective-permute-start.26) | collective-permute-done | bytes 262176 | tf_op jit(solution)/shard_map/ppermute | solution.py:235
  77.3 0.8 %fusion.3 = bf16[32,4096]{1,0:T(8,128)(2,1)} fusion(f32[64,4096]{1,0:T(8,128)S(1)} %convert_add_fusion, bf16[32,4096]{1,0:T(8,128)(2,1)S(1)} %collective-permute-done.28, bf16[32,4096]{1,0:T(8,128)(2,1)S(1)} %collective-permute-done.26, bf16[32,2048]{1,0:T(8,128)(2,1)S(1)} %collective-permute-done.27, bf16[32,1024]{1,0:T(8,128)(2,1)S(1)} %collective-permute-done.25, ...), kind=kLoop, calls=%fused_computation.6 | loop fusion | flops 1572864 | bytes 1572864 | tf_op jit(solution)/shard_map/convert_element_type | solution.py:264
  (50 shorter events, 1.8 us)
Async XLA Ops:
  0.6 12.1 %collective-permute-start.1 = (bf16[32,4096]{1,0:T(8,128)(2,1)}, bf16[32,4096]{1,0:T(8,128)(2,1)S(1)}, u32[]{:S(2)}, u32[]{:S(2)}) collective-permute-start(bf16[32,4096]{1,0:T(8,128)(2,1)} %refs_0_.3), channel_id=1, source_target_pairs={{0,4},{1,5},{2,6},{3,7},{4,0},{5,1},{6,2},{7,3},{8,12},{9,13},{10,... | collective-permute-start | bytes 786440 | tf_op jit(solution)/shard_map/ppermute | solution.py:235
  3.7 9.0 %collective-permute-start.2 = (bf16[32,4096]{1,0:T(8,128)(2,1)}, bf16[32,4096]{1,0:T(8,128)(2,1)S(1)}, u32[]{:S(2)}, u32[]{:S(2)}) collective-permute-start(bf16[32,4096]{1,0:T(8,128)(2,1)} %refs_0_.3), channel_id=1, source_target_pairs={{0,2},{1,3},{2,0},{3,1},{4,6},{5,7},{6,4},{7,5},{8,10},{9,11},{10,... | collective-permute-start | bytes 786440 | tf_op jit(solution)/shard_map/ppermute | solution.py:235
  5.2 7.5 %collective-permute-start.3 = (bf16[32,4096]{1,0:T(8,128)(2,1)}, bf16[32,4096]{1,0:T(8,128)(2,1)S(1)}, u32[]{:S(2)}, u32[]{:S(2)}) collective-permute-start(bf16[32,4096]{1,0:T(8,128)(2,1)} %refs_0_.3), channel_id=1, source_target_pairs={{0,1},{1,0},{2,3},{3,2},{4,5},{5,4},{6,7},{7,6},{8,9},{9,8},{10,11... | collective-permute-start | bytes 786440 | tf_op jit(solution)/shard_map/ppermute | solution.py:235
  5.2 15.5 %collective-permute-start = (bf16[32,4096]{1,0:T(8,128)(2,1)}, bf16[32,4096]{1,0:T(8,128)(2,1)S(1)}, u32[]{:S(2)}, u32[]{:S(2)}) collective-permute-start(bf16[32,4096]{1,0:T(8,128)(2,1)} %refs_0_.3), channel_id=1, source_target_pairs={{0,8},{1,9},{2,10},{3,11},{4,12},{5,13},{6,14},{7,15},{8,0},{9,1},... | collective-permute-start | bytes 786440 | tf_op jit(solution)/shard_map/ppermute | solution.py:235
  7.8 16.7 %copy-start.4 = (bf16[8,1024]{1,0:T(8,128)(2,1)S(1)}, bf16[8,1024]{1,0:T(8,128)(2,1)}, u32[]{:S(2)}) copy-start(bf16[8,1024]{1,0:T(8,128)(2,1)} %refs_6_.7) | copy-start | bytes 49156
  7.8 16.7 %copy-start.7 = (s32[8]{0:T(128)S(1)}, s32[8]{0:T(128)}, u32[]{:S(2)}) copy-start(s32[8]{0:T(128)} %ranks.1) | copy-start | bytes 100
  12.8 8.2 %collective-permute-start.4 = (bf16[32,4096]{1,0:T(8,128)(2,1)S(1)}, bf16[32,4096]{1,0:T(8,128)(2,1)S(1)}, u32[]{:S(2)}, u32[]{:S(2)}) collective-permute-start(bf16[32,4096]{1,0:T(8,128)(2,1)S(1)} %collective-permute-done.1.refs_0_), channel_id=1, source_target_pairs={{0,2},{1,3},{2,0},{3,1},{4,6},{5,7},{6,4},{7,5},{8,10},{9,11},{10,... | collective-permute-start | bytes 786440 | tf_op jit(solution)/shard_map/ppermute | solution.py:235
  16.0 4.9 %collective-permute-start.6 = (bf16[32,4096]{1,0:T(8,128)(2,1)S(1)}, bf16[32,4096]{1,0:T(8,128)(2,1)S(1)}, u32[]{:S(2)}, u32[]{:S(2)}) collective-permute-start(bf16[32,4096]{1,0:T(8,128)(2,1)S(1)} %collective-permute-done.1.refs_0_), channel_id=1, source_target_pairs={{0,1},{1,0},{2,3},{3,2},{4,5},{5,4},{6,7},{7,6},{8,9},{9,8},{10,11... | collective-permute-start | bytes 786440 | tf_op jit(solution)/shard_map/ppermute | solution.py:235
  16.0 4.9 %collective-permute-start.5 = (bf16[32,4096]{1,0:T(8,128)(2,1)S(1)}, bf16[32,4096]{1,0:T(8,128)(2,1)S(1)}, u32[]{:S(2)}, u32[]{:S(2)}) collective-permute-start(bf16[32,4096]{1,0:T(8,128)(2,1)S(1)} %collective-permute-done.2.refs_1_), channel_id=1, source_target_pairs={{0,1},{1,0},{2,3},{3,2},{4,5},{5,4},{6,7},{7,6},{8,9},{9,8},{10,11... | collective-permute-start | bytes 786440 | tf_op jit(solution)/shard_map/ppermute | solution.py:235
  16.5 3.4 %copy-start = (bf16[4096,1024]{1,0:T(8,128)(2,1)S(1)}, bf16[4096,1024]{1,0:T(8,128)(2,1)}, u32[]{:S(2)}) copy-start(bf16[4096,1024]{1,0:T(8,128)(2,1)} %refs_0_) | copy-start | bytes 25165828
  19.9 4.6 %copy-start.2 = (bf16[8,4096]{1,0:T(8,128)(2,1)S(1)}, bf16[8,4096]{1,0:T(8,128)(2,1)}, u32[]{:S(2)}) copy-start(bf16[8,4096]{1,0:T(8,128)(2,1)} %refs_5_.7) | copy-start | bytes 196612
  19.9 4.6 %copy-start.3 = (bf16[8,4096]{1,0:T(8,128)(2,1)S(1)}, bf16[8,4096]{1,0:T(8,128)(2,1)}, u32[]{:S(2)}) copy-start(bf16[8,4096]{1,0:T(8,128)(2,1)} %refs_8_.7) | copy-start | bytes 196612
  19.9 4.6 %copy-start.5 = (bf16[8,1024]{1,0:T(8,128)(2,1)S(1)}, bf16[8,1024]{1,0:T(8,128)(2,1)}, u32[]{:S(2)}) copy-start(bf16[8,1024]{1,0:T(8,128)(2,1)} %refs_7_.7) | copy-start | bytes 49156
  19.9 6.8 %copy-start.1 = (bf16[1024,4096]{1,0:T(8,128)(2,1)S(1)}, bf16[1024,4096]{1,0:T(8,128)(2,1)}, u32[]{:S(2)}) copy-start(bf16[1024,4096]{1,0:T(8,128)(2,1)} %refs_0_.2) | copy-start | bytes 25165828
  20.9 4.2 %collective-permute-start.8 = (bf16[32,4096]{1,0:T(8,128)(2,1)S(1)}, bf16[32,4096]{1,0:T(8,128)(2,1)S(1)}, u32[]{:S(2)}, u32[]{:S(2)}) collective-permute-start(bf16[32,4096]{1,0:T(8,128)(2,1)S(1)} %collective-permute-done.4.refs_1_), channel_id=1, source_target_pairs={{0,1},{1,0},{2,3},{3,2},{4,5},{5,4},{6,7},{7,6},{8,9},{9,8},{10,11... | collective-permute-start | bytes 786440 | tf_op jit(solution)/shard_map/ppermute | solution.py:235
  20.9 14.3 %collective-permute-start.10 = (bf16[32,4096]{1,0:T(8,128)(2,1)S(1)}, bf16[32,4096]{1,0:T(8,128)(2,1)S(1)}, u32[]{:S(2)}, u32[]{:S(2)}) collective-permute-start(bf16[32,4096]{1,0:T(8,128)(2,1)S(1)} %collective-permute-done.refs_0_), channel_id=1, source_target_pairs={{0,2},{1,3},{2,0},{3,1},{4,6},{5,7},{6,4},{7,5},{8,10},{9,11},{10,... | collective-permute-start | bytes 786440 | tf_op jit(solution)/shard_map/ppermute | solution.py:235
  22.7 12.5 %collective-permute-start.11 = (bf16[32,4096]{1,0:T(8,128)(2,1)S(1)}, bf16[32,4096]{1,0:T(8,128)(2,1)S(1)}, u32[]{:S(2)}, u32[]{:S(2)}) collective-permute-start(bf16[32,4096]{1,0:T(8,128)(2,1)S(1)} %collective-permute-done.refs_0_), channel_id=1, source_target_pairs={{0,6},{1,7},{2,4},{3,5},{4,2},{5,3},{6,0},{7,1},{8,14},{9,15},{10,... | collective-permute-start | bytes 786440 | tf_op jit(solution)/shard_map/ppermute | solution.py:235
  22.7 12.5 %collective-permute-start.12 = (bf16[32,4096]{1,0:T(8,128)(2,1)S(1)}, bf16[32,4096]{1,0:T(8,128)(2,1)S(1)}, u32[]{:S(2)}, u32[]{:S(2)}) collective-permute-start(bf16[32,4096]{1,0:T(8,128)(2,1)S(1)} %collective-permute-done.refs_0_), channel_id=1, source_target_pairs={{0,1},{1,0},{2,3},{3,2},{4,5},{5,4},{6,7},{7,6},{8,9},{9,8},{10,11... | collective-permute-start | bytes 786440 | tf_op jit(solution)/shard_map/ppermute | solution.py:235
  22.9 13.6 %collective-permute-start.9 = (bf16[32,4096]{1,0:T(8,128)(2,1)S(1)}, bf16[32,4096]{1,0:T(8,128)(2,1)S(1)}, u32[]{:S(2)}, u32[]{:S(2)}) collective-permute-start(bf16[32,4096]{1,0:T(8,128)(2,1)S(1)} %collective-permute-done.refs_0_), channel_id=1, source_target_pairs={{0,4},{1,5},{2,6},{3,7},{4,0},{5,1},{6,2},{7,3},{8,12},{9,13},{10,... | collective-permute-start | bytes 786440 | tf_op jit(solution)/shard_map/ppermute | solution.py:235
  25.1 8.1 %collective-permute-start.7 = (bf16[8,10368]{1,0:T(8,128)(2,1)S(1)}, bf16[8,10368]{1,0:T(8,128)(2,1)S(1)}, u32[]{:S(2)}, u32[]{:S(2)}) collective-permute-start(bf16[8,10368]{1,0:T(8,128)(2,1)S(1)} %shard_map.113.refs_0_), channel_id=1, source_target_pairs={{0,16},{16,0},{1,17},{17,1},{2,18},{18,2},{3,19},{19,3},{4,20},{20... | collective-permute-start | bytes 497672 | tf_op jit(solution)/shard_map/ppermute | solution.py:276
  27.2 3.0 %copy-start.6 = (bf16[32,4096]{1,0:T(8,128)(2,1)S(1)}, bf16[32,4096]{1,0:T(8,128)(2,1)}, u32[]{:S(2)}) copy-start(bf16[32,4096]{1,0:T(8,128)(2,1)} %refs_0_.3) | copy-start | bytes 786436
  36.5 5.7 %collective-permute-start.14 = (bf16[64,4096]{1,0:T(8,128)(2,1)S(1)}, bf16[64,4096]{1,0:T(8,128)(2,1)S(1)}, u32[]{:S(2)}, u32[]{:S(2)}) collective-permute-start(bf16[64,4096]{1,0:T(8,128)(2,1)S(1)} %get-tuple-element.100), channel_id=1, source_target_pairs={{0,1},{1,0},{2,3},{3,2},{4,5},{5,4},{6,7},{7,6},{8,9},{9,8},{10,11... | collective-permute-start | bytes 1572872 | tf_op jit(solution)/shard_map/ppermute | solution.py:235
  36.5 2.3 %collective-permute-start.15 = (bf16[32,4096]{1,0:T(8,128)(2,1)S(1)}, bf16[32,4096]{1,0:T(8,128)(2,1)S(1)}, u32[]{:S(2)}, u32[]{:S(2)}) collective-permute-start(bf16[32,4096]{1,0:T(8,128)(2,1)S(1)} %collective-permute-done.9.refs_0_), channel_id=1, source_target_pairs={{0,1},{1,0},{2,3},{3,2},{4,5},{5,4},{6,7},{7,6},{8,9},{9,8},{10,11... | collective-permute-start | bytes 786440 | tf_op jit(solution)/shard_map/ppermute | solution.py:235
  37.0 2.1 %collective-permute-start.16 = (bf16[32,4096]{1,0:T(8,128)(2,1)S(1)}, bf16[32,4096]{1,0:T(8,128)(2,1)S(1)}, u32[]{:S(2)}, u32[]{:S(2)}) collective-permute-start(bf16[32,4096]{1,0:T(8,128)(2,1)S(1)} %collective-permute-done.11.refs_1_), channel_id=1, source_target_pairs={{0,1},{1,0},{2,3},{3,2},{4,5},{5,4},{6,7},{7,6},{8,9},{9,8},{10,11... | collective-permute-start | bytes 786440 | tf_op jit(solution)/shard_map/ppermute | solution.py:235
  37.0 5.1 %collective-permute-start.13 = (bf16[32,4096]{1,0:T(8,128)(2,1)S(1)}, bf16[32,4096]{1,0:T(8,128)(2,1)S(1)}, u32[]{:S(2)}, u32[]{:S(2)}) collective-permute-start(bf16[32,4096]{1,0:T(8,128)(2,1)S(1)} %collective-permute-done.10.refs_1_), channel_id=1, source_target_pairs={{0,1},{1,0},{2,3},{3,2},{4,5},{5,4},{6,7},{7,6},{8,9},{9,8},{10,11... | collective-permute-start | bytes 786440 | tf_op jit(solution)/shard_map/ppermute | solution.py:235
  42.2 2.0 %collective-permute-start.17 = (bf16[64,4096]{1,0:T(8,128)(2,1)S(1)}, bf16[64,4096]{1,0:T(8,128)(2,1)S(1)}, u32[]{:S(2)}, u32[]{:S(2)}) collective-permute-start(bf16[64,4096]{1,0:T(8,128)(2,1)S(1)} %get-tuple-element.106), channel_id=1, source_target_pairs={{0,1},{1,0},{2,3},{3,2},{4,5},{5,4},{6,7},{7,6},{8,9},{9,8},{10,11... | collective-permute-start | bytes 1572872 | tf_op jit(solution)/shard_map/ppermute | solution.py:235
  42.5 10.1 %collective-permute-start.18 = (bf16[32,4096]{1,0:T(8,128)(2,1)S(1)}, bf16[32,4096]{1,0:T(8,128)(2,1)S(1)}, u32[]{:S(2)}, u32[]{:S(2)}) collective-permute-start(bf16[32,4096]{1,0:T(8,128)(2,1)S(1)} %get-tuple-element.112), channel_id=1, source_target_pairs={{0,4},{1,5},{2,6},{3,7},{4,0},{5,1},{6,2},{7,3},{8,12},{9,13},{10,... | collective-permute-start | bytes 786440 | tf_op jit(solution)/shard_map/ppermute | solution.py:235
  44.3 8.4 %collective-permute-start.19 = (bf16[32,4096]{1,0:T(8,128)(2,1)S(1)}, bf16[32,4096]{1,0:T(8,128)(2,1)S(1)}, u32[]{:S(2)}, u32[]{:S(2)}) collective-permute-start(bf16[32,4096]{1,0:T(8,128)(2,1)S(1)} %get-tuple-element.113), channel_id=1, source_target_pairs={{0,2},{1,3},{2,0},{3,1},{4,6},{5,7},{6,4},{7,5},{8,10},{9,11},{10,... | collective-permute-start | bytes 786440 | tf_op jit(solution)/shard_map/ppermute | solution.py:235
  46.1 6.5 %collective-permute-start.20 = (bf16[32,1024]{1,0:T(8,128)(2,1)S(1)}, bf16[32,1024]{1,0:T(8,128)(2,1)S(1)}, u32[]{:S(2)}, u32[]{:S(2)}) collective-permute-start(bf16[32,1024]{1,0:T(8,128)(2,1)S(1)} %get-tuple-element.125), channel_id=1, source_target_pairs={{0,4},{1,5},{2,6},{3,7},{4,0},{5,1},{6,2},{7,3},{8,12},{9,13},{10,... | collective-permute-start | bytes 196616 | tf_op jit(solution)/shard_map/ppermute | solution.py:235
  52.7 1.9 %collective-permute-start.22 = (bf16[64,4096]{1,0:T(8,128)(2,1)S(1)}, bf16[64,4096]{1,0:T(8,128)(2,1)S(1)}, u32[]{:S(2)}, u32[]{:S(2)}) collective-permute-start(bf16[64,4096]{1,0:T(8,128)(2,1)S(1)} %get-tuple-element.131), channel_id=1, source_target_pairs={{0,1},{1,0},{2,3},{3,2},{4,5},{5,4},{6,7},{7,6},{8,9},{9,8},{10,11... | collective-permute-start | bytes 1572872 | tf_op jit(solution)/shard_map/ppermute | solution.py:235
  52.7 10.3 %collective-permute-start.24 = (bf16[64,4096]{1,0:T(8,128)(2,1)S(1)}, bf16[64,4096]{1,0:T(8,128)(2,1)S(1)}, u32[]{:S(2)}, u32[]{:S(2)}) collective-permute-start(bf16[64,4096]{1,0:T(8,128)(2,1)S(1)} %get-tuple-element.136), channel_id=1, source_target_pairs={{0,1},{1,0},{2,3},{3,2},{4,5},{5,4},{6,7},{7,6},{8,9},{9,8},{10,11... | collective-permute-start | bytes 1572872 | tf_op jit(solution)/shard_map/ppermute | solution.py:235
  53.3 9.7 %collective-permute-start.21 = (bf16[32,4096]{1,0:T(8,128)(2,1)S(1)}, bf16[32,4096]{1,0:T(8,128)(2,1)S(1)}, u32[]{:S(2)}, u32[]{:S(2)}) collective-permute-start(bf16[32,4096]{1,0:T(8,128)(2,1)S(1)} %add_convert_fusion.1), channel_id=1, source_target_pairs={{0,4},{1,5},{2,6},{3,7},{4,0},{5,1},{6,2},{7,3},{8,12},{9,13},{10,... | collective-permute-start | bytes 786440 | tf_op jit(solution)/shard_map/ppermute | solution.py:235
  54.7 8.4 %collective-permute-start.23 = (bf16[32,4096]{1,0:T(8,128)(2,1)S(1)}, bf16[32,4096]{1,0:T(8,128)(2,1)S(1)}, u32[]{:S(2)}, u32[]{:S(2)}) collective-permute-start(bf16[32,4096]{1,0:T(8,128)(2,1)S(1)} %get-tuple-element.135), channel_id=1, source_target_pairs={{0,2},{1,3},{2,0},{3,1},{4,6},{5,7},{6,4},{7,5},{8,10},{9,11},{10,... | collective-permute-start | bytes 786440 | tf_op jit(solution)/shard_map/ppermute | solution.py:235
  56.5 6.4 %collective-permute-start.25 = (bf16[32,1024]{1,0:T(8,128)(2,1)S(1)}, bf16[32,1024]{1,0:T(8,128)(2,1)S(1)}, u32[]{:S(2)}, u32[]{:S(2)}) collective-permute-start(bf16[32,1024]{1,0:T(8,128)(2,1)S(1)} %get-tuple-element.141), channel_id=1, source_target_pairs={{0,4},{1,5},{2,6},{3,7},{4,0},{5,1},{6,2},{7,3},{8,12},{9,13},{10,... | collective-permute-start | bytes 196616 | tf_op jit(solution)/shard_map/ppermute | solution.py:235
  63.2 14.1 %collective-permute-start.26 = (bf16[32,4096]{1,0:T(8,128)(2,1)S(1)}, bf16[32,4096]{1,0:T(8,128)(2,1)S(1)}, u32[]{:S(2)}, u32[]{:S(2)}) collective-permute-start(bf16[32,4096]{1,0:T(8,128)(2,1)S(1)} %add_convert_fusion), channel_id=1, source_target_pairs={{0,8},{1,9},{2,10},{3,11},{4,12},{5,13},{6,14},{7,15},{8,0},{9,1},... | collective-permute-start | bytes 786440 | tf_op jit(solution)/shard_map/ppermute | solution.py:235
  65.5 11.8 %collective-permute-start.28 = (bf16[32,4096]{1,0:T(8,128)(2,1)S(1)}, bf16[32,4096]{1,0:T(8,128)(2,1)S(1)}, u32[]{:S(2)}, u32[]{:S(2)}) collective-permute-start(bf16[32,4096]{1,0:T(8,128)(2,1)S(1)} %fusion), channel_id=1, source_target_pairs={{0,2},{1,3},{2,0},{3,1},{4,6},{5,7},{6,4},{7,5},{8,10},{9,11},{10,... | collective-permute-start | bytes 786440 | tf_op jit(solution)/shard_map/ppermute | solution.py:235
  67.2 8.7 %collective-permute-start.27 = (bf16[32,2048]{1,0:T(8,128)(2,1)S(1)}, bf16[32,2048]{1,0:T(8,128)(2,1)S(1)}, u32[]{:S(2)}, u32[]{:S(2)}) collective-permute-start(bf16[32,2048]{1,0:T(8,128)(2,1)S(1)} %get-tuple-element.148), channel_id=1, source_target_pairs={{0,4},{1,5},{2,6},{3,7},{4,0},{5,1},{6,2},{7,3},{8,12},{9,13},{10,... | collective-permute-start | bytes 393224 | tf_op jit(solution)/shard_map/ppermute | solution.py:235
